TPU v7x, 32 devices: a whole 2x2x4 slice. The times are simulated.
32 devices in a mesh: dp: 8 (over z, y), fsdp: 4 (over x, core).
Axes of the slice: x: 2, y: 2, z: 4, core: 2. Of those that a mesh axis runs over, the one named last changes fastest.
Arguments:
- block_input: bfloat16 [64, 128, 1536], P(('dp', 'fsdp')), may hold values from -6 to 6
- caption: bfloat16 [64, 256, 4096], P(('dp', 'fsdp')), may hold values from -6 to 6
- modulation: float32 [64, 4, 1536], P(('dp', 'fsdp')), may hold values from -2.5 to 2.5
- segment_ids: int32 [64, 128], P(('dp', 'fsdp')), may hold values from 0 to 127, as said below
- pos_row: int32 [64, 128], P(('dp', 'fsdp')), may hold values from 0 to 63
- pos_col: int32 [64, 128], P(('dp', 'fsdp')), may hold values from 0 to 10
- caption_len: int32 [64], P(('dp', 'fsdp')), may hold values from 64 to 256, as said below
- gain_attn: bfloat16 [1536], P('fsdp'), may hold values from 0.25 to 1.75
- w_query: bfloat16 [1536, 1536], P('fsdp'), may hold values from -0.15625 to 0.15625
- w_key: bfloat16 [1536, 1536], P('fsdp'), may hold values from -0.15625 to 0.15625
- w_value: bfloat16 [1536, 1536], P('fsdp'), may hold values from -0.15625 to 0.15625
- gain_query: bfloat16 [64], P('fsdp'), may hold values from 0.25 to 1.75
- gain_key: bfloat16 [64], P('fsdp'), may hold values from 0.25 to 1.75
- w_cap_key: bfloat16 [4096, 1536], P('fsdp'), may hold values from -0.09375 to 0.09375
- w_cap_value: bfloat16 [4096, 1536], P('fsdp'), may hold values from -0.09375 to 0.09375
- gain_cap_key: bfloat16 [64], P('fsdp'), may hold values from 0.25 to 1.75
- head_gate: bfloat16 [24], P('fsdp'), may hold values from -3 to 3
- w_out: bfloat16 [1536, 1536], P('fsdp'), may hold values from -0.625 to 0.625
- gain_ffn: bfloat16 [1536], P('fsdp'), may hold values from 0.25 to 1.75
- w_gate: bfloat16 [1536, 4096], P('fsdp'), may hold values from -0.15625 to 0.15625
- w_up: bfloat16 [1536, 4096], P('fsdp'), may hold values from -0.15625 to 0.15625
- w_down: bfloat16 [4096, 1536], P('fsdp'), may hold values from -0.09375 to 0.09375
- cotangent: bfloat16 [64, 128, 1536], P(('dp', 'fsdp')), may hold values from -6 to 6
Outputs:
- block_out: bfloat16 [64, 128, 1536], P(('dp', 'fsdp'))
- input_grad: bfloat16 [64, 128, 1536], P(('dp', 'fsdp'))
- modulation_grad: float32 [64, 4, 1536], P(('dp', 'fsdp'))
- grad_gain_attn: float32 [1536], P('fsdp')
- grad_w_query: float32 [1536, 1536], P('fsdp', 'dp')
- grad_w_key: float32 [1536, 1536], P('fsdp', 'dp')
- grad_w_value: float32 [1536, 1536], P('fsdp', 'dp')
- grad_gain_query: float32 [64], P('fsdp')
- grad_gain_key: float32 [64], P('fsdp')
- grad_w_cap_key: float32 [4096, 1536], P('fsdp', 'dp')
- grad_w_cap_value: float32 [4096, 1536], P('fsdp', 'dp')
- grad_gain_cap_key: float32 [64], P('fsdp')
- grad_head_gate: float32 [24], P('fsdp')
- grad_w_out: float32 [1536, 1536], P('fsdp', 'dp')
- grad_gain_ffn: float32 [1536], P('fsdp')
- grad_w_gate: float32 [1536, 4096], P('fsdp', 'dp')
- grad_w_up: float32 [1536, 4096], P('fsdp', 'dp')
- grad_w_down: float32 [4096, 1536], P('fsdp', 'dp')
Inputs may be any that keep to these rules, and one draw needn't show every extreme that they name: `segment_ids`: within a row the ids start at 0 and rise by at most one from token to token; each image, a run of equal ids, lays its tokens out in raster order on a grid 2 to 11 columns wide, which pos_row and pos_col give. Caption positions from caption_len on are padding.
All inputs are finite; a program needn't handle non-finite values.
Results may differ from a plain program's by a relative error of at most 0.018.
Values may be sent and summed in bfloat16 or wider, within the bound.
No kernel may reach another device: no remote copies, remote signals or barrier semaphores. Data moves between devices by JAX's collectives and lax.ppermute only.
A program may use at most 384 MiB of HBM per device.

v0:
```python
import math

import jax
import jax.numpy as jnp
from jax import lax
from jax.sharding import PartitionSpec as P

EPSILON = 1e-06
NEGATIVE = -1e30


def angle_tables(rows_pos, cols_pos, head_size):
    quarter = head_size // 4
    frequency = jnp.exp(jnp.arange(quarter, dtype=jnp.float32) * (-math.log(10000.0) / quarter))
    row_angle = rows_pos.astype(jnp.float32)[..., None] * frequency
    col_angle = cols_pos.astype(jnp.float32)[..., None] * frequency
    angles = jnp.concatenate([row_angle, row_angle, col_angle, col_angle], axis=-1)[:, :, None, :]
    return (jnp.cos(angles), jnp.sin(angles))


def quarter_turn(values):
    shaped = values.reshape(values.shape[:-1] + (2, 2, values.shape[-1] // 4))
    turned = jnp.stack([-shaped[..., 1, :], shaped[..., 0, :]], axis=-2)
    return turned.reshape(values.shape)


def rms_scale(values):
    inverse = lax.rsqrt(jnp.mean(values * values, axis=-1, keepdims=True) + EPSILON)
    return (values * inverse, inverse)


def rms_back(incoming, normed, inverse):
    return inverse * (incoming - normed * jnp.mean(incoming * normed, axis=-1, keepdims=True))


def product(operand, weight_matrix):
    return jnp.einsum("...c,ce->...e", operand, weight_matrix, preferred_element_type=jnp.float32)


def product_back(incoming, weight_matrix):
    return jnp.einsum("...e,ce->...c", incoming, weight_matrix, preferred_element_type=jnp.float32)


def outer_sum(operand, incoming):
    return jnp.einsum("rsc,rse->ce", operand, incoming, preferred_element_type=jnp.float32)


def head_norm(projected, gain_vec, head_size):
    per_head = projected.reshape(
        projected.shape[:-1] + (projected.shape[-1] // head_size, head_size)
    )
    normed, inverse = rms_scale(per_head)
    return (normed * gain_vec, normed, inverse)


def head_norm_back(incoming, normed, inverse, gain_vec):
    grad_gain = jnp.sum(incoming * normed, axis=(0, 1, 2))
    grad_projected = rms_back(incoming * gain_vec, normed, inverse)
    return (
        grad_gain,
        grad_projected.reshape(grad_projected.shape[:2] + (-1,)).astype(jnp.bfloat16),
    )


def attend_weights(queries, keys, allowed, scaling):
    scores = (
        jnp.einsum("rqhd,rkhd->rhqk", queries, keys, preferred_element_type=jnp.float32) * scaling
    )
    return jax.nn.softmax(jnp.where(allowed, scores, NEGATIVE), axis=-1)


def attend_back(weights, grad_output, values, queries, keys, scaling):
    grad_weights = jnp.einsum(
        "rqhd,rkhd->rhqk", grad_output, values, preferred_element_type=jnp.float32
    )
    centre = jnp.sum(grad_weights * weights, axis=-1, keepdims=True)
    grad_scores = (weights * (grad_weights - centre)).astype(jnp.bfloat16)
    grad_values = jnp.einsum(
        "rhqk,rqhd->rkhd",
        weights.astype(jnp.bfloat16),
        grad_output,
        preferred_element_type=jnp.float32,
    ).astype(jnp.bfloat16)
    grad_queries = (
        jnp.einsum("rhqk,rkhd->rqhd", grad_scores, keys, preferred_element_type=jnp.float32)
        * scaling
    )
    grad_keys = (
        jnp.einsum("rhqk,rqhd->rkhd", grad_scores, queries, preferred_element_type=jnp.float32)
        * scaling
    )
    return (grad_queries, grad_keys, grad_values)


def unrotate(incoming, cos_table, sin_table):
    return incoming * cos_table - quarter_turn(incoming * sin_table)


def shards(
    block_input,
    caption,
    modulation,
    segment_ids,
    pos_row,
    pos_col,
    caption_len,
    gain_attn,
    w_query,
    w_key,
    w_value,
    gain_query,
    gain_key,
    w_cap_key,
    w_cap_value,
    gain_cap_key,
    head_gate,
    w_out,
    gain_ffn,
    w_gate,
    w_up,
    w_down,
    cotangent,
):
    attn_full = (
        lax.all_gather(gain_attn, "fsdp", axis=0, tiled=True),
        lax.all_gather(w_query, "fsdp", axis=0, tiled=True),
        lax.all_gather(w_key, "fsdp", axis=0, tiled=True),
        lax.all_gather(w_value, "fsdp", axis=0, tiled=True),
        lax.all_gather(gain_query, "fsdp", axis=0, tiled=True),
        lax.all_gather(gain_key, "fsdp", axis=0, tiled=True),
        lax.all_gather(w_cap_key, "fsdp", axis=0, tiled=True),
        lax.all_gather(w_cap_value, "fsdp", axis=0, tiled=True),
        lax.all_gather(gain_cap_key, "fsdp", axis=0, tiled=True),
        lax.all_gather(head_gate, "fsdp", axis=0, tiled=True),
        lax.all_gather(w_out, "fsdp", axis=0, tiled=True),
    )
    (
        full_gain_attn,
        full_query,
        full_key,
        full_value,
        full_gain_query,
        full_gain_key,
        full_cap_key,
        full_cap_value,
        full_gain_cap,
        full_head_gate,
        full_out,
    ) = attn_full
    inputs = block_input.astype(jnp.float32)
    head_size = full_gain_query.shape[0]
    scaling = 1.0 / math.sqrt(head_size)
    cos_table, sin_table = angle_tables(pos_row, pos_col, head_size)
    same_segment = (segment_ids[:, :, None] == segment_ids[:, None, :])[:, None, :, :]
    cap_positions = jnp.arange(caption.shape[1], dtype=jnp.int32)
    caption_mask = (cap_positions[None, :] < caption_len[:, None])[:, None, None, :]
    scale_attn = 1.0 + modulation[:, 0][:, None, :]
    tanh_attn = jnp.tanh(modulation[:, 1])[:, None, :]
    scale_ffn = 1.0 + modulation[:, 2][:, None, :]
    tanh_ffn = jnp.tanh(modulation[:, 3])[:, None, :]
    normed_in, inverse_in = rms_scale(inputs)
    attn_in = (normed_in * full_gain_attn.astype(jnp.float32) * scale_attn).astype(jnp.bfloat16)
    query_raw = product(attn_in, full_query)
    key_raw = product(attn_in, full_key)
    value_heads = product(attn_in, full_value).astype(jnp.bfloat16)
    value_heads = value_heads.reshape(value_heads.shape[:2] + (-1, head_size))
    query_gain = full_gain_query.astype(jnp.float32)
    key_gain = full_gain_key.astype(jnp.float32)
    cap_gain = full_gain_cap.astype(jnp.float32)
    query_scaled, query_normed, query_inverse = head_norm(query_raw, query_gain, head_size)
    queries = (query_scaled * cos_table + quarter_turn(query_scaled) * sin_table).astype(
        jnp.bfloat16
    )
    key_scaled, key_normed, key_inverse = head_norm(key_raw, key_gain, head_size)
    keys = (key_scaled * cos_table + quarter_turn(key_scaled) * sin_table).astype(jnp.bfloat16)
    cap_key_raw = product(caption, full_cap_key)
    cap_scaled, cap_normed, cap_inverse = head_norm(cap_key_raw, cap_gain, head_size)
    cap_keys = cap_scaled.astype(jnp.bfloat16)
    cap_values = product(caption, full_cap_value).astype(jnp.bfloat16)
    cap_values = cap_values.reshape(cap_values.shape[:2] + (-1, head_size))
    self_weights = attend_weights(queries, keys, same_segment, scaling)
    self_out = jnp.einsum(
        "rhqk,rkhd->rqhd",
        self_weights.astype(jnp.bfloat16),
        value_heads,
        preferred_element_type=jnp.float32,
    )
    cross_weights = attend_weights(queries, cap_keys, caption_mask, scaling)
    cross_out = jnp.einsum(
        "rhqk,rkhd->rqhd",
        cross_weights.astype(jnp.bfloat16),
        cap_values,
        preferred_element_type=jnp.float32,
    )
    head_tanh = jnp.tanh(full_head_gate.astype(jnp.float32))[:, None]
    mixed = (self_out + head_tanh * cross_out).astype(jnp.bfloat16)
    mixed = mixed.reshape(mixed.shape[:2] + (-1,))
    attn_branch = product(mixed, full_out)
    hidden = inputs + tanh_attn * attn_branch
    ffn_full = (
        lax.all_gather(gain_ffn, "fsdp", axis=0, tiled=True),
        lax.all_gather(w_gate, "fsdp", axis=0, tiled=True),
        lax.all_gather(w_up, "fsdp", axis=0, tiled=True),
        lax.all_gather(w_down, "fsdp", axis=0, tiled=True),
    )
    normed_mid, inverse_mid = rms_scale(hidden)
    ffn_in = (normed_mid * ffn_full[0].astype(jnp.float32) * scale_ffn).astype(jnp.bfloat16)
    gate_proj = product(ffn_in, ffn_full[1])
    up_proj = product(ffn_in, ffn_full[2])
    activated = (jax.nn.silu(gate_proj) * up_proj).astype(jnp.bfloat16)
    ffn_branch = product(activated, ffn_full[3])
    block_out = (hidden + tanh_ffn * ffn_branch).astype(jnp.bfloat16)
    ffn_back = (
        lax.all_gather(gain_ffn, "fsdp", axis=0, tiled=True),
        lax.all_gather(w_gate, "fsdp", axis=0, tiled=True),
        lax.all_gather(w_up, "fsdp", axis=0, tiled=True),
        lax.all_gather(w_down, "fsdp", axis=0, tiled=True),
    )
    upstream = cotangent.astype(jnp.float32)
    grad_ffn_branch = (upstream * tanh_ffn).astype(jnp.bfloat16)
    grad_mod_ffn_gate = jnp.sum(upstream * ffn_branch, axis=1) * (
        1.0 - tanh_ffn[:, 0] * tanh_ffn[:, 0]
    )
    gate_again = product(ffn_in, ffn_back[1])
    up_again = product(ffn_in, ffn_back[2])
    sigmoid_gate = jax.nn.sigmoid(gate_again)
    silu_gate = gate_again * sigmoid_gate
    activated_again = (silu_gate * up_again).astype(jnp.bfloat16)
    grad_down_w = outer_sum(activated_again, grad_ffn_branch)
    grad_act = product_back(grad_ffn_branch, ffn_back[3])
    grad_gate = (
        grad_act * up_again * sigmoid_gate * (1.0 + gate_again * (1.0 - sigmoid_gate))
    ).astype(jnp.bfloat16)
    grad_up = (grad_act * silu_gate).astype(jnp.bfloat16)
    grad_gate_w = outer_sum(ffn_in, grad_gate)
    grad_up_w = outer_sum(ffn_in, grad_up)
    grad_ffn_in = product_back(grad_gate, ffn_back[1]) + product_back(grad_up, ffn_back[2])
    ffn_gain_back = ffn_back[0].astype(jnp.float32)
    grad_ffn_gain = jnp.sum(grad_ffn_in * normed_mid * scale_ffn, axis=(0, 1))
    grad_mod_ffn_scale = jnp.sum(grad_ffn_in * normed_mid * ffn_gain_back, axis=1)
    grad_hidden = upstream + rms_back(
        grad_ffn_in * ffn_gain_back * scale_ffn, normed_mid, inverse_mid
    )
    ffn_parts = (
        lax.psum_scatter(
            grad_ffn_gain.astype(jnp.bfloat16), "fsdp", scatter_dimension=0, tiled=True
        ).astype(jnp.float32),
        lax.psum_scatter(
            grad_gate_w.astype(jnp.bfloat16), "fsdp", scatter_dimension=0, tiled=True
        ).astype(jnp.float32),
        lax.psum_scatter(
            grad_up_w.astype(jnp.bfloat16), "fsdp", scatter_dimension=0, tiled=True
        ).astype(jnp.float32),
        lax.psum_scatter(
            grad_down_w.astype(jnp.bfloat16), "fsdp", scatter_dimension=0, tiled=True
        ).astype(jnp.float32),
    )
    attn_back = (
        lax.all_gather(gain_attn, "fsdp", axis=0, tiled=True),
        lax.all_gather(w_query, "fsdp", axis=0, tiled=True),
        lax.all_gather(w_key, "fsdp", axis=0, tiled=True),
        lax.all_gather(w_value, "fsdp", axis=0, tiled=True),
        lax.all_gather(gain_query, "fsdp", axis=0, tiled=True),
        lax.all_gather(gain_key, "fsdp", axis=0, tiled=True),
        lax.all_gather(w_cap_key, "fsdp", axis=0, tiled=True),
        lax.all_gather(w_cap_value, "fsdp", axis=0, tiled=True),
        lax.all_gather(gain_cap_key, "fsdp", axis=0, tiled=True),
        lax.all_gather(head_gate, "fsdp", axis=0, tiled=True),
        lax.all_gather(w_out, "fsdp", axis=0, tiled=True),
    )
    (
        back_gain_attn,
        back_query,
        back_key,
        back_value,
        back_gain_query,
        back_gain_key,
        back_cap_key,
        back_cap_value,
        back_gain_cap,
        back_head_gate,
        back_out,
    ) = attn_back
    grad_attn_branch = (grad_hidden * tanh_attn).astype(jnp.bfloat16)
    grad_mod_attn_gate = jnp.sum(grad_hidden * attn_branch, axis=1) * (
        1.0 - tanh_attn[:, 0] * tanh_attn[:, 0]
    )
    grad_out_w = outer_sum(mixed, grad_attn_branch)
    grad_mixed = product_back(grad_attn_branch, back_out).astype(jnp.bfloat16)
    grad_mixed = grad_mixed.reshape(grad_mixed.shape[:2] + (-1, head_size))
    grad_mixed_float = grad_mixed.astype(jnp.float32)
    back_tanh = jnp.tanh(back_head_gate.astype(jnp.float32))[:, None]
    grad_gate_heads = jnp.sum(grad_mixed_float * cross_out, axis=(0, 1, 3)) * (
        1.0 - back_tanh[:, 0] * back_tanh[:, 0]
    )
    grad_cross = (back_tanh * grad_mixed_float).astype(jnp.bfloat16)
    self_again = attend_weights(queries, keys, same_segment, scaling)
    cross_again = attend_weights(queries, cap_keys, caption_mask, scaling)
    grad_q_self, grad_keys_turned, grad_values = attend_back(
        self_again, grad_mixed, value_heads, queries, keys, scaling
    )
    grad_q_cross, grad_cap_keys, grad_cap_values = attend_back(
        cross_again, grad_cross, cap_values, queries, cap_keys, scaling
    )
    grad_queries = unrotate(grad_q_self + grad_q_cross, cos_table, sin_table)
    grad_keys_plain = unrotate(grad_keys_turned, cos_table, sin_table)
    grad_query_gain, grad_query_raw = head_norm_back(
        grad_queries, query_normed, query_inverse, back_gain_query.astype(jnp.float32)
    )
    grad_key_gain, grad_key_raw = head_norm_back(
        grad_keys_plain, key_normed, key_inverse, back_gain_key.astype(jnp.float32)
    )
    grad_cap_gain, grad_cap_raw = head_norm_back(
        grad_cap_keys, cap_normed, cap_inverse, back_gain_cap.astype(jnp.float32)
    )
    grad_values_flat = grad_values.reshape(grad_values.shape[:2] + (-1,))
    grad_cap_values_flat = grad_cap_values.reshape(grad_cap_values.shape[:2] + (-1,))
    grad_query_w = outer_sum(attn_in, grad_query_raw)
    grad_key_w = outer_sum(attn_in, grad_key_raw)
    grad_value_w = outer_sum(attn_in, grad_values_flat)
    grad_cap_key_w = outer_sum(caption, grad_cap_raw)
    grad_cap_value_w = outer_sum(caption, grad_cap_values_flat)
    grad_attn_in = (
        product_back(grad_query_raw, back_query)
        + product_back(grad_key_raw, back_key)
        + product_back(grad_values_flat, back_value)
    )
    back_gain_in = back_gain_attn.astype(jnp.float32)
    grad_gain_in = jnp.sum(grad_attn_in * normed_in * scale_attn, axis=(0, 1))
    grad_mod_attn_scale = jnp.sum(grad_attn_in * normed_in * back_gain_in, axis=1)
    input_grad = (
        grad_hidden + rms_back(grad_attn_in * back_gain_in * scale_attn, normed_in, inverse_in)
    ).astype(jnp.bfloat16)
    modulation_grad = jnp.stack(
        [grad_mod_attn_scale, grad_mod_attn_gate, grad_mod_ffn_scale, grad_mod_ffn_gate], axis=1
    )
    attn_parts = (
        lax.psum_scatter(
            grad_gain_in.astype(jnp.bfloat16), "fsdp", scatter_dimension=0, tiled=True
        ).astype(jnp.float32),
        lax.psum_scatter(
            grad_query_w.astype(jnp.bfloat16), "fsdp", scatter_dimension=0, tiled=True
        ).astype(jnp.float32),
        lax.psum_scatter(
            grad_key_w.astype(jnp.bfloat16), "fsdp", scatter_dimension=0, tiled=True
        ).astype(jnp.float32),
        lax.psum_scatter(
            grad_value_w.astype(jnp.bfloat16), "fsdp", scatter_dimension=0, tiled=True
        ).astype(jnp.float32),
        lax.psum_scatter(
            grad_query_gain.astype(jnp.bfloat16), "fsdp", scatter_dimension=0, tiled=True
        ).astype(jnp.float32),
        lax.psum_scatter(
            grad_key_gain.astype(jnp.bfloat16), "fsdp", scatter_dimension=0, tiled=True
        ).astype(jnp.float32),
        lax.psum_scatter(
            grad_cap_key_w.astype(jnp.bfloat16), "fsdp", scatter_dimension=0, tiled=True
        ).astype(jnp.float32),
        lax.psum_scatter(
            grad_cap_value_w.astype(jnp.bfloat16), "fsdp", scatter_dimension=0, tiled=True
        ).astype(jnp.float32),
        lax.psum_scatter(
            grad_cap_gain.astype(jnp.bfloat16), "fsdp", scatter_dimension=0, tiled=True
        ).astype(jnp.float32),
        lax.psum_scatter(
            grad_gate_heads.astype(jnp.bfloat16), "fsdp", scatter_dimension=0, tiled=True
        ).astype(jnp.float32),
        lax.psum_scatter(
            grad_out_w.astype(jnp.bfloat16), "fsdp", scatter_dimension=0, tiled=True
        ).astype(jnp.float32),
    )
    matrices = (
        lax.psum_scatter(attn_parts[1], "dp", scatter_dimension=1, tiled=True),
        lax.psum_scatter(attn_parts[2], "dp", scatter_dimension=1, tiled=True),
        lax.psum_scatter(attn_parts[3], "dp", scatter_dimension=1, tiled=True),
        lax.psum_scatter(attn_parts[6], "dp", scatter_dimension=1, tiled=True),
        lax.psum_scatter(attn_parts[7], "dp", scatter_dimension=1, tiled=True),
        lax.psum_scatter(attn_parts[10], "dp", scatter_dimension=1, tiled=True),
        lax.psum_scatter(ffn_parts[1], "dp", scatter_dimension=1, tiled=True),
        lax.psum_scatter(ffn_parts[2], "dp", scatter_dimension=1, tiled=True),
        lax.psum_scatter(ffn_parts[3], "dp", scatter_dimension=1, tiled=True),
    )
    gains = lax.psum(
        (attn_parts[0], attn_parts[4], attn_parts[5], attn_parts[8], attn_parts[9], ffn_parts[0]),
        "dp",
    )
    return (
        block_out,
        input_grad,
        modulation_grad,
        gains[0],
        matrices[0],
        matrices[1],
        matrices[2],
        gains[1],
        gains[2],
        matrices[3],
        matrices[4],
        gains[3],
        gains[4],
        matrices[5],
        gains[5],
        matrices[6],
        matrices[7],
        matrices[8],
    )


def solution(mesh):
    return jax.shard_map(
        shards,
        mesh=mesh,
        in_specs=(
            P(("dp", "fsdp"), None, None),
            P(("dp", "fsdp"), None, None),
            P(("dp", "fsdp"), None, None),
            P(("dp", "fsdp"), None),
            P(("dp", "fsdp"), None),
            P(("dp", "fsdp"), None),
            P(("dp", "fsdp")),
            P("fsdp"),
            P("fsdp", None),
            P("fsdp", None),
            P("fsdp", None),
            P("fsdp"),
            P("fsdp"),
            P("fsdp", None),
            P("fsdp", None),
            P("fsdp"),
            P("fsdp"),
            P("fsdp", None),
            P("fsdp"),
            P("fsdp", None),
            P("fsdp", None),
            P("fsdp", None),
            P(("dp", "fsdp"), None, None),
        ),
        out_specs=(
            P(("dp", "fsdp"), None, None),
            P(("dp", "fsdp"), None, None),
            P(("dp", "fsdp"), None, None),
            P("fsdp"),
            P("fsdp", "dp"),
            P("fsdp", "dp"),
            P("fsdp", "dp"),
            P("fsdp"),
            P("fsdp"),
            P("fsdp", "dp"),
            P("fsdp", "dp"),
            P("fsdp"),
            P("fsdp"),
            P("fsdp", "dp"),
            P("fsdp"),
            P("fsdp", "dp"),
            P("fsdp", "dp"),
            P("fsdp", "dp"),
        ),
        check_vma=False,
    )
```

profile of v0, /device:TPU:0, one launch (start us, length us, event | category | flops | bytes accessed | tf_op | source)
XLA Modules:
  0.0 2274.2 jit_solution(742960472135385495)
XLA Ops:
  16.5 8.5 all-reduce.12
  40.8 9.1 all-gather.12.cloned.1.call-done
  54.9 34.1 %all-gather.16.cloned.1.call-done = bf16[1536,1536]{1,0:T(8,128)(2,1)} async-done(((bf16[384,1536]{1,0:T(8,128)(2,1)}), bf16[1536,1536]{1,0:T(8,128)(2,1)}) %all-gather.16.cloned.1.call-update) | async-done | bytes 4718608 | tf_op jit(solution)/shard_map/all_gather | solution.py:127
  95.3 32.8 %all-gather.14.cloned.1.call-done = bf16[1536,1536]{1,0:T(8,128)(2,1)} async-done(((bf16[384,1536]{1,0:T(8,128)(2,1)}), bf16[1536,1536]{1,0:T(8,128)(2,1)}) %all-gather.14.cloned.1.call-update) | async-done | bytes 4718608 | tf_op jit(solution)/shard_map/all_gather | solution.py:126
  138.2 73.4 %all-gather.18.cloned.1.call-done = bf16[4096,1536]{1,0:T(8,128)(2,1)} async-done(((bf16[1024,1536]{1,0:T(8,128)(2,1)}), bf16[4096,1536]{1,0:T(8,128)(2,1)}) %all-gather.18.cloned.1.call-update) | async-done | bytes 12582928 | tf_op jit(solution)/shard_map/all_gather | solution.py:132
  211.7 10.9 fusion.45
  224.1 71.0 %all-gather.20.cloned.1.call-done = bf16[4096,1536]{1,0:T(8,128)(2,1)} async-done(((bf16[1024,1536]{1,0:T(8,128)(2,1)}), bf16[4096,1536]{1,0:T(8,128)(2,1)}) %all-gather.20.cloned.1.call-update) | async-done | bytes 12582928 | tf_op jit(solution)/shard_map/all_gather | solution.py:131
  295.2 11.1 fusion.16
  307.0 6.2 fusion.121
  320.6 13.5 all-gather.22.cloned.1.call-done
  334.1 5.4 multiply_reduce_fusion.13
  341.8 76.0 %all-gather.28.cloned.1.call-done = bf16[4096,1536]{1,0:T(8,128)(2,1)} async-done(((bf16[1024,1536]{1,0:T(8,128)(2,1)}), bf16[4096,1536]{1,0:T(8,128)(2,1)}) %all-gather.28.cloned.1.call-update) | async-done | bytes 12582928 | tf_op jit(solution)/shard_map/all_gather | solution.py:204
  417.8 10.4 fusion.4
  428.2 73.3 %all-gather.26.cloned.1.call-done = bf16[1536,4096]{1,0:T(8,128)(2,1)} async-done(((bf16[384,4096]{1,0:T(8,128)(2,1)}), bf16[1536,4096]{1,0:T(8,128)(2,1)}) %all-gather.26.cloned.1.call-update) | async-done | bytes 12582928 | tf_op jit(solution)/shard_map/all_gather | solution.py:203
  501.5 10.4 fusion.10
  511.9 73.3 %all-gather.24.cloned.1.call-done = bf16[1536,4096]{1,0:T(8,128)(2,1)} async-done(((bf16[384,4096]{1,0:T(8,128)(2,1)}), bf16[1536,4096]{1,0:T(8,128)(2,1)}) %all-gather.24.cloned.1.call-update) | async-done | bytes 12582928 | tf_op jit(solution)/shard_map/all_gather | solution.py:202
  585.2 14.0 multiply_convert_fusion.2
  599.2 9.2 fusion.8
  608.4 10.8 multiply_reduce_fusion.3
  619.3 11.2 fusion.79
  688.3 9.6 fusion.2
  703.2 9.6 fusion.3
  713.9 9.3 bitcast_convert_fusion.2
  723.4 8.1 bitcast_convert_fusion.1
  733.2 7.6 bitcast_convert_fusion
  743.7 18.1 reduce-scatter.31.cloned.1.call-done
  764.7 47.5 %reduce-scatter.33.cloned.1.call-done = bf16[384,1536]{1,0:T(8,128)(2,1)} async-done(((bf16[1536,1536]{1,0:T(8,128)(2,1)}), bf16[384,1536]{1,0:T(8,128)(2,1)}) %reduce-scatter.33.cloned.1.call-update) | async-done | bytes 1179664 | tf_op jit(solution)/shard_map/reduce_scatter | solution.py:347
  815.0 47.8 %reduce-scatter.43.cloned.1.call-done = bf16[384,1536]{1,0:T(8,128)(2,1)} async-done(((bf16[1536,1536]{1,0:T(8,128)(2,1)}), bf16[384,1536]{1,0:T(8,128)(2,1)}) %reduce-scatter.43.cloned.1.call-update) | async-done | bytes 1179664 | tf_op jit(solution)/shard_map/reduce_scatter | solution.py:368
  865.6 98.7 %reduce-scatter.35.cloned.1.call-done = bf16[1024,1536]{0,1:T(8,128)(2,1)} async-done(((bf16[4096,1536]{0,1:T(8,128)(2,1)}), bf16[1024,1536]{0,1:T(8,128)(2,1)}) %reduce-scatter.35.cloned.1.call-update) | async-done | bytes 3145744 | tf_op jit(solution)/shard_map/reduce_scatter | solution.py:356
  964.3 5.3 convert_element_type.285
  969.7 96.1 %reduce-scatter.39.cloned.1.call-done = bf16[1024,1536]{0,1:T(8,128)(2,1)} async-done(((bf16[4096,1536]{0,1:T(8,128)(2,1)}), bf16[1024,1536]{0,1:T(8,128)(2,1)}) %reduce-scatter.39.cloned.1.call-update) | async-done | bytes 3145744 | tf_op jit(solution)/shard_map/reduce_scatter | solution.py:359
  1065.8 5.4 convert_element_type.290
  1071.2 96.1 %reduce-scatter.45.cloned.1.call-done = bf16[384,4096]{1,0:T(8,128)(2,1)} async-done(((bf16[1536,4096]{1,0:T(8,128)(2,1)}), bf16[384,4096]{1,0:T(8,128)(2,1)}) %reduce-scatter.45.cloned.1.call-update) | async-done | bytes 3145744 | tf_op jit(solution)/shard_map/reduce_scatter | solution.py:248
  1167.3 5.3 convert_element_type.300
  1172.7 96.1 %reduce-scatter.49.cloned.1.call-done = bf16[384,4096]{1,0:T(8,128)(2,1)} async-done(((bf16[1536,4096]{1,0:T(8,128)(2,1)}), bf16[384,4096]{1,0:T(8,128)(2,1)}) %reduce-scatter.49.cloned.1.call-update) | async-done | bytes 3145744 | tf_op jit(solution)/shard_map/reduce_scatter | solution.py:251
  1274.4 95.9 %reduce-scatter.53.cloned.1.call-done = bf16[1024,1536]{1,0:T(8,128)(2,1)} async-done(((bf16[4096,1536]{1,0:T(8,128)(2,1)}), bf16[1024,1536]{1,0:T(8,128)(2,1)}) %reduce-scatter.53.cloned.1.call-update) | async-done | bytes 3145744 | tf_op jit(solution)/shard_map/reduce_scatter | solution.py:254
  1370.3 5.4 copy.173
  1390.1 10.9 all-reduce.11
  1401.5 22.2 all-reduce.10
  1426.5 17.5 reduce-scatter.55.cloned.1.call-done
  1444.0 72.0 %reduce-scatter.57.cloned.1.call-done = f32[192,384]{1,0:T(8,128)} async-done(((f32[1536,384]{1,0:T(8,128)}), f32[192,384]{1,0:T(8,128)}) %reduce-scatter.57.cloned.1.call-update) | async-done | bytes 294928
  1516.0 72.1 %reduce-scatter.59.cloned.1.call-done = f32[192,384]{1,0:T(8,128)} async-done(((f32[1536,384]{1,0:T(8,128)}), f32[192,384]{1,0:T(8,128)}) %reduce-scatter.59.cloned.1.call-update) | async-done | bytes 294928
  1588.2 72.1 %reduce-scatter.61.cloned.1.call-done = f32[192,384]{1,0:T(8,128)} async-done(((f32[1536,384]{1,0:T(8,128)}), f32[192,384]{1,0:T(8,128)}) %reduce-scatter.61.cloned.1.call-update) | async-done | bytes 294928
  1660.3 121.2 %reduce-scatter.37.cloned.1.call-done = f32[1024,192]{0,1:T(8,128)} async-done(((f32[1024,1536]{0,1:T(8,128)}), f32[1024,192]{0,1:T(8,128)}) %reduce-scatter.37.cloned.1.call-update) | async-done | bytes 786448 | tf_op jit(solution)/shard_map/reduce_scatter | solution.py:376
  1781.5 121.1 %reduce-scatter.41.cloned.1.call-done = f32[1024,192]{0,1:T(8,128)} async-done(((f32[1024,1536]{0,1:T(8,128)}), f32[1024,192]{0,1:T(8,128)}) %reduce-scatter.41.cloned.1.call-update) | async-done | bytes 786448 | tf_op jit(solution)/shard_map/reduce_scatter | solution.py:377
  1902.6 121.8 %reduce-scatter.47.cloned.1.call-done = f32[384,512]{1,0:T(8,128)} async-done(((f32[384,4096]{1,0:T(8,128)}), f32[384,512]{1,0:T(8,128)}) %reduce-scatter.47.cloned.1.call-update) | async-done | bytes 786448 | tf_op jit(solution)/shard_map/reduce_scatter | solution.py:379
  2024.4 121.6 %reduce-scatter.51.cloned.1.call-done = f32[384,512]{1,0:T(8,128)} async-done(((f32[384,4096]{1,0:T(8,128)}), f32[384,512]{1,0:T(8,128)}) %reduce-scatter.51.cloned.1.call-update) | async-done | bytes 786448 | tf_op jit(solution)/shard_map/reduce_scatter | solution.py:380
  2145.9 121.1 %reduce-scatter.63.cloned.1.call-done = f32[192,1024]{1,0:T(8,128)} async-done(((f32[1536,1024]{1,0:T(8,128)}), f32[192,1024]{1,0:T(8,128)}) %reduce-scatter.63.cloned.1.call-update) | async-done | bytes 786448
  (321 shorter events, 154.7 us)
Async XLA Ops:
  7.2 42.7 %all-gather.12.cloned.1.call-start = ((), (), s32[]{:S(2)}) async-start(), calls=%async_computation.18 | async-start | bytes 5898240 | tf_op jit(solution)/shard_map/all_gather | solution.py:128
  7.9 81.1 %all-gather.16.cloned.1.call-start = ((), (), s32[]{:S(2)}) async-start(), calls=%async_computation.20 | async-start | bytes 5898240 | tf_op jit(solution)/shard_map/all_gather | solution.py:127
  8.7 119.4 %all-gather.14.cloned.1.call-start = ((), (), s32[]{:S(2)}) async-start(), calls=%async_computation.19 | async-start | bytes 5898240 | tf_op jit(solution)/shard_map/all_gather | solution.py:126
  9.4 202.2 %all-gather.18.cloned.1.call-start = ((), (), s32[]{:S(2)}) async-start(), calls=%async_computation.21 | async-start | bytes 15728640 | tf_op jit(solution)/shard_map/all_gather | solution.py:132
  10.0 285.2 %all-gather.20.cloned.1.call-start = ((), (), s32[]{:S(2)}) async-start(), calls=%async_computation.22 | async-start | bytes 15728640 | tf_op jit(solution)/shard_map/all_gather | solution.py:131
  10.6 323.5 %all-gather.22.cloned.1.call-start = ((), (), s32[]{:S(2)}) async-start(), calls=%async_computation.23 | async-start | bytes 5898240 | tf_op jit(solution)/shard_map/all_gather | solution.py:135
  11.2 406.6 %all-gather.28.cloned.1.call-start = ((), (), s32[]{:S(2)}) async-start(), calls=%async_computation.26 | async-start | bytes 15728640 | tf_op jit(solution)/shard_map/all_gather | solution.py:204
  11.9 489.6 %all-gather.26.cloned.1.call-start = ((), (), s32[]{:S(2)}) async-start(), calls=%async_computation.25 | async-start | bytes 15728640 | tf_op jit(solution)/shard_map/all_gather | solution.py:203
  12.7 13.5 copy-start.51
  12.7 18.7 copy-start.52
  12.7 18.7 copy-start.53
  12.7 19.2 copy-start.54
  12.7 25.2 %copy-start = (bf16[2,128,1536]{2,1,0:T(8,128)(2,1)S(1)}, bf16[2,128,1536]{2,1,0:T(8,128)(2,1)}, u32[]{:S(2)}) copy-start(bf16[2,128,1536]{2,1,0:T(8,128)(2,1)} %param.23) | copy-start | bytes 2359300
  12.8 25.9 %copy-start.63 = (s32[2]{0:T(128)S(1)}, s32[2]{0:T(128)}, u32[]{:S(2)}) copy-start(s32[2]{0:T(128)} %param.29) | copy-start | bytes 28
  12.8 26.6 %copy-start.48 = (s32[2,128]{1,0:T(2,128)S(1)}, s32[2,128]{1,0:T(2,128)}, u32[]{:S(2)}) copy-start(s32[2,128]{1,0:T(2,128)} %param.26) | copy-start | bytes 3076
  12.8 27.3 %copy-start.40 = (f32[2,4,1536]{2,1,0:T(4,128)S(1)}, f32[2,4,1536]{2,1,0:T(4,128)}, u32[]{:S(2)}) copy-start(f32[2,4,1536]{2,1,0:T(4,128)} %param.25) | copy-start | bytes 147460
  12.8 572.4 %all-gather.24.cloned.1.call-start = ((), (), s32[]{:S(2)}) async-start(), calls=%async_computation.24 | async-start | bytes 15728640 | tf_op jit(solution)/shard_map/all_gather | solution.py:202
  13.5 727.4 %reduce-scatter.29.cloned.1.call-start = ((), (), s32[]{:S(2)}) async-start(), calls=%async_computation.27 | async-start | bytes 5898240 | tf_op jit(solution)/shard_map/reduce_scatter | solution.py:341
  25.0 28.7 %copy-start.64 = (bf16[24]{0:T(256)(128)(2,1)}, bf16[24]{0:T(256)(128)(2,1)S(1)}, u32[]{:S(2)}) copy-start(bf16[24]{0:T(256)(128)(2,1)S(1)} %get-tuple-element.99) | copy-start | bytes 148
  25.0 28.7 %copy-start.66 = (bf16[64]{0:T(256)(128)(2,1)}, bf16[64]{0:T(256)(128)(2,1)S(1)}, u32[]{:S(2)}) copy-start(bf16[64]{0:T(256)(128)(2,1)S(1)} %get-tuple-element.98) | copy-start | bytes 388
  40.1 13.6 copy-start.35
  40.1 13.6 copy-start.37
  93.2 39.9 %copy-start.4 = (f32[2,128,1536]{1,2,0:T(8,128)}, f32[2,128,1536]{1,2,0:T(8,128)S(1)}, u32[]{:S(2)}) copy-start(f32[2,128,1536]{1,2,0:T(8,128)S(1)} %fusion.27) | copy-start | bytes 4718596
  334.1 6.6 copy-start.41
  599.2 9.2 copy-start.27
  599.2 9.2 copy-start.28
  599.2 9.2 copy-start.16
  608.4 23.3 %slice-start.2 = ((s8[4718592]{0:T(1024)(128)(4,1)}), s8[4194304]{0:T(1024)(128)(4,1)S(1)}, s32[]{:S(2)}) async-start(s8[4718592]{0:T(1024)(128)(4,1)} %bitcast.257), calls=%async_computation.47 | async-start | bytes 8388608
  619.3 12.4 slice-start.3
  663.3 98.6 %reduce-scatter.31.cloned.1.call-start = ((), (), s32[]{:S(2)}) async-start(), calls=%async_computation.28 | async-start | bytes 5898240 | tf_op jit(solution)/shard_map/reduce_scatter | solution.py:344
  668.6 143.6 %reduce-scatter.33.cloned.1.call-start = ((), (), s32[]{:S(2)}) async-start(), calls=%async_computation.29 | async-start | bytes 5898240 | tf_op jit(solution)/shard_map/reduce_scatter | solution.py:347
  676.7 186.0 %reduce-scatter.43.cloned.1.call-start = ((), (), s32[]{:S(2)}) async-start(), calls=%async_computation.34 | async-start | bytes 5898240 | tf_op jit(solution)/shard_map/reduce_scatter | solution.py:368
  682.0 282.3 %reduce-scatter.35.cloned.1.call-start = ((), (), s32[]{:S(2)}) async-start(), calls=%async_computation.30 | async-start | bytes 15728640 | tf_op jit(solution)/shard_map/reduce_scatter | solution.py:356
  697.9 367.8 %reduce-scatter.39.cloned.1.call-start = ((), (), s32[]{:S(2)}) async-start(), calls=%async_computation.32 | async-start | bytes 15728640 | tf_op jit(solution)/shard_map/reduce_scatter | solution.py:359
  712.8 454.5 %reduce-scatter.45.cloned.1.call-start = ((), (), s32[]{:S(2)}) async-start(), calls=%async_computation.35 | async-start | bytes 15728640 | tf_op jit(solution)/shard_map/reduce_scatter | solution.py:248
  723.1 545.7 %reduce-scatter.49.cloned.1.call-start = ((), (), s32[]{:S(2)}) async-start(), calls=%async_computation.37 | async-start | bytes 15728640 | tf_op jit(solution)/shard_map/reduce_scatter | solution.py:251
  731.5 638.8 %reduce-scatter.53.cloned.1.call-start = ((), (), s32[]{:S(2)}) async-start(), calls=%async_computation.39 | async-start | bytes 15728640 | tf_op jit(solution)/shard_map/reduce_scatter | solution.py:254
  740.8 703.2 %reduce-scatter.55.cloned.1.call-start = ((), (), s32[]{:S(2)}) async-start(), calls=%async_computation.40 | async-start | bytes 2654208
  743.7 772.3 %reduce-scatter.57.cloned.1.call-start = ((), (), s32[]{:S(2)}) async-start(), calls=%async_computation.41 | async-start | bytes 2654208
  764.6 823.6 %reduce-scatter.59.cloned.1.call-start = ((), (), s32[]{:S(2)}) async-start(), calls=%async_computation.42 | async-start | bytes 2654208
  814.9 845.4 %reduce-scatter.61.cloned.1.call-start = ((), (), s32[]{:S(2)}) async-start(), calls=%async_computation.43 | async-start | bytes 2654208
  865.5 915.9 %reduce-scatter.37.cloned.1.call-start = ((), (), s32[]{:S(2)}) async-start(), calls=%async_computation.31 | async-start | bytes 7077888 | tf_op jit(solution)/shard_map/reduce_scatter | solution.py:376
  969.6 933.0 %reduce-scatter.41.cloned.1.call-start = ((), (), s32[]{:S(2)}) async-start(), calls=%async_computation.33 | async-start | bytes 7077888 | tf_op jit(solution)/shard_map/reduce_scatter | solution.py:377
  1071.2 953.2 %reduce-scatter.47.cloned.1.call-start = ((), (), s32[]{:S(2)}) async-start(), calls=%async_computation.36 | async-start | bytes 7077888 | tf_op jit(solution)/shard_map/reduce_scatter | solution.py:379
  1172.7 973.3 %reduce-scatter.51.cloned.1.call-start = ((), (), s32[]{:S(2)}) async-start(), calls=%async_computation.38 | async-start | bytes 7077888 | tf_op jit(solution)/shard_map/reduce_scatter | solution.py:380
  1274.1 992.9 %reduce-scatter.63.cloned.1.call-start = ((), (), s32[]{:S(2)}) async-start(), calls=%async_computation.44 | async-start | bytes 7077888
  1377.9 7.9 slice-start.4
  1389.1 34.7 %copy-start.14 = (f32[2,128,1536]{2,1,0:T(8,128)S(1)}, f32[2,128,1536]{2,1,0:T(8,128)}, u32[]{:S(2)}) copy-start(f32[2,128,1536]{2,1,0:T(8,128)} %copy-done.13) | copy-start | bytes 4718596
  (56 other events, 137.2 us)
Sparse Core Ops, SparseCore 0:
  9.6 40.2 all-gather.11
  51.5 37.5 all-gather.15
  90.6 37.4 all-gather.13
  129.5 82.1 all-gather.17
  213.1 82.0 all-gather.19
  296.6 37.4 all-gather.21
  335.6 82.0 all-gather.27
  419.3 82.0 all-gather.25
  503.1 82.0 all-gather.23
  663.4 47.8 reduce-scatter.28
  713.9 47.8 reduce-scatter.30
  764.3 47.8 reduce-scatter.32
  814.8 47.8 reduce-scatter.42
  865.2 99.0 reduce-scatter.34
  966.7 99.0 reduce-scatter.38
  1068.2 99.0 reduce-scatter.44
  1169.7 99.0 reduce-scatter.48
  1271.3 99.0 reduce-scatter.52
  1374.4 69.5 reduce-scatter.54
  1447.9 68.0 reduce-scatter.56
  1520.1 68.0 reduce-scatter.58
  1592.2 68.0 reduce-scatter.60
  1664.5 116.9 reduce-scatter.36
  1785.5 117.0 reduce-scatter.40
  1906.8 117.5 reduce-scatter.46
  2028.4 117.4 reduce-scatter.50
  2149.9 117.0 reduce-scatter.62
where the time goes:
time: 2280 us; the launch traced here: 2270 us
  waiting for transfers between devices  1900 us (83%)
  matrix products  218 us (10%)
  blocking collectives  52 us (2%)
  other arithmetic  44.2 us (2%)
  local copies, waits for them, and re-layouts  40 us (2%)
    unnamed x32, waiting for transfers between devices  361 us
    reduce_scatter x1, waiting for transfers between devices, shards(): lax.psum_scatter(ffn_parts[1], 'dp', scatter_dimension=1, tiled=True)  122 us
    reduce_scatter x1, waiting for transfers between devices, shards(): lax.psum_scatter(ffn_parts[2], 'dp', scatter_dimension=1, tiled=True)  122 us
    reduce_scatter x1, waiting for transfers between devices, shards(): lax.psum_scatter(attn_parts[6], 'dp', scatter_dimension=1, tiled=True)  121 us
    reduce_scatter x1, waiting for transfers between devices, shards(): lax.psum_scatter(attn_parts[7], 'dp', scatter_dimension=1, tiled=True)  121 us
    reduce_scatter x1, waiting for transfers between devices, shards(): lax.psum_scatter(grad_cap_key_w.astype(jnp.bfloat16), 'fsdp', scatter_dim...  98.7 us
    reduce_scatter x1, waiting for transfers between devices, shards(): lax.psum_scatter(grad_up_w.astype(jnp.bfloat16), 'fsdp', scatter_dimensio...  96.1 us
    reduce_scatter x1, waiting for transfers between devices, shards(): lax.psum_scatter(grad_cap_value_w.astype(jnp.bfloat16), 'fsdp', scatter_d...  96.1 us
  transfers between devices with their start and end apart: 27, of which 26 were waited for; matrix products, arithmetic and copies ran while one was open for 9% of the time, Pallas kernels for 0%

commit v1 on v0

v1 whole, which is shorter than its diff:
```python
import math

import jax
import jax.numpy as jnp
from jax import lax
from jax.sharding import PartitionSpec as P

EPSILON = 1e-06
NEGATIVE = -1e30
BF16 = jnp.bfloat16
F32 = jnp.float32


def angle_tables(rows_pos, cols_pos, head_size):
    quarter = head_size // 4
    frequency = jnp.exp(jnp.arange(quarter, dtype=F32) * (-math.log(10000.0) / quarter))
    row_angle = rows_pos.astype(F32)[..., None] * frequency
    col_angle = cols_pos.astype(F32)[..., None] * frequency
    angles = jnp.concatenate([row_angle, row_angle, col_angle, col_angle], axis=-1)[:, :, None, :]
    return (jnp.cos(angles), jnp.sin(angles))


def quarter_turn(values):
    shaped = values.reshape(values.shape[:-1] + (2, 2, values.shape[-1] // 4))
    turned = jnp.stack([-shaped[..., 1, :], shaped[..., 0, :]], axis=-2)
    return turned.reshape(values.shape)


def rms_scale(values):
    inverse = lax.rsqrt(jnp.mean(values * values, axis=-1, keepdims=True) + EPSILON)
    return (values * inverse, inverse)


def rms_back(incoming, normed, inverse):
    return inverse * (incoming - normed * jnp.mean(incoming * normed, axis=-1, keepdims=True))


def dot(left, right):
    return jnp.einsum("tc,ce->te", left, right, preferred_element_type=F32)


def dot_back(incoming, weight):
    return jnp.einsum("te,ce->tc", incoming, weight, preferred_element_type=F32)


def dot_tokens(left, right):
    return jnp.einsum("tc,te->ce", left, right, preferred_element_type=F32)


def head_norm(projected, gain_vec, head_size):
    per_head = projected.reshape(
        projected.shape[:-1] + (projected.shape[-1] // head_size, head_size)
    )
    normed, inverse = rms_scale(per_head)
    return (normed * gain_vec, normed, inverse)


def head_norm_back(incoming, normed, inverse, gain_vec):
    grad_gain = jnp.sum(incoming * normed, axis=(0, 1, 2))
    grad_projected = rms_back(incoming * gain_vec, normed, inverse)
    return (
        grad_gain,
        grad_projected.reshape(-1, grad_projected.shape[2] * grad_projected.shape[3]).astype(BF16),
    )


def attend_weights(queries, keys, allowed, scaling):
    scores = jnp.einsum("rqhd,rkhd->rhqk", queries, keys, preferred_element_type=F32) * scaling
    return jax.nn.softmax(jnp.where(allowed, scores, NEGATIVE), axis=-1)


def attend_back(weights, grad_output, values, queries, keys, scaling):
    grad_weights = jnp.einsum("rqhd,rkhd->rhqk", grad_output, values, preferred_element_type=F32)
    centre = jnp.sum(grad_weights * weights, axis=-1, keepdims=True)
    grad_scores = (weights * (grad_weights - centre)).astype(BF16)
    grad_values = jnp.einsum(
        "rhqk,rqhd->rkhd", weights.astype(BF16), grad_output, preferred_element_type=F32
    ).astype(BF16)
    grad_queries = (
        jnp.einsum("rhqk,rkhd->rqhd", grad_scores, keys, preferred_element_type=F32) * scaling
    )
    grad_keys = (
        jnp.einsum("rhqk,rqhd->rkhd", grad_scores, queries, preferred_element_type=F32) * scaling
    )
    return (grad_queries, grad_keys, grad_values)


def unrotate(incoming, cos_table, sin_table):
    return incoming * cos_table - quarter_turn(incoming * sin_table)


class Place:
    def __init__(self, mesh):
        self.copies = mesh.shape["dp"]
        self.shards = mesh.shape["fsdp"]
        self.top_step = self.copies // 2
        self.team_step = self.copies // 4
        self.low = self.copies // 4

    def locate(self):
        self.dp = lax.axis_index("dp")
        self.fsdp = lax.axis_index("fsdp")
        self.side = self.fsdp // 2
        self.core = self.fsdp % 2
        self.top = self.dp // self.top_step
        self.team = (self.dp // self.team_step) % 2
        self.lane = self.dp % 2
        self.quarter = 2 * self.core + self.team

    def swap(self, value, dp=0, fsdp=0):
        if not dp:
            pairs = [(i, i ^ fsdp) for i in range(self.shards)]
            return lax.ppermute(value, "fsdp", pairs)
        if not fsdp:
            pairs = [(i, i ^ dp) for i in range(self.copies)]
            return lax.ppermute(value, "dp", pairs)
        return self.route(value, lambda d, f: (d ^ dp, f ^ fsdp))

    def route(self, value, target):
        pairs = []
        for d in range(self.copies):
            for f in range(self.shards):
                to = target(d, f)
                if to is not None:
                    pairs.append((d * self.shards + f, to[0] * self.shards + to[1]))
        return lax.ppermute(value, ("dp", "fsdp"), pairs)

    def bits(self, d, f):
        return ((d // self.team_step) % 2, f // 2, f % 2, d % 2)


    def gather_tokens(self, block):
        mine = jnp.concatenate([block, self.swap(block, dp=self.team_step)], axis=0)
        return jnp.concatenate([mine, self.swap(mine, fsdp=1)], axis=0)

    def reduce_tokens(self, pairs, product):
        half = pairs[0][0].shape[0] // 2
        block = half // 2

        def part(start, stop):
            return sum(product(left[start:stop], right) for left, right in pairs)

        away = self.swap(part(half, 2 * half).astype(BF16), fsdp=1).astype(F32)
        other = self.swap((part(block, half) + away[block:]).astype(BF16), dp=self.team_step)
        return part(0, block) + away[:block] + other.astype(F32)


    def columns(self, shard):
        width = shard.shape[1] // 4

        def cut(quarter):
            return lax.dynamic_slice_in_dim(shard, quarter * width, width, axis=1)

        near = self.swap(cut(2 * (1 - self.core) + self.team), fsdp=1)
        sent = cut(2 * (self.core ^ self.lane) + self.team)
        across = self.route(sent, lambda d, f: (d, f ^ 2 ^ (d % 2)))
        far = self.swap(across, dp=1)
        full = jnp.zeros((4,) + near.shape, shard.dtype)
        full = lax.dynamic_update_index_in_dim(full, cut(self.quarter), self.fsdp, 0)
        full = lax.dynamic_update_index_in_dim(full, near, self.fsdp ^ 1, 0)
        full = lax.dynamic_update_index_in_dim(full, across, self.fsdp ^ 2 ^ self.lane, 0)
        full = lax.dynamic_update_index_in_dim(full, far, self.fsdp ^ 3 ^ self.lane, 0)
        return full.reshape(-1, width)

    def rows(self, shard):
        half = shard.shape[0] // 2

        def near_target(d, f):
            team, side, core, _ = self.bits(d, f)
            return (d, 2 * side + side) if core == team and side != team else None

        def far_target(d, f):
            team, side, core, _ = self.bits(d, f)
            return (d, 2 * (1 - side) + side) if core == team else None

        near = self.route(shard, near_target)
        piece = lax.dynamic_slice_in_dim(shard, self.lane * half, half, axis=0)
        across = self.route(piece, far_target)
        far = self.swap(across, dp=1)
        first = jnp.where(self.lane == 0, across, far)
        second = jnp.where(self.lane == 0, far, across)
        home = jnp.where(self.side == self.team, shard, near)
        return jnp.where(
            self.core == self.side, home, jnp.concatenate([first, second], axis=0)
        )


    def halve(self, value, axis, keep, dp=0, fsdp=0):
        sent = lax.dynamic_index_in_dim(value, 1 - keep, axis, keepdims=False)
        kept = lax.dynamic_index_in_dim(value, keep, axis, keepdims=False)
        got = self.swap(sent.astype(BF16), dp=dp, fsdp=fsdp)
        return kept.astype(F32) + got.astype(F32)

    def halve_low(self, value):
        step = self.low // 2
        while step:
            value = value.reshape((2, step) + value.shape[1:])
            value = self.halve(value, 0, (self.dp // step) % 2, dp=step)
            step //= 2
        return value[0]

    def columns_back(self, grad, side_first):
        columns, rows = grad.shape
        value = grad.reshape(self.low, columns // self.low, 2, rows // 2)
        if side_first:
            value = self.halve(value, 2, self.side, fsdp=2)
            value = self.halve_low(value)
        else:
            value = self.halve_low(value)
            value = self.halve(value, 1, self.side, fsdp=2)
        value = value.astype(BF16).reshape(columns // self.low, 2, rows // 4)
        own = lax.dynamic_index_in_dim(value, self.core, 1, keepdims=False)
        got = self.swap(
            lax.dynamic_index_in_dim(value, 1 - self.core, 1, keepdims=False), fsdp=1
        )
        straight = self.core == self.top
        sent = jnp.where(straight, got, own)
        kept = jnp.where(straight, own, got)
        total = kept.astype(F32) + self.swap(sent, dp=self.top_step).astype(F32)
        return total.T

    def rows_back(self, grad, side_first):
        columns, rows = grad.shape
        value = grad.astype(BF16).reshape(2, 2, self.low, columns // self.copies, rows)
        own = lax.dynamic_index_in_dim(value, self.core, 1, keepdims=False)
        got = self.swap(
            lax.dynamic_index_in_dim(value, 1 - self.core, 1, keepdims=False), fsdp=1
        )
        straight = self.core == self.side

        def cross(kept, sent):
            return kept.astype(F32) + self.swap(sent, fsdp=2).astype(F32)

        kept = jnp.where(straight, own, got)
        sent = jnp.where(straight, got, own)
        if side_first:
            value = self.halve_low(jnp.moveaxis(cross(kept, sent), 1, 0))
        else:
            both = jnp.stack([kept, sent], axis=0)
            both = self.halve_low(jnp.moveaxis(both, 2, 0))
            value = cross(both[0], both[1].astype(BF16))
        value = self.halve(value, 0, self.top, dp=self.top_step)

        def turn(d, f):
            team, _, core, _ = self.bits(d, f)
            return (d ^ self.team_step, f ^ 1) if core != team else (d, f)

        value = self.route(value.astype(BF16), turn)
        return value.astype(F32).T


def layer(
    place,
    block_input,
    caption,
    modulation,
    segment_ids,
    pos_row,
    pos_col,
    caption_len,
    gain_attn,
    w_query,
    w_key,
    w_value,
    gain_query,
    gain_key,
    w_cap_key,
    w_cap_value,
    gain_cap_key,
    head_gate,
    w_out,
    gain_ffn,
    w_gate,
    w_up,
    w_down,
    cotangent,
):
    place.locate()
    rows, tokens, width = block_input.shape
    cap_tokens = caption.shape[1]
    head_size = gain_query.shape[0] * place.shards
    scaling = 1.0 / math.sqrt(head_size)
    team_rows = 4 * rows

    small = (gain_attn, gain_ffn, gain_query, gain_key, gain_cap_key, head_gate)
    packed = lax.all_gather(jnp.concatenate(small), "fsdp", axis=0).astype(F32)
    full_small, at = [], 0
    for vector in small:
        full_small.append(packed[:, at : at + vector.shape[0]].reshape(-1))
        at += vector.shape[0]
    full_gain_attn, full_gain_ffn, query_gain, key_gain, cap_gain, full_head_gate = full_small
    heads = full_head_gate.shape[0] // 4

    inputs = block_input.astype(F32)
    scale_attn = 1.0 + modulation[:, 0][:, None, :]
    tanh_attn = jnp.tanh(modulation[:, 1])[:, None, :]
    scale_ffn = 1.0 + modulation[:, 2][:, None, :]
    tanh_ffn = jnp.tanh(modulation[:, 3])[:, None, :]
    normed_in, inverse_in = rms_scale(inputs)
    attn_in = (normed_in * full_gain_attn * scale_attn).astype(BF16).reshape(-1, width)
    upstream = cotangent.astype(F32)
    grad_ffn_branch = (upstream * tanh_ffn).astype(BF16).reshape(-1, width)

    attn_in = place.gather_tokens(attn_in)
    marks = jnp.concatenate(
        [segment_ids, pos_row, pos_col, jnp.broadcast_to(caption_len[:, None], (rows, 128))], axis=1
    )
    marks = place.gather_tokens(marks)
    segment_ids, pos_row, pos_col = (marks[:, i * tokens : (i + 1) * tokens] for i in range(3))
    caption_len = marks[:, 3 * tokens]
    caption = place.gather_tokens(caption.reshape(-1, caption.shape[-1]))
    grad_ffn_branch = place.gather_tokens(grad_ffn_branch)

    w_query, w_key, w_value = (place.columns(w) for w in (w_query, w_key, w_value))
    w_cap_key, w_cap_value = (place.columns(w) for w in (w_cap_key, w_cap_value))
    w_out = place.rows(w_out)
    w_gate, w_up = (place.columns(w) for w in (w_gate, w_up))
    w_down = place.rows(w_down)

    cos_table, sin_table = angle_tables(pos_row, pos_col, head_size)
    same_segment = (segment_ids[:, :, None] == segment_ids[:, None, :])[:, None, :, :]
    cap_positions = jnp.arange(cap_tokens, dtype=jnp.int32)
    caption_mask = (cap_positions[None, :] < caption_len[:, None])[:, None, None, :]

    def by_row(flat):
        return flat.reshape(team_rows, -1, flat.shape[-1])

    def by_head(flat):
        return flat.reshape(team_rows, -1, heads, head_size)

    query_raw = by_row(dot(attn_in, w_query))
    key_raw = by_row(dot(attn_in, w_key))
    value_heads = by_head(dot(attn_in, w_value).astype(BF16))
    query_scaled, query_normed, query_inverse = head_norm(query_raw, query_gain, head_size)
    queries = (query_scaled * cos_table + quarter_turn(query_scaled) * sin_table).astype(BF16)
    key_scaled, key_normed, key_inverse = head_norm(key_raw, key_gain, head_size)
    keys = (key_scaled * cos_table + quarter_turn(key_scaled) * sin_table).astype(BF16)
    cap_key_raw = by_row(dot(caption, w_cap_key))
    cap_scaled, cap_normed, cap_inverse = head_norm(cap_key_raw, cap_gain, head_size)
    cap_keys = cap_scaled.astype(BF16)
    cap_values = by_head(dot(caption, w_cap_value).astype(BF16))
    self_weights = attend_weights(queries, keys, same_segment, scaling)
    self_out = jnp.einsum(
        "rhqk,rkhd->rqhd", self_weights.astype(BF16), value_heads, preferred_element_type=F32
    )
    cross_weights = attend_weights(queries, cap_keys, caption_mask, scaling)
    cross_out = jnp.einsum(
        "rhqk,rkhd->rqhd", cross_weights.astype(BF16), cap_values, preferred_element_type=F32
    )
    head_tanh = jnp.tanh(
        lax.dynamic_slice_in_dim(full_head_gate, place.quarter * heads, heads)
    )[:, None]
    mixed = (self_out + head_tanh * cross_out).astype(BF16).reshape(-1, heads * head_size)
    attn_branch = place.reduce_tokens([(mixed, w_out)], dot).reshape(inputs.shape)
    hidden = inputs + tanh_attn * attn_branch

    normed_mid, inverse_mid = rms_scale(hidden)
    ffn_in = (normed_mid * full_gain_ffn * scale_ffn).astype(BF16).reshape(-1, width)
    ffn_in = place.gather_tokens(ffn_in)
    gate_proj = dot(ffn_in, w_gate)
    up_proj = dot(ffn_in, w_up)
    sigmoid_gate = jax.nn.sigmoid(gate_proj)
    silu_gate = gate_proj * sigmoid_gate
    activated = (silu_gate * up_proj).astype(BF16)
    grad_act = dot_back(grad_ffn_branch, w_down)
    grad_gate = (
        grad_act * up_proj * sigmoid_gate * (1.0 + gate_proj * (1.0 - sigmoid_gate))
    ).astype(BF16)
    grad_up = (grad_act * silu_gate).astype(BF16)
    grad_ffn_in = place.reduce_tokens([(grad_gate, w_gate), (grad_up, w_up)], dot_back)
    grad_ffn_in = grad_ffn_in.reshape(inputs.shape)
    grad_w_down = place.rows_back(dot_tokens(grad_ffn_branch, activated), False)
    grad_w_gate = place.columns_back(dot_tokens(grad_gate, ffn_in), True)
    grad_w_up = place.columns_back(dot_tokens(grad_up, ffn_in), False)
    ffn_branch = place.reduce_tokens([(activated, w_down)], dot).reshape(inputs.shape)
    block_out = (hidden + tanh_ffn * ffn_branch).astype(BF16)
    grad_mod_ffn_gate = jnp.sum(upstream * ffn_branch, axis=1) * (
        1.0 - tanh_ffn[:, 0] * tanh_ffn[:, 0]
    )
    grad_ffn_gain = jnp.sum(grad_ffn_in * normed_mid * scale_ffn, axis=(0, 1))
    grad_mod_ffn_scale = jnp.sum(grad_ffn_in * normed_mid * full_gain_ffn, axis=1)
    grad_hidden = upstream + rms_back(
        grad_ffn_in * full_gain_ffn * scale_ffn, normed_mid, inverse_mid
    )

    grad_attn_branch = (grad_hidden * tanh_attn).astype(BF16).reshape(-1, width)
    grad_attn_branch = place.gather_tokens(grad_attn_branch)
    grad_mod_attn_gate = jnp.sum(grad_hidden * attn_branch, axis=1) * (
        1.0 - tanh_attn[:, 0] * tanh_attn[:, 0]
    )
    grad_mixed = by_head(dot_back(grad_attn_branch, w_out).astype(BF16))
    grad_w_out = place.rows_back(dot_tokens(grad_attn_branch, mixed), True)
    grad_mixed_float = grad_mixed.astype(F32)
    grad_head_gate = jnp.sum(grad_mixed_float * cross_out, axis=(0, 1, 3)) * (
        1.0 - head_tanh[:, 0] * head_tanh[:, 0]
    )
    grad_cross = (head_tanh * grad_mixed_float).astype(BF16)
    grad_q_self, grad_keys_turned, grad_values = attend_back(
        self_weights, grad_mixed, value_heads, queries, keys, scaling
    )
    grad_q_cross, grad_cap_keys, grad_cap_values = attend_back(
        cross_weights, grad_cross, cap_values, queries, cap_keys, scaling
    )
    grad_queries = unrotate(grad_q_self + grad_q_cross, cos_table, sin_table)
    grad_keys_plain = unrotate(grad_keys_turned, cos_table, sin_table)
    grad_query_gain, grad_query = head_norm_back(
        grad_queries, query_normed, query_inverse, query_gain
    )
    grad_key_gain, grad_key = head_norm_back(grad_keys_plain, key_normed, key_inverse, key_gain)
    grad_cap_gain, grad_cap = head_norm_back(grad_cap_keys, cap_normed, cap_inverse, cap_gain)
    grad_value = grad_values.reshape(-1, heads * head_size)
    grad_cap_value = grad_cap_values.reshape(-1, heads * head_size)
    grad_w_cap_key = place.columns_back(dot_tokens(grad_cap, caption), True)
    grad_w_cap_value = place.columns_back(dot_tokens(grad_cap_value, caption), False)
    grad_w_query = place.columns_back(dot_tokens(grad_query, attn_in), True)
    grad_w_key = place.columns_back(dot_tokens(grad_key, attn_in), False)
    grad_w_value = place.columns_back(dot_tokens(grad_value, attn_in), True)
    grad_attn_in = place.reduce_tokens(
        [(grad_query, w_query), (grad_key, w_key), (grad_value, w_value)], dot_back
    ).reshape(inputs.shape)
    grad_gain_in = jnp.sum(grad_attn_in * normed_in * scale_attn, axis=(0, 1))
    grad_mod_attn_scale = jnp.sum(grad_attn_in * normed_in * full_gain_attn, axis=1)
    input_grad = (
        grad_hidden + rms_back(grad_attn_in * full_gain_attn * scale_attn, normed_in, inverse_in)
    ).astype(BF16)
    modulation_grad = jnp.stack(
        [grad_mod_attn_scale, grad_mod_attn_gate, grad_mod_ffn_scale, grad_mod_ffn_gate], axis=1
    )

    head_part = jnp.zeros_like(full_head_gate)
    head_part = lax.dynamic_update_slice_in_dim(
        head_part, grad_head_gate, place.quarter * heads, axis=0
    )
    parts = (
        grad_gain_in,
        grad_ffn_gain,
        grad_query_gain,
        grad_key_gain,
        grad_cap_gain,
        head_part,
    )
    summed = lax.psum(jnp.concatenate(parts), ("dp", "fsdp"))
    gains, at = [], 0
    for vector in parts:
        size = vector.shape[0] // place.shards
        gains.append(lax.dynamic_slice_in_dim(summed, at + place.fsdp * size, size))
        at += vector.shape[0]
    return (
        block_out,
        input_grad,
        modulation_grad,
        gains[0],
        grad_w_query,
        grad_w_key,
        grad_w_value,
        gains[2],
        gains[3],
        grad_w_cap_key,
        grad_w_cap_value,
        gains[4],
        gains[5],
        grad_w_out,
        gains[1],
        grad_w_gate,
        grad_w_up,
        grad_w_down,
    )


def solution(mesh):
    def shards(*arrays):
        return layer(Place(mesh), *arrays)

    rows = P(("dp", "fsdp"), None, None)
    marks = P(("dp", "fsdp"), None)
    vector = P("fsdp")
    weight = P("fsdp", None)
    grad = P("fsdp", "dp")
    return jax.shard_map(
        shards,
        mesh=mesh,
        in_specs=(
            (rows, rows, rows, marks, marks, marks, P(("dp", "fsdp")), vector)
            + (weight, weight, weight, vector, vector, weight, weight, vector, vector, weight)
            + (vector, weight, weight, weight, rows)
        ),
        out_specs=(
            (rows, rows, rows, vector, grad, grad, grad, vector, vector, grad, grad, vector)
            + (vector, grad, vector, grad, grad, grad)
        ),
        check_vma=False,
    )
```

time: 2280 us -> 995 us (0.44)
  waiting for transfers between devices: 1900 us -> 324 us
  local copies, waits for them, and re-layouts: 40 us -> 215 us
  starting transfers between devices: 1.73 us -> 81.7 us
  other arithmetic: 44.2 us -> 120 us
  matrix products: 218 us -> 184 us
    reduce_scatter x13 -> x0, waiting for transfers between devices: 1080 us -> none  [the longest x1 122 us: shards(): lax.psum_scatter(ffn_parts[1], 'dp', scatter_dimension=1, tiled=True)]
    all_gather x9 -> x0, waiting for transfers between devices: 457 us -> none  [the longest x1 76 us: shards(): lax.all_gather(w_down, 'fsdp', axis=0, tiled=True)]
    unnamed x32 -> x0, waiting for transfers between devices: 361 us -> none
    ppermute x0 -> x85, waiting for transfers between devices: none -> 324 us  [the longest x37 278 us: swap(): return lax.ppermute(value, 'dp', pairs)]
    ppermute x0 -> x85, starting transfers between devices: none -> 81.7 us  [the longest x37 40.6 us: swap(): return lax.ppermute(value, 'dp', pairs)]
    dynamic_slice x0 -> x31, local copies, waits for them, and re-layouts: none -> 56.8 us  [the longest x9 18.1 us: columns_back(): own = lax.dynamic_index_in_dim(value, self.core, 1, keepdims=False)]
    dynamic_update_slice x0 -> x28, local copies, waits for them, and re-layouts: none -> 28.9 us  [the longest x7 9.33 us: columns(): full = lax.dynamic_update_index_in_dim(full, near, self.fsdp ^ 1, 0)]
    dot_general x31 -> x45, matrix products: 196 us -> 168 us  [the longest x13 60.3 us: dot(): return jnp.einsum('tc,ce->te', left, right, preferred_element_type=F32)]
  transfers between devices with their start and end apart: 27 -> 85, of which waited for: 26 -> 28; matrix products, arithmetic and copies ran while one was open for 9% -> 48% of each run, Pallas kernels for 0% -> 0%
where the time goes in v1:
time: 995 us; the launch traced here: 984 us
  waiting for transfers between devices  324 us (33%)
  local copies, waits for them, and re-layouts  215 us (22%)
  matrix products  184 us (18%)
  other arithmetic  120 us (12%)
  starting transfers between devices  81.7 us (8%)
  blocking collectives  54.8 us (6%)
    ppermute x37, waiting for transfers between devices, swap(): return lax.ppermute(value, 'dp', pairs)  278 us
    dot_general x13, matrix products, dot(): return jnp.einsum('tc,ce->te', left, right, preferred_element_type=F32)  60.3 us
    dot_general x9, matrix products, dot_tokens(): return jnp.einsum('tc,te->ce', left, right, preferred_element_type=F32)  48.3 us
    dot_general x17, matrix products, dot_back(): return jnp.einsum('te,ce->tc', incoming, weight, preferred_element_type=F32)  45.8 us
    ppermute x37, starting transfers between devices, swap(): return lax.ppermute(value, 'dp', pairs)  40.6 us
    psum x1, blocking collectives, layer(): summed = lax.psum(jnp.concatenate(parts), ('dp', 'fsdp'))  37.9 us
    ppermute x13, waiting for transfers between devices, route(): return lax.ppermute(value, ('dp', 'fsdp'), pairs)  36.4 us
    unnamed x369, local copies, waits for them, and re-layouts  33.7 us
  transfers between devices with their start and end apart: 85, of which 28 were waited for; matrix products, arithmetic and copies ran while one was open for 48% of the time, Pallas kernels for 0%

profile of v1, /device:TPU:0, one launch (start us, length us, event | category | flops | bytes accessed | tf_op | source)
XLA Modules:
  0.0 984.4 jit_solution(5097146901221809301)
XLA Ops:
  11.3 16.9 %all-reduce = bf16[3288]{0:T(1024)(128)(2,1)S(1)} all-reduce(bf16[3288]{0:T(1024)(128)(2,1)S(1)} %dynamic-update-slice), channel_id=2, replica_groups=mesh['dp'=8,'fsdp'=4] {'fsdp'}, use_global_device_ids=true, to_apply=%add | all-reduce | flops 3288 | bytes 13152
  53.1 46.6 %collective-permute-done.5 = s32[2,512]{1,0:T(2,128)S(1)} collective-permute-done((s32[2,512]{1,0:T(2,128)S(1)}, s32[2,512]{1,0:T(2,128)S(1)}, u32[]{:S(2)}, u32[]{:S(2)}) %collective-permute-start.5) | collective-permute-done | bytes 4128 | tf_op jit(solution)/shard_map/ppermute | solution.py:116
  108.1 6.9 collective-permute-done.8
  115.1 5.3 collective-permute-done.11
  122.4 7.8 pad_maximum_fusion.1
  136.8 5.1 collective-permute-done.12
  141.9 5.7 collective-permute-done.4
  164.4 9.8 collective-permute-done
  183.7 15.6 %collective-permute-done.20 = bf16[1024,384]{1,0:T(8,128)(2,1)S(1)} collective-permute-done((bf16[1024,384]{1,0:T(8,128)(2,1)S(1)}, bf16[1024,384]{1,0:T(8,128)(2,1)S(1)}, u32[]{:S(2)}, u32[]{:S(2)}) %collective-permute-start.20) | collective-permute-done | bytes 786464 | tf_op jit(solution)/shard_map/ppermute | solution.py:116
  200.4 4.7 copy.71
  205.1 10.9 %collective-permute-done.17 = bf16[1024,384]{1,0:T(8,128)(2,1)} collective-permute-done((bf16[1024,384]{1,0:T(8,128)(2,1)}, bf16[1024,384]{1,0:T(8,128)(2,1)}, u32[]{:S(2)}, u32[]{:S(2)}) %collective-permute-start.17) | collective-permute-done | bytes 786464 | tf_op jit(solution)/shard_map/ppermute | solution.py:116
  238.6 25.4 %convolution_convert_fusion.4 = bf16[2048,384]{1,0:T(8,128)(2,1)S(1)} fusion(bf16[4096,384]{1,0:T(8,128)(2,1)} %bitcast.650, bf16[1024,4096]{1,0:T(8,128)(2,1)} %collective-permute-done.14, bf16[512,4096]{1,0:T(8,128)(2,1)} %collective-permute-done.13, bf16[512,4096]{1,0:T(8,128)(2,1)} %bitcast.616), kind=kOutput, calls=%fused_computation.72 | convolution fusion | flops 6493569024 | bytes 21495808 | tf_op jit(solution)/shard_map/tc,ce->te/dot_general | solution.py:39
  266.5 14.3 %fusion.165 = (bf16[4096,2048]{0,1:T(8,128)(2,1)}, bf16[2048,4096]{1,0:T(8,128)(2,1)S(1)}) fusion(bf16[1024,4096]{1,0:T(8,128)(2,1)} %collective-permute-done.14, bf16[512,4096]{1,0:T(8,128)(2,1)} %collective-permute-done.13, bf16[512,4096]{1,0:T(8,128)(2,1)} %bitcast.617), kind=kLoop, calls=%fused_computation.441 | loop fusion | flops 50331648 | bytes 50331648 | tf_op jit(solution)/shard_map/tc,te->ce/dot_general | solution.py:47
  280.8 6.7 multiply_reduce_fusion.2
  287.6 6.8 fusion.176
  294.5 4.7 fusion.64
  311.0 5.5 collective-permute-start.35
  326.5 24.1 %collective-permute-done.29 = bf16[384,1024]{1,0:T(8,128)(2,1)S(1)} collective-permute-done((bf16[384,1024]{1,0:T(8,128)(2,1)S(1)}, bf16[384,1024]{1,0:T(8,128)(2,1)S(1)}, u32[]{:S(2)}, u32[]{:S(2)}) %collective-permute-start.29) | collective-permute-done | bytes 786464 | tf_op jit(solution)/shard_map/ppermute | solution.py:126
  357.1 14.8 %collective-permute-done.30 = bf16[384,1024]{1,0:T(8,128)(2,1)S(1)} collective-permute-done((bf16[384,1024]{1,0:T(8,128)(2,1)S(1)}, bf16[384,1024]{1,0:T(8,128)(2,1)S(1)}, u32[]{:S(2)}, u32[]{:S(2)}) %collective-permute-start.30) | collective-permute-done | bytes 786464 | tf_op jit(solution)/shard_map/ppermute | solution.py:116
  372.9 4.7 copy.97
  377.6 27.8 %collective-permute-done.36 = bf16[512,1536]{1,0:T(8,128)(2,1)} collective-permute-done((bf16[512,1536]{1,0:T(8,128)(2,1)}, bf16[512,1536]{1,0:T(8,128)(2,1)}, u32[]{:S(2)}, u32[]{:S(2)}) %collective-permute-start.36) | collective-permute-done | bytes 1572896 | tf_op jit(solution)/shard_map/ppermute | solution.py:116
  412.7 8.5 fusion.76
  422.7 22.3 %copy.107 = bf16[4096,2048]{1,0:T(8,128)(2,1)} copy(bf16[4096,2048]{0,1:T(8,128)(2,1)} %get-tuple-element.54) | data formatting | bytes 33554432 | tf_op jit(solution)/shard_map/tc,te->ce/dot_general | solution.py:47
  445.0 5.4 fusion.162
  450.4 7.9 multiply_convert_fusion.2
  460.2 5.1 fusion.12
  468.9 7.2 fusion.161
  476.1 8.4 reshape.513
  484.5 5.6 constant_dynamic-slice_fusion.8
  493.5 7.2 fusion.160
  500.7 8.3 reshape_reshape.2
  514.1 5.8 convolution_convert_fusion
  564.7 11.4 %collective-permute-done.38 = bf16[256,1536]{1,0:T(8,128)(2,1)S(1)} collective-permute-done((bf16[256,1536]{1,0:T(8,128)(2,1)S(1)}, bf16[256,1536]{1,0:T(8,128)(2,1)S(1)}, u32[]{:S(2)}, u32[]{:S(2)}) %collective-permute-start.38) | collective-permute-done | bytes 786464 | tf_op jit(solution)/shard_map/ppermute | solution.py:116
  615.3 9.2 collective-permute-done.82
  628.7 21.7 %collective-permute-done.75 = bf16[512,384]{0,1:T(8,128)(2,1)S(1)} collective-permute-done((bf16[512,384]{0,1:T(8,128)(2,1)S(1)}, bf16[512,384]{0,1:T(8,128)(2,1)S(1)}, u32[]{:S(2)}, u32[]{:S(2)}) %collective-permute-start.75) | collective-permute-done | bytes 393248 | tf_op jit(solution)/shard_map/ppermute | solution.py:116
  651.4 7.4 collective-permute-done.79
  659.8 6.7 collective-permute-done.83
  667.4 4.6 collective-permute-start.84
  734.6 10.3 %fusion.183 = f32[2,192,2,2048]{3,1,2,0:T(8,128)S(1)} fusion(bf16[2,192,2048,1]{2,1,3,0:T(8,128)(2,1)S(1)} %bitcast.658, bf16[2,2048,2048,1]{2,1,0,3:T(8,128)(2,1)} %bitcast.612), kind=kOutput, calls=%fused_computation.459 | convolution fusion | flops 6442450944 | bytes 24641536 | tf_op jit(solution)/shard_map/tc,te->ce/dot_general | solution.py:47
  751.0 10.3 %fusion.184 = f32[2,192,2,2048]{3,1,2,0:T(8,128)S(1)} fusion(bf16[2,192,2048,1]{2,1,3,0:T(8,128)(2,1)S(1)} %bitcast.657, bf16[2,2048,2048,1]{2,1,0,3:T(8,128)(2,1)} %bitcast.613), kind=kOutput, calls=%fused_computation.460 | convolution fusion | flops 6442450944 | bytes 24641536 | tf_op jit(solution)/shard_map/tc,te->ce/dot_general | solution.py:47
  784.5 32.7 %collective-permute-done.48 = bf16[1,192,768]{2,1,0:T(8,128)(2,1)S(1)} collective-permute-done((bf16[1,192,768]{2,1,0:T(8,128)(2,1)S(1)}, bf16[1,192,768]{2,1,0:T(8,128)(2,1)S(1)}, u32[]{:S(2)}, u32[]{:S(2)}) %collective-permute-start.48) | collective-permute-done | bytes 294944 | tf_op jit(solution)/shard_map/ppermute | solution.py:116
  843.0 9.4 collective-permute-done.50
  853.1 5.2 collective-permute-done.54
  868.0 4.6 collective-permute-start.46
  882.2 8.5 collective-permute-done.46
  907.5 37.9 %psum.7 = f32[3288]{0:T(1024)S(1)} all-reduce(f32[3288]{0:T(1024)S(1)} %concatenate.85), channel_id=1, replica_groups=mesh['dp'=8,'fsdp'=4] {'dp','fsdp'}, use_global_device_ids=true, to_apply=%region_25.26 | all-reduce | flops 3288 | bytes 26304 | tf_op jit(solution)/shard_map/psum | solution.py:442
  952.3 22.9 %collective-permute-done.62 = bf16[192,1024]{1,0:T(8,128)(2,1)S(1)} collective-permute-done((bf16[192,1024]{1,0:T(8,128)(2,1)S(1)}, bf16[192,1024]{1,0:T(8,128)(2,1)S(1)}, u32[]{:S(2)}, u32[]{:S(2)}) %collective-permute-start.62) | collective-permute-done | bytes 393248 | tf_op jit(solution)/shard_map/ppermute | solution.py:116
  976.4 6.4 collective-permute-done.66
  (801 shorter events, 408.4 us)
Async XLA Ops:
  3.7 151.8 %collective-permute-start.15 = (bf16[1024,384]{1,0:T(8,128)(2,1)}, bf16[1024,384]{1,0:T(8,128)(2,1)}, u32[]{:S(2)}, u32[]{:S(2)}) collective-permute-start(bf16[1024,384]{1,0:T(8,128)(2,1)} %get-tuple-element.74), channel_id=1, source_target_pairs={{0,1},{1,0},{2,3},{3,2},{4,5},{5,4},{6,7},{7,6},{8,9},{9,8},{10,11... | collective-permute-start | bytes 2359304 | tf_op jit(solution)/shard_map/ppermute | solution.py:113
  4.1 153.7 %collective-permute-start.16 = (bf16[1024,384]{1,0:T(8,128)(2,1)}, bf16[1024,384]{1,0:T(8,128)(2,1)}, u32[]{:S(2)}, u32[]{:S(2)}) collective-permute-start(bf16[1024,384]{1,0:T(8,128)(2,1)} %get-tuple-element.73), channel_id=1, source_target_pairs={{0,2},{1,3},{2,0},{3,1},{4,7},{5,6},{6,5},{7,4},{8,10},{9,11},{10,... | collective-permute-start | bytes 2359304 | tf_op jit(solution)/shard_map/ppermute | solution.py:126
  6.6 114.2 %collective-permute-start.13 = (bf16[512,4096]{1,0:T(8,128)(2,1)}, bf16[512,4096]{1,0:T(8,128)(2,1)}, u32[]{:S(2)}, u32[]{:S(2)}) collective-permute-start(bf16[512,4096]{1,0:T(8,128)(2,1)} %bitcast.614), channel_id=1, source_target_pairs={{0,8},{4,12},{8,0},{12,4},{16,24},{20,28},{24,16},{28,20},{1,9},{5... | collective-permute-start | bytes 12582920 | tf_op jit(solution)/shard_map/ppermute | solution.py:116
  8.3 91.4 %collective-permute-start.5 = (s32[2,512]{1,0:T(2,128)S(1)}, s32[2,512]{1,0:T(2,128)S(1)}, u32[]{:S(2)}, u32[]{:S(2)}) collective-permute-start(s32[2,512]{1,0:T(2,128)S(1)} %pad_add_fusion.2), channel_id=1, source_target_pairs={{0,8},{4,12},{8,0},{12,4},{16,24},{20,28},{24,16},{28,20},{1,9},{5... | collective-permute-start | bytes 12296 | tf_op jit(solution)/shard_map/ppermute | solution.py:116
  9.7 95.3 %collective-permute-start.7 = (bf16[384,384]{1,0:T(8,128)(2,1)}, bf16[384,384]{1,0:T(8,128)(2,1)}, u32[]{:S(2)}, u32[]{:S(2)}) collective-permute-start(bf16[384,384]{1,0:T(8,128)(2,1)} %get-tuple-element.91), channel_id=1, source_target_pairs={{0,1},{1,0},{2,3},{3,2},{4,5},{5,4},{6,7},{7,6},{8,9},{9,8},{10,11... | collective-permute-start | bytes 884744 | tf_op jit(solution)/shard_map/ppermute | solution.py:113
  130.1 108.5 %collective-permute-start.14 = (bf16[1024,4096]{1,0:T(8,128)(2,1)}, bf16[1024,4096]{1,0:T(8,128)(2,1)}, u32[]{:S(2)}, u32[]{:S(2)}) collective-permute-start(bf16[1024,4096]{1,0:T(8,128)(2,1)} %pad_maximum_fusion.1), channel_id=1, source_target_pairs={{0,1},{1,0},{2,3},{3,2},{4,5},{5,4},{6,7},{7,6},{8,9},{9,8},{10,11... | collective-permute-start | bytes 25165832 | tf_op jit(solution)/shard_map/ppermute | solution.py:113
  174.2 235.9 %collective-permute-start.34 = (bf16[1024,1536]{1,0:T(8,128)(2,1)}, bf16[1024,1536]{1,0:T(8,128)(2,1)}, u32[]{:S(2)}, u32[]{:S(2)}) collective-permute-start(bf16[1024,1536]{1,0:T(8,128)(2,1)} %param.44), channel_id=1, source_target_pairs={{2,3},{6,7},{9,8},{13,12},{18,19},{22,23},{25,24},{29,28}} | collective-permute-start | bytes 9437192 | tf_op jit(solution)/shard_map/ppermute | solution.py:126
  178.0 41.5 %collective-permute-start.1 = (bf16[512,1536]{1,0:T(8,128)(2,1)}, bf16[512,1536]{1,0:T(8,128)(2,1)}, u32[]{:S(2)}, u32[]{:S(2)}) collective-permute-start(bf16[512,1536]{1,0:T(8,128)(2,1)} %pad_maximum_fusion.6), channel_id=1, source_target_pairs={{0,1},{1,0},{2,3},{3,2},{4,5},{5,4},{6,7},{7,6},{8,9},{9,8},{10,11... | collective-permute-start | bytes 4718600 | tf_op jit(solution)/shard_map/ppermute | solution.py:113
  180.9 35.0 %collective-permute-start.17 = (bf16[1024,384]{1,0:T(8,128)(2,1)}, bf16[1024,384]{1,0:T(8,128)(2,1)}, u32[]{:S(2)}, u32[]{:S(2)}) collective-permute-start(bf16[1024,384]{1,0:T(8,128)(2,1)} %collective-permute-done.16), channel_id=1, source_target_pairs={{0,4},{4,0},{8,12},{12,8},{16,20},{20,16},{24,28},{28,24},{1,5},{5... | collective-permute-start | bytes 2359304 | tf_op jit(solution)/shard_map/ppermute | solution.py:116
  199.4 119.8 %collective-permute-start.31 = (bf16[384,1024]{1,0:T(8,128)(2,1)}, bf16[384,1024]{1,0:T(8,128)(2,1)}, u32[]{:S(2)}, u32[]{:S(2)}) collective-permute-start(bf16[384,1024]{1,0:T(8,128)(2,1)} %get-tuple-element.68), channel_id=1, source_target_pairs={{0,1},{1,0},{2,3},{3,2},{4,5},{5,4},{6,7},{7,6},{8,9},{9,8},{10,11... | collective-permute-start | bytes 2359304 | tf_op jit(solution)/shard_map/ppermute | solution.py:113
  216.0 104.6 %collective-permute-start.32 = (bf16[384,1024]{1,0:T(8,128)(2,1)}, bf16[384,1024]{1,0:T(8,128)(2,1)}, u32[]{:S(2)}, u32[]{:S(2)}) collective-permute-start(bf16[384,1024]{1,0:T(8,128)(2,1)} %get-tuple-element.67), channel_id=1, source_target_pairs={{0,2},{1,3},{2,0},{3,1},{4,7},{5,6},{6,5},{7,4},{8,10},{9,11},{10,... | collective-permute-start | bytes 2359304 | tf_op jit(solution)/shard_map/ppermute | solution.py:126
  219.5 91.5 %collective-permute-start.39 = (bf16[256,1536]{1,0:T(8,128)(2,1)}, bf16[256,1536]{1,0:T(8,128)(2,1)}, u32[]{:S(2)}, u32[]{:S(2)}) collective-permute-start(bf16[256,1536]{1,0:T(8,128)(2,1)} %bitcast.68), channel_id=1, source_target_pairs={{0,8},{4,12},{8,0},{12,4},{16,24},{20,28},{24,16},{28,20},{1,9},{5... | collective-permute-start | bytes 2359304 | tf_op jit(solution)/shard_map/ppermute | solution.py:116
  311.0 41.1 %collective-permute-start.35 = (bf16[512,1536]{1,0:T(8,128)(2,1)}, bf16[512,1536]{1,0:T(8,128)(2,1)}, u32[]{:S(2)}, u32[]{:S(2)}) collective-permute-start(bf16[512,1536]{1,0:T(8,128)(2,1)} %constant_dynamic-slice_fusion.22), channel_id=1, source_target_pairs={{0,2},{2,1},{4,6},{6,5},{9,10},{11,9},{13,14},{15,13},{16,18},{18,... | collective-permute-start | bytes 4718600 | tf_op jit(solution)/shard_map/ppermute | solution.py:126
  320.5 30.1 %collective-permute-start.29 = (bf16[384,1024]{1,0:T(8,128)(2,1)S(1)}, bf16[384,1024]{1,0:T(8,128)(2,1)S(1)}, u32[]{:S(2)}, u32[]{:S(2)}) collective-permute-start(bf16[384,1024]{1,0:T(8,128)(2,1)S(1)} %copy-done.97), channel_id=1, source_target_pairs={{0,2},{1,3},{2,0},{3,1},{4,7},{5,6},{6,5},{7,4},{8,10},{9,11},{10,... | collective-permute-start | bytes 2359304 | tf_op jit(solution)/shard_map/ppermute | solution.py:126
  322.1 29.5 %collective-permute-start.33 = (bf16[384,1024]{1,0:T(8,128)(2,1)}, bf16[384,1024]{1,0:T(8,128)(2,1)S(1)}, u32[]{:S(2)}, u32[]{:S(2)}) collective-permute-start(bf16[384,1024]{1,0:T(8,128)(2,1)} %collective-permute-done.32), channel_id=1, source_target_pairs={{0,4},{4,0},{8,12},{12,8},{16,20},{20,16},{24,28},{28,24},{1,5},{5... | collective-permute-start | bytes 2359304 | tf_op jit(solution)/shard_map/ppermute | solution.py:116
  325.2 28.7 %collective-permute-start.25 = (bf16[256,1536]{1,0:T(8,128)(2,1)S(1)}, bf16[256,1536]{1,0:T(8,128)(2,1)S(1)}, u32[]{:S(2)}, u32[]{:S(2)}) collective-permute-start(bf16[256,1536]{1,0:T(8,128)(2,1)S(1)} %fusion.24), channel_id=1, source_target_pairs={{0,8},{4,12},{8,0},{12,4},{16,24},{20,28},{24,16},{28,20},{1,9},{5... | collective-permute-start | bytes 2359304 | tf_op jit(solution)/shard_map/ppermute | solution.py:116
  350.6 62.1 %collective-permute-start.40 = (bf16[512,1536]{1,0:T(8,128)(2,1)}, bf16[512,1536]{1,0:T(8,128)(2,1)}, u32[]{:S(2)}, u32[]{:S(2)}) collective-permute-start(bf16[512,1536]{1,0:T(8,128)(2,1)} %pad_maximum_fusion.10), channel_id=1, source_target_pairs={{0,1},{1,0},{2,3},{3,2},{4,5},{5,4},{6,7},{7,6},{8,9},{9,8},{10,11... | collective-permute-start | bytes 4718600 | tf_op jit(solution)/shard_map/ppermute | solution.py:113
  352.2 53.2 %collective-permute-start.36 = (bf16[512,1536]{1,0:T(8,128)(2,1)}, bf16[512,1536]{1,0:T(8,128)(2,1)}, u32[]{:S(2)}, u32[]{:S(2)}) collective-permute-start(bf16[512,1536]{1,0:T(8,128)(2,1)} %collective-permute-done.35), channel_id=1, source_target_pairs={{0,4},{4,0},{8,12},{12,8},{16,20},{20,16},{24,28},{28,24},{1,5},{5... | collective-permute-start | bytes 4718600 | tf_op jit(solution)/shard_map/ppermute | solution.py:116
  357.1 50.3 %collective-permute-start.26 = (bf16[256,1536]{1,0:T(8,128)(2,1)}, bf16[256,1536]{1,0:T(8,128)(2,1)}, u32[]{:S(2)}, u32[]{:S(2)}) collective-permute-start(bf16[256,1536]{1,0:T(8,128)(2,1)} %bitcast.56), channel_id=1, source_target_pairs={{0,8},{4,12},{8,0},{12,4},{16,24},{20,28},{24,16},{28,20},{1,9},{5... | collective-permute-start | bytes 2359304 | tf_op jit(solution)/shard_map/ppermute | solution.py:116
  410.1 34.9 %collective-permute-start.27 = (bf16[512,1536]{1,0:T(8,128)(2,1)}, bf16[512,1536]{1,0:T(8,128)(2,1)}, u32[]{:S(2)}, u32[]{:S(2)}) collective-permute-start(bf16[512,1536]{1,0:T(8,128)(2,1)} %pad_maximum_fusion.9), channel_id=1, source_target_pairs={{0,1},{1,0},{2,3},{3,2},{4,5},{5,4},{6,7},{7,6},{8,9},{9,8},{10,11... | collective-permute-start | bytes 4718600 | tf_op jit(solution)/shard_map/ppermute | solution.py:113
  465.3 69.1 %collective-permute-start.41 = (bf16[512,1536]{1,0:T(8,128)(2,1)}, bf16[512,1536]{1,0:T(8,128)(2,1)}, u32[]{:S(2)}, u32[]{:S(2)}) collective-permute-start(bf16[512,1536]{1,0:T(8,128)(2,1)} %fusion.12), channel_id=1, source_target_pairs={{0,1},{1,0},{2,3},{3,2},{4,5},{5,4},{6,7},{7,6},{8,9},{9,8},{10,11... | collective-permute-start | bytes 4718600 | tf_op jit(solution)/shard_map/ppermute | solution.py:113
  468.9 70.7 %collective-permute-start.37 = (bf16[512,1536]{1,0:T(8,128)(2,1)}, bf16[512,1536]{1,0:T(8,128)(2,1)}, u32[]{:S(2)}, u32[]{:S(2)}) collective-permute-start(bf16[512,1536]{1,0:T(8,128)(2,1)} %convolution_convert_fusion.1), channel_id=1, source_target_pairs={{0,1},{1,0},{2,3},{3,2},{4,5},{5,4},{6,7},{7,6},{8,9},{9,8},{10,11... | collective-permute-start | bytes 4718600 | tf_op jit(solution)/shard_map/ppermute | solution.py:113
  491.5 53.0 %collective-permute-start.72 = (bf16[2,512,768]{2,1,0:T(8,128)(2,1)}, bf16[2,512,768]{2,1,0:T(8,128)(2,1)}, u32[]{:S(2)}, u32[]{:S(2)}) collective-permute-start(bf16[2,512,768]{2,1,0:T(8,128)(2,1)} %bitcast.583), channel_id=1, source_target_pairs={{0,2},{1,3},{2,0},{3,1},{4,6},{5,7},{6,4},{7,5},{8,10},{9,11},{10,... | collective-permute-start | bytes 4718600 | tf_op jit(solution)/shard_map/ppermute | solution.py:113
  513.3 37.6 %collective-permute-start.76 = (bf16[1,512,2,768]{3,1,2,0:T(8,128)(2,1)}, bf16[1,512,2,768]{3,1,2,0:T(8,128)(2,1)}, u32[]{:S(2)}, u32[]{:S(2)}) collective-permute-start(bf16[1,512,2,768]{3,1,2,0:T(8,128)(2,1)} %bitcast.584), channel_id=1, source_target_pairs={{0,4},{4,0},{8,12},{12,8},{16,20},{20,16},{24,28},{28,24},{1,5},{5... | collective-permute-start | bytes 4718600 | tf_op jit(solution)/shard_map/ppermute | solution.py:116
  522.6 31.6 %collective-permute-start.80 = (bf16[2,2,192,1024]{3,2,0,1:T(8,128)(2,1)}, bf16[2,2,192,1024]{3,2,0,1:T(8,128)(2,1)}, u32[]{:S(2)}, u32[]{:S(2)}) collective-permute-start(bf16[2,2,192,1024]{3,2,0,1:T(8,128)(2,1)} %bitcast.585), channel_id=1, source_target_pairs={{0,1},{1,0},{2,3},{3,2},{4,5},{5,4},{6,7},{7,6},{8,9},{9,8},{10,11... | collective-permute-start | bytes 4718600 | tf_op jit(solution)/shard_map/ppermute | solution.py:113
  542.9 33.3 %collective-permute-start.38 = (bf16[256,1536]{1,0:T(8,128)(2,1)S(1)}, bf16[256,1536]{1,0:T(8,128)(2,1)S(1)}, u32[]{:S(2)}, u32[]{:S(2)}) collective-permute-start(bf16[256,1536]{1,0:T(8,128)(2,1)S(1)} %fusion.26), channel_id=1, source_target_pairs={{0,8},{4,12},{8,0},{12,4},{16,24},{20,28},{24,16},{28,20},{1,9},{5... | collective-permute-start | bytes 2359304 | tf_op jit(solution)/shard_map/ppermute | solution.py:116
  546.4 35.9 %collective-permute-start.73 = (bf16[1,512,768]{2,1,0:T(8,128)(2,1)S(1)}, bf16[1,512,768]{2,1,0:T(8,128)(2,1)S(1)}, u32[]{:S(2)}, u32[]{:S(2)}) collective-permute-start(bf16[1,512,768]{2,1,0:T(8,128)(2,1)S(1)} %dynamic-slice_convert_fusion.3), channel_id=1, source_target_pairs={{0,4},{4,0},{8,12},{12,8},{16,20},{20,16},{24,28},{28,24},{1,5},{5... | collective-permute-start | bytes 2359304 | tf_op jit(solution)/shard_map/ppermute | solution.py:116
  553.6 42.1 %collective-permute-start.77 = (bf16[512,768]{1,0:T(8,128)(2,1)}, bf16[512,768]{1,0:T(8,128)(2,1)}, u32[]{:S(2)}, u32[]{:S(2)}) collective-permute-start(bf16[512,768]{1,0:T(8,128)(2,1)} %fusion.82), channel_id=1, source_target_pairs={{0,2},{1,3},{2,0},{3,1},{4,6},{5,7},{6,4},{7,5},{8,10},{9,11},{10,... | collective-permute-start | bytes 2359304 | tf_op jit(solution)/shard_map/ppermute | solution.py:113
  558.1 43.0 %collective-permute-start.81 = (bf16[1,2,2,192,1024]{4,3,2,1,0:T(8,128)(2,1)}, bf16[1,2,2,192,1024]{4,3,2,1,0:T(8,128)(2,1)}, u32[]{:S(2)}, u32[]{:S(2)}) collective-permute-start(bf16[1,2,2,192,1024]{4,3,2,1,0:T(8,128)(2,1)} %fusion.49), channel_id=1, source_target_pairs={{0,4},{4,0},{8,12},{12,8},{16,20},{20,16},{24,28},{28,24},{1,5},{5... | collective-permute-start | bytes 4718600 | tf_op jit(solution)/shard_map/ppermute | solution.py:116
  582.0 28.2 %collective-permute-start.43 = (bf16[256,1536]{1,0:T(8,128)(2,1)}, bf16[256,1536]{1,0:T(8,128)(2,1)}, u32[]{:S(2)}, u32[]{:S(2)}) collective-permute-start(bf16[256,1536]{1,0:T(8,128)(2,1)} %bitcast.70), channel_id=1, source_target_pairs={{0,8},{4,12},{8,0},{12,4},{16,24},{20,28},{24,16},{28,20},{1,9},{5... | collective-permute-start | bytes 2359304 | tf_op jit(solution)/shard_map/ppermute | solution.py:116
  611.8 60.3 %collective-permute-start.44 = (bf16[512,1536]{1,0:T(8,128)(2,1)S(1)}, bf16[512,1536]{1,0:T(8,128)(2,1)S(1)}, u32[]{:S(2)}, u32[]{:S(2)}) collective-permute-start(bf16[512,1536]{1,0:T(8,128)(2,1)S(1)} %pad_maximum_fusion.11), channel_id=1, source_target_pairs={{0,1},{1,0},{2,3},{3,2},{4,5},{5,4},{6,7},{7,6},{8,9},{9,8},{10,11... | collective-permute-start | bytes 4718600 | tf_op jit(solution)/shard_map/ppermute | solution.py:113
  612.2 38.2 %collective-permute-start.75 = (bf16[512,384]{0,1:T(8,128)(2,1)S(1)}, bf16[512,384]{0,1:T(8,128)(2,1)S(1)}, u32[]{:S(2)}, u32[]{:S(2)}) collective-permute-start(bf16[512,384]{0,1:T(8,128)(2,1)S(1)} %bitcast_select_fusion.6), channel_id=1, source_target_pairs={{0,16},{4,20},{8,24},{12,28},{16,0},{20,4},{24,8},{28,12},{1,17},{... | collective-permute-start | bytes 1179656 | tf_op jit(solution)/shard_map/ppermute | solution.py:116
  614.9 43.9 %collective-permute-start.79 = (bf16[512,384]{0,1:T(8,128)(2,1)S(1)}, bf16[512,384]{0,1:T(8,128)(2,1)S(1)}, u32[]{:S(2)}, u32[]{:S(2)}) collective-permute-start(bf16[512,384]{0,1:T(8,128)(2,1)S(1)} %bitcast_select_fusion.4), channel_id=1, source_target_pairs={{0,16},{4,20},{8,24},{12,28},{16,0},{20,4},{24,8},{28,12},{1,17},{... | collective-permute-start | bytes 1179656 | tf_op jit(solution)/shard_map/ppermute | solution.py:116
  626.0 40.5 %collective-permute-start.83 = (bf16[192,1024]{1,0:T(8,128)(2,1)S(1)}, bf16[192,1024]{1,0:T(8,128)(2,1)S(1)}, u32[]{:S(2)}, u32[]{:S(2)}) collective-permute-start(bf16[192,1024]{1,0:T(8,128)(2,1)S(1)} %fusion.107), channel_id=1, source_target_pairs={{0,16},{4,20},{8,24},{12,28},{16,0},{20,4},{24,8},{28,12},{1,17},{... | collective-permute-start | bytes 1179656 | tf_op jit(solution)/shard_map/ppermute | solution.py:116
  667.4 100.6 %collective-permute-start.84 = (bf16[192,1024]{1,0:T(8,128)(2,1)}, bf16[192,1024]{1,0:T(8,128)(2,1)}, u32[]{:S(2)}, u32[]{:S(2)}) collective-permute-start(bf16[192,1024]{1,0:T(8,128)(2,1)} %fusion.86), channel_id=1, source_target_pairs={{0,0},{1,8},{2,2},{3,10},{4,4},{5,12},{6,6},{7,14},{8,1},{9,9},{10... | collective-permute-start | bytes 1179656 | tf_op jit(solution)/shard_map/ppermute | solution.py:126
  717.4 147.9 %collective-permute-start.45 = (bf16[512,1536]{1,0:T(8,128)(2,1)}, bf16[512,1536]{1,0:T(8,128)(2,1)}, u32[]{:S(2)}, u32[]{:S(2)}) collective-permute-start(bf16[512,1536]{1,0:T(8,128)(2,1)} %fusion.13), channel_id=1, source_target_pairs={{0,1},{1,0},{2,3},{3,2},{4,5},{5,4},{6,7},{7,6},{8,9},{9,8},{10,11... | collective-permute-start | bytes 4718600 | tf_op jit(solution)/shard_map/ppermute | solution.py:113
  724.0 50.6 %collective-permute-start.47 = (bf16[2,192,768]{2,1,0:T(8,128)(2,1)}, bf16[2,192,768]{2,1,0:T(8,128)(2,1)}, u32[]{:S(2)}, u32[]{:S(2)}) collective-permute-start(bf16[2,192,768]{2,1,0:T(8,128)(2,1)} %fusion.92), channel_id=1, source_target_pairs={{0,2},{1,3},{2,0},{3,1},{4,6},{5,7},{6,4},{7,5},{8,10},{9,11},{10,... | collective-permute-start | bytes 1769480 | tf_op jit(solution)/shard_map/ppermute | solution.py:113
  727.7 48.9 %collective-permute-start.51 = (bf16[1,192,2,768]{3,1,2,0:T(8,128)(2,1)}, bf16[1,192,2,768]{3,1,2,0:T(8,128)(2,1)}, u32[]{:S(2)}, u32[]{:S(2)}) collective-permute-start(bf16[1,192,2,768]{3,1,2,0:T(8,128)(2,1)} %dynamic-slice_convert_fusion.7), channel_id=1, source_target_pairs={{0,4},{4,0},{8,12},{12,8},{16,20},{20,16},{24,28},{28,24},{1,5},{5... | collective-permute-start | bytes 1769480 | tf_op jit(solution)/shard_map/ppermute | solution.py:116
  730.7 48.3 %collective-permute-start.55 = (bf16[2,192,768]{2,1,0:T(8,128)(2,1)S(1)}, bf16[2,192,768]{2,1,0:T(8,128)(2,1)}, u32[]{:S(2)}, u32[]{:S(2)}) collective-permute-start(bf16[2,192,768]{2,1,0:T(8,128)(2,1)S(1)} %fusion.93), channel_id=1, source_target_pairs={{0,2},{1,3},{2,0},{3,1},{4,6},{5,7},{6,4},{7,5},{8,10},{9,11},{10,... | collective-permute-start | bytes 1769480 | tf_op jit(solution)/shard_map/ppermute | solution.py:113
  768.0 104.6 %collective-permute-start.59 = (bf16[2,192,2048]{2,1,0:T(8,128)(2,1)}, bf16[2,192,2048]{2,1,0:T(8,128)(2,1)}, u32[]{:S(2)}, u32[]{:S(2)}) collective-permute-start(bf16[2,192,2048]{2,1,0:T(8,128)(2,1)} %fusion.45), channel_id=1, source_target_pairs={{0,2},{1,3},{2,0},{3,1},{4,6},{5,7},{6,4},{7,5},{8,10},{9,11},{10,... | collective-permute-start | bytes 4718600 | tf_op jit(solution)/shard_map/ppermute | solution.py:113
  774.7 101.4 %collective-permute-start.63 = (bf16[1,192,2,2048]{3,1,2,0:T(8,128)(2,1)}, bf16[1,192,2,2048]{3,1,2,0:T(8,128)(2,1)}, u32[]{:S(2)}, u32[]{:S(2)}) collective-permute-start(bf16[1,192,2,2048]{3,1,2,0:T(8,128)(2,1)} %dynamic-slice_convert_fusion), channel_id=1, source_target_pairs={{0,4},{4,0},{8,12},{12,8},{16,20},{20,16},{24,28},{28,24},{1,5},{5... | collective-permute-start | bytes 4718600 | tf_op jit(solution)/shard_map/ppermute | solution.py:116
  779.0 38.2 %collective-permute-start.48 = (bf16[1,192,768]{2,1,0:T(8,128)(2,1)S(1)}, bf16[1,192,768]{2,1,0:T(8,128)(2,1)S(1)}, u32[]{:S(2)}, u32[]{:S(2)}) collective-permute-start(bf16[1,192,768]{2,1,0:T(8,128)(2,1)S(1)} %dynamic-slice_convert_fusion.13), channel_id=1, source_target_pairs={{0,4},{4,0},{8,12},{12,8},{16,20},{20,16},{24,28},{28,24},{1,5},{5... | collective-permute-start | bytes 884744 | tf_op jit(solution)/shard_map/ppermute | solution.py:116
  782.6 41.0 %collective-permute-start.52 = (bf16[192,768]{1,0:T(8,128)(2,1)}, bf16[192,768]{1,0:T(8,128)(2,1)}, u32[]{:S(2)}, u32[]{:S(2)}) collective-permute-start(bf16[192,768]{1,0:T(8,128)(2,1)} %fusion.118), channel_id=1, source_target_pairs={{0,2},{1,3},{2,0},{3,1},{4,6},{5,7},{6,4},{7,5},{8,10},{9,11},{10,... | collective-permute-start | bytes 884744 | tf_op jit(solution)/shard_map/ppermute | solution.py:113
  868.0 22.6 %collective-permute-start.46 = (bf16[256,1536]{1,0:T(8,128)(2,1)S(1)}, bf16[256,1536]{1,0:T(8,128)(2,1)S(1)}, u32[]{:S(2)}, u32[]{:S(2)}) collective-permute-start(bf16[256,1536]{1,0:T(8,128)(2,1)S(1)} %fusion.25), channel_id=1, source_target_pairs={{0,8},{4,12},{8,0},{12,4},{16,24},{20,28},{24,16},{28,20},{1,9},{5... | collective-permute-start | bytes 2359304 | tf_op jit(solution)/shard_map/ppermute | solution.py:116
  898.8 46.7 %collective-permute-start.61 = (bf16[192,1024]{1,0:T(8,128)(2,1)}, bf16[192,1024]{1,0:T(8,128)(2,1)}, u32[]{:S(2)}, u32[]{:S(2)}) collective-permute-start(bf16[192,1024]{1,0:T(8,128)(2,1)} %bitcast.591), channel_id=1, source_target_pairs={{0,1},{1,0},{2,3},{3,2},{4,5},{5,4},{6,7},{7,6},{8,9},{9,8},{10,11... | collective-permute-start | bytes 1179656 | tf_op jit(solution)/shard_map/ppermute | solution.py:113
  907.3 40.9 %collective-permute-start.65 = (bf16[192,1024]{1,0:T(8,128)(2,1)S(1)}, bf16[192,1024]{1,0:T(8,128)(2,1)S(1)}, u32[]{:S(2)}, u32[]{:S(2)}) collective-permute-start(bf16[192,1024]{1,0:T(8,128)(2,1)S(1)} %bitcast.681), channel_id=1, source_target_pairs={{0,1},{1,0},{2,3},{3,2},{4,5},{5,4},{6,7},{7,6},{8,9},{9,8},{10,11... | collective-permute-start | bytes 1179656 | tf_op jit(solution)/shard_map/ppermute | solution.py:113
  946.6 28.6 %collective-permute-start.62 = (bf16[192,1024]{1,0:T(8,128)(2,1)S(1)}, bf16[192,1024]{1,0:T(8,128)(2,1)S(1)}, u32[]{:S(2)}, u32[]{:S(2)}) collective-permute-start(bf16[192,1024]{1,0:T(8,128)(2,1)S(1)} %broadcast_select_fusion.5), channel_id=1, source_target_pairs={{0,16},{4,20},{8,24},{12,28},{16,0},{20,4},{24,8},{28,12},{1,17},{... | collective-permute-start | bytes 1179656 | tf_op jit(solution)/shard_map/ppermute | solution.py:116
  948.4 34.4 %collective-permute-start.66 = (bf16[192,1024]{1,0:T(8,128)(2,1)S(1)}, bf16[192,1024]{1,0:T(8,128)(2,1)S(1)}, u32[]{:S(2)}, u32[]{:S(2)}) collective-permute-start(bf16[192,1024]{1,0:T(8,128)(2,1)S(1)} %broadcast_select_fusion.4), channel_id=1, source_target_pairs={{0,16},{4,20},{8,24},{12,28},{16,0},{20,4},{24,8},{28,12},{1,17},{... | collective-permute-start | bytes 1179656 | tf_op jit(solution)/shard_map/ppermute | solution.py:116
  (215 other events, 1792.9 us)

commit v2 on v1

v2 whole, which is shorter than its diff:
```python
import functools
import math

import jax
import jax.numpy as jnp
from jax import lax
from jax.experimental import pallas as pl
from jax.experimental.pallas import tpu as pltpu
from jax.sharding import PartitionSpec as P

EPSILON = 1e-06
NEGATIVE = -1e30
BF16 = jnp.bfloat16
F32 = jnp.float32


def rms_scale(values):
    inverse = lax.rsqrt(jnp.mean(values * values, axis=-1, keepdims=True) + EPSILON)
    return (values * inverse, inverse)


def rms_back(incoming, normed, inverse):
    return inverse * (incoming - normed * jnp.mean(incoming * normed, axis=-1, keepdims=True))


def dot(left, right):
    return jnp.einsum("tc,ce->te", left, right, preferred_element_type=F32)


def dot_back(incoming, weight):
    return jnp.einsum("te,ce->tc", incoming, weight, preferred_element_type=F32)


def dot_tokens(left, right):
    return jnp.einsum("tc,te->ce", left, right, preferred_element_type=F32)


def after(value, *others):
    if not others:
        return value
    return lax.optimization_barrier((value,) + others)[0]


def quarter_turn(values):
    heads, size, tokens = values.shape
    parts = values.reshape(heads, 2, 2, size // 4, tokens)
    turned = jnp.concatenate([-parts[:, :, 1:], parts[:, :, :1]], axis=2)
    return turned.reshape(heads, size, tokens)


def head_norm(raw):
    inverse = lax.rsqrt(jnp.mean(raw * raw, axis=1, keepdims=True) + EPSILON)
    return raw * inverse, inverse


def head_norm_back(incoming, normed, inverse, gain):
    scaled = incoming * gain
    return inverse * (scaled - normed * jnp.mean(scaled * normed, axis=1, keepdims=True))


def dot00(left, right):
    return lax.dot_general(left, right, (((0,), (0,)), ((), ())), preferred_element_type=F32)


def dot11(left, right):
    return lax.dot_general(left, right, (((1,), (1,)), ((), ())), preferred_element_type=F32)


def dot10(left, right):
    return lax.dot_general(left, right, (((1,), (0,)), ((), ())), preferred_element_type=F32)


def softmax0(scores):
    top = jnp.max(scores, axis=0, keepdims=True)
    raised = jnp.exp(scores - top)
    return raised * (1.0 / jnp.sum(raised, axis=0, keepdims=True))


def row_state(qkv, cap, cos_table, sin_table, marks, gains, heads, size):
    tokens, cap_tokens = qkv.shape[0], cap.shape[0]
    across = heads * size
    qkv = qkv.T
    cap = cap.T

    def split(values, at):
        return values[at * across : (at + 1) * across].reshape(heads, size, -1)

    query_normed, query_inverse = head_norm(split(qkv, 0))
    key_normed, key_inverse = head_norm(split(qkv, 1))
    cap_normed, cap_inverse = head_norm(split(cap, 0))

    def rotate(values):
        return (values * cos_table + quarter_turn(values) * sin_table).astype(BF16)

    segment = marks[0:1]
    key_segment = jnp.broadcast_to(segment, (tokens, tokens)).T
    return {
        "queries": rotate(query_normed * gains[0]),
        "keys": rotate(key_normed * gains[1]),
        "values": split(qkv, 2).astype(BF16),
        "cap_keys": (cap_normed * gains[2][:, :1]).astype(BF16),
        "cap_values": split(cap, 1).astype(BF16),
        "norms": (query_normed, query_inverse, key_normed, key_inverse, cap_normed, cap_inverse),
        "same": key_segment == segment,
        "in_use": lax.broadcasted_iota(jnp.int32, (cap_tokens, tokens), 0).astype(F32)
        < marks[1:2],
    }


def forward_kernel(
    heads, size, qkv_ref, cap_ref, cos_ref, sin_ref, marks_ref, gains_ref, tanh_ref, mixed_ref, cross_ref
):
    state = row_state(
        qkv_ref[...], cap_ref[...], cos_ref[...], sin_ref[...], marks_ref[0], gains_ref[...], heads, size
    )
    scaling = 1.0 / math.sqrt(size)
    mixed = []
    for head in range(heads):
        queries = state["queries"][head]
        scores = dot00(state["keys"][head], queries) * scaling
        weights = softmax0(jnp.where(state["same"], scores, NEGATIVE)).astype(BF16)
        self_out = dot10(state["values"][head], weights)
        scores = dot00(state["cap_keys"][head], queries) * scaling
        weights = softmax0(jnp.where(state["in_use"], scores, NEGATIVE)).astype(BF16)
        cross_out = dot10(state["cap_values"][head], weights)
        cross_ref[head * size : (head + 1) * size, :] = cross_out
        mixed.append(self_out + tanh_ref[head] * cross_out)
    mixed_ref[...] = jnp.concatenate(mixed, axis=0).T.astype(BF16)


def backward_kernel(
    heads,
    size,
    qkv_ref,
    cap_ref,
    cos_ref,
    sin_ref,
    marks_ref,
    gains_ref,
    tanh_ref,
    cross_ref,
    grad_ref,
    turned_ref,
    plain_ref,
    cap_grad_ref,
    gain_grad_ref,
    gate_grad_ref,
):
    step = pl.program_id(0)
    cap = cap_ref[...]
    crossed = cross_ref[...]
    gains = gains_ref[...]
    cos_table, sin_table = cos_ref[...], sin_ref[...]
    state = row_state(qkv_ref[...], cap, cos_table, sin_table, marks_ref[0], gains, heads, size)
    scaling = 1.0 / math.sqrt(size)
    across = heads * size
    grad_q, grad_k, grad_cap_k, gate = [], [], [], []
    for head in range(heads):
        span = slice(head * size, (head + 1) * size)
        queries, keys, values = (state[name][head] for name in ("queries", "keys", "values"))
        cap_keys, cap_values = state["cap_keys"][head], state["cap_values"][head]
        grad_out = grad_ref[span, :]
        grad_float = grad_out.astype(F32)
        gate.append(jnp.sum(grad_float * crossed[span], axis=0, keepdims=True))
        grad_cross = (tanh_ref[head] * grad_float).astype(BF16)

        def back(weights, grad_output, held):
            grad_weights = dot00(held, grad_output)
            centre = jnp.sum(grad_weights * weights, axis=0, keepdims=True)
            return (weights * (grad_weights - centre)).astype(BF16)

        scores = dot00(keys, queries) * scaling
        weights = softmax0(jnp.where(state["same"], scores, NEGATIVE))
        grad_scores = back(weights, grad_out, values)
        grad_value = dot11(grad_out, weights.astype(BF16))
        at = 2 * across + head * size
        turned_ref[at : at + size, :] = grad_value.astype(BF16)
        grad_query = dot10(keys, grad_scores)
        grad_k.append(dot11(queries, grad_scores) * scaling)

        scores = dot00(cap_keys, queries) * scaling
        weights = softmax0(jnp.where(state["in_use"], scores, NEGATIVE))
        grad_scores = back(weights, grad_cross, cap_values)
        grad_cap_value = dot11(grad_cross, weights.astype(BF16))
        cap_grad_ref[across + head * size : across + (head + 1) * size, :] = grad_cap_value.astype(
            BF16
        )
        grad_q.append((grad_query + dot10(cap_keys, grad_scores)) * scaling)
        grad_cap_k.append(dot11(queries, grad_scores) * scaling)

    def stacked(parts):
        return jnp.concatenate(parts, axis=0).reshape(heads, size, -1)

    def unrotate(incoming):
        return incoming * cos_table - quarter_turn(incoming * sin_table)

    normed = state["norms"]
    grad_q, grad_k = unrotate(stacked(grad_q)), unrotate(stacked(grad_k))
    grad_cap_k = stacked(grad_cap_k)
    turned_ref[0:across, :] = (
        head_norm_back(grad_q, normed[0], normed[1], gains[0]).reshape(across, -1).astype(BF16)
    )
    turned_ref[across : 2 * across, :] = (
        head_norm_back(grad_k, normed[2], normed[3], gains[1]).reshape(across, -1).astype(BF16)
    )
    cap_grad_ref[0:across, :] = (
        head_norm_back(grad_cap_k, normed[4], normed[5], gains[2][:, :1])
        .reshape(across, -1)
        .astype(BF16)
    )
    plain_ref[...] = turned_ref[...].astype(F32).T.astype(BF16)
    tokens = grad_q.shape[-1]
    cap_part = jnp.sum(grad_cap_k * normed[4], axis=0)
    gain_part = jnp.stack(
        [
            jnp.sum(grad_q * normed[0], axis=0),
            jnp.sum(grad_k * normed[2], axis=0),
            sum(cap_part[:, i : i + tokens] for i in range(0, cap_part.shape[1], tokens)),
        ]
    )
    gate_part = jnp.stack(gate)

    @pl.when(step == 0)
    def _():
        gain_grad_ref[...] = gain_part
        gate_grad_ref[...] = gate_part

    @pl.when(step > 0)
    def _():
        gain_grad_ref[...] += gain_part
        gate_grad_ref[...] += gate_part


def row_specs(row_of, sizes, across):
    size, tokens, cap_tokens = sizes
    return [
        pl.BlockSpec((tokens, 3 * across), lambda i: (row_of(i), 0)),
        pl.BlockSpec((cap_tokens, 2 * across), lambda i: (i, 0)),
        pl.BlockSpec((size, tokens), lambda i: (0, row_of(i))),
        pl.BlockSpec((size, tokens), lambda i: (0, row_of(i))),
        pl.BlockSpec((1, 8, tokens), lambda i: (row_of(i), 0, 0)),
    ]


def whole(shape):
    return pl.BlockSpec(shape, lambda i: (0,) * len(shape))


def attend(row_of, heads, sizes, qkv, cap, cos_table, sin_table, marks, gains, tanh):
    size, tokens, cap_tokens = sizes
    rows = cap.shape[0] // cap_tokens
    across = heads * size
    return pl.pallas_call(
        functools.partial(forward_kernel, heads, size),
        grid=(rows,),
        in_specs=row_specs(row_of, sizes, across) + [whole(gains.shape), whole(tanh.shape)],
        out_specs=[
            pl.BlockSpec((tokens, across), lambda i: (i, 0)),
            pl.BlockSpec((across, tokens), lambda i: (0, i)),
        ],
        out_shape=[
            jax.ShapeDtypeStruct((rows * tokens, across), BF16),
            jax.ShapeDtypeStruct((across, rows * tokens), F32),
        ],
        compiler_params=pltpu.CompilerParams(vmem_limit_bytes=32 * 1024 * 1024),
        cost_estimate=pl.CostEstimate(
            flops=rows * across * tokens * (tokens + cap_tokens) * 16,
            bytes_accessed=rows * across * (tokens * 18 + cap_tokens * 8),
            transcendentals=rows * heads * tokens * (tokens + cap_tokens),
        ),
    )(qkv, cap, cos_table, sin_table, marks, gains, tanh)


def attend_back(row_of, first, heads, sizes, qkv, cap, cos_table, sin_table, marks, gains, tanh, crossed, grad):
    size, tokens, cap_tokens = sizes
    rows = cap.shape[0] // cap_tokens
    across = heads * size
    out_shape = [
        jax.ShapeDtypeStruct((3 * across, rows * tokens), BF16),
        jax.ShapeDtypeStruct((rows * tokens, 3 * across), BF16),
        jax.ShapeDtypeStruct((2 * across, rows * cap_tokens), BF16),
        jax.ShapeDtypeStruct((3, size, tokens), F32),
        jax.ShapeDtypeStruct((heads, 1, tokens), F32),
    ]
    return pl.pallas_call(
        functools.partial(backward_kernel, heads, size),
        grid=(rows,),
        in_specs=row_specs(row_of, sizes, across)
        + [
            whole(gains.shape),
            whole(tanh.shape),
            pl.BlockSpec((across, tokens), lambda i: (0, i)),
            pl.BlockSpec((across, tokens), lambda i: (0, row_of(i) - first)),
        ],
        out_specs=[
            pl.BlockSpec((3 * across, tokens), lambda i: (0, row_of(i) - first)),
            pl.BlockSpec((tokens, 3 * across), lambda i: (row_of(i) - first, 0)),
            pl.BlockSpec((2 * across, cap_tokens), lambda i: (0, i)),
            whole(out_shape[3].shape),
            whole(out_shape[4].shape),
        ],
        out_shape=out_shape,
        compiler_params=pltpu.CompilerParams(vmem_limit_bytes=40 * 1024 * 1024),
        cost_estimate=pl.CostEstimate(
            flops=rows * across * tokens * (tokens + cap_tokens) * 40,
            bytes_accessed=rows * across * (tokens * 30 + cap_tokens * 12),
            transcendentals=rows * heads * tokens * (tokens + cap_tokens),
        ),
    )(qkv, cap, cos_table, sin_table, marks, gains, tanh, crossed, grad)


def join_kernel(widths, rows, chunks, place_ref, *refs):
    shards = refs[: len(widths)]
    near = refs[len(widths)]
    pieces = refs[len(widths) + 1 : len(widths) + 1 + 2 * chunks]
    out, sems = refs[-2:]
    copies = []

    def copy(source, row, count, column, width):
        target = out.at[pl.ds(pl.multiple_of(row, 16), count), pl.ds(column, width)]
        copies.append(pltpu.make_async_copy(source, target, sems.at[len(copies)]))
        copies[-1].start()

    at = 0
    for shard, width in zip(shards, widths):
        begin = pl.multiple_of(place_ref[4] * width, 128)
        copy(shard.at[:, pl.ds(begin, width)], place_ref[0] * rows, rows, at, width)
        at += width
    copy(near, place_ref[1] * rows, rows, 0, at)
    part = rows // chunks
    for chunk in range(chunks):
        for kind in range(2):
            row = place_ref[2 + kind] * rows + chunk * part
            copy(pieces[2 * chunk + kind], row, part, 0, at)
    for item in copies:
        item.wait()


def join(place_index, shards, near, pieces):
    widths = tuple(shard.shape[1] // 4 for shard in shards)
    rows = near.shape[0]
    chunks = len(pieces) // 2
    count = len(shards) + 1 + len(pieces)
    return pl.pallas_call(
        functools.partial(join_kernel, widths, rows, chunks),
        grid_spec=pltpu.PrefetchScalarGridSpec(
            num_scalar_prefetch=1,
            grid=(1,),
            in_specs=[pl.BlockSpec(memory_space=pl.ANY)] * count,
            out_specs=pl.BlockSpec((4 * rows, sum(widths)), lambda i, place: (0, 0)),
            scratch_shapes=[pltpu.SemaphoreType.DMA((count,))],
        ),
        out_shape=jax.ShapeDtypeStruct((4 * rows, sum(widths)), near.dtype),
        compiler_params=pltpu.CompilerParams(vmem_limit_bytes=32 * 1024 * 1024),
        cost_estimate=pl.CostEstimate(
            flops=0, bytes_accessed=16 * rows * sum(widths), transcendentals=0
        ),
    )(place_index, *shards, near, *pieces)


class Flow:
    def __init__(self, steps):
        self.steps = steps
        self.sent = next(steps)
        self.result = None

    def step(self, *others):
        try:
            self.sent = self.steps.send(others)
        except StopIteration as stop:
            self.result = stop.value


class Place:
    def __init__(self, mesh):
        self.copies = mesh.shape["dp"]
        self.shards = mesh.shape["fsdp"]
        self.top_step = self.copies // 2
        self.team_step = self.copies // 4
        self.low = self.copies // 4
        self.last = {}
        self.wave, self.before = [], ()
        self.links = {"fsdp": "x", "dp": "y"}

    def locate(self):
        self.dp = lax.axis_index("dp")
        self.fsdp = lax.axis_index("fsdp")
        self.side = self.fsdp // 2
        self.core = self.fsdp % 2
        self.top = self.dp // self.top_step
        self.team = (self.dp // self.team_step) % 2
        self.lane = self.dp % 2
        self.quarter = 2 * self.core + self.team

    def swap(self, value, dp=0, fsdp=0, link=None):
        return self.route(value, lambda d, f: (d ^ dp, f ^ fsdp), link)

    def route(self, value, target, link=None):
        pairs = []
        for d in range(self.copies):
            for f in range(self.shards):
                to = target(d, f)
                if to is not None:
                    pairs.append((d * self.shards + f, to[0] * self.shards + to[1]))
        value = after(value, *self.before, *self.last.get(link, ()))
        self.operand = value
        value = lax.ppermute(value, ("dp", "fsdp"), pairs)
        if link is not None:
            self.last[link] = (value,)
        self.wave.append(value)
        return value

    def next_wave(self, *computed):
        self.before, self.wave = tuple(self.wave) + computed, []

    def hold(self, value):
        return after(value, *self.before)

    def end_waves(self):
        self.before, self.wave = (), []

    def bits(self, d, f):
        return ((d // self.team_step) % 2, f // 2, f % 2, d % 2)

    def team_swap(self, value):
        return self.swap(value, dp=self.team_step, link="z")

    def core_swap(self, value):
        return self.swap(value, fsdp=1, link="c")


    def gather_tokens(self, block):
        near = self.core_swap(block)
        far = self.team_swap(block)
        near = jnp.concatenate([block, near], axis=0)
        return near, jnp.concatenate([far, self.core_swap(far)], axis=0)

    def reduce_tokens(self, near, far, right, product):
        own, near = jnp.split(near, 2, axis=0)
        far, last = jnp.split(far, 2, axis=0)
        last = self.core_swap(product(last, right).astype(BF16))
        far = self.team_swap((product(far, right) + last.astype(F32)).astype(BF16))
        self.reducing = self.operand
        near = self.core_swap(product(near, right).astype(BF16))
        return product(own, right) + near.astype(F32) + far.astype(F32)


    def cut_columns(self, shards):
        def cut(quarter):
            parts = []
            for shard in shards:
                width = shard.shape[1] // 4
                parts.append(lax.dynamic_slice_in_dim(shard, quarter * width, width, axis=1))
            return jnp.concatenate(parts, axis=1)

        return cut(2 * (self.core ^ self.lane) + self.team), cut(2 * (1 - self.core) + self.team)

    def side_swap(self, piece):
        return self.route(piece, lambda d, f: (d, f ^ 2 ^ (d % 2)))

    def lane_swap(self, piece):
        return self.swap(piece, dp=1)

    def join_columns(self, shards, near, pieces):
        index = [self.fsdp, self.fsdp ^ 1, self.fsdp ^ 2 ^ self.lane, self.fsdp ^ 3 ^ self.lane]
        return join(jnp.stack(index + [self.quarter]).astype(jnp.int32), shards, near, pieces)

    def rows_side_swap(self, shard):
        def target(d, f):
            team, side, core, _ = self.bits(d, f)
            return (d, 2 * (1 - side) + side) if core == team else None

        return self.route(self.part(shard, self.lane, 0), target)

    def rows_lane_swap(self, piece):
        def target(d, f):
            _, side, core, _ = self.bits(d, f)
            return (d ^ 1, f) if core != side else None

        return self.route(piece, target)

    def rows_core_swap(self, shard):
        def target(d, f):
            team, side, core, _ = self.bits(d, f)
            return (d, 2 * side + side) if core == team and side != team else None

        return self.route(shard, target, "c")

    def join_rows(self, shard, near, across, far):
        first = jnp.where(self.lane == 0, across, far)
        second = jnp.where(self.lane == 0, far, across)
        home = jnp.where(self.side == self.team, shard, near)
        return jnp.where(self.core == self.side, home, jnp.concatenate([first, second], axis=0))


    def part(self, value, index, axis):
        if isinstance(value, tuple):
            return tuple(self.part(array, index, axis) for array in value)
        size = value.shape[axis] // 2
        return lax.dynamic_slice_in_dim(value, index * size, size, axis=axis)

    def summed(self, arrays):
        return sum(array.astype(F32) for array in arrays).astype(BF16)

    def halves(self, value, axis, keep):
        sent = self.summed([self.part(array, 1 - keep, axis) for array in value])
        return sent, [self.part(array, keep, axis) for array in value]

    def low_steps(self):
        step = self.low // 2
        while step:
            yield step, (self.dp // step) % 2
            step //= 2

    def both_ways(self, first, second, first_way, second_way):
        got_first = self.swap(first, link=self.links[first_way[0]], **dict([first_way]))
        sent = (self.operand,)
        got_second = self.swap(second, link=self.links[second_way[0]], **dict([second_way]))
        others = yield sent + (self.operand,)
        return after(got_first, *others), after(got_second, *others)

    def spread(self, first, second, place):
        (step, keep), *lows = self.low_steps()
        side, low = ("fsdp", 2), ("dp", step)
        sent = first[0](1 - place), second[0](1 - keep)
        first, second = [first[1](place)], [second[1](keep)]
        got = yield from self.both_ways(*sent, side, low)
        first.append(got[0])
        second.append(got[1])
        sent_first, first = self.halves(first, 0, keep)
        sent_second, second = self.halves(second, 1, place)
        got = yield from self.both_ways(sent_first, sent_second, low, side)
        first.append(got[0])
        second.append(got[1])
        for step, keep in lows:
            sent_first, first = self.halves(first, 0, keep)
            sent_second, second = self.halves(second, 0, keep)
            first.append(self.swap(sent_first, dp=step))
            second.append(self.swap(sent_second, dp=step))
        return first, second

    def finish(self, own, sent):
        got = self.core_swap(sent)
        others = yield (self.operand,)
        got = after(got, *others)
        straight = self.core == self.top
        sent = jnp.where(straight, got, own)
        kept = jnp.where(straight, own, got)
        got = self.swap(sent, dp=self.top_step, link="w")
        others = yield (self.operand,)
        return kept.astype(F32) + after(got, *others).astype(F32)

    def pair_back(self, product, lefts, left_axis, right):
        def by_side(index):
            return product(lefts[0], self.part(right, index, 1)).astype(BF16)

        def by_low(index):
            return product(self.part(lefts[1], index, left_axis), right).astype(BF16)

        first, second = yield from self.spread((by_side, by_side), (by_low, by_low), self.side)

        def both(index):
            return jnp.concatenate(
                [self.summed([self.part(array, index, 1) for array in value]) for value in (first, second)]
            )

        value = yield from self.finish(both(self.core), both(1 - self.core))
        return [part.T for part in jnp.split(value, 2, axis=0)]

    def split_rows(self, right):
        columns = right.shape[1] // 4

        def block(index):
            return lax.dynamic_slice_in_dim(right, index * columns, columns, axis=1)

        return (
            block(2 * self.side),
            block(2 * (1 - self.side)),
            jnp.concatenate([block(1), block(3)], axis=1),
        )

    def split_back(self, product, left, left_axis, right, count):
        this_side, other_side, low_rows = right

        def by_low(index):
            return product(self.part(left, index, left_axis), low_rows).astype(BF16)

        first, second = yield from self.spread(
            (
                lambda index: product(left, other_side).astype(BF16),
                lambda index: product(left, this_side).astype(BF16),
            ),
            (by_low, by_low),
            self.side,
        )
        first, second = self.summed(first), self.summed(second)
        own = jnp.where(self.core == 0, first, second)
        sent = jnp.where(self.core == 0, second, first)
        value = yield from self.finish(own, sent)
        return [part.T for part in jnp.split(value, count, axis=0)]

    def rows_back(self, grad):
        columns, rows = grad.shape
        value = grad.reshape(2, 2, columns // 4, rows)
        own = lax.dynamic_index_in_dim(value, self.core, 1, keepdims=False)
        sent = lax.dynamic_index_in_dim(value, 1 - self.core, 1, keepdims=False)
        got = self.core_swap(sent)
        others = yield (self.operand,)
        got = after(got, *others)
        straight = self.core == self.side
        kept = jnp.where(straight, own, got)
        sent = jnp.where(straight, got, own)
        wide = jnp.concatenate([kept[1], sent[1]], axis=1)
        pieces = sent[0], kept[0]

        def by_low(index):
            return self.part(wide, index, 0)

        first, second = yield from self.spread(
            (lambda index: pieces[0], lambda index: pieces[1]), (by_low, by_low), 0
        )
        first, second = self.summed(first), self.summed(second)
        sent = jnp.where(self.top == 0, second, first)
        got = self.swap(sent, dp=self.top_step, link="w")
        others = yield (self.operand,)
        value = self.summed([jnp.where(self.top == 0, first, second), after(got, *others)])

        def turn(d, f):
            team, _, core, _ = self.bits(d, f)
            return (d ^ self.team_step, f ^ 1) if core != team else (d, f)

        got = self.route(value, turn)
        others = yield (self.operand,)
        return after(got, *others).astype(F32).T

    def total(self, value):
        for bit in (1, 2):
            value = value + self.swap(value, fsdp=bit)
        step = 1
        while step < self.copies:
            value = value + self.swap(value, dp=step)
            step *= 2
        return value


def layer(
    place,
    block_input,
    caption,
    modulation,
    segment_ids,
    pos_row,
    pos_col,
    caption_len,
    gain_attn,
    w_query,
    w_key,
    w_value,
    gain_query,
    gain_key,
    w_cap_key,
    w_cap_value,
    gain_cap_key,
    head_gate,
    w_out,
    gain_ffn,
    w_gate,
    w_up,
    w_down,
    cotangent,
):
    place.locate()
    rows, tokens, width = block_input.shape
    cap_tokens = caption.shape[1]
    size = gain_query.shape[0] * place.shards
    team_rows = 4 * rows

    cap_flat = caption.reshape(-1, caption.shape[-1])
    cap_pieces = jnp.split(cap_flat, 4, axis=0)
    qkv_shards, cap_shards, ffn_shards = (w_query, w_key, w_value), (w_cap_key, w_cap_value), (w_gate, w_up)
    qkv_sent, qkv_near = place.cut_columns(qkv_shards)
    cap_sent, cap_w_near = place.cut_columns(cap_shards)
    ffn_sent, ffn_w_near = place.cut_columns(ffn_shards)
    cap_sent, ffn_sent = jnp.split(cap_sent, 2, axis=0), jnp.split(ffn_sent, 2, axis=0)
    qkv_side = place.side_swap(qkv_sent)
    far_pieces = [place.team_swap(cap_pieces[0])]

    small = (gain_attn, gain_ffn, gain_query, gain_key, gain_cap_key, head_gate)
    piece = jnp.concatenate(small)
    pair = jnp.stack([piece, place.core_swap(piece)])
    other = place.swap(pair, fsdp=2)
    packed = jnp.zeros((place.shards,) + piece.shape, piece.dtype)
    for part, index in ((pair[0], 0), (pair[1], 1), (other[0], 2), (other[1], 3)):
        packed = lax.dynamic_update_index_in_dim(packed, part, place.fsdp ^ index, 0)
    packed = packed.astype(F32)
    full_small, at = [], 0
    for vector in small:
        full_small.append(packed[:, at : at + vector.shape[0]].reshape(-1))
        at += vector.shape[0]
    full_gain_attn, full_gain_ffn, query_gain, key_gain, cap_gain, full_head_gate = full_small
    heads = full_head_gate.shape[0] // 4
    across = heads * size
    sizes = (size, tokens, cap_tokens)
    cap_core = place.core_swap(cap_flat)
    cap_near = jnp.concatenate([cap_flat, cap_core], axis=0)

    inputs = block_input.astype(F32)
    scale_attn = 1.0 + modulation[:, 0][:, None, :]
    tanh_attn = jnp.tanh(modulation[:, 1])[:, None, :]
    scale_ffn = 1.0 + modulation[:, 2][:, None, :]
    tanh_ffn = jnp.tanh(modulation[:, 3])[:, None, :]
    normed_in, inverse_in = rms_scale(inputs)
    attn_in = (normed_in * full_gain_attn * scale_attn).astype(BF16).reshape(-1, width)
    upstream = cotangent.astype(F32)
    grad_branch = (upstream * tanh_ffn).astype(BF16).reshape(-1, width)

    marks = jnp.stack(
        [segment_ids, pos_row, pos_col, jnp.broadcast_to(caption_len[:, None], (rows, tokens))],
        axis=-1,
    ).astype(BF16)
    marks = jnp.pad(marks.reshape(-1, 4), ((0, 0), (0, 124)))
    marked = jnp.concatenate([attn_in, marks], axis=1)

    place.next_wave()
    cap_side = [place.side_swap(cap_sent[0])]
    qkv_lane = place.lane_swap(qkv_side)
    far = place.team_swap(marked)
    qkv_near = place.core_swap(qkv_near)
    near = place.core_swap(marked)

    place.next_wave()
    cap_side.append(place.side_swap(cap_sent[1]))
    cap_lane = [place.lane_swap(cap_side[0])]
    far_pieces.append(place.team_swap(cap_pieces[1]))
    gathered = [
        jnp.concatenate([marked, near], axis=0),
        jnp.concatenate([far, place.core_swap(far)], axis=0),
    ]
    attn_near, attn_far = (part[:, :width] for part in gathered)
    marks = jnp.concatenate([part[:, width : width + 4] for part in gathered]).astype(F32)
    attn_all = jnp.concatenate([attn_near, attn_far], axis=0)
    cap_w_near = place.core_swap(cap_w_near)
    w_qkv = place.join_columns(qkv_shards, qkv_near, [place.hold(qkv_side), qkv_lane])

    place.next_wave(w_qkv)
    out_side = place.rows_side_swap(w_out)
    ffn_side = [place.side_swap(ffn_sent[0])]
    cap_lane.append(place.lane_swap(cap_side[1]))
    far_pieces.append(place.team_swap(cap_pieces[2]))
    cap_first = jnp.concatenate(far_pieces[:2], axis=0)
    cap_first = jnp.concatenate([cap_first, place.core_swap(cap_first)], axis=0)
    quarter_size = size // 4
    frequency = jnp.exp(
        jnp.arange(quarter_size, dtype=F32) * (-math.log(10000.0) / quarter_size)
    )
    marks = place.hold(marks)
    row_angle = frequency[:, None] * marks[:, 1][None, :]
    col_angle = frequency[:, None] * marks[:, 2][None, :]
    angles = jnp.concatenate([row_angle, row_angle, col_angle, col_angle], axis=0)
    cos_table, sin_table = jnp.cos(angles), jnp.sin(angles)
    marks = jnp.stack([marks[:, 0], marks[:, 3]]).reshape(2, team_rows, tokens)
    marks = jnp.pad(jnp.moveaxis(marks, 0, 1), ((0, 0), (0, 6), (0, 0)))
    gains = jnp.broadcast_to(
        jnp.stack([query_gain, key_gain, cap_gain])[:, :, None], (3, size, tokens)
    )
    head_tanh = jnp.tanh(lax.dynamic_slice_in_dim(full_head_gate, place.quarter * heads, heads))
    tanh_table = jnp.broadcast_to(head_tanh[:, None, None], (heads, 1, tokens))
    tables = (cos_table, sin_table, marks, gains, tanh_table)
    qkv_raw = dot(place.hold(attn_all), w_qkv)

    half = team_rows // 2

    def near_row(i):
        return i

    def far_row(i):
        return half + (i % 2) * rows + i // 2

    def second_row(i):
        return half + i * rows + 1

    place.next_wave(qkv_raw, cos_table)
    ffn_side.append(place.side_swap(ffn_sent[1]))
    out_lane = place.rows_lane_swap(out_side)
    ffn_lane = [place.lane_swap(ffn_side[0])]
    far_pieces.append(place.team_swap(cap_pieces[3]))
    ffn_w_near = place.core_swap(ffn_w_near)
    w_cap = place.join_columns(
        cap_shards, cap_w_near, [place.hold(cap_side[0]), cap_lane[0], cap_side[1], cap_lane[1]]
    )
    cap_raw_near = dot(cap_near, w_cap)
    mixed_near, cross_near = attend(near_row, heads, sizes, qkv_raw, cap_raw_near, *tables)

    place.next_wave(mixed_near)
    cap_second = jnp.concatenate(far_pieces[2:], axis=0)
    cap_second = jnp.concatenate([cap_second, place.core_swap(cap_second)], axis=0)
    down_side = place.rows_side_swap(w_down)
    ffn_lane.append(place.lane_swap(ffn_side[1]))
    far = place.team_swap(grad_branch)
    out_near = place.rows_core_swap(w_out)
    w_out = place.join_rows(w_out, out_near, place.hold(out_side), out_lane)
    branch_near = jnp.concatenate([grad_branch, place.core_swap(grad_branch)], axis=0)
    cap_raw_first = dot(place.hold(cap_first), w_cap)
    mixed_first, cross_first = attend(far_row, heads, sizes, qkv_raw, cap_raw_first, *tables)

    place.next_wave(mixed_first)
    down_lane = place.rows_lane_swap(down_side)
    place.end_waves()
    cap_raw_second = dot(cap_second, w_cap)
    mixed_second, cross_second = attend(second_row, heads, sizes, qkv_raw, cap_raw_second, *tables)
    mixed_far = jnp.concatenate(
        [mixed_first[:tokens], mixed_second[:tokens], mixed_first[tokens:], mixed_second[tokens:]]
    )
    cap_far = jnp.concatenate([cap_first, cap_second], axis=0)
    cap_raw_far = jnp.concatenate([cap_raw_first, cap_raw_second], axis=0)
    cross_far = jnp.concatenate([cross_first, cross_second], axis=1)
    attn_branch = place.reduce_tokens(mixed_near, mixed_far, w_out, dot).reshape(inputs.shape)
    down_near = place.rows_core_swap(w_down)
    w_down = place.join_rows(w_down, down_near, down_side, down_lane)
    w_ffn = place.join_columns(
        ffn_shards, ffn_w_near, [ffn_side[0], ffn_lane[0], ffn_side[1], ffn_lane[1]]
    )
    branch_far = jnp.concatenate([far, place.core_swap(far)], axis=0)
    hidden = inputs + tanh_attn * attn_branch

    normed_mid, inverse_mid = rms_scale(hidden)
    ffn_in = (normed_mid * full_gain_ffn * scale_ffn).astype(BF16).reshape(-1, width)
    ffn_near, ffn_far = place.gather_tokens(ffn_in)

    def middle(ffn_in, grad_branch):
        grad_act = dot_back(grad_branch, w_down)
        inner = grad_act.shape[1]
        gate_up = dot(ffn_in, w_ffn)
        gate_proj, up_proj = gate_up[:, :inner], gate_up[:, inner:]
        sigmoid_gate = jax.nn.sigmoid(gate_proj)
        silu_gate = gate_proj * sigmoid_gate
        activated = (silu_gate * up_proj).astype(BF16)
        grad_gate = (
            grad_act * up_proj * sigmoid_gate * (1.0 + gate_proj * (1.0 - sigmoid_gate))
        ).astype(BF16)
        grad_up = (grad_act * silu_gate).astype(BF16)
        return activated, jnp.concatenate([grad_gate, grad_up], axis=1)

    act_near, grad_near = middle(ffn_near, branch_near)
    act_far, grad_far = middle(ffn_far, branch_far)
    grad_ffn_in = place.reduce_tokens(grad_near, grad_far, w_ffn, dot_back)
    grad_ffn_in = grad_ffn_in.reshape(inputs.shape)
    inner = act_near.shape[1]
    grad_far, act_far = after(grad_far, place.reducing), after(act_far, place.reducing)

    def halves_product(left, right):
        return dot_tokens(left[0], right[0]) + dot_tokens(left[1], right[1])

    ffn = Flow(
        place.pair_back(
            halves_product,
            [(grad_near[:, at : at + inner], grad_far[:, at : at + inner]) for at in (0, inner)],
            1,
            (ffn_near, ffn_far),
        )
    )
    grad_down = halves_product((branch_near, branch_far), (act_near, act_far)).astype(BF16)
    down = Flow(place.rows_back(grad_down))
    grad_ffn_gain = jnp.sum(grad_ffn_in * normed_mid * scale_ffn, axis=(0, 1))
    grad_mod_ffn_scale = jnp.sum(grad_ffn_in * normed_mid * full_gain_ffn, axis=1)
    grad_hidden = upstream + rms_back(
        grad_ffn_in * full_gain_ffn * scale_ffn, normed_mid, inverse_mid
    )

    grad_attn_branch = (grad_hidden * tanh_attn).astype(BF16).reshape(-1, width)
    attn_grad_near, attn_grad_far = place.gather_tokens(grad_attn_branch)
    grad_mod_attn_gate = jnp.sum(grad_hidden * attn_branch, axis=1) * (
        1.0 - tanh_attn[:, 0] * tanh_attn[:, 0]
    )

    def heads_back(row_of, first, cap_raw, crossed, grad):
        grad_mixed = dot_back(w_out, grad).astype(BF16)
        return attend_back(
            row_of, first, heads, sizes, qkv_raw, cap_raw, *tables, crossed, grad_mixed
        )

    cap_all = jnp.concatenate([cap_near, cap_far], axis=0)
    cap_right = place.split_rows(cap_all)
    attn_right = place.split_rows(attn_all)
    near = heads_back(near_row, 0, cap_raw_near, cross_near, attn_grad_near)
    ffn.step(near[0])
    attn_grad_far = after(attn_grad_far, *ffn.sent)
    far = heads_back(far_row, half, cap_raw_far, cross_far, attn_grad_far)
    ffn.step(far[0])
    down.step(far[0])

    def mix(grads, count):
        grads = jnp.concatenate(grads, axis=1)
        shaped = grads.reshape(count, place.low, -1, grads.shape[1])
        return jnp.moveaxis(shaped, 0, 1).reshape(grads.shape)

    grad_cap = after(mix((near[2], far[2]), 2), *down.sent)
    cap = Flow(place.split_back(dot, grad_cap, 0, cap_right, 2))
    near_plain, far_plain = (after(part, *cap.sent) for part in (near[1], far[1]))
    grad_attn_in = place.reduce_tokens(near_plain, far_plain, w_qkv, dot_back).reshape(inputs.shape)
    attn_grad_all = jnp.concatenate([attn_grad_near, attn_grad_far], axis=0)
    mixed_all = after(jnp.concatenate([mixed_near, mixed_far], axis=0), *cap.sent)
    ffn.step()
    out = Flow(place.rows_back(dot_tokens(attn_grad_all, mixed_all).astype(BF16)))
    down.step()
    cap.step()
    qkv = Flow(place.split_back(dot, mix((near[0], far[0]), 3), 0, attn_right, 3))
    ffn.step()
    down.step()
    cap.step()
    out.step()
    qkv.step()
    down.step()
    out.step()
    ffn_branch = place.reduce_tokens(act_near, after(act_far, *cap.sent), w_down, dot)
    ffn_branch = ffn_branch.reshape(inputs.shape)
    flows = [down, cap, qkv, out]
    while any(flow.result is None for flow in flows):
        for flow in flows:
            if flow.result is None:
                flow.step()
    block_out = (hidden + tanh_ffn * ffn_branch).astype(BF16)
    grad_mod_ffn_gate = jnp.sum(upstream * ffn_branch, axis=1) * (
        1.0 - tanh_ffn[:, 0] * tanh_ffn[:, 0]
    )
    gate_parts = near[4] + far[4]
    gain_parts = jnp.sum(near[3] + far[3], axis=2)
    grad_head_gate = jnp.sum(gate_parts, axis=(1, 2)) * (1.0 - head_tanh * head_tanh)
    grad_gain_in = jnp.sum(grad_attn_in * normed_in * scale_attn, axis=(0, 1))
    grad_mod_attn_scale = jnp.sum(grad_attn_in * normed_in * full_gain_attn, axis=1)
    input_grad = (
        grad_hidden + rms_back(grad_attn_in * full_gain_attn * scale_attn, normed_in, inverse_in)
    ).astype(BF16)
    modulation_grad = jnp.stack(
        [grad_mod_attn_scale, grad_mod_attn_gate, grad_mod_ffn_scale, grad_mod_ffn_gate], axis=1
    )

    head_part = jnp.zeros_like(full_head_gate)
    head_part = lax.dynamic_update_slice_in_dim(
        head_part, grad_head_gate, place.quarter * heads, axis=0
    )
    parts = (
        grad_gain_in,
        grad_ffn_gain,
        gain_parts[0],
        gain_parts[1],
        gain_parts[2],
        head_part,
    )
    summed = place.total(jnp.concatenate(parts))
    vectors, at = [], 0
    for vector in parts:
        length = vector.shape[0] // place.shards
        vectors.append(lax.dynamic_slice_in_dim(summed, at + place.fsdp * length, length))
        at += vector.shape[0]
    return (
        block_out,
        input_grad,
        modulation_grad,
        vectors[0],
        qkv.result[0],
        qkv.result[1],
        qkv.result[2],
        vectors[2],
        vectors[3],
        cap.result[0],
        cap.result[1],
        vectors[4],
        vectors[5],
        out.result,
        vectors[1],
        ffn.result[0],
        ffn.result[1],
        down.result,
    )


def solution(mesh):
    def shards(*arrays):
        return layer(Place(mesh), *arrays)

    rows = P(("dp", "fsdp"), None, None)
    marks = P(("dp", "fsdp"), None)
    vector = P("fsdp")
    weight = P("fsdp", None)
    grad = P("fsdp", "dp")
    return jax.shard_map(
        shards,
        mesh=mesh,
        in_specs=(
            (rows, rows, rows, marks, marks, marks, P(("dp", "fsdp")), vector)
            + (weight, weight, weight, vector, vector, weight, weight, vector, vector, weight)
            + (vector, weight, weight, weight, rows)
        ),
        out_specs=(
            (rows, rows, rows, vector, grad, grad, grad, vector, vector, grad, grad, vector)
            + (vector, grad, vector, grad, grad, grad)
        ),
        check_vma=False,
    )
```

time: 995 us -> 665 us (0.67)
  local copies, waits for them, and re-layouts: 215 us -> 90 us
  waiting for transfers between devices: 324 us -> 229 us
  matrix products: 184 us -> 128 us
  blocking collectives: 54.8 us -> 0 us
  Pallas kernels: 0 us -> 53.2 us
  other arithmetic: 120 us -> 72.2 us
    ppermute x85 -> x89, waiting for transfers between devices: 324 us -> 229 us  [route(): value = lax.ppermute(value, ('dp', 'fsdp'), pairs)]
    pallas_call x0 -> x8, Pallas kernels: none -> 53.2 us  [the longest x2 30.3 us: attend_back(): pl.pallas_call(functools.partial(backward_kernel, heads, size), grid=(row...]
    psum x1 -> x0, blocking collectives: 37.9 us -> none  [layer(): summed = lax.psum(jnp.concatenate(parts), ('dp', 'fsdp'))]
    dynamic_slice x31 -> x10, local copies, waits for them, and re-layouts: 56.8 us -> 19.1 us  [the longest x4 8.15 us: cut(): lax.dynamic_slice_in_dim(shard, quarter * width, width, axis=1)]
    dynamic_update_slice x28 -> x4, local copies, waits for them, and re-layouts: 28.9 us -> 0.2 us  [layer(): lax.dynamic_update_index_in_dim(packed, part, place.fsdp ^ index, 0)]
    dot_general x2 -> x0, local copies, waits for them, and re-layouts: 26.9 us -> none  [dot_tokens(): return jnp.einsum('tc,te->ce', left, right, preferred_element_type=F32)]
    dot_general x9 -> x11, matrix products: 48.3 us -> 22.9 us  [dot_tokens(): return jnp.einsum('tc,te->ce', left, right, preferred_element_type=F32)]
    convert_element_type x30 -> x0, local copies, waits for them, and re-layouts: 23.8 us -> none  [the longest x15 8.85 us: halve(): got = self.swap(sent.astype(BF16), dp=dp, fsdp=fsdp)]
  transfers between devices with their start and end apart: 85 -> 89, of which waited for: 28 -> 28; matrix products, arithmetic and copies ran while one was open for 48% -> 36% of each run, Pallas kernels for 0% -> 8%
where the time goes in v2:
time: 665 us; the launch traced here: 657 us
  waiting for transfers between devices  229 us (34%)
  matrix products  128 us (19%)
  local copies, waits for them, and re-layouts  90 us (14%)
  starting transfers between devices  80.7 us (12%)
  other arithmetic  72.2 us (11%)
  Pallas kernels  53.2 us (8%)
    ppermute x89, waiting for transfers between devices, route(): value = lax.ppermute(value, ('dp', 'fsdp'), pairs)  229 us
    ppermute x89, starting transfers between devices, route(): value = lax.ppermute(value, ('dp', 'fsdp'), pairs)  80.7 us
    dot_general x22, matrix products, dot(): return jnp.einsum('tc,ce->te', left, right, preferred_element_type=F32)  74.8 us
    unnamed x314, local copies, waits for them, and re-layouts  45.4 us
    dot_general x12, matrix products, dot_back(): return jnp.einsum('te,ce->tc', incoming, weight, preferred_element_type=F32)  30.6 us
    pallas_call x2, Pallas kernels, attend_back(): pl.pallas_call(functools.partial(backward_kernel, heads, size), grid=(row...  30.3 us
    dot_general x11, matrix products, dot_tokens(): return jnp.einsum('tc,te->ce', left, right, preferred_element_type=F32)  22.9 us
    pallas_call x3, Pallas kernels, attend(): pl.pallas_call(functools.partial(forward_kernel, heads, size), grid=(rows...  16 us
  transfers between devices with their start and end apart: 89, of which 28 were waited for; matrix products, arithmetic and copies ran while one was open for 36% of the time, Pallas kernels for 8%

profile of v2, /device:TPU:0, one launch (start us, length us, event | category | flops | bytes accessed | tf_op | source)
XLA Modules:
  0.0 656.6 jit_solution(8550367076804793846)
XLA Ops:
  0.7 4.2 concatenate.141
  52.7 4.6 constant_dynamic-update-slice_fusion.13
  57.4 13.0 %collective-permute-done.8.refs_3_ = bf16[512,768]{1,0:T(8,128)(2,1)} collective-permute-done((bf16[512,768]{1,0:T(8,128)(2,1)}, bf16[512,768]{1,0:T(8,128)(2,1)}, u32[]{:S(2)}, u32[]{:S(2)}) %collective-permute-start.8) | collective-permute-done | bytes 786464 | tf_op jit(solution)/shard_map/ppermute | solution.py:407
  71.2 4.8 constant_dynamic-update-slice_fusion.12
  89.6 12.0 %collective-permute-done.13 = bf16[128,4096]{1,0:T(8,128)(2,1)S(1)} collective-permute-done((bf16[128,4096]{1,0:T(8,128)(2,1)S(1)}, bf16[128,4096]{1,0:T(8,128)(2,1)S(1)}, u32[]{:S(2)}, u32[]{:S(2)}) %collective-permute-start.13) | collective-permute-done | bytes 1048608 | tf_op jit(solution)/shard_map/ppermute | solution.py:407
  107.2 3.8 collective-permute-start.15
  115.4 4.5 fusion.195.qkv_ref
  119.9 3.4 collective-permute-done.15
  123.3 12.1 %collective-permute-done.16.refs_3_ = bf16[192,2048]{1,0:T(8,128)(2,1)} collective-permute-done((bf16[192,2048]{1,0:T(8,128)(2,1)S(1)}, bf16[192,2048]{1,0:T(8,128)(2,1)}, u32[]{:S(2)}, u32[]{:S(2)}) %collective-permute-start.16) | collective-permute-done | bytes 786464 | tf_op jit(solution)/shard_map/ppermute | solution.py:407
  145.8 8.6 %fusion.cap_ref = f32[1024,768]{1,0:T(8,128)S(1)} fusion(bf16[4096,768]{1,0:T(8,128)(2,1)S(1)} %shard_map.359, bf16[512,4096]{1,0:T(8,128)(2,1)} %collective-permute-done.4, bf16[512,4096]{1,0:T(8,128)(2,1)S(1)} %bitcast.192), kind=kOutput, calls=%fused_computation | convolution fusion | flops 6459228160 | bytes 17825792 | tf_op jit(solution)/shard_map/tc,ce->te/dot_general | solution.py:27
  154.6 7.9 %shard_map.360 = (bf16[512,384]{1,0:T(8,128)(2,1)S(1)}, f32[384,512]{1,0:T(8,128)S(1)}) custom-call(f32[1024,1152]{1,0:T(8,128)S(1)} %fusion.195.qkv_ref, f32[1024,768]{1,0:T(8,128)S(1)} %fusion.cap_ref, f32[64,1024]{1,0:T(8,128)S(1)} %get-tuple-element.364.cos_ref, f32[64,1024]{1,0:T(8,128)S(1)} %get-tuple-element.363.sin_ref, ...), custom_call_target="tpu_custom_call" | custom-call | flops 1207959552 | bytes 6684672 | tf_op jit(solution)/shard_map/pallas_call | solution.py:253
  162.5 5.9 collective-permute-done.23
  173.4 3.4 fusion.196.cap_ref
  176.9 4.0 shard_map.361
  183.9 4.7 fusion.6.cap_ref
  188.6 4.0 shard_map.362
  208.7 8.9 %collective-permute-done.30 = bf16[256,1536]{1,0:T(8,128)(2,1)S(1)} collective-permute-done((bf16[256,1536]{1,0:T(8,128)(2,1)S(1)}, bf16[256,1536]{1,0:T(8,128)(2,1)S(1)}, u32[]{:S(2)}, u32[]{:S(2)}) %collective-permute-start.30) | collective-permute-done | bytes 786464 | tf_op jit(solution)/shard_map/ppermute | solution.py:407
  222.4 3.1 constant_dynamic-update-slice_fusion.6
  227.8 6.0 fusion.185
  235.2 11.2 %collective-permute-done.31 = bf16[256,1536]{1,0:T(8,128)(2,1)S(1)} collective-permute-done((bf16[256,1536]{1,0:T(8,128)(2,1)S(1)}, bf16[256,1536]{1,0:T(8,128)(2,1)S(1)}, u32[]{:S(2)}, u32[]{:S(2)}) %collective-permute-start.31) | collective-permute-done | bytes 786464 | tf_op jit(solution)/shard_map/ppermute | solution.py:407
  254.5 14.0 %collective-permute-done.38 = bf16[256,1536]{1,0:T(8,128)(2,1)} collective-permute-done((bf16[256,1536]{1,0:T(8,128)(2,1)S(1)}, bf16[256,1536]{1,0:T(8,128)(2,1)}, u32[]{:S(2)}, u32[]{:S(2)}) %collective-permute-start.38) | collective-permute-done | bytes 786464 | tf_op jit(solution)/shard_map/ppermute | solution.py:407
  273.3 5.0 fusion.115
  278.3 5.0 multiply_convert_fusion.1
  286.5 5.3 fusion.197
  291.8 6.4 multiply_convert_fusion.2
  298.3 4.0 convolution_convert_fusion.4
  320.6 4.5 fusion.198
  325.1 4.6 add_convert_fusion
  336.8 3.3 fusion.32
  345.3 17.0 %collective-permute-done.45 = bf16[256,1536]{1,0:T(8,128)(2,1)} collective-permute-done((bf16[256,1536]{1,0:T(8,128)(2,1)S(1)}, bf16[256,1536]{1,0:T(8,128)(2,1)}, u32[]{:S(2)}, u32[]{:S(2)}) %collective-permute-start.45) | collective-permute-done | bytes 786464 | tf_op jit(solution)/shard_map/ppermute | solution.py:407
  363.2 15.2 %shard_map.364 = (bf16[1152,512]{1,0:T(8,128)(2,1)S(1)}, bf16[512,1152]{1,0:T(8,128)(2,1)S(1)}, bf16[768,1024]{1,0:T(8,128)(2,1)S(1)}, f32[3,64,128]{2,1,0:T(8,128)S(1)}, f32[6,1,128]{2,1,0:T(1,128)S(1)}) custom-call(f32[1024,1152]{1,0:T(8,128)S(1)} %fusion.195.qkv_ref, f32[1024,768]{1,0:T(8,128)S(1)} %fusion.cap_ref, ...), custom_call_target="tpu_custom_call" | custom-call | flops 3019898880 | bytes 10616832 | tf_op jit(solution)/shard_map/pallas_call | solution.py:285
  388.5 15.1 %shard_map.365 = (bf16[1152,512]{1,0:T(8,128)(2,1)S(1)}, bf16[512,1152]{1,0:T(8,128)(2,1)S(1)}, bf16[768,1024]{1,0:T(8,128)(2,1)S(1)}, f32[3,64,128]{2,1,0:T(8,128)S(1)}, f32[6,1,128]{2,1,0:T(1,128)S(1)}) custom-call(f32[1024,1152]{1,0:T(8,128)S(1)} %fusion.195.qkv_ref, f32[1024,768]{1,0:T(8,128)S(1)} %pad_maximum_fusion.5.cap_ref, ...), custom_call_target="tpu_custom_call" | custom-call | flops 3019898880 | bytes 10616832 | tf_op jit(solution)/shard_map/pallas_call | solution.py:285
  424.1 6.7 %fusion.46 = bf16[768,1024]{1,0:T(8,128)(2,1)} fusion(bf16[768,2048]{1,0:T(8,128)(2,1)S(1)} %bitcast.205, bf16[2048,4096]{1,0:T(8,128)(2,1)} %constant_dynamic-update-slice_fusion.6, s32[]{:T(128)S(6)} %select_n.418), kind=kOutput, calls=%fused_computation.113 | convolution fusion | flops 3222011904 | bytes 8912900 | tf_op jit(solution)/shard_map/tc,ce->te/dot_general | solution.py:27
  430.8 6.9 %fusion.43 = bf16[768,1024]{1,0:T(8,128)(2,1)} fusion(bf16[768,2048]{1,0:T(8,128)(2,1)S(1)} %bitcast.206, bf16[2048,4096]{1,0:T(8,128)(2,1)} %constant_dynamic-update-slice_fusion.6, s32[]{:T(128)S(6)} %select_n.417), kind=kOutput, calls=%fused_computation.112 | convolution fusion | flops 3222011904 | bytes 8912900 | tf_op jit(solution)/shard_map/tc,ce->te/dot_general | solution.py:27
  438.0 6.6 %fusion.24 = bf16[384,2048]{1,0:T(8,128)(2,1)} fusion(bf16[2048,1024]{1,0:T(8,128)(2,1)S(1)} %copy-done.57, bf16[2048,1024]{1,0:T(8,128)(2,1)S(1)} %copy-done.56, bf16[768,2048]{1,0:T(8,128)(2,1)} %bitcast.207, s32[]{:T(128)S(6)} %select_n.413), kind=kOutput, calls=%fused_computation.43 | convolution fusion | flops 3238789120 | bytes 11534340 | tf_op jit(solution)/shard_map/tc,ce->te/dot_general | solution.py:27
  448.7 5.0 fusion.25
  470.2 20.9 %collective-permute-done.82 = bf16[1024,384]{1,0:T(8,128)(2,1)S(1)} collective-permute-done((bf16[1024,384]{1,0:T(8,128)(2,1)S(1)}, bf16[1024,384]{1,0:T(8,128)(2,1)S(1)}, u32[]{:S(2)}, u32[]{:S(2)}) %collective-permute-start.82) | collective-permute-done | bytes 786464 | tf_op jit(solution)/shard_map/ppermute | solution.py:407
  492.5 10.3 %collective-permute-done.66 = bf16[256,1536]{1,0:T(8,128)(2,1)S(1)} collective-permute-done((bf16[256,1536]{1,0:T(8,128)(2,1)S(1)}, bf16[256,1536]{1,0:T(8,128)(2,1)S(1)}, u32[]{:S(2)}, u32[]{:S(2)}) %collective-permute-start.66) | collective-permute-done | bytes 786464 | tf_op jit(solution)/shard_map/ppermute | solution.py:407
  512.8 3.6 collective-permute-done.69
  526.8 3.2 collective-permute-done.72
  536.6 13.3 %collective-permute-done.83 = bf16[192,1024]{1,0:T(8,128)(2,1)S(1)} collective-permute-done((bf16[192,1024]{1,0:T(8,128)(2,1)S(1)}, bf16[192,1024]{1,0:T(8,128)(2,1)S(1)}, u32[]{:S(2)}, u32[]{:S(2)}) %collective-permute-start.83) | collective-permute-done | bytes 393248 | tf_op jit(solution)/shard_map/ppermute | solution.py:407
  561.7 15.2 %collective-permute-done.73 = bf16[1152,384]{1,0:T(8,128)(2,1)S(1)} collective-permute-done((bf16[1152,384]{1,0:T(8,128)(2,1)S(1)}, bf16[1152,384]{1,0:T(8,128)(2,1)S(1)}, u32[]{:S(2)}, u32[]{:S(2)}) %collective-permute-start.73) | collective-permute-done | bytes 884768 | tf_op jit(solution)/shard_map/ppermute | solution.py:407
  581.4 4.9 collective-permute-done.75
  591.5 5.2 collective-permute-done.78
  598.1 17.6 %collective-permute-done.84 = bf16[384,1024]{1,0:T(8,128)(2,1)S(1)} collective-permute-done((bf16[384,1024]{1,0:T(8,128)(2,1)S(1)}, bf16[384,1024]{1,0:T(8,128)(2,1)S(1)}, u32[]{:S(2)}, u32[]{:S(2)}) %collective-permute-start.84) | collective-permute-done | bytes 786464 | tf_op jit(solution)/shard_map/ppermute | solution.py:407
  617.7 6.7 %collective-permute-done.85 = bf16[192,384]{1,0:T(8,128)(2,1)S(1)} collective-permute-done((bf16[192,384]{1,0:T(8,128)(2,1)S(1)}, bf16[192,384]{1,0:T(8,128)(2,1)S(1)}, u32[]{:S(2)}, u32[]{:S(2)}) %collective-permute-start.85) | collective-permute-done | bytes 147488 | tf_op jit(solution)/shard_map/ppermute | solution.py:407
  626.5 3.9 collective-permute-start.79
  636.3 18.7 %collective-permute-done.86 = bf16[576,384]{1,0:T(8,128)(2,1)S(1)} collective-permute-done((bf16[576,384]{1,0:T(8,128)(2,1)S(1)}, bf16[576,384]{1,0:T(8,128)(2,1)S(1)}, u32[]{:S(2)}, u32[]{:S(2)}) %collective-permute-start.86) | collective-permute-done | bytes 442400 | tf_op jit(solution)/shard_map/ppermute | solution.py:407
  (654 shorter events, 274.8 us)
Async XLA Ops:
  4.9 19.8 %collective-permute-start = (bf16[822]{0:T(1024)(128)(2,1)S(1)}, bf16[822]{0:T(1024)(128)(2,1)S(1)}, u32[]{:S(2)}, u32[]{:S(2)}) collective-permute-start(bf16[822]{0:T(1024)(128)(2,1)S(1)} %concatenate.141), channel_id=1, source_target_pairs={{0,1},{1,0},{2,3},{3,2},{4,5},{5,4},{6,7},{7,6},{8,9},{9,8},{10,11... | collective-permute-start | bytes 4940 | tf_op jit(solution)/shard_map/ppermute | solution.py:407
  9.8 28.9 %collective-permute-start.2 = (bf16[384,1152]{1,0:T(8,128)(2,1)}, bf16[384,1152]{1,0:T(8,128)(2,1)}, u32[]{:S(2)}, u32[]{:S(2)}) collective-permute-start(bf16[384,1152]{1,0:T(8,128)(2,1)} %pad_maximum_fusion.28), channel_id=1, source_target_pairs={{0,2},{1,3},{2,0},{3,1},{4,7},{5,6},{6,5},{7,4},{8,10},{9,11},{10,... | collective-permute-start | bytes 2654216 | tf_op jit(solution)/shard_map/ppermute | solution.py:407
  14.6 25.5 %collective-permute-start.3 = (bf16[128,4096]{1,0:T(8,128)(2,1)}, bf16[128,4096]{1,0:T(8,128)(2,1)}, u32[]{:S(2)}, u32[]{:S(2)}) collective-permute-start(bf16[128,4096]{1,0:T(8,128)(2,1)} %get-tuple-element.307), channel_id=1, source_target_pairs={{0,8},{1,9},{2,10},{3,11},{4,12},{5,13},{6,14},{7,15},{8,0},{9,1},... | collective-permute-start | bytes 3145736 | tf_op jit(solution)/shard_map/ppermute | solution.py:407
  46.9 23.4 %collective-permute-start.7 = (bf16[256,1664]{0,1:T(8,128)(2,1)}, bf16[256,1664]{0,1:T(8,128)(2,1)}, u32[]{:S(2)}, u32[]{:S(2)}) collective-permute-start(bf16[256,1664]{0,1:T(8,128)(2,1)} %pad_maximum_fusion.30), channel_id=1, source_target_pairs={{0,8},{1,9},{2,10},{3,11},{4,12},{5,13},{6,14},{7,15},{8,0},{9,1},... | collective-permute-start | bytes 2555912 | tf_op jit(solution)/shard_map/ppermute | solution.py:407
  48.5 22.1 %collective-permute-start.9 = (bf16[384,1152]{1,0:T(8,128)(2,1)}, bf16[384,1152]{1,0:T(8,128)(2,1)}, u32[]{:S(2)}, u32[]{:S(2)}) collective-permute-start(bf16[384,1152]{1,0:T(8,128)(2,1)} %collective-permute-done.2.refs_4_), channel_id=1, source_target_pairs={{0,4},{1,5},{2,6},{3,7},{4,0},{5,1},{6,2},{7,3},{8,12},{9,13},{10,... | collective-permute-start | bytes 2654216 | tf_op jit(solution)/shard_map/ppermute | solution.py:407
  50.0 20.6 %collective-permute-start.6 = (bf16[256,1664]{0,1:T(8,128)(2,1)}, bf16[256,1664]{0,1:T(8,128)(2,1)}, u32[]{:S(2)}, u32[]{:S(2)}) collective-permute-start(bf16[256,1664]{0,1:T(8,128)(2,1)} %pad_maximum_fusion.30), channel_id=1, source_target_pairs={{0,1},{1,0},{2,3},{3,2},{4,5},{5,4},{6,7},{7,6},{8,9},{9,8},{10,11... | collective-permute-start | bytes 2555912 | tf_op jit(solution)/shard_map/ppermute | solution.py:407
  50.3 20.1 %collective-permute-start.8 = (bf16[512,768]{1,0:T(8,128)(2,1)}, bf16[512,768]{1,0:T(8,128)(2,1)}, u32[]{:S(2)}, u32[]{:S(2)}) collective-permute-start(bf16[512,768]{1,0:T(8,128)(2,1)} %get-tuple-element.132), channel_id=1, source_target_pairs={{0,2},{1,3},{2,0},{3,1},{4,7},{5,6},{6,5},{7,4},{8,10},{9,11},{10,... | collective-permute-start | bytes 2359304 | tf_op jit(solution)/shard_map/ppermute | solution.py:407
  76.0 25.6 %collective-permute-start.13 = (bf16[128,4096]{1,0:T(8,128)(2,1)S(1)}, bf16[128,4096]{1,0:T(8,128)(2,1)S(1)}, u32[]{:S(2)}, u32[]{:S(2)}) collective-permute-start(bf16[128,4096]{1,0:T(8,128)(2,1)S(1)} %copy-done.96), channel_id=1, source_target_pairs={{0,8},{1,9},{2,10},{3,11},{4,12},{5,13},{6,14},{7,15},{8,0},{9,1},... | collective-permute-start | bytes 3145736 | tf_op jit(solution)/shard_map/ppermute | solution.py:407
  76.5 27.0 %collective-permute-start.14 = (bf16[1024,768]{1,0:T(8,128)(2,1)S(1)}, bf16[1024,768]{1,0:T(8,128)(2,1)S(1)}, u32[]{:S(2)}, u32[]{:S(2)}) collective-permute-start(bf16[1024,768]{1,0:T(8,128)(2,1)S(1)} %copy-done.80), channel_id=1, source_target_pairs={{0,1},{1,0},{2,3},{3,2},{4,5},{5,4},{6,7},{7,6},{8,9},{9,8},{10,11... | collective-permute-start | bytes 4718600 | tf_op jit(solution)/shard_map/ppermute | solution.py:407
  80.3 23.1 %collective-permute-start.11 = (bf16[512,768]{1,0:T(8,128)(2,1)S(1)}, bf16[512,768]{1,0:T(8,128)(2,1)S(1)}, u32[]{:S(2)}, u32[]{:S(2)}) collective-permute-start(bf16[512,768]{1,0:T(8,128)(2,1)S(1)} %copy-done.106), channel_id=1, source_target_pairs={{0,2},{1,3},{2,0},{3,1},{4,7},{5,6},{6,5},{7,4},{8,10},{9,11},{10,... | collective-permute-start | bytes 2359304 | tf_op jit(solution)/shard_map/ppermute | solution.py:407
  80.9 22.6 %collective-permute-start.12 = (bf16[512,768]{1,0:T(8,128)(2,1)}, bf16[512,768]{1,0:T(8,128)(2,1)S(1)}, u32[]{:S(2)}, u32[]{:S(2)}) collective-permute-start(bf16[512,768]{1,0:T(8,128)(2,1)} %collective-permute-done.8.refs_3_), channel_id=1, source_target_pairs={{0,4},{1,5},{2,6},{3,7},{4,0},{5,1},{6,2},{7,3},{8,12},{9,13},{10,... | collective-permute-start | bytes 2359304 | tf_op jit(solution)/shard_map/ppermute | solution.py:407
  103.5 34.6 %collective-permute-start.19 = (bf16[256,4096]{1,0:T(8,128)(2,1)S(1)}, bf16[256,4096]{1,0:T(8,128)(2,1)S(1)}, u32[]{:S(2)}, u32[]{:S(2)}) collective-permute-start(bf16[256,4096]{1,0:T(8,128)(2,1)S(1)} %pad_maximum_fusion.13), channel_id=1, source_target_pairs={{0,1},{1,0},{2,3},{3,2},{4,5},{5,4},{6,7},{7,6},{8,9},{9,8},{10,11... | collective-permute-start | bytes 6291464 | tf_op jit(solution)/shard_map/ppermute | solution.py:407
  111.0 24.4 %collective-permute-start.16 = (bf16[192,2048]{1,0:T(8,128)(2,1)S(1)}, bf16[192,2048]{1,0:T(8,128)(2,1)}, u32[]{:S(2)}, u32[]{:S(2)}) collective-permute-start(bf16[192,2048]{1,0:T(8,128)(2,1)S(1)} %copy-done.105), channel_id=1, source_target_pairs={{0,2},{1,3},{2,0},{3,1},{4,7},{5,6},{6,5},{7,4},{8,10},{9,11},{10,... | collective-permute-start | bytes 2359304 | tf_op jit(solution)/shard_map/ppermute | solution.py:407
  111.8 23.6 %collective-permute-start.17 = (bf16[512,768]{1,0:T(8,128)(2,1)S(1)}, bf16[512,768]{1,0:T(8,128)(2,1)S(1)}, u32[]{:S(2)}, u32[]{:S(2)}) collective-permute-start(bf16[512,768]{1,0:T(8,128)(2,1)S(1)} %collective-permute-done.11.refs_5_), channel_id=1, source_target_pairs={{0,4},{1,5},{2,6},{3,7},{4,0},{5,1},{6,2},{7,3},{8,12},{9,13},{10,... | collective-permute-start | bytes 2359304 | tf_op jit(solution)/shard_map/ppermute | solution.py:407
  112.6 25.6 %collective-permute-start.18 = (bf16[128,4096]{1,0:T(8,128)(2,1)S(1)}, bf16[128,4096]{1,0:T(8,128)(2,1)S(1)}, u32[]{:S(2)}, u32[]{:S(2)}) collective-permute-start(bf16[128,4096]{1,0:T(8,128)(2,1)S(1)} %copy-done.95), channel_id=1, source_target_pairs={{0,8},{1,9},{2,10},{3,11},{4,12},{5,13},{6,14},{7,15},{8,0},{9,1},... | collective-permute-start | bytes 3145736 | tf_op jit(solution)/shard_map/ppermute | solution.py:407
  138.2 33.0 %collective-permute-start.21 = (bf16[192,1536]{1,0:T(8,128)(2,1)}, bf16[192,1536]{1,0:T(8,128)(2,1)}, u32[]{:S(2)}, u32[]{:S(2)}) collective-permute-start(bf16[192,1536]{1,0:T(8,128)(2,1)} %collective-permute-done.15), channel_id=1, source_target_pairs={{1,5},{2,6},{5,1},{6,2},{9,13},{10,14},{13,9},{14,10},{17,21},{18,... | collective-permute-start | bytes 1769480 | tf_op jit(solution)/shard_map/ppermute | solution.py:407
  139.9 31.2 %collective-permute-start.20 = (bf16[192,2048]{1,0:T(8,128)(2,1)}, bf16[192,2048]{1,0:T(8,128)(2,1)}, u32[]{:S(2)}, u32[]{:S(2)}) collective-permute-start(bf16[192,2048]{1,0:T(8,128)(2,1)} %get-tuple-element.149), channel_id=1, source_target_pairs={{0,2},{1,3},{2,0},{3,1},{4,7},{5,6},{6,5},{7,4},{8,10},{9,11},{10,... | collective-permute-start | bytes 2359304 | tf_op jit(solution)/shard_map/ppermute | solution.py:407
  142.4 28.8 %collective-permute-start.22 = (bf16[192,2048]{1,0:T(8,128)(2,1)}, bf16[192,2048]{1,0:T(8,128)(2,1)}, u32[]{:S(2)}, u32[]{:S(2)}) collective-permute-start(bf16[192,2048]{1,0:T(8,128)(2,1)} %collective-permute-done.16.refs_3_), channel_id=1, source_target_pairs={{0,4},{1,5},{2,6},{3,7},{4,0},{5,1},{6,2},{7,3},{8,12},{9,13},{10,... | collective-permute-start | bytes 2359304 | tf_op jit(solution)/shard_map/ppermute | solution.py:407
  142.4 26.0 %collective-permute-start.23 = (bf16[128,4096]{1,0:T(8,128)(2,1)}, bf16[128,4096]{1,0:T(8,128)(2,1)}, u32[]{:S(2)}, u32[]{:S(2)}) collective-permute-start(bf16[128,4096]{1,0:T(8,128)(2,1)} %get-tuple-element.152), channel_id=1, source_target_pairs={{0,8},{1,9},{2,10},{3,11},{4,12},{5,13},{6,14},{7,15},{8,0},{9,1},... | collective-permute-start | bytes 3145736 | tf_op jit(solution)/shard_map/ppermute | solution.py:407
  142.7 28.5 %collective-permute-start.24 = (bf16[384,2048]{1,0:T(8,128)(2,1)}, bf16[384,2048]{1,0:T(8,128)(2,1)S(1)}, u32[]{:S(2)}, u32[]{:S(2)}) collective-permute-start(bf16[384,2048]{1,0:T(8,128)(2,1)} %pad_maximum_fusion.18), channel_id=1, source_target_pairs={{0,1},{1,0},{2,3},{3,2},{4,5},{5,4},{6,7},{7,6},{8,9},{9,8},{10,11... | collective-permute-start | bytes 4718600 | tf_op jit(solution)/shard_map/ppermute | solution.py:407
  206.2 27.6 %collective-permute-start.36 = (bf16[512,1536]{1,0:T(8,128)(2,1)}, bf16[512,1536]{1,0:T(8,128)(2,1)}, u32[]{:S(2)}, u32[]{:S(2)}) collective-permute-start(bf16[512,1536]{1,0:T(8,128)(2,1)} %constant_dynamic-slice_fusion), channel_id=1, source_target_pairs={{0,2},{2,1},{4,6},{6,5},{9,10},{11,9},{13,14},{15,13},{16,18},{18,... | collective-permute-start | bytes 4718600 | tf_op jit(solution)/shard_map/ppermute | solution.py:407
  221.4 30.0 %collective-permute-start.32 = (bf16[1024,1536]{1,0:T(8,128)(2,1)}, bf16[1024,1536]{1,0:T(8,128)(2,1)S(1)}, u32[]{:S(2)}, u32[]{:S(2)}) collective-permute-start(bf16[1024,1536]{1,0:T(8,128)(2,1)} %param.44), channel_id=1, source_target_pairs={{2,3},{6,7},{9,8},{13,12},{18,19},{22,23},{25,24},{29,28}} | collective-permute-start | bytes 9437192 | tf_op jit(solution)/shard_map/ppermute | solution.py:407
  226.1 20.2 %collective-permute-start.31 = (bf16[256,1536]{1,0:T(8,128)(2,1)S(1)}, bf16[256,1536]{1,0:T(8,128)(2,1)S(1)}, u32[]{:S(2)}, u32[]{:S(2)}) collective-permute-start(bf16[256,1536]{1,0:T(8,128)(2,1)S(1)} %fusion.33), channel_id=1, source_target_pairs={{0,8},{1,9},{2,10},{3,11},{4,12},{5,13},{6,14},{7,15},{8,0},{9,1},... | collective-permute-start | bytes 2359304 | tf_op jit(solution)/shard_map/ppermute | solution.py:407
  308.4 28.4 %collective-permute-start.42 = (bf16[256,1536]{1,0:T(8,128)(2,1)}, bf16[256,1536]{1,0:T(8,128)(2,1)}, u32[]{:S(2)}, u32[]{:S(2)}) collective-permute-start(bf16[256,1536]{1,0:T(8,128)(2,1)} %fusion.35), channel_id=1, source_target_pairs={{0,8},{1,9},{2,10},{3,11},{4,12},{5,13},{6,14},{7,15},{8,0},{9,1},... | collective-permute-start | bytes 2359304 | tf_op jit(solution)/shard_map/ppermute | solution.py:407
  313.6 23.0 %collective-permute-start.41 = (bf16[256,1536]{1,0:T(8,128)(2,1)}, bf16[256,1536]{1,0:T(8,128)(2,1)}, u32[]{:S(2)}, u32[]{:S(2)}) collective-permute-start(bf16[256,1536]{1,0:T(8,128)(2,1)} %convolution_convert_fusion.3), channel_id=1, source_target_pairs={{0,1},{1,0},{2,3},{3,2},{4,5},{5,4},{6,7},{7,6},{8,9},{9,8},{10,11... | collective-permute-start | bytes 2359304 | tf_op jit(solution)/shard_map/ppermute | solution.py:407
  316.0 62.4 %collective-permute-start.47 = (bf16[1024,768]{1,0:T(8,128)(2,1)}, bf16[1024,768]{1,0:T(8,128)(2,1)}, u32[]{:S(2)}, u32[]{:S(2)}) collective-permute-start(bf16[1024,768]{1,0:T(8,128)(2,1)} %add_convert_fusion.1), channel_id=1, source_target_pairs={{0,2},{1,3},{2,0},{3,1},{4,6},{5,7},{6,4},{7,5},{8,10},{9,11},{10,... | collective-permute-start | bytes 4718600 | tf_op jit(solution)/shard_map/ppermute | solution.py:407
  319.5 59.0 %collective-permute-start.48 = (bf16[512,1536]{1,0:T(8,128)(2,1)}, bf16[512,1536]{1,0:T(8,128)(2,1)}, u32[]{:S(2)}, u32[]{:S(2)}) collective-permute-start(bf16[512,1536]{1,0:T(8,128)(2,1)} %fusion.22), channel_id=1, source_target_pairs={{0,4},{1,5},{2,6},{3,7},{4,0},{5,1},{6,2},{7,3},{8,12},{9,13},{10,... | collective-permute-start | bytes 4718600 | tf_op jit(solution)/shard_map/ppermute | solution.py:407
  342.3 20.0 %collective-permute-start.45 = (bf16[256,1536]{1,0:T(8,128)(2,1)S(1)}, bf16[256,1536]{1,0:T(8,128)(2,1)}, u32[]{:S(2)}, u32[]{:S(2)}) collective-permute-start(bf16[256,1536]{1,0:T(8,128)(2,1)S(1)} %bitcast.216), channel_id=1, source_target_pairs={{0,8},{1,9},{2,10},{3,11},{4,12},{5,13},{6,14},{7,15},{8,0},{9,1},... | collective-permute-start | bytes 2359304 | tf_op jit(solution)/shard_map/ppermute | solution.py:407
  342.4 19.9 %collective-permute-start.44 = (bf16[256,1536]{1,0:T(8,128)(2,1)S(1)}, bf16[256,1536]{1,0:T(8,128)(2,1)S(1)}, u32[]{:S(2)}, u32[]{:S(2)}) collective-permute-start(bf16[256,1536]{1,0:T(8,128)(2,1)S(1)} %bitcast.217), channel_id=1, source_target_pairs={{0,1},{1,0},{2,3},{3,2},{4,5},{5,4},{6,7},{7,6},{8,9},{9,8},{10,11... | collective-permute-start | bytes 2359304 | tf_op jit(solution)/shard_map/ppermute | solution.py:407
  362.3 22.7 %collective-permute-start.46 = (bf16[256,1536]{1,0:T(8,128)(2,1)}, bf16[256,1536]{1,0:T(8,128)(2,1)S(1)}, u32[]{:S(2)}, u32[]{:S(2)}) collective-permute-start(bf16[256,1536]{1,0:T(8,128)(2,1)} %collective-permute-done.45), channel_id=1, source_target_pairs={{0,1},{1,0},{2,3},{3,2},{4,5},{5,4},{6,7},{7,6},{8,9},{9,8},{10,11... | collective-permute-start | bytes 2359304 | tf_op jit(solution)/shard_map/ppermute | solution.py:407
  382.0 22.8 %collective-permute-start.49 = (bf16[512,768]{1,0:T(8,128)(2,1)}, bf16[512,768]{1,0:T(8,128)(2,1)}, u32[]{:S(2)}, u32[]{:S(2)}) collective-permute-start(bf16[512,768]{1,0:T(8,128)(2,1)} %add_convert_fusion.8), channel_id=1, source_target_pairs={{0,2},{1,3},{2,0},{3,1},{4,6},{5,7},{6,4},{7,5},{8,10},{9,11},{10,... | collective-permute-start | bytes 2359304 | tf_op jit(solution)/shard_map/ppermute | solution.py:407
  383.9 29.5 %collective-permute-start.50 = (bf16[512,768]{1,0:T(8,128)(2,1)S(1)}, bf16[512,768]{1,0:T(8,128)(2,1)}, u32[]{:S(2)}, u32[]{:S(2)}) collective-permute-start(bf16[512,768]{1,0:T(8,128)(2,1)S(1)} %add_convert_fusion.9), channel_id=1, source_target_pairs={{0,4},{1,5},{2,6},{3,7},{4,0},{5,1},{6,2},{7,3},{8,12},{9,13},{10,... | collective-permute-start | bytes 2359304 | tf_op jit(solution)/shard_map/ppermute | solution.py:407
  420.9 32.8 %collective-permute-start.59 = (bf16[1024,384]{1,0:T(8,128)(2,1)}, bf16[1024,384]{1,0:T(8,128)(2,1)S(1)}, u32[]{:S(2)}, u32[]{:S(2)}) collective-permute-start(bf16[1024,384]{1,0:T(8,128)(2,1)} %pad_maximum_fusion.34), channel_id=1, source_target_pairs={{0,1},{1,0},{2,3},{3,2},{4,5},{5,4},{6,7},{7,6},{8,9},{9,8},{10,11... | collective-permute-start | bytes 2359304 | tf_op jit(solution)/shard_map/ppermute | solution.py:407
  423.1 33.5 %collective-permute-start.53 = (bf16[384,1024]{1,0:T(8,128)(2,1)}, bf16[384,1024]{1,0:T(8,128)(2,1)}, u32[]{:S(2)}, u32[]{:S(2)}) collective-permute-start(bf16[384,1024]{1,0:T(8,128)(2,1)} %get-tuple-element.195), channel_id=1, source_target_pairs={{0,2},{1,3},{2,0},{3,1},{4,6},{5,7},{6,4},{7,5},{8,10},{9,11},{10,... | collective-permute-start | bytes 2359304 | tf_op jit(solution)/shard_map/ppermute | solution.py:407
  423.2 33.4 %collective-permute-start.51 = (bf16[192,2048]{1,0:T(8,128)(2,1)}, bf16[192,2048]{1,0:T(8,128)(2,1)S(1)}, u32[]{:S(2)}, u32[]{:S(2)}) collective-permute-start(bf16[192,2048]{1,0:T(8,128)(2,1)} %get-tuple-element.196), channel_id=1, source_target_pairs={{0,4},{1,5},{2,6},{3,7},{4,0},{5,1},{6,2},{7,3},{8,12},{9,13},{10,... | collective-permute-start | bytes 2359304 | tf_op jit(solution)/shard_map/ppermute | solution.py:407
  453.9 37.1 %collective-permute-start.82 = (bf16[1024,384]{1,0:T(8,128)(2,1)S(1)}, bf16[1024,384]{1,0:T(8,128)(2,1)S(1)}, u32[]{:S(2)}, u32[]{:S(2)}) collective-permute-start(bf16[1024,384]{1,0:T(8,128)(2,1)S(1)} %broadcast_select_fusion.2), channel_id=1, source_target_pairs={{0,16},{1,17},{2,18},{3,19},{4,20},{5,21},{6,22},{7,23},{8,24},{9,... | collective-permute-start | bytes 2359304 | tf_op jit(solution)/shard_map/ppermute | solution.py:407
  456.6 63.7 %collective-permute-start.52 = (bf16[384,2048]{1,0:T(8,128)(2,1)}, bf16[384,2048]{1,0:T(8,128)(2,1)}, u32[]{:S(2)}, u32[]{:S(2)}) collective-permute-start(bf16[384,2048]{1,0:T(8,128)(2,1)} %fusion.25), channel_id=1, source_target_pairs={{0,4},{1,5},{2,6},{3,7},{4,0},{5,1},{6,2},{7,3},{8,12},{9,13},{10,... | collective-permute-start | bytes 4718600 | tf_op jit(solution)/shard_map/ppermute | solution.py:407
  457.7 63.7 %collective-permute-start.54 = (bf16[768,1024]{1,0:T(8,128)(2,1)}, bf16[768,1024]{1,0:T(8,128)(2,1)}, u32[]{:S(2)}, u32[]{:S(2)}) collective-permute-start(bf16[768,1024]{1,0:T(8,128)(2,1)} %fusion.43), channel_id=1, source_target_pairs={{0,2},{1,3},{2,0},{3,1},{4,6},{5,7},{6,4},{7,5},{8,10},{9,11},{10,... | collective-permute-start | bytes 4718600 | tf_op jit(solution)/shard_map/ppermute | solution.py:407
  466.0 26.5 %collective-permute-start.61 = (bf16[256,1536]{1,0:T(8,128)(2,1)S(1)}, bf16[256,1536]{1,0:T(8,128)(2,1)S(1)}, u32[]{:S(2)}, u32[]{:S(2)}) collective-permute-start(bf16[256,1536]{1,0:T(8,128)(2,1)S(1)} %convolution_convert_fusion.9), channel_id=1, source_target_pairs={{0,1},{1,0},{2,3},{3,2},{4,5},{5,4},{6,7},{7,6},{8,9},{9,8},{10,11... | collective-permute-start | bytes 2359304 | tf_op jit(solution)/shard_map/ppermute | solution.py:407
  466.1 36.7 %collective-permute-start.66 = (bf16[256,1536]{1,0:T(8,128)(2,1)S(1)}, bf16[256,1536]{1,0:T(8,128)(2,1)S(1)}, u32[]{:S(2)}, u32[]{:S(2)}) collective-permute-start(bf16[256,1536]{1,0:T(8,128)(2,1)S(1)} %fusion.36), channel_id=1, source_target_pairs={{0,8},{1,9},{2,10},{3,11},{4,12},{5,13},{6,14},{7,15},{8,0},{9,1},... | collective-permute-start | bytes 2359304 | tf_op jit(solution)/shard_map/ppermute | solution.py:407
  512.1 24.3 %collective-permute-start.62 = (bf16[2,384,384]{2,1,0:T(8,128)(2,1)}, bf16[2,384,384]{2,1,0:T(8,128)(2,1)S(1)}, u32[]{:S(2)}, u32[]{:S(2)}) collective-permute-start(bf16[2,384,384]{2,1,0:T(8,128)(2,1)} %dynamic-slice_bitcast_fusion.1), channel_id=1, source_target_pairs={{0,1},{1,0},{2,3},{3,2},{4,5},{5,4},{6,7},{7,6},{8,9},{9,8},{10,11... | collective-permute-start | bytes 1769480 | tf_op jit(solution)/shard_map/ppermute | solution.py:407
  555.2 21.6 %collective-permute-start.73 = (bf16[1152,384]{1,0:T(8,128)(2,1)S(1)}, bf16[1152,384]{1,0:T(8,128)(2,1)S(1)}, u32[]{:S(2)}, u32[]{:S(2)}) collective-permute-start(bf16[1152,384]{1,0:T(8,128)(2,1)S(1)} %copy-done.137), channel_id=1, source_target_pairs={{0,2},{1,3},{2,0},{3,1},{4,6},{5,7},{6,4},{7,5},{8,10},{9,11},{10,... | collective-permute-start | bytes 2654216 | tf_op jit(solution)/shard_map/ppermute | solution.py:407
  556.8 21.6 %collective-permute-start.74 = (bf16[576,768]{1,0:T(8,128)(2,1)S(1)}, bf16[576,768]{1,0:T(8,128)(2,1)S(1)}, u32[]{:S(2)}, u32[]{:S(2)}) collective-permute-start(bf16[576,768]{1,0:T(8,128)(2,1)S(1)} %copy-done.138), channel_id=1, source_target_pairs={{0,4},{1,5},{2,6},{3,7},{4,0},{5,1},{6,2},{7,3},{8,12},{9,13},{10,... | collective-permute-start | bytes 2654216 | tf_op jit(solution)/shard_map/ppermute | solution.py:407
  560.9 26.9 %collective-permute-start.64 = (bf16[256,1536]{1,0:T(8,128)(2,1)S(1)}, bf16[256,1536]{1,0:T(8,128)(2,1)S(1)}, u32[]{:S(2)}, u32[]{:S(2)}) collective-permute-start(bf16[256,1536]{1,0:T(8,128)(2,1)S(1)} %convolution_convert_fusion.2), channel_id=1, source_target_pairs={{0,1},{1,0},{2,3},{3,2},{4,5},{5,4},{6,7},{7,6},{8,9},{9,8},{10,11... | collective-permute-start | bytes 2359304 | tf_op jit(solution)/shard_map/ppermute | solution.py:407
  579.6 36.0 %collective-permute-start.84 = (bf16[384,1024]{1,0:T(8,128)(2,1)S(1)}, bf16[384,1024]{1,0:T(8,128)(2,1)S(1)}, u32[]{:S(2)}, u32[]{:S(2)}) collective-permute-start(bf16[384,1024]{1,0:T(8,128)(2,1)S(1)} %broadcast_select_fusion.3), channel_id=1, source_target_pairs={{0,16},{1,17},{2,18},{3,19},{4,20},{5,21},{6,22},{7,23},{8,24},{9,... | collective-permute-start | bytes 2359304 | tf_op jit(solution)/shard_map/ppermute | solution.py:407
  589.0 37.5 %collective-permute-start.65 = (bf16[256,1536]{1,0:T(8,128)(2,1)S(1)}, bf16[256,1536]{1,0:T(8,128)(2,1)S(1)}, u32[]{:S(2)}, u32[]{:S(2)}) collective-permute-start(bf16[256,1536]{1,0:T(8,128)(2,1)S(1)} %copy-done.139), channel_id=1, source_target_pairs={{0,1},{1,0},{2,3},{3,2},{4,5},{5,4},{6,7},{7,6},{8,9},{9,8},{10,11... | collective-permute-start | bytes 2359304 | tf_op jit(solution)/shard_map/ppermute | solution.py:407
  589.0 41.4 %collective-permute-start.67 = (bf16[256,1536]{1,0:T(8,128)(2,1)S(1)}, bf16[256,1536]{1,0:T(8,128)(2,1)S(1)}, u32[]{:S(2)}, u32[]{:S(2)}) collective-permute-start(bf16[256,1536]{1,0:T(8,128)(2,1)S(1)} %fusion.34), channel_id=1, source_target_pairs={{0,8},{1,9},{2,10},{3,11},{4,12},{5,13},{6,14},{7,15},{8,0},{9,1},... | collective-permute-start | bytes 2359304 | tf_op jit(solution)/shard_map/ppermute | solution.py:407
  632.5 22.5 %collective-permute-start.86 = (bf16[576,384]{1,0:T(8,128)(2,1)S(1)}, bf16[576,384]{1,0:T(8,128)(2,1)S(1)}, u32[]{:S(2)}, u32[]{:S(2)}) collective-permute-start(bf16[576,384]{1,0:T(8,128)(2,1)S(1)} %broadcast_select_fusion.10), channel_id=1, source_target_pairs={{0,16},{1,17},{2,18},{3,19},{4,20},{5,21},{6,22},{7,23},{8,24},{9,... | collective-permute-start | bytes 1327112 | tf_op jit(solution)/shard_map/ppermute | solution.py:407
  (189 other events, 1692.0 us)

commit v3 on v2

v3 whole, which is shorter than its diff:
```python
import functools
import math

import jax
import jax.numpy as jnp
from jax import lax
from jax.experimental import pallas as pl
from jax.experimental.pallas import tpu as pltpu
from jax.sharding import PartitionSpec as P

EPSILON = 1e-06
NEGATIVE = -1e30
BF16 = jnp.bfloat16
F32 = jnp.float32
SMALL_COST = pl.CostEstimate(flops=1024, bytes_accessed=1024, transcendentals=0)


def rms_scale(values):
    inverse = lax.rsqrt(jnp.mean(values * values, axis=-1, keepdims=True) + EPSILON)
    return (values * inverse, inverse)


def rms_back(incoming, normed, inverse):
    return inverse * (incoming - normed * jnp.mean(incoming * normed, axis=-1, keepdims=True))


def dot(left, right):
    return jnp.einsum("tc,ce->te", left, right, preferred_element_type=F32)


def dot_back(incoming, weight):
    return jnp.einsum("te,ce->tc", incoming, weight, preferred_element_type=F32)


def dot_tokens(left, right):
    return jnp.einsum("tc,te->ce", left, right, preferred_element_type=F32)


def after(value, *others):
    if not others:
        return value
    return lax.optimization_barrier((value,) + others)[0]


def join_rows_kernel(place_ref, shard, near, across, far, out, sems):
    half = across.shape[0]
    source, lane = place_ref[0], place_ref[1]

    def copy(piece, row, count, sem):
        item = pltpu.make_async_copy(piece, out.at[pl.ds(row, count)], sem)
        item.start()
        return item

    @pl.when(source == 0)
    def _():
        copy(shard, 0, 2 * half, sems.at[0]).wait()

    @pl.when(source == 1)
    def _():
        copy(near, 0, 2 * half, sems.at[0]).wait()

    @pl.when(source == 2)
    def _():
        first = copy(across, pl.multiple_of(lane * half, 16), half, sems.at[0])
        second = copy(far, pl.multiple_of((1 - lane) * half, 16), half, sems.at[1])
        first.wait()
        second.wait()


def join_rows(index, shard, near, across, far):
    return pl.pallas_call(
        join_rows_kernel,
        grid_spec=pltpu.PrefetchScalarGridSpec(
            num_scalar_prefetch=1,
            grid=(1,),
            in_specs=[pl.BlockSpec(memory_space=pl.ANY)] * 4,
            out_specs=pl.BlockSpec(shard.shape, lambda i, place: (0, 0)),
            scratch_shapes=[pltpu.SemaphoreType.DMA((2,))],
        ),
        out_shape=jax.ShapeDtypeStruct(shard.shape, shard.dtype),
        compiler_params=pltpu.CompilerParams(vmem_limit_bytes=32 * 1024 * 1024),
        cost_estimate=SMALL_COST,
    )(index, shard, near, across, far)


def quarter_turn(values):
    heads, size, tokens = values.shape
    parts = values.reshape(heads, 2, 2, size // 4, tokens)
    turned = jnp.concatenate([-parts[:, :, 1:], parts[:, :, :1]], axis=2)
    return turned.reshape(heads, size, tokens)


def head_norm(raw):
    inverse = lax.rsqrt(jnp.mean(raw * raw, axis=1, keepdims=True) + EPSILON)
    return raw * inverse, inverse


def head_norm_back(incoming, normed, inverse, gain):
    scaled = incoming * gain
    return inverse * (scaled - normed * jnp.mean(scaled * normed, axis=1, keepdims=True))


def dot00(left, right):
    return lax.dot_general(left, right, (((0,), (0,)), ((), ())), preferred_element_type=F32)


def dot11(left, right):
    return lax.dot_general(left, right, (((1,), (1,)), ((), ())), preferred_element_type=F32)


def dot10(left, right):
    return lax.dot_general(left, right, (((1,), (0,)), ((), ())), preferred_element_type=F32)


def softmax0(scores):
    top = jnp.max(scores, axis=0, keepdims=True)
    raised = jnp.exp(scores - top)
    return raised * (1.0 / jnp.sum(raised, axis=0, keepdims=True))


def row_state(qkv, cap, cos_table, sin_table, marks, gains, heads, size):
    tokens, cap_tokens = qkv.shape[0], cap.shape[0]
    across = heads * size
    qkv = qkv.T
    cap = cap.T

    def split(values, at):
        return values[at * across : (at + 1) * across].reshape(heads, size, -1)

    query_normed, query_inverse = head_norm(split(qkv, 0))
    key_normed, key_inverse = head_norm(split(qkv, 1))
    cap_normed, cap_inverse = head_norm(split(cap, 0))

    def rotate(values):
        return (values * cos_table + quarter_turn(values) * sin_table).astype(BF16)

    segment = marks[0:1]
    key_segment = jnp.broadcast_to(segment, (tokens, tokens)).T
    return {
        "queries": rotate(query_normed * gains[0]),
        "keys": rotate(key_normed * gains[1]),
        "values": split(qkv, 2).astype(BF16),
        "cap_keys": (cap_normed * gains[2][:, :1]).astype(BF16),
        "cap_values": split(cap, 1).astype(BF16),
        "norms": (query_normed, query_inverse, key_normed, key_inverse, cap_normed, cap_inverse),
        "same": key_segment == segment,
        "in_use": lax.broadcasted_iota(jnp.int32, (cap_tokens, tokens), 0).astype(F32)
        < marks[1:2],
    }


def forward_kernel(
    heads,
    size,
    half,
    qkv_ref,
    first_ref,
    second_ref,
    weight_ref,
    cos_ref,
    sin_ref,
    marks_ref,
    gains_ref,
    tanh_ref,
    raw_ref,
    mixed_ref,
    cross_ref,
):
    step = pl.program_id(0)

    @pl.when(step < half)
    def _():
        raw_ref[...] = dot10(first_ref[...], weight_ref[...])

    @pl.when(step >= half)
    def _():
        raw_ref[...] = dot10(second_ref[...], weight_ref[...])

    state = row_state(
        qkv_ref[...], raw_ref[...], cos_ref[...], sin_ref[...], marks_ref[0], gains_ref[...], heads, size
    )
    scaling = 1.0 / math.sqrt(size)
    mixed = []
    for head in range(heads):
        queries = state["queries"][head]
        scores = dot00(state["keys"][head], queries) * scaling
        weights = softmax0(jnp.where(state["same"], scores, NEGATIVE)).astype(BF16)
        self_out = dot10(state["values"][head], weights)
        scores = dot00(state["cap_keys"][head], queries) * scaling
        weights = softmax0(jnp.where(state["in_use"], scores, NEGATIVE)).astype(BF16)
        cross_out = dot10(state["cap_values"][head], weights)
        cross_ref[head * size : (head + 1) * size, :] = cross_out
        mixed.append(self_out + tanh_ref[head] * cross_out)
    mixed_ref[...] = jnp.concatenate(mixed, axis=0).T.astype(BF16)


def backward_kernel(
    heads,
    size,
    qkv_ref,
    cap_ref,
    cos_ref,
    sin_ref,
    marks_ref,
    gains_ref,
    tanh_ref,
    cross_ref,
    grad_ref,
    turned_ref,
    plain_ref,
    cap_grad_ref,
    gain_grad_ref,
    gate_grad_ref,
):
    step = pl.program_id(0)
    cap = cap_ref[...]
    crossed = cross_ref[...]
    gains = gains_ref[...]
    cos_table, sin_table = cos_ref[...], sin_ref[...]
    state = row_state(qkv_ref[...], cap, cos_table, sin_table, marks_ref[0], gains, heads, size)
    scaling = 1.0 / math.sqrt(size)
    across = heads * size
    grad_q, grad_k, grad_cap_k, gate = [], [], [], []
    for head in range(heads):
        span = slice(head * size, (head + 1) * size)
        queries, keys, values = (state[name][head] for name in ("queries", "keys", "values"))
        cap_keys, cap_values = state["cap_keys"][head], state["cap_values"][head]
        grad_out = grad_ref[span, :]
        grad_float = grad_out.astype(F32)
        gate.append(jnp.sum(grad_float * crossed[span], axis=0, keepdims=True))
        grad_cross = (tanh_ref[head] * grad_float).astype(BF16)

        def back(weights, grad_output, held):
            grad_weights = dot00(held, grad_output)
            centre = jnp.sum(grad_weights * weights, axis=0, keepdims=True)
            return (weights * (grad_weights - centre)).astype(BF16)

        scores = dot00(keys, queries) * scaling
        weights = softmax0(jnp.where(state["same"], scores, NEGATIVE))
        grad_scores = back(weights, grad_out, values)
        grad_value = dot11(grad_out, weights.astype(BF16))
        at = 2 * across + head * size
        turned_ref[at : at + size, :] = grad_value.astype(BF16)
        grad_query = dot10(keys, grad_scores)
        grad_k.append(dot11(queries, grad_scores) * scaling)

        scores = dot00(cap_keys, queries) * scaling
        weights = softmax0(jnp.where(state["in_use"], scores, NEGATIVE))
        grad_scores = back(weights, grad_cross, cap_values)
        grad_cap_value = dot11(grad_cross, weights.astype(BF16))
        cap_grad_ref[across + head * size : across + (head + 1) * size, :] = grad_cap_value.astype(
            BF16
        )
        grad_q.append((grad_query + dot10(cap_keys, grad_scores)) * scaling)
        grad_cap_k.append(dot11(queries, grad_scores) * scaling)

    def stacked(parts):
        return jnp.concatenate(parts, axis=0).reshape(heads, size, -1)

    def unrotate(incoming):
        return incoming * cos_table - quarter_turn(incoming * sin_table)

    normed = state["norms"]
    grad_q, grad_k = unrotate(stacked(grad_q)), unrotate(stacked(grad_k))
    grad_cap_k = stacked(grad_cap_k)
    turned_ref[0:across, :] = (
        head_norm_back(grad_q, normed[0], normed[1], gains[0]).reshape(across, -1).astype(BF16)
    )
    turned_ref[across : 2 * across, :] = (
        head_norm_back(grad_k, normed[2], normed[3], gains[1]).reshape(across, -1).astype(BF16)
    )
    cap_grad_ref[0:across, :] = (
        head_norm_back(grad_cap_k, normed[4], normed[5], gains[2][:, :1])
        .reshape(across, -1)
        .astype(BF16)
    )
    plain_ref[...] = turned_ref[...].astype(F32).T.astype(BF16)
    tokens = grad_q.shape[-1]
    cap_part = jnp.sum(grad_cap_k * normed[4], axis=0)
    gain_part = jnp.stack(
        [
            jnp.sum(grad_q * normed[0], axis=0),
            jnp.sum(grad_k * normed[2], axis=0),
            sum(cap_part[:, i : i + tokens] for i in range(0, cap_part.shape[1], tokens)),
        ]
    )
    gate_part = jnp.stack(gate)

    @pl.when(step == 0)
    def _():
        gain_grad_ref[...] = gain_part
        gate_grad_ref[...] = gate_part

    @pl.when(step > 0)
    def _():
        gain_grad_ref[...] += gain_part
        gate_grad_ref[...] += gate_part


def row_specs(row_of, sizes, across):
    size, tokens, cap_tokens = sizes
    return [
        pl.BlockSpec((tokens, 3 * across), lambda i: (row_of(i), 0)),
        pl.BlockSpec((cap_tokens, 2 * across), lambda i: (i, 0)),
        pl.BlockSpec((size, tokens), lambda i: (0, row_of(i))),
        pl.BlockSpec((size, tokens), lambda i: (0, row_of(i))),
        pl.BlockSpec((1, 8, tokens), lambda i: (row_of(i), 0, 0)),
    ]


def whole(shape):
    return pl.BlockSpec(shape, lambda i: (0,) * len(shape))


def attend(row_of, heads, sizes, qkv, caps, weight, cos_table, sin_table, marks, gains, tanh):
    size, tokens, cap_tokens = sizes
    half = caps[0].shape[0] // cap_tokens
    rows = 2 * half
    across = heads * size
    width = caps[0].shape[1]
    specs = row_specs(row_of, sizes, across)
    return pl.pallas_call(
        functools.partial(forward_kernel, heads, size, half),
        grid=(rows,),
        in_specs=[
            specs[0],
            pl.BlockSpec((cap_tokens, width), lambda i: (jnp.minimum(i, half - 1), 0)),
            pl.BlockSpec((cap_tokens, width), lambda i: (jnp.maximum(i - half, 0), 0)),
            whole(weight.shape),
            *specs[2:],
            whole(gains.shape),
            whole(tanh.shape),
        ],
        out_specs=[
            pl.BlockSpec((cap_tokens, 2 * across), lambda i: (i, 0)),
            pl.BlockSpec((tokens, across), lambda i: (i, 0)),
            pl.BlockSpec((across, tokens), lambda i: (0, i)),
        ],
        out_shape=[
            jax.ShapeDtypeStruct((rows * cap_tokens, 2 * across), F32),
            jax.ShapeDtypeStruct((rows * tokens, across), BF16),
            jax.ShapeDtypeStruct((across, rows * tokens), F32),
        ],
        compiler_params=pltpu.CompilerParams(vmem_limit_bytes=48 * 1024 * 1024),
        cost_estimate=SMALL_COST,
    )(qkv, caps[0], caps[1], weight, cos_table, sin_table, marks, gains, tanh)


def attend_back(row_of, first, heads, sizes, qkv, cap, cos_table, sin_table, marks, gains, tanh, crossed, grad):
    size, tokens, cap_tokens = sizes
    rows = cap.shape[0] // cap_tokens
    across = heads * size
    out_shape = [
        jax.ShapeDtypeStruct((3 * across, rows * tokens), BF16),
        jax.ShapeDtypeStruct((rows * tokens, 3 * across), BF16),
        jax.ShapeDtypeStruct((2 * across, rows * cap_tokens), BF16),
        jax.ShapeDtypeStruct((3, size, tokens), F32),
        jax.ShapeDtypeStruct((heads, 1, tokens), F32),
    ]
    return pl.pallas_call(
        functools.partial(backward_kernel, heads, size),
        grid=(rows,),
        in_specs=row_specs(row_of, sizes, across)
        + [
            whole(gains.shape),
            whole(tanh.shape),
            pl.BlockSpec((across, tokens), lambda i: (0, i)),
            pl.BlockSpec((across, tokens), lambda i: (0, row_of(i) - first)),
        ],
        out_specs=[
            pl.BlockSpec((3 * across, tokens), lambda i: (0, row_of(i) - first)),
            pl.BlockSpec((tokens, 3 * across), lambda i: (row_of(i) - first, 0)),
            pl.BlockSpec((2 * across, cap_tokens), lambda i: (0, i)),
            whole(out_shape[3].shape),
            whole(out_shape[4].shape),
        ],
        out_shape=out_shape,
        compiler_params=pltpu.CompilerParams(vmem_limit_bytes=40 * 1024 * 1024),
        cost_estimate=SMALL_COST,
    )(qkv, cap, cos_table, sin_table, marks, gains, tanh, crossed, grad)


def outer_kernel(counts, place_ref, *refs):
    lefts, rights = refs[: len(counts)], refs[len(counts) : -1]
    total, at = None, 0
    for left, count in zip(lefts, counts):
        begin = 0
        for right in rights[at : at + count]:
            end = begin + right.shape[0]
            part = dot10(left[:, begin:end], right[...])
            total = part if total is None else total + part
            begin = end
        at += count
    refs[-1][...] = total.astype(BF16)


def outer(lefts, rights, left_index, left_blocks, column_blocks, width):
    counts = tuple(len(group) for group in rights)
    flat = [piece for group in rights for piece in group]
    rows = lefts[0].shape[0] // left_blocks
    count = len(column_blocks)
    index = jnp.stack([left_index] + list(column_blocks)).astype(jnp.int32)
    tokens = sum(left.shape[1] for left in lefts)
    return pl.pallas_call(
        functools.partial(outer_kernel, counts),
        grid_spec=pltpu.PrefetchScalarGridSpec(
            num_scalar_prefetch=1,
            grid=(count,),
            in_specs=[
                pl.BlockSpec((rows, left.shape[1]), lambda i, place: (place[0], 0)) for left in lefts
            ]
            + [pl.BlockSpec((right.shape[0], width), lambda i, place: (0, place[1 + i])) for right in flat],
            out_specs=pl.BlockSpec((rows, width), lambda i, place: (0, i)),
        ),
        out_shape=jax.ShapeDtypeStruct((rows, count * width), BF16),
        compiler_params=pltpu.CompilerParams(vmem_limit_bytes=40 * 1024 * 1024),
        cost_estimate=SMALL_COST,
    )(index, *lefts, *flat)


def middle_kernel(inner, ffn_ref, gate_ref, up_ref, branch_ref, down_ref, act_ref, grad_ref):
    block = gate_ref.shape[1]
    grad_act = dot11(branch_ref[...], down_ref[...])
    gate = dot10(ffn_ref[...], gate_ref[...])
    up = dot10(ffn_ref[...], up_ref[...])
    sigmoid = 1.0 / (1.0 + jnp.exp(-gate))
    silu = gate * sigmoid
    at = pl.multiple_of(pl.program_id(0) * block, 128)
    act_ref[...] = (silu * up).astype(BF16)
    grad_ref[:, pl.ds(at, block)] = (grad_act * up * sigmoid * (1.0 + gate * (1.0 - sigmoid))).astype(BF16)
    grad_ref[:, pl.ds(at + inner, block)] = (grad_act * silu).astype(BF16)


def middle(ffn_in, w_ffn, grad_branch, w_down):
    tokens, width = ffn_in.shape
    inner = w_down.shape[0]
    block = 256
    steps = inner // block

    def whole(shape):
        return pl.BlockSpec(shape, lambda i: (0,) * len(shape))

    return pl.pallas_call(
        functools.partial(middle_kernel, inner),
        grid=(steps,),
        in_specs=[
            whole((tokens, width)),
            pl.BlockSpec((width, block), lambda i: (0, i)),
            pl.BlockSpec((width, block), lambda i: (0, i + steps)),
            whole((tokens, width)),
            pl.BlockSpec((block, width), lambda i: (i, 0)),
        ],
        out_specs=[
            pl.BlockSpec((tokens, block), lambda i: (0, i)),
            whole((tokens, 2 * inner)),
        ],
        out_shape=[
            jax.ShapeDtypeStruct((tokens, inner), BF16),
            jax.ShapeDtypeStruct((tokens, 2 * inner), BF16),
        ],
        compiler_params=pltpu.CompilerParams(vmem_limit_bytes=40 * 1024 * 1024),
        cost_estimate=SMALL_COST,
    )(ffn_in, w_ffn, w_ffn, grad_branch, w_down)


def outer_tokens_kernel(count, place_ref, *refs):
    total = None
    for left, right in zip(refs[:count], refs[count:-1]):
        part = dot00(left[...], right[...])
        total = part if total is None else total + part
    refs[-1][...] = total.astype(BF16)


def outer_tokens(lefts, rights, left_block, blocks, right_block, right_blocks):
    block = 256
    columns = rights[0].shape[1] // right_blocks
    index = jnp.stack([jnp.asarray(left_block), jnp.asarray(right_block)]).astype(jnp.int32)
    return pl.pallas_call(
        functools.partial(outer_tokens_kernel, len(lefts)),
        grid_spec=pltpu.PrefetchScalarGridSpec(
            num_scalar_prefetch=1,
            grid=(blocks,),
            in_specs=[
                pl.BlockSpec((left.shape[0], block), lambda i, place: (0, place[0] + i)) for left in lefts
            ]
            + [
                pl.BlockSpec((right.shape[0], columns), lambda i, place: (0, place[1]))
                for right in rights
            ],
            out_specs=pl.BlockSpec((block, columns), lambda i, place: (i, 0)),
        ),
        out_shape=jax.ShapeDtypeStruct((blocks * block, columns), BF16),
        compiler_params=pltpu.CompilerParams(vmem_limit_bytes=40 * 1024 * 1024),
        cost_estimate=SMALL_COST,
    )(index, *lefts, *rights)


def join_kernel(widths, rows, chunks, place_ref, *refs):
    shards = refs[: len(widths)]
    near = refs[len(widths)]
    pieces = refs[len(widths) + 1 : len(widths) + 1 + 2 * chunks]
    out, sems = refs[-2:]
    copies = []

    def copy(source, row, count, column, width):
        target = out.at[pl.ds(pl.multiple_of(row, 16), count), pl.ds(column, width)]
        copies.append(pltpu.make_async_copy(source, target, sems.at[len(copies)]))
        copies[-1].start()

    at = 0
    for shard, width in zip(shards, widths):
        begin = pl.multiple_of(place_ref[4] * width, 128)
        copy(shard.at[:, pl.ds(begin, width)], place_ref[0] * rows, rows, at, width)
        at += width
    copy(near, place_ref[1] * rows, rows, 0, at)
    part = rows // chunks
    for chunk in range(chunks):
        for kind in range(2):
            row = place_ref[2 + kind] * rows + chunk * part
            copy(pieces[2 * chunk + kind], row, part, 0, at)
    for item in copies:
        item.wait()


def join(place_index, shards, near, pieces):
    widths = tuple(shard.shape[1] // 4 for shard in shards)
    rows = near.shape[0]
    chunks = len(pieces) // 2
    count = len(shards) + 1 + len(pieces)
    return pl.pallas_call(
        functools.partial(join_kernel, widths, rows, chunks),
        grid_spec=pltpu.PrefetchScalarGridSpec(
            num_scalar_prefetch=1,
            grid=(1,),
            in_specs=[pl.BlockSpec(memory_space=pl.ANY)] * count,
            out_specs=pl.BlockSpec((4 * rows, sum(widths)), lambda i, place: (0, 0)),
            scratch_shapes=[pltpu.SemaphoreType.DMA((count,))],
        ),
        out_shape=jax.ShapeDtypeStruct((4 * rows, sum(widths)), near.dtype),
        compiler_params=pltpu.CompilerParams(vmem_limit_bytes=32 * 1024 * 1024),
        cost_estimate=SMALL_COST,
    )(place_index, *shards, near, *pieces)


class Flow:
    def __init__(self, steps):
        self.steps = steps
        self.result = None
        self.waiting = next(steps)

    def step(self, values):
        if self.result is not None:
            return
        try:
            self.waiting = self.steps.send(values)
        except StopIteration as stop:
            self.waiting, self.result = (), stop.value


class Place:
    def __init__(self, mesh):
        self.copies = mesh.shape["dp"]
        self.shards = mesh.shape["fsdp"]
        self.top_step = self.copies // 2
        self.team_step = self.copies // 4
        self.low = self.copies // 4
        self.last = {}
        self.before, self.token = (), ()

    def locate(self):
        self.dp = lax.axis_index("dp")
        self.fsdp = lax.axis_index("fsdp")
        self.side = self.fsdp // 2
        self.core = self.fsdp % 2
        self.top = self.dp // self.top_step
        self.team = (self.dp // self.team_step) % 2
        self.lane = self.dp % 2
        self.quarter = 2 * self.core + self.team

    def swap(self, value, dp=0, fsdp=0, link=None):
        return self.route(value, lambda d, f: (d ^ dp, f ^ fsdp), link)

    def route(self, value, target, link=None):
        pairs = []
        for d in range(self.copies):
            for f in range(self.shards):
                to = target(d, f)
                if to is not None:
                    pairs.append((d * self.shards + f, to[0] * self.shards + to[1]))
        value = after(value, *self.before, *self.last.get(link, ()))
        self.operand = value
        value = lax.ppermute(value, ("dp", "fsdp"), pairs)
        if link is not None:
            self.last[link] = (value,)
        return value

    def next_wave(self, *others):
        self.before = others

    def arrive(self, *values):
        values = lax.optimization_barrier(values)
        self.before = values
        return values

    def meet(self, flows, *values):
        waiting = [array for flow in flows for array in flow.waiting]
        arrived = self.arrive(*waiting, *values)
        self.done(*arrived[len(waiting) :])
        at = 0
        for flow in flows:
            count = len(flow.waiting)
            flow.step(arrived[at : at + count])
            at += count
        return arrived[at:]

    def held(self, value):
        if isinstance(value, tuple):
            return tuple(self.held(part) for part in value)
        return after(value, *self.token)

    def done(self, *values):
        self.token = values

    def bits(self, d, f):
        return ((d // self.team_step) % 2, f // 2, f % 2, d % 2)

    def team_swap(self, value):
        return self.swap(value, dp=self.team_step, link="z")

    def core_swap(self, value):
        return self.swap(value, fsdp=1, link="c")


    def cut_columns(self, shards):
        def cut(quarter):
            parts = []
            for shard in shards:
                width = shard.shape[1] // 4
                parts.append(lax.dynamic_slice_in_dim(shard, quarter * width, width, axis=1))
            return jnp.concatenate(parts, axis=1)

        return cut(2 * (self.core ^ self.lane) + self.team), cut(2 * (1 - self.core) + self.team)

    def side_swap(self, piece):
        return self.route(piece, lambda d, f: (d, f ^ 2 ^ (d % 2)), "x")

    def lane_swap(self, piece):
        return self.swap(piece, dp=1, link="y")

    def join_columns(self, shards, near, pieces):
        index = [self.fsdp, self.fsdp ^ 1, self.fsdp ^ 2 ^ self.lane, self.fsdp ^ 3 ^ self.lane]
        return join(jnp.stack(index + [self.quarter]).astype(jnp.int32), shards, near, pieces)

    def rows_side_swap(self, shard):
        def target(d, f):
            team, side, core, _ = self.bits(d, f)
            return (d, 2 * (1 - side) + side) if core == team else None

        return self.route(shard, target, "x")

    def rows_lane_swap(self, piece):
        def target(d, f):
            _, side, core, _ = self.bits(d, f)
            return (d ^ 1, f) if core != side else None

        return self.route(piece, target, "y")

    def rows_core_swap(self, shard):
        def target(d, f):
            team, side, core, _ = self.bits(d, f)
            return (d, 2 * side + side) if core == team and side != team else None

        return self.route(shard, target, "c")

    def join_rows(self, shard, near, across, far):
        source = jnp.where(
            self.core != self.side, 2, jnp.where(self.side == self.team, 0, 1)
        )
        return join_rows(jnp.stack([source, self.lane]).astype(jnp.int32), shard, near, across, far)


    def part(self, value, index, axis):
        if isinstance(value, tuple):
            return tuple(self.part(array, index, axis) for array in value)
        size = value.shape[axis] // 2
        return lax.dynamic_slice_in_dim(value, index * size, size, axis=axis)

    def summed(self, arrays):
        return sum(array.astype(F32) for array in arrays).astype(BF16)

    def halves(self, value, axis, keep):
        sent = self.summed([self.part(array, 1 - keep, axis) for array in value])
        return sent, [self.part(array, keep, axis) for array in value]

    def low_steps(self):
        step = self.low // 2
        while step:
            yield step, (self.dp // step) % 2
            step //= 2

    def spread(self, first, second, place, chunks=1, ahead=False):
        (step, keep), *lows = self.low_steps()
        side, low, kept = [], [], ()
        sents = [(first[0](1 - place, i), second[0](1 - keep, i)) for i in range(chunks)]
        if chunks > 1:
            kept = tuple(first[1](place, i) for i in range(chunks))
            kept += tuple(second[1](keep, i) for i in range(chunks))
        if ahead:
            sents = [(yield sents[0])]
        for chunk in range(chunks):
            first_got = self.swap(sents[chunk][0], fsdp=2)
            operands = (self.operand,)
            second_got = self.swap(sents[chunk][1], dp=step)
            self.operands = operands + (self.operand,)
            rest = tuple(part for pair in sents[chunk + 1 :] for part in pair)
            if not kept:
                yield first_got, second_got
                kept = first[1](place, 0), second[1](keep, 0)
            arrived = yield (first_got, second_got) + kept + rest
            side.append(arrived[0])
            low.append(arrived[1])
            kept, rest = arrived[2 : 2 + len(kept)], arrived[2 + len(kept) :]
            sents[chunk + 1 :] = [rest[i : i + 2] for i in range(0, len(rest), 2)]

        def joined(parts):
            return parts[0] if chunks == 1 else jnp.concatenate(parts, axis=0)

        if chunks == 2 and not lows:
            pairs = (kept[:chunks], side)
            sent_first = self.summed([jnp.where(keep == 0, pair[1], pair[0]) for pair in pairs])
            first = [jnp.where(keep == 0, pair[0], pair[1]) for pair in pairs]
        else:
            sent_first, first = self.halves([joined(kept[:chunks]), joined(side)], 0, keep)
        second = [joined(kept[chunks:]), joined(low)]
        sent_second, second = self.halves(second, 1, place)
        got = yield self.swap(sent_first, dp=step), self.swap(sent_second, fsdp=2)
        first.append(got[0])
        second.append(got[1])
        for step, keep in lows:
            sent_first, first = self.halves(first, 0, keep)
            sent_second, second = self.halves(second, 0, keep)
            first.append(self.swap(sent_first, dp=step))
            second.append(self.swap(sent_second, dp=step))
        return first, second

    def finish(self, own, sent, parts, apart=False):
        got = self.core_swap(sent)
        if apart:
            (got,) = yield (got,)
        straight = self.core == self.top
        sent = jnp.split(jnp.where(straight, got, own), parts, axis=0)
        kept = jnp.split(jnp.where(straight, own, got), parts, axis=0)
        totals = []
        for part in range(parts):
            (got,) = yield (self.swap(sent[part], dp=self.top_step),)
            totals.append(kept[part].astype(F32) + got.astype(F32))
        return totals

    def pair_back(self, by_side, by_low):
        first, second = yield from self.spread((by_side, by_side), (by_low, by_low), self.side, 2)

        def both(index):
            return jnp.concatenate(
                [self.summed([self.part(array, index, 1) for array in value]) for value in (first, second)]
            )

        value = yield from self.finish(both(self.core), both(1 - self.core), 2, True)
        return [part.T for part in value]

    def split_back(self, by_side, by_low, count, parts, ahead=False):
        yield ()
        first, second = yield from self.spread(
            (by_side, by_side), (by_low, by_low), self.side, 1, ahead
        )
        first, second = self.summed(first), self.summed(second)
        own = jnp.where(self.core == 0, first, second)
        sent = jnp.where(self.core == 0, second, first)
        value = yield from self.finish(own, sent, parts)
        return [part.T for total in value for part in jnp.split(total, count // parts, axis=0)]

    def rows_back(self, grad):
        columns, rows = grad.shape
        value = grad.reshape(2, 2, columns // 4, rows)
        own = lax.dynamic_index_in_dim(value, self.core, 1, keepdims=False)
        sent = lax.dynamic_index_in_dim(value, 1 - self.core, 1, keepdims=False)
        got = self.core_swap(sent)
        straight = self.core == self.side
        kept = jnp.where(straight, own, got)
        sent = jnp.where(straight, got, own)
        wide = jnp.concatenate([kept[1], sent[1]], axis=1)
        pieces = sent[0], kept[0]
        *pieces, wide = yield (*pieces, wide)

        def by_low(index, _):
            return self.part(wide, index, 0)

        first, second = yield from self.spread(
            (lambda *_: pieces[0], lambda *_: pieces[1]), (by_low, by_low), 0
        )
        first, second = self.summed(first), self.summed(second)
        sent = jnp.where(self.top == 0, second, first)
        (got,) = yield (self.swap(sent, dp=self.top_step),)
        value = self.summed([jnp.where(self.top == 0, first, second), got])

        def turn(d, f):
            team, _, core, _ = self.bits(d, f)
            return (d ^ self.team_step, f ^ 1) if core != team else (d, f)

        (got,) = yield (self.route(value, turn),)
        return got.astype(F32).T

    def total(self, value):
        for bit in (1, 2):
            value = value + self.swap(value, fsdp=bit)
        step = 1
        while step < self.top_step:
            value = value + self.swap(value, dp=step)
            step *= 2
        got = self.swap(value, dp=step)
        return lambda: value + self.held(got)


def layer(
    place,
    block_input,
    caption,
    modulation,
    segment_ids,
    pos_row,
    pos_col,
    caption_len,
    gain_attn,
    w_query,
    w_key,
    w_value,
    gain_query,
    gain_key,
    w_cap_key,
    w_cap_value,
    gain_cap_key,
    head_gate,
    w_out,
    gain_ffn,
    w_gate,
    w_up,
    w_down,
    cotangent,
):
    place.locate()
    rows, tokens, width = block_input.shape
    cap_tokens = caption.shape[1]
    size = gain_query.shape[0] * place.shards
    team_rows = 4 * rows

    qkv_shards, cap_shards, ffn_shards = (w_query, w_key, w_value), (w_cap_key, w_cap_value), (w_gate, w_up)
    qkv_sent, qkv_near = place.cut_columns(qkv_shards)
    qkv_side = place.side_swap(qkv_sent)
    cap_pieces = [caption[0, : cap_tokens // 2], caption[0, cap_tokens // 2 :]]
    cap_pieces += [caption[1, : cap_tokens // 2], caption[1, cap_tokens // 2 :]]
    far_pieces = [place.team_swap(cap_pieces[0])]

    small = (gain_attn, gain_ffn, gain_query, gain_key, gain_cap_key, head_gate)
    piece = after(jnp.concatenate(small), qkv_sent)
    pair = jnp.stack([piece, place.core_swap(piece)])
    other = place.swap(pair, fsdp=2)
    packed = jnp.zeros((place.shards,) + piece.shape, piece.dtype)
    for part, index in ((pair[0], 0), (pair[1], 1), (other[0], 2), (other[1], 3)):
        packed = lax.dynamic_update_index_in_dim(packed, part, place.fsdp ^ index, 0)
    packed = packed.astype(F32)
    full_small, at = [], 0
    for vector in small:
        full_small.append(packed[:, at : at + vector.shape[0]].reshape(-1))
        at += vector.shape[0]
    full_gain_attn, full_gain_ffn, query_gain, key_gain, cap_gain, full_head_gate = full_small
    heads = full_head_gate.shape[0] // 4
    across = heads * size
    sizes = (size, tokens, cap_tokens)

    cap_own = caption.reshape(-1, caption.shape[-1])
    cap_core = place.core_swap(cap_own)
    cap_sent, cap_w_near = place.cut_columns(cap_shards)
    cap_sent = jnp.split(cap_sent, 2, axis=0)
    ffn_sent, ffn_w_near = place.cut_columns(ffn_shards)
    ffn_sent = jnp.split(ffn_sent, 2, axis=0)
    half_out, half_down = w_out.shape[0] // 2, w_down.shape[0] // 2
    rows_sent = jnp.concatenate(
        [place.part(w_out, place.lane, 0), place.part(w_down, place.lane, 0)], axis=0
    )

    inputs = block_input.astype(F32)
    scale_attn = 1.0 + modulation[:, 0][:, None, :]
    tanh_attn = jnp.tanh(modulation[:, 1])[:, None, :]
    scale_ffn = 1.0 + modulation[:, 2][:, None, :]
    tanh_ffn = jnp.tanh(modulation[:, 3])[:, None, :]
    upstream = cotangent.astype(F32)
    grad_branch = (upstream * tanh_ffn).astype(BF16).reshape(-1, width)
    normed_in, inverse_in = rms_scale(inputs)
    attn_in = (normed_in * full_gain_attn * scale_attn).astype(BF16).reshape(-1, width)

    own_tokens = rows * tokens
    marks = jnp.stack(
        [segment_ids, pos_row, pos_col, jnp.broadcast_to(caption_len[:, None], (rows, tokens))]
    )
    marks = marks.astype(BF16).reshape(4, own_tokens)
    marks = jnp.pad(marks, ((0, 12), (0, width - own_tokens)))
    marked = jnp.concatenate([attn_in, marks], axis=0)

    qkv_side, far_piece = place.arrive(qkv_side, far_pieces[0])
    far_pieces = [far_piece]
    cap_side = place.side_swap(cap_sent[0])
    qkv_lane = place.lane_swap(qkv_side)
    marked_far = place.team_swap(marked)
    place.before = ()
    qkv_near = place.core_swap(qkv_near)
    marked_near = place.core_swap(marked)

    cap_side, qkv_lane, marked_far = place.arrive(cap_side, qkv_lane, marked_far)
    cap_pairs = [cap_side]
    next_side = place.side_swap(cap_sent[1])
    cap_lane = place.lane_swap(cap_side)
    far_piece = place.team_swap(cap_pieces[1])
    place.before = ()
    marked_last = place.core_swap(marked_far)
    cap_w_near = place.core_swap(cap_w_near)
    blocks = (marked, marked_near, marked_far, marked_last)
    attn_all = jnp.concatenate([block[:own_tokens] for block in blocks], axis=0)
    marks = jnp.concatenate([block[own_tokens:, :own_tokens] for block in blocks], axis=1).astype(F32)
    w_qkv = place.join_columns(qkv_shards, qkv_near, [qkv_side, qkv_lane])

    next_side, cap_lane, far_piece, attn_all, w_qkv = place.arrive(
        next_side, cap_lane, far_piece, attn_all, w_qkv
    )
    cap_pairs += [cap_lane, next_side]
    far_pieces.append(far_piece)
    rows_side = place.rows_side_swap(rows_sent)
    cap_lane = place.lane_swap(next_side)
    far_piece = place.team_swap(cap_pieces[2])
    place.before = ()
    far_first = jnp.concatenate(far_pieces, axis=0)
    far_first_core = place.core_swap(far_first)
    ffn_w_near = place.core_swap(ffn_w_near)
    qkv_raw = dot(attn_all, w_qkv)

    quarter_size = size // 4
    frequency = jnp.exp(
        jnp.arange(quarter_size, dtype=F32) * (-math.log(10000.0) / quarter_size)
    )
    row_angle = frequency[:, None] * marks[1][None, :]
    col_angle = frequency[:, None] * marks[2][None, :]
    angles = jnp.concatenate([row_angle, row_angle, col_angle, col_angle], axis=0)
    cos_table, sin_table = jnp.cos(angles), jnp.sin(angles)
    marks = jnp.stack([marks[0], marks[3]]).reshape(2, team_rows, tokens)
    marks = jnp.pad(jnp.moveaxis(marks, 0, 1), ((0, 0), (0, 6), (0, 0)))
    gains = jnp.broadcast_to(
        jnp.stack([query_gain, key_gain, cap_gain])[:, :, None], (3, size, tokens)
    )
    head_tanh = jnp.tanh(lax.dynamic_slice_in_dim(full_head_gate, place.quarter * heads, heads))
    tanh_table = jnp.broadcast_to(head_tanh[:, None, None], (heads, 1, tokens))
    tables = (cos_table, sin_table, marks, gains, tanh_table)
    half = team_rows // 2

    def far_row(i):
        return half + (i % rows) * rows + i // rows

    def rows_from(first):
        return lambda i: first + i

    rows_side, cap_lane, far_piece, qkv_raw, cos_table = place.arrive(
        rows_side, cap_lane, far_piece, qkv_raw, cos_table
    )
    tables = (cos_table,) + tables[1:]
    cap_pairs.append(cap_lane)
    far_pieces = [far_piece]
    ffn_side = place.side_swap(ffn_sent[0])
    rows_lane = place.rows_lane_swap(rows_side)
    far_piece = place.team_swap(cap_pieces[3])
    w_cap = place.join_columns(cap_shards, cap_w_near, cap_pairs)
    out_near = place.rows_core_swap(w_out)
    branch_core = place.core_swap(grad_branch)
    place.before = ()
    near_raw, mixed_near, near_crossed = attend(
        rows_from(0), heads, sizes, qkv_raw, (cap_own, cap_core), w_cap, *tables
    )

    ffn_side, rows_lane, far_piece, mixed_near = place.arrive(ffn_side, rows_lane, far_piece, mixed_near)
    ffn_pairs = [ffn_side]
    far_pieces.append(far_piece)
    next_side = place.side_swap(ffn_sent[1])
    ffn_lane = place.lane_swap(ffn_side)
    branch_far = place.team_swap(grad_branch)
    place.before = ()
    far_second = jnp.concatenate(far_pieces, axis=0)
    far_second_core = place.core_swap(far_second)
    down_near = place.rows_core_swap(w_down)
    w_out = place.join_rows(w_out, out_near, rows_side[:half_out], rows_lane[:half_out])
    first_raw, mixed_first, first_crossed = attend(
        lambda i: half + i * rows, heads, sizes, qkv_raw, (far_first, far_first_core), w_cap, *tables
    )
    second_raw, mixed_second, second_crossed = attend(
        lambda i: half + 1 + i * rows,
        heads,
        sizes,
        qkv_raw,
        (far_second, far_second_core),
        w_cap,
        *tables,
    )
    next_side, ffn_lane, branch_far, mixed_second = place.arrive(
        next_side, ffn_lane, branch_far, mixed_second
    )
    ffn_pairs += [ffn_lane, next_side]
    place.before = ()
    place.done(mixed_second)
    far_raw = jnp.concatenate([first_raw, second_raw], axis=0)
    far_crossed = jnp.concatenate([first_crossed, second_crossed], axis=1)
    mixed_blocks = (
        *jnp.split(mixed_near, 2, axis=0),
        jnp.concatenate([mixed_first[:tokens], mixed_second[:tokens]], axis=0),
        jnp.concatenate([mixed_first[tokens:], mixed_second[tokens:]], axis=0),
    )
    def far_sum(blocks, right, product):
        last = place.core_swap(product(place.held(blocks[3]), right).astype(BF16))
        far = product(place.held(blocks[2]), right) + last.astype(F32)
        return place.team_swap(far.astype(BF16))

    def near_sum(blocks, right, product):
        got = place.core_swap(product(place.held(blocks[1]), right).astype(BF16))
        return product(place.held(blocks[0]), right) + got.astype(F32)

    attn_far_sum = far_sum(mixed_blocks, w_out, dot)
    ffn_pairs.append(place.lane_swap(next_side))
    w_down = place.join_rows(w_down, down_near, rows_side[half_out:], rows_lane[half_out:])
    branch_near = jnp.concatenate([grad_branch, branch_core], axis=0)
    branch_far = jnp.concatenate([branch_far, place.core_swap(branch_far)], axis=0)
    w_ffn = place.join_columns(ffn_shards, ffn_w_near, ffn_pairs)
    attn_near_sum = near_sum(mixed_blocks, w_out, dot)
    attn_far_sum, attn_near_sum, w_ffn, w_down = place.arrive(
        attn_far_sum, attn_near_sum, w_ffn, w_down
    )
    place.before = ()
    attn_branch = (attn_near_sum + attn_far_sum.astype(F32)).reshape(inputs.shape)
    hidden = inputs + tanh_attn * attn_branch

    normed_mid, inverse_mid = rms_scale(hidden)
    ffn_in = (normed_mid * full_gain_ffn * scale_ffn).astype(BF16).reshape(-1, width)

    ffn_far = place.team_swap(ffn_in)
    ffn_near = jnp.concatenate([ffn_in, place.core_swap(ffn_in)], axis=0)
    act_near, grad_near = middle(ffn_near, w_ffn, branch_near, w_down)
    place.done(act_near, grad_near)
    ffn_far = place.held(ffn_far)
    ffn_far = jnp.concatenate([ffn_far, place.core_swap(ffn_far)], axis=0)
    act_far, grad_far = middle(ffn_far, w_ffn, branch_far, w_down)
    place.done(act_far, grad_far)
    grad_blocks = (*jnp.split(grad_near, 2, axis=0), *jnp.split(grad_far, 2, axis=0))
    act_blocks = (*jnp.split(act_near, 2, axis=0), *jnp.split(act_far, 2, axis=0))
    blocks = act_near.shape[1] // 256

    def gate_by_side(side, chunk):
        lefts = place.held((grad_near, grad_far))
        each = blocks // 2
        return outer_tokens(lefts, (ffn_near, ffn_far), chunk * each, each, side, 2)

    def up_by_low(index, chunk):
        lefts = place.held((grad_near, grad_far))
        each = blocks // 4
        first = blocks + index * (blocks // 2) + chunk * each
        return outer_tokens(lefts, (ffn_near, ffn_far), first, each, 0, 1)

    ffn_far_sum = far_sum(grad_blocks, w_ffn, dot_back)
    ffn = Flow(place.pair_back(gate_by_side, up_by_low))
    ffn_near_sum = near_sum(grad_blocks, w_ffn, dot_back)
    ffn_far_sum, ffn_near_sum = place.meet([ffn], ffn_far_sum, ffn_near_sum)
    place.before = ()
    grad_ffn_in = (ffn_near_sum + ffn_far_sum.astype(F32)).reshape(inputs.shape)
    grad_ffn_gain = jnp.sum(grad_ffn_in * normed_mid * scale_ffn, axis=(0, 1))
    grad_mod_ffn_scale = jnp.sum(grad_ffn_in * normed_mid * full_gain_ffn, axis=1)
    grad_hidden = upstream + rms_back(
        grad_ffn_in * full_gain_ffn * scale_ffn, normed_mid, inverse_mid
    )

    grad_attn_branch = (grad_hidden * tanh_attn).astype(BF16).reshape(-1, width)
    grad_mod_attn_gate = jnp.sum(grad_hidden * attn_branch, axis=1) * (
        1.0 - tanh_attn[:, 0] * tanh_attn[:, 0]
    )
    attn_grad_far = place.team_swap(grad_attn_branch)
    attn_grad_near = jnp.concatenate([grad_attn_branch, place.core_swap(grad_attn_branch)], axis=0)

    def heads_back(row_of, first, cap_raw, crossed, grad):
        grad_mixed = dot_back(w_out, grad).astype(BF16)
        result = attend_back(
            row_of, first, heads, sizes, qkv_raw, cap_raw, *tables, crossed, grad_mixed
        )
        return list(result)

    near = heads_back(rows_from(0), 0, near_raw, near_crossed, attn_grad_near)
    attn_grad_far, near[0] = place.meet([ffn], attn_grad_far, near[0])
    place.before = ()
    place.done(place.operand)
    attn_grad_far = jnp.concatenate([attn_grad_far, place.core_swap(attn_grad_far)], axis=0)
    grad_down = outer_tokens(
        (branch_near, branch_far), place.held((act_near, act_far)), 0, width // 256, 0, 1
    )
    down = Flow(place.rows_back(grad_down))
    far = heads_back(far_row, half, far_raw, far_crossed, attn_grad_far)
    attn_grad_all = jnp.concatenate([attn_grad_near, attn_grad_far], axis=0)
    mixed_all = jnp.concatenate(mixed_blocks, axis=0)

    def mix(grads, count):
        shaped = grads.reshape(count, place.low, -1, grads.shape[1])
        return jnp.moveaxis(shaped, 0, 1).reshape(grads.shape)

    cap_lefts = []
    cap_rights = (cap_own, cap_core), (far_first, far_first_core, far_second, far_second_core)
    block = min(512, caption.shape[2] // 4)
    per = caption.shape[2] // 4 // block

    def cap_by_side(side, _):
        lefts = place.held(tuple(cap_lefts))
        return outer(lefts, cap_rights, 0, 1, [2 * per * side + i for i in range(per)], block)

    def cap_by_low(index, _):
        lefts = place.held(tuple(cap_lefts))
        columns = [start * per + i for start in (1, 3) for i in range(per)]
        return outer(lefts, cap_rights, index, 2, columns, block)

    far[0], far[2] = place.meet([ffn, down], far[0], far[2])
    down.step(())
    cap_lefts += [mix(near[2], 2), mix(far[2], 2)]
    cap = Flow(place.split_back(cap_by_side, cap_by_low, 2, 2))
    cap.step(())
    place.meet([ffn, down], *place.operands)
    place.done(place.before[0])
    place.before = ()
    cap.step(())
    cap_kept = cap.waiting[2:]
    branch_far_sum = far_sum(act_blocks, w_down, dot)
    branch_near_sum = near_sum(act_blocks, w_down, dot)
    out = Flow(place.rows_back(dot_tokens(attn_grad_all, place.held(mixed_all)).astype(BF16)))
    branch_near_sum, *_ = place.meet([ffn, cap, out], branch_near_sum, *cap_kept)
    out.step(())
    place.before = ()
    plain = (*jnp.split(near[1], 2, axis=0), *jnp.split(far[1], 2, axis=0))
    plain = place.held(plain)
    attn_far_sum = far_sum(plain, w_qkv, dot_back)
    attn_near_sum = near_sum(plain, w_qkv, dot_back)
    turned = mix(jnp.concatenate([near[0], far[0]], axis=1), 3)
    columns = width // 4
    low_rows = jnp.concatenate([attn_all[:, i * columns : (i + 1) * columns] for i in (1, 3)], axis=1)

    def qkv_by_side(side, _):
        right = lax.dynamic_slice_in_dim(attn_all, 2 * side * columns, columns, axis=1)
        return dot(place.held(turned), right).astype(BF16)

    def qkv_by_low(index, _):
        return dot(place.part(place.held(turned), index, 0), low_rows).astype(BF16)

    qkv = Flow(place.split_back(qkv_by_side, qkv_by_low, 3, 1, True))
    qkv.step(())
    branch_far_sum, attn_near_sum = place.meet(
        [ffn, cap, down, qkv], branch_far_sum, attn_near_sum
    )
    qkv.step(())
    (attn_far_sum,) = place.meet([qkv, out], attn_far_sum)
    grad_attn_in = (attn_near_sum + attn_far_sum.astype(F32)).reshape(inputs.shape)
    grad_gain_in = jnp.sum(grad_attn_in * normed_in * scale_attn, axis=(0, 1))
    grad_mod_attn_scale = jnp.sum(grad_attn_in * normed_in * full_gain_attn, axis=1)
    input_grad = (
        grad_hidden + rms_back(grad_attn_in * full_gain_attn * scale_attn, normed_in, inverse_in)
    ).astype(BF16)
    gate_parts = near[4] + far[4]
    gain_parts = jnp.sum(near[3] + far[3], axis=2)
    grad_head_gate = jnp.sum(gate_parts, axis=(1, 2)) * (1.0 - head_tanh * head_tanh)
    ffn_branch = (branch_near_sum + branch_far_sum.astype(F32)).reshape(inputs.shape)
    block_out = (hidden + tanh_ffn * ffn_branch).astype(BF16)
    grad_mod_ffn_gate = jnp.sum(upstream * ffn_branch, axis=1) * (
        1.0 - tanh_ffn[:, 0] * tanh_ffn[:, 0]
    )
    grad_gain_in, input_grad, block_out = place.meet(
        [cap, out, down, qkv], grad_gain_in, input_grad, block_out
    )
    place.before = ()
    head_part = jnp.zeros_like(full_head_gate)
    head_part = lax.dynamic_update_slice_in_dim(
        head_part, grad_head_gate, place.quarter * heads, axis=0
    )
    parts = (
        grad_gain_in,
        grad_ffn_gain,
        gain_parts[0],
        gain_parts[1],
        gain_parts[2],
        head_part,
    )
    small_grads = jnp.concatenate(parts)
    summed = place.total(after(small_grads, place.operand))
    for flow in (ffn, down, cap, out, qkv):
        for _ in range(4):
            flow.step(flow.waiting)
    summed = summed()
    modulation_grad = jnp.stack(
        [grad_mod_attn_scale, grad_mod_attn_gate, grad_mod_ffn_scale, grad_mod_ffn_gate], axis=1
    )

    vectors, at = [], 0
    for vector in parts:
        length = vector.shape[0] // place.shards
        vectors.append(lax.dynamic_slice_in_dim(summed, at + place.fsdp * length, length))
        at += vector.shape[0]
    return (
        block_out,
        input_grad,
        modulation_grad,
        vectors[0],
        qkv.result[0],
        qkv.result[1],
        qkv.result[2],
        vectors[2],
        vectors[3],
        cap.result[0],
        cap.result[1],
        vectors[4],
        vectors[5],
        out.result,
        vectors[1],
        ffn.result[0],
        ffn.result[1],
        down.result,
    )


def solution(mesh):
    def shards(*arrays):
        return layer(Place(mesh), *arrays)

    rows = P(("dp", "fsdp"), None, None)
    marks = P(("dp", "fsdp"), None)
    vector = P("fsdp")
    weight = P("fsdp", None)
    grad = P("fsdp", "dp")
    return jax.shard_map(
        shards,
        mesh=mesh,
        in_specs=(
            (rows, rows, rows, marks, marks, marks, P(("dp", "fsdp")), vector)
            + (weight, weight, weight, vector, vector, weight, weight, vector, vector, weight)
            + (vector, weight, weight, weight, rows)
        ),
        out_specs=(
            (rows, rows, rows, vector, grad, grad, grad, vector, vector, grad, grad, vector)
            + (vector, grad, vector, grad, grad, grad)
        ),
        check_vma=False,
    )
```

time: 665 us -> 632 us (0.950)
  Pallas kernels: 53.2 us -> 145 us
  matrix products: 128 us -> 52.4 us
  waiting for transfers between devices: 229 us -> 166 us
  local copies, waits for them, and re-layouts: 90 us -> 100 us
    pallas_call x3 -> x20, Pallas kernels: 16 us -> 109 us  [the longest x3 42.5 us: attend(): pl.pallas_call(functools.partial(forward_kernel, heads, size, half), grid...]
    ppermute x89 -> x91, waiting for transfers between devices: 229 us -> 166 us  [route(): value = lax.ppermute(value, ('dp', 'fsdp'), pairs)]
    dot_general x22 -> x13, matrix products: 74.8 us -> 27.1 us  [dot(): return jnp.einsum('tc,ce->te', left, right, preferred_element_type=F32)]
    dot_general x11 -> x1, matrix products: 22.9 us -> 3.22 us  [dot_tokens(): return jnp.einsum('tc,te->ce', left, right, preferred_element_type=F32)]
    slice x6 -> x13, local copies, waits for them, and re-layouts: 0.48 us -> 12.3 us  [the longest x1 2.66 us: layer(): attn_all[:, i * columns:(i + 1) * columns]]
    dot_general x12 -> x10, matrix products: 30.6 us -> 22 us  [dot_back(): return jnp.einsum('te,ce->tc', incoming, weight, preferred_element_type=F32)]
    concatenate x13 -> x10, other arithmetic: 15.2 us -> 8.94 us  [the longest x1 2.04 us: layer(): ffn_near = jnp.concatenate([ffn_in, place.core_swap(ffn_in)], axis=0)]
    unnamed x314 -> x418, local copies, waits for them, and re-layouts: 45.4 us -> 46.7 us
  transfers between devices with their start and end apart: 89 -> 91, of which waited for: 28 -> 28; matrix products, arithmetic and copies ran while one was open for 36% -> 27% of each run, Pallas kernels for 8% -> 22%
where the time goes in v3:
time: 632 us; the launch traced here: 623 us
  waiting for transfers between devices  166 us (26%)
  Pallas kernels  145 us (23%)
  local copies, waits for them, and re-layouts  100 us (16%)
  starting transfers between devices  80.6 us (13%)
  other arithmetic  75.5 us (12%)
  matrix products  52.4 us (8%)
    ppermute x91, waiting for transfers between devices, route(): value = lax.ppermute(value, ('dp', 'fsdp'), pairs)  166 us
    ppermute x91, starting transfers between devices, route(): value = lax.ppermute(value, ('dp', 'fsdp'), pairs)  80.6 us
    unnamed x418, local copies, waits for them, and re-layouts  46.7 us
    pallas_call x3, Pallas kernels, attend(): pl.pallas_call(functools.partial(forward_kernel, heads, size, half), grid...  42.5 us
    pallas_call x2, Pallas kernels, attend_back(): pl.pallas_call(functools.partial(backward_kernel, heads, size), grid=(row...  29.6 us
    dot_general x13, matrix products, dot(): return jnp.einsum('tc,ce->te', left, right, preferred_element_type=F32)  27.1 us
    pallas_call x4, Pallas kernels, outer(): pl.pallas_call(functools.partial(outer_kernel, counts), grid_spec=pltpu.P...  24.5 us
    dot_general x10, matrix products, dot_back(): return jnp.einsum('te,ce->tc', incoming, weight, preferred_element_type=F32)  22 us
  transfers between devices with their start and end apart: 91, of which 28 were waited for; matrix products, arithmetic and copies ran while one was open for 27% of the time, Pallas kernels for 22%

profile of v3, /device:TPU:0, one launch (start us, length us, event | category | flops | bytes accessed | tf_op | source)
XLA Modules:
  0.0 623.4 jit_solution(11983818385282134829)
XLA Ops:
  5.7 2.6 collective-permute-start
  8.5 4.6 slice_bitcast_fusion
  20.9 7.9 %collective-permute-done.5 = bf16[2,822]{1,0:T(2,128)(2,1)S(1)} collective-permute-done((bf16[2,822]{1,0:T(2,128)(2,1)S(1)}, bf16[2,822]{1,0:T(2,128)(2,1)S(1)}, u32[]{:S(2)}, u32[]{:S(2)}) %collective-permute-start.5) | collective-permute-done | bytes 3320 | tf_op jit(solution)/shard_map/ppermute | solution.py:592
  31.3 7.5 %collective-permute-done.1 = bf16[128,4096]{1,0:T(8,128)(2,1)} collective-permute-done((bf16[128,4096]{1,0:T(8,128)(2,1)}, bf16[128,4096]{1,0:T(8,128)(2,1)}, u32[]{:S(2)}, u32[]{:S(2)}) %collective-permute-start.1) | collective-permute-done | bytes 1048608 | tf_op jit(solution)/shard_map/ppermute | solution.py:592
  44.2 19.0 %collective-permute-done.2.refs_3_ = bf16[512,768]{1,0:T(8,128)(2,1)} collective-permute-done((bf16[512,768]{1,0:T(8,128)(2,1)S(1)}, bf16[512,768]{1,0:T(8,128)(2,1)}, u32[]{:S(2)}, u32[]{:S(2)}) %collective-permute-start.2) | collective-permute-done | bytes 786464 | tf_op jit(solution)/shard_map/ppermute | solution.py:592
  80.1 7.7 %collective-permute-done.8.refs_4_ = bf16[512,768]{1,0:T(8,128)(2,1)S(1)} collective-permute-done((bf16[512,768]{1,0:T(8,128)(2,1)}, bf16[512,768]{1,0:T(8,128)(2,1)S(1)}, u32[]{:S(2)}, u32[]{:S(2)}) %collective-permute-start.8) | collective-permute-done | bytes 786464 | tf_op jit(solution)/shard_map/ppermute | solution.py:592
  87.9 5.4 collective-permute-done.9
  99.3 4.3 collective-permute-start.14
  109.8 5.8 fusion.95.qkv_ref
  115.6 10.6 %collective-permute-done.15.refs_6_ = bf16[512,768]{1,0:T(8,128)(2,1)S(1)} collective-permute-done((bf16[512,768]{1,0:T(8,128)(2,1)S(1)}, bf16[512,768]{1,0:T(8,128)(2,1)S(1)}, u32[]{:S(2)}, u32[]{:S(2)}) %collective-permute-start.15) | collective-permute-done | bytes 786464 | tf_op jit(solution)/shard_map/ppermute | solution.py:592
  127.0 3.3 collective-permute-done.16
  150.1 2.7 copy-done.1
  152.9 19.6 %shard_map.361 = (f32[1024,768]{1,0:T(8,128)S(1)}, bf16[512,384]{1,0:T(8,128)(2,1)S(1)}, f32[384,512]{1,0:T(8,128)S(1)}) custom-call(f32[1024,1152]{1,0:T(8,128)} %fusion.95.qkv_ref, bf16[512,4096]{1,0:T(8,128)(2,1)} %bitcast.204, bf16[512,4096]{1,0:T(8,128)(2,1)} %collective-permute-done.10.second_ref.refs_3_, bf16[4096,768]{1,0:T(8,128)(2,1)} %copy-done.1, ...), custom_call_target="tpu_custom_call" | custom-call | flops 1024 | bytes 1024 | tf_op jit(solution)/shard_map/pallas_call | solution.py:322
  189.2 11.3 %shard_map.360 = (f32[512,768]{1,0:T(8,128)S(1)}, bf16[256,384]{1,0:T(8,128)(2,1)S(1)}, f32[384,256]{1,0:T(8,128)S(1)}) custom-call(f32[1024,1152]{1,0:T(8,128)} %fusion.95.qkv_ref, bf16[256,4096]{1,0:T(8,128)(2,1)S(1)} %constant_dynamic-update-slice_fusion.first_ref.refs_4_, bf16[256,4096]{1,0:T(8,128)(2,1)} %collective-permute-done.18.second_ref.refs_5_, ...), custom_call_target="tpu_custom_call" | custom-call | flops 1024 | bytes 1024 | tf_op jit(solution)/shard_map/pallas_call | solution.py:322
  204.5 11.6 %shard_map.362 = (f32[512,768]{1,0:T(8,128)S(1)}, bf16[256,384]{1,0:T(8,128)(2,1)S(1)}, f32[384,256]{1,0:T(8,128)S(1)}) custom-call(f32[1024,1152]{1,0:T(8,128)} %fusion.95.qkv_ref, bf16[256,4096]{1,0:T(8,128)(2,1)S(1)} %copy-done.5, bf16[256,4096]{1,0:T(8,128)(2,1)} %copy-done.7, bf16[4096,768]{1,0:T(8,128)(2,1)} %copy-done.1, ...), custom_call_target="tpu_custom_call" | custom-call | flops 1024 | bytes 1024 | tf_op jit(solution)/shard_map/pallas_call | solution.py:322
  233.8 7.2 %collective-permute-done.34.refs_6_ = bf16[192,2048]{1,0:T(8,128)(2,1)} collective-permute-done((bf16[192,2048]{1,0:T(8,128)(2,1)}, bf16[192,2048]{1,0:T(8,128)(2,1)}, u32[]{:S(2)}, u32[]{:S(2)}) %collective-permute-start.34) | collective-permute-done | bytes 786464 | tf_op jit(solution)/shard_map/ppermute | solution.py:592
  241.0 2.7 shard_map.364.gate_ref.up_ref
  243.7 2.7 copy-done
  257.7 2.7 fusion.79
  263.7 8.0 %shard_map.366 = (bf16[512,1024]{1,0:T(8,128)(2,1)S(1)}, bf16[512,2048]{1,0:T(8,128)(2,1)S(1)}) custom-call(bf16[512,1536]{1,0:T(8,128)(2,1)S(1)} %pad_maximum_fusion.6.ffn_ref.refs_2_, bf16[1536,2048]{1,0:T(8,128)(2,1)} %copy-done, bf16[1536,2048]{1,0:T(8,128)(2,1)} %copy-done, bf16[512,1536]{1,0:T(8,128)(2,1)S(1)} %pad_maximum_fusion.7.branch_ref.refs_0_, ...), custom_call_target="tpu_custom_call" | custom-call | flops 1024 | bytes 1024 | tf_op jit(solution)/shard_map/pallas_call | solution.py:443
  271.7 4.8 collective-permute-done.36
  281.9 7.8 %shard_map.367 = (bf16[512,1024]{1,0:T(8,128)(2,1)S(1)}, bf16[512,2048]{1,0:T(8,128)(2,1)S(1)}) custom-call(bf16[512,1536]{1,0:T(8,128)(2,1)S(1)} %constant_dynamic-update-slice_fusion.4.ffn_ref.refs_3_, bf16[1536,2048]{1,0:T(8,128)(2,1)} %copy-done, bf16[1536,2048]{1,0:T(8,128)(2,1)} %copy-done, ...), custom_call_target="tpu_custom_call" | custom-call | flops 1024 | bytes 1024 | tf_op jit(solution)/shard_map/pallas_call | solution.py:443
  298.9 2.7 convolution_convert_fusion.4
  301.6 2.7 fusion.13
  308.8 2.5 shard_map.374
  318.8 3.6 convolution_add_fusion.6
  339.8 14.7 %shard_map.376 = (bf16[1152,512]{1,0:T(8,128)(2,1)S(1)}, bf16[512,1152]{1,0:T(8,128)(2,1)S(1)}, bf16[768,1024]{1,0:T(8,128)(2,1)S(1)}, f32[3,64,128]{2,1,0:T(8,128)S(1)}, f32[6,1,128]{2,1,0:T(1,128)S(1)}) custom-call(f32[1024,1152]{1,0:T(8,128)S(1)} %bitcast.190, f32[1024,768]{1,0:T(8,128)S(1)} %copy-done.32, f32[64,1024]{1,0:T(8,128)S(1)} %copy-done.19, ...), custom_call_target="tpu_custom_call" | custom-call | flops 1024 | bytes 1024 | tf_op jit(solution)/shard_map/pallas_call | solution.py:360
  359.2 5.4 shard_map.377
  375.9 14.9 %shard_map.378 = (bf16[1152,512]{1,0:T(8,128)(2,1)S(1)}, bf16[512,1152]{1,0:T(8,128)(2,1)S(1)}, bf16[768,1024]{1,0:T(8,128)(2,1)S(1)}, f32[3,64,128]{2,1,0:T(8,128)S(1)}, f32[6,1,128]{2,1,0:T(1,128)S(1)}) custom-call(f32[1024,1152]{1,0:T(8,128)S(1)} %bitcast.190, f32[1024,768]{1,0:T(8,128)S(1)} %copy-done.17, f32[64,1024]{1,0:T(8,128)S(1)} %copy-done.19, ...), custom_call_target="tpu_custom_call" | custom-call | flops 1024 | bytes 1024 | tf_op jit(solution)/shard_map/pallas_call | solution.py:360
  404.4 6.3 %shard_map.380 = bf16[384,2048]{1,0:T(8,128)(2,1)S(1)} custom-call(s32[5]{0:T(128)S(1)} %copy-done.65, bf16[768,1024]{1,0:T(8,128)(2,1)S(1)} %bitcast.191, bf16[768,1024]{1,0:T(8,128)(2,1)S(1)} %bitcast.195, bf16[512,4096]{1,0:T(8,128)(2,1)} %bitcast.205, bf16[512,4096]{1,0:T(8,128)(2,1)} %collective-permute-done.10.second_ref.refs_3_, ...), custom_call_target="tpu_custom_call" | custom-call | flops 1024 | bytes 1024 | tf_op jit(solution)/shard_map/pallas_call | solution.py:404
  410.8 5.9 shard_map.379
  424.1 3.2 fusion.8
  431.8 2.6 collective-permute-start.54
  436.4 6.3 %shard_map.382 = bf16[384,2048]{1,0:T(8,128)(2,1)S(1)} custom-call(s32[5]{0:T(128)S(1)} %stack.186.place_ref, bf16[768,1024]{1,0:T(8,128)(2,1)S(1)} %bitcast.193, bf16[768,1024]{1,0:T(8,128)(2,1)S(1)} %bitcast.197, bf16[512,4096]{1,0:T(8,128)(2,1)} %bitcast.207, bf16[512,4096]{1,0:T(8,128)(2,1)} %collective-permute-done.10.second_ref.refs_3_, ...), custom_call_target="tpu_custom_call" | custom-call | flops 1024 | bytes 1024 | tf_op jit(solution)/shard_map/pallas_call | solution.py:404
  442.8 5.8 shard_map.381
  455.3 2.7 collective-permute-done.55
  474.3 7.2 %collective-permute-done.65 = bf16[256,1536]{1,0:T(8,128)(2,1)S(1)} collective-permute-done((bf16[256,1536]{1,0:T(8,128)(2,1)S(1)}, bf16[256,1536]{1,0:T(8,128)(2,1)S(1)}, u32[]{:S(2)}, u32[]{:S(2)}) %collective-permute-start.65) | collective-permute-done | bytes 786464 | tf_op jit(solution)/shard_map/ppermute | solution.py:592
  481.6 2.6 collective-permute-start.60
  488.7 10.0 %collective-permute-done.63 = bf16[192,1024]{1,0:T(8,128)(2,1)S(1)} collective-permute-done((bf16[192,1024]{1,0:T(8,128)(2,1)S(1)}, bf16[192,1024]{1,0:T(8,128)(2,1)S(1)}, u32[]{:S(2)}, u32[]{:S(2)}) %collective-permute-start.63) | collective-permute-done | bytes 393248 | tf_op jit(solution)/shard_map/ppermute | solution.py:592
  504.9 3.4 broadcast_select_fusion.5
  522.4 10.1 %collective-permute-done.72 = bf16[384,384]{1,0:T(8,128)(2,1)S(1)} collective-permute-done((bf16[384,384]{1,0:T(8,128)(2,1)S(1)}, bf16[384,384]{1,0:T(8,128)(2,1)S(1)}, u32[]{:S(2)}, u32[]{:S(2)}) %collective-permute-start.72) | collective-permute-done | bytes 294944 | tf_op jit(solution)/shard_map/ppermute | solution.py:592
  541.2 10.3 %collective-permute-done.77 = bf16[192,1024]{1,0:T(8,128)(2,1)} collective-permute-done((bf16[192,1024]{1,0:T(8,128)(2,1)S(1)}, bf16[192,1024]{1,0:T(8,128)(2,1)}, u32[]{:S(2)}, u32[]{:S(2)}) %collective-permute-start.77) | collective-permute-done | bytes 393248 | tf_op jit(solution)/shard_map/ppermute | solution.py:592
  553.2 4.0 collective-permute-done.75
  557.3 2.5 collective-permute-done.69
  564.8 2.9 collective-permute-start.87
  568.0 14.5 %collective-permute-done.88 = bf16[192,384]{1,0:T(8,128)(2,1)} collective-permute-done((bf16[192,384]{1,0:T(8,128)(2,1)}, bf16[192,384]{1,0:T(8,128)(2,1)}, u32[]{:S(2)}, u32[]{:S(2)}) %collective-permute-start.88) | collective-permute-done | bytes 147488 | tf_op jit(solution)/shard_map/ppermute | solution.py:592
  591.9 3.5 collective-permute-start.84
  601.8 18.2 %collective-permute-done.85 = f32[3288]{0:T(1024)S(1)} collective-permute-done((f32[3288]{0:T(1024)S(1)}, f32[3288]{0:T(1024)S(1)}, u32[]{:S(2)}, u32[]{:S(2)}) %collective-permute-start.85) | collective-permute-done | bytes 13184 | tf_op jit(solution)/shard_map/ppermute | solution.py:592
  (786 shorter events, 290.9 us)
Async XLA Ops:
  5.7 25.6 %collective-permute-start = (bf16[384,1152]{1,0:T(8,128)(2,1)}, bf16[384,1152]{1,0:T(8,128)(2,1)S(1)}, u32[]{:S(2)}, u32[]{:S(2)}) collective-permute-start(bf16[384,1152]{1,0:T(8,128)(2,1)} %pad_maximum_fusion.12), channel_id=1, source_target_pairs={{0,2},{1,3},{2,0},{3,1},{4,7},{5,6},{6,5},{7,4},{8,10},{9,11},{10,... | collective-permute-start | bytes 2654216 | tf_op jit(solution)/shard_map/ppermute | solution.py:592
  8.3 20.6 %collective-permute-start.10 = (bf16[512,4096]{1,0:T(8,128)(2,1)}, bf16[512,4096]{1,0:T(8,128)(2,1)}, u32[]{:S(2)}, u32[]{:S(2)}) collective-permute-start(bf16[512,4096]{1,0:T(8,128)(2,1)} %bitcast.203), channel_id=1, source_target_pairs={{0,1},{1,0},{2,3},{3,2},{4,5},{5,4},{6,7},{7,6},{8,9},{9,8},{10,11... | collective-permute-start | bytes 12582920 | tf_op jit(solution)/shard_map/ppermute | solution.py:592
  13.1 25.7 %collective-permute-start.1 = (bf16[128,4096]{1,0:T(8,128)(2,1)}, bf16[128,4096]{1,0:T(8,128)(2,1)}, u32[]{:S(2)}, u32[]{:S(2)}) collective-permute-start(bf16[128,4096]{1,0:T(8,128)(2,1)} %get-tuple-element.548), channel_id=1, source_target_pairs={{0,8},{1,9},{2,10},{3,11},{4,12},{5,13},{6,14},{7,15},{8,0},{9,1},... | collective-permute-start | bytes 3145736 | tf_op jit(solution)/shard_map/ppermute | solution.py:592
  38.8 24.3 %collective-permute-start.6 = (bf16[272,1536]{1,0:T(8,128)(2,1)S(1)}, bf16[272,1536]{1,0:T(8,128)(2,1)S(1)}, u32[]{:S(2)}, u32[]{:S(2)}) collective-permute-start(bf16[272,1536]{1,0:T(8,128)(2,1)S(1)} %pad_maximum_fusion.14), channel_id=1, source_target_pairs={{0,8},{1,9},{2,10},{3,11},{4,12},{5,13},{6,14},{7,15},{8,0},{9,1},... | collective-permute-start | bytes 2506760 | tf_op jit(solution)/shard_map/ppermute | solution.py:592
  40.4 22.8 %collective-permute-start.3 = (bf16[384,1152]{1,0:T(8,128)(2,1)S(1)}, bf16[384,1152]{1,0:T(8,128)(2,1)S(1)}, u32[]{:S(2)}, u32[]{:S(2)}) collective-permute-start(bf16[384,1152]{1,0:T(8,128)(2,1)S(1)} %collective-permute-done.refs_4_), channel_id=1, source_target_pairs={{0,4},{1,5},{2,6},{3,7},{4,0},{5,1},{6,2},{7,3},{8,12},{9,13},{10,... | collective-permute-start | bytes 2654216 | tf_op jit(solution)/shard_map/ppermute | solution.py:592
  42.0 22.1 %collective-permute-start.12 = (bf16[272,1536]{1,0:T(8,128)(2,1)S(1)}, bf16[272,1536]{1,0:T(8,128)(2,1)S(1)}, u32[]{:S(2)}, u32[]{:S(2)}) collective-permute-start(bf16[272,1536]{1,0:T(8,128)(2,1)S(1)} %pad_maximum_fusion.14), channel_id=1, source_target_pairs={{0,1},{1,0},{2,3},{3,2},{4,5},{5,4},{6,7},{7,6},{8,9},{9,8},{10,11... | collective-permute-start | bytes 2506760 | tf_op jit(solution)/shard_map/ppermute | solution.py:592
  67.4 27.2 %collective-permute-start.17 = (bf16[1024,768]{1,0:T(8,128)(2,1)}, bf16[1024,768]{1,0:T(8,128)(2,1)}, u32[]{:S(2)}, u32[]{:S(2)}) collective-permute-start(bf16[1024,768]{1,0:T(8,128)(2,1)} %pad_maximum_fusion.4), channel_id=1, source_target_pairs={{0,1},{1,0},{2,3},{3,2},{4,5},{5,4},{6,7},{7,6},{8,9},{9,8},{10,11... | collective-permute-start | bytes 4718600 | tf_op jit(solution)/shard_map/ppermute | solution.py:592
  67.5 25.8 %collective-permute-start.9 = (bf16[128,4096]{1,0:T(8,128)(2,1)}, bf16[128,4096]{1,0:T(8,128)(2,1)}, u32[]{:S(2)}, u32[]{:S(2)}) collective-permute-start(bf16[128,4096]{1,0:T(8,128)(2,1)} %get-tuple-element.263), channel_id=1, source_target_pairs={{0,8},{1,9},{2,10},{3,11},{4,12},{5,13},{6,14},{7,15},{8,0},{9,1},... | collective-permute-start | bytes 3145736 | tf_op jit(solution)/shard_map/ppermute | solution.py:592
  99.3 31.0 %collective-permute-start.14 = (bf16[704,1536]{1,0:T(8,128)(2,1)}, bf16[704,1536]{1,0:T(8,128)(2,1)}, u32[]{:S(2)}, u32[]{:S(2)}) collective-permute-start(bf16[704,1536]{1,0:T(8,128)(2,1)} %pad_maximum_fusion.3), channel_id=1, source_target_pairs={{0,2},{2,1},{4,6},{6,5},{9,10},{11,9},{13,14},{15,13},{16,18},{18,... | collective-permute-start | bytes 6488072 | tf_op jit(solution)/shard_map/ppermute | solution.py:592
  107.8 22.6 %collective-permute-start.16 = (bf16[128,4096]{1,0:T(8,128)(2,1)S(1)}, bf16[128,4096]{1,0:T(8,128)(2,1)S(1)}, u32[]{:S(2)}, u32[]{:S(2)}) collective-permute-start(bf16[128,4096]{1,0:T(8,128)(2,1)S(1)} %copy-done.119), channel_id=1, source_target_pairs={{0,8},{1,9},{2,10},{3,11},{4,12},{5,13},{6,14},{7,15},{8,0},{9,1},... | collective-permute-start | bytes 3145736 | tf_op jit(solution)/shard_map/ppermute | solution.py:592
  108.6 24.4 %collective-permute-start.25 = (bf16[384,2048]{1,0:T(8,128)(2,1)S(1)}, bf16[384,2048]{1,0:T(8,128)(2,1)S(1)}, u32[]{:S(2)}, u32[]{:S(2)}) collective-permute-start(bf16[384,2048]{1,0:T(8,128)(2,1)S(1)} %pad_maximum_fusion.5), channel_id=1, source_target_pairs={{0,1},{1,0},{2,3},{3,2},{4,5},{5,4},{6,7},{7,6},{8,9},{9,8},{10,11... | collective-permute-start | bytes 4718600 | tf_op jit(solution)/shard_map/ppermute | solution.py:592
  130.3 44.2 %collective-permute-start.20 = (bf16[704,1536]{1,0:T(8,128)(2,1)}, bf16[704,1536]{1,0:T(8,128)(2,1)}, u32[]{:S(2)}, u32[]{:S(2)}) collective-permute-start(bf16[704,1536]{1,0:T(8,128)(2,1)} %collective-permute-done.14), channel_id=1, source_target_pairs={{1,5},{2,6},{5,1},{6,2},{9,13},{10,14},{13,9},{14,10},{17,21},{18,... | collective-permute-start | bytes 6488072 | tf_op jit(solution)/shard_map/ppermute | solution.py:592
  134.2 39.2 %collective-permute-start.26 = (bf16[384,1536]{1,0:T(8,128)(2,1)}, bf16[384,1536]{1,0:T(8,128)(2,1)}, u32[]{:S(2)}, u32[]{:S(2)}) collective-permute-start(bf16[384,1536]{1,0:T(8,128)(2,1)} %shard.2), channel_id=1, source_target_pairs={{2,3},{6,7},{9,8},{13,12},{18,19},{22,23},{25,24},{29,28}} | collective-permute-start | bytes 3538952 | tf_op jit(solution)/shard_map/ppermute | solution.py:592
  137.1 37.4 %collective-permute-start.21 = (bf16[128,4096]{1,0:T(8,128)(2,1)}, bf16[128,4096]{1,0:T(8,128)(2,1)}, u32[]{:S(2)}, u32[]{:S(2)}) collective-permute-start(bf16[128,4096]{1,0:T(8,128)(2,1)} %get-tuple-element.286), channel_id=1, source_target_pairs={{0,8},{1,9},{2,10},{3,11},{4,12},{5,13},{6,14},{7,15},{8,0},{9,1},... | collective-permute-start | bytes 3145736 | tf_op jit(solution)/shard_map/ppermute | solution.py:592
  140.2 34.3 %collective-permute-start.19 = (bf16[192,2048]{1,0:T(8,128)(2,1)}, bf16[192,2048]{1,0:T(8,128)(2,1)}, u32[]{:S(2)}, u32[]{:S(2)}) collective-permute-start(bf16[192,2048]{1,0:T(8,128)(2,1)} %get-tuple-element.284), channel_id=1, source_target_pairs={{0,2},{1,3},{2,0},{3,1},{4,7},{5,6},{6,5},{7,4},{8,10},{9,11},{10,... | collective-permute-start | bytes 2359304 | tf_op jit(solution)/shard_map/ppermute | solution.py:592
  182.0 35.7 %collective-permute-start.29 = (bf16[1024,1536]{1,0:T(8,128)(2,1)}, bf16[1024,1536]{1,0:T(8,128)(2,1)}, u32[]{:S(2)}, u32[]{:S(2)}) collective-permute-start(bf16[1024,1536]{1,0:T(8,128)(2,1)} %shard.3), channel_id=1, source_target_pairs={{2,3},{6,7},{9,8},{13,12},{18,19},{22,23},{25,24},{29,28}} | collective-permute-start | bytes 9437192 | tf_op jit(solution)/shard_map/ppermute | solution.py:592
  184.3 31.9 %collective-permute-start.24 = (bf16[256,1536]{1,0:T(8,128)(2,1)}, bf16[256,1536]{1,0:T(8,128)(2,1)}, u32[]{:S(2)}, u32[]{:S(2)}) collective-permute-start(bf16[256,1536]{1,0:T(8,128)(2,1)} %bitcast.19), channel_id=1, source_target_pairs={{0,8},{1,9},{2,10},{3,11},{4,12},{5,13},{6,14},{7,15},{8,0},{9,1},... | collective-permute-start | bytes 2359304 | tf_op jit(solution)/shard_map/ppermute | solution.py:592
  184.7 31.4 %collective-permute-start.23 = (bf16[192,2048]{1,0:T(8,128)(2,1)}, bf16[192,2048]{1,0:T(8,128)(2,1)}, u32[]{:S(2)}, u32[]{:S(2)}) collective-permute-start(bf16[192,2048]{1,0:T(8,128)(2,1)} %collective-permute-done.19.refs_3_), channel_id=1, source_target_pairs={{0,4},{1,5},{2,6},{3,7},{4,0},{5,1},{6,2},{7,3},{8,12},{9,13},{10,... | collective-permute-start | bytes 2359304 | tf_op jit(solution)/shard_map/ppermute | solution.py:592
  186.4 29.7 %collective-permute-start.22 = (bf16[192,2048]{1,0:T(8,128)(2,1)}, bf16[192,2048]{1,0:T(8,128)(2,1)}, u32[]{:S(2)}, u32[]{:S(2)}) collective-permute-start(bf16[192,2048]{1,0:T(8,128)(2,1)} %get-tuple-element.292), channel_id=1, source_target_pairs={{0,2},{1,3},{2,0},{3,1},{4,7},{5,6},{6,5},{7,4},{8,10},{9,11},{10,... | collective-permute-start | bytes 2359304 | tf_op jit(solution)/shard_map/ppermute | solution.py:592
  222.9 26.0 %collective-permute-start.33 = (bf16[256,1536]{1,0:T(8,128)(2,1)}, bf16[256,1536]{1,0:T(8,128)(2,1)}, u32[]{:S(2)}, u32[]{:S(2)}) collective-permute-start(bf16[256,1536]{1,0:T(8,128)(2,1)} %convolution_convert_fusion.6), channel_id=1, source_target_pairs={{0,1},{1,0},{2,3},{3,2},{4,5},{5,4},{6,7},{7,6},{8,9},{9,8},{10,11... | collective-permute-start | bytes 2359304 | tf_op jit(solution)/shard_map/ppermute | solution.py:592
  225.3 26.0 %collective-permute-start.31 = (bf16[256,1536]{1,0:T(8,128)(2,1)}, bf16[256,1536]{1,0:T(8,128)(2,1)}, u32[]{:S(2)}, u32[]{:S(2)}) collective-permute-start(bf16[256,1536]{1,0:T(8,128)(2,1)} %fusion.11), channel_id=1, source_target_pairs={{0,8},{1,9},{2,10},{3,11},{4,12},{5,13},{6,14},{7,15},{8,0},{9,1},... | collective-permute-start | bytes 2359304 | tf_op jit(solution)/shard_map/ppermute | solution.py:592
  295.3 27.1 %collective-permute-start.39 = (bf16[256,1536]{1,0:T(8,128)(2,1)S(1)}, bf16[256,1536]{1,0:T(8,128)(2,1)}, u32[]{:S(2)}, u32[]{:S(2)}) collective-permute-start(bf16[256,1536]{1,0:T(8,128)(2,1)S(1)} %shard_map.369), channel_id=1, source_target_pairs={{0,4},{1,5},{2,6},{3,7},{4,0},{5,1},{6,2},{7,3},{8,12},{9,13},{10,... | collective-permute-start | bytes 2359304 | tf_op jit(solution)/shard_map/ppermute | solution.py:592
  298.0 24.3 %collective-permute-start.38 = (bf16[512,768]{1,0:T(8,128)(2,1)S(1)}, bf16[512,768]{1,0:T(8,128)(2,1)}, u32[]{:S(2)}, u32[]{:S(2)}) collective-permute-start(bf16[512,768]{1,0:T(8,128)(2,1)S(1)} %shard_map.368), channel_id=1, source_target_pairs={{0,2},{1,3},{2,0},{3,1},{4,6},{5,7},{6,4},{7,5},{8,10},{9,11},{10,... | collective-permute-start | bytes 2359304 | tf_op jit(solution)/shard_map/ppermute | solution.py:592
  330.3 24.2 %collective-permute-start.45 = (bf16[256,1536]{1,0:T(8,128)(2,1)}, bf16[256,1536]{1,0:T(8,128)(2,1)}, u32[]{:S(2)}, u32[]{:S(2)}) collective-permute-start(bf16[256,1536]{1,0:T(8,128)(2,1)} %bitcast.31), channel_id=1, source_target_pairs={{0,8},{1,9},{2,10},{3,11},{4,12},{5,13},{6,14},{7,15},{8,0},{9,1},... | collective-permute-start | bytes 2359304 | tf_op jit(solution)/shard_map/ppermute | solution.py:592
  331.3 23.2 %collective-permute-start.44 = (bf16[256,1536]{1,0:T(8,128)(2,1)}, bf16[256,1536]{1,0:T(8,128)(2,1)S(1)}, u32[]{:S(2)}, u32[]{:S(2)}) collective-permute-start(bf16[256,1536]{1,0:T(8,128)(2,1)} %shard_map.375), channel_id=1, source_target_pairs={{0,4},{1,5},{2,6},{3,7},{4,0},{5,1},{6,2},{7,3},{8,12},{9,13},{10,... | collective-permute-start | bytes 2359304 | tf_op jit(solution)/shard_map/ppermute | solution.py:592
  332.4 22.2 %collective-permute-start.43 = (bf16[512,768]{1,0:T(8,128)(2,1)S(1)}, bf16[512,768]{1,0:T(8,128)(2,1)S(1)}, u32[]{:S(2)}, u32[]{:S(2)}) collective-permute-start(bf16[512,768]{1,0:T(8,128)(2,1)S(1)} %shard_map.374), channel_id=1, source_target_pairs={{0,2},{1,3},{2,0},{3,1},{4,6},{5,7},{6,4},{7,5},{8,10},{9,11},{10,... | collective-permute-start | bytes 2359304 | tf_op jit(solution)/shard_map/ppermute | solution.py:592
  359.1 34.7 %collective-permute-start.48 = (bf16[512,768]{1,0:T(8,128)(2,1)}, bf16[512,768]{1,0:T(8,128)(2,1)}, u32[]{:S(2)}, u32[]{:S(2)}) collective-permute-start(bf16[512,768]{1,0:T(8,128)(2,1)} %add_convert_fusion.5), channel_id=1, source_target_pairs={{0,2},{1,3},{2,0},{3,1},{4,6},{5,7},{6,4},{7,5},{8,10},{9,11},{10,... | collective-permute-start | bytes 2359304 | tf_op jit(solution)/shard_map/ppermute | solution.py:592
  364.8 26.1 %collective-permute-start.50 = (bf16[2,384,1024]{2,1,0:T(8,128)(2,1)S(1)}, bf16[2,384,1024]{2,1,0:T(8,128)(2,1)}, u32[]{:S(2)}, u32[]{:S(2)}) collective-permute-start(bf16[2,384,1024]{2,1,0:T(8,128)(2,1)S(1)} %dynamic-slice_bitcast_fusion), channel_id=1, source_target_pairs={{0,1},{1,0},{2,3},{3,2},{4,5},{5,4},{6,7},{7,6},{8,9},{9,8},{10,11... | collective-permute-start | bytes 4718600 | tf_op jit(solution)/shard_map/ppermute | solution.py:592
  367.5 26.3 %collective-permute-start.47 = (bf16[512,768]{1,0:T(8,128)(2,1)}, bf16[512,768]{1,0:T(8,128)(2,1)}, u32[]{:S(2)}, u32[]{:S(2)}) collective-permute-start(bf16[512,768]{1,0:T(8,128)(2,1)} %add_convert_fusion.6), channel_id=1, source_target_pairs={{0,4},{1,5},{2,6},{3,7},{4,0},{5,1},{6,2},{7,3},{8,12},{9,13},{10,... | collective-permute-start | bytes 2359304 | tf_op jit(solution)/shard_map/ppermute | solution.py:592
  394.9 21.8 %collective-permute-start.53 = (bf16[192,2048]{1,0:T(8,128)(2,1)}, bf16[192,2048]{1,0:T(8,128)(2,1)S(1)}, u32[]{:S(2)}, u32[]{:S(2)}) collective-permute-start(bf16[192,2048]{1,0:T(8,128)(2,1)} %get-tuple-element.381), channel_id=1, source_target_pairs={{0,4},{1,5},{2,6},{3,7},{4,0},{5,1},{6,2},{7,3},{8,12},{9,13},{10,... | collective-permute-start | bytes 2359304 | tf_op jit(solution)/shard_map/ppermute | solution.py:592
  394.9 21.8 %collective-permute-start.52 = (bf16[384,1024]{1,0:T(8,128)(2,1)S(1)}, bf16[384,1024]{1,0:T(8,128)(2,1)}, u32[]{:S(2)}, u32[]{:S(2)}) collective-permute-start(bf16[384,1024]{1,0:T(8,128)(2,1)S(1)} %get-tuple-element.380), channel_id=1, source_target_pairs={{0,2},{1,3},{2,0},{3,1},{4,6},{5,7},{6,4},{7,5},{8,10},{9,11},{10,... | collective-permute-start | bytes 2359304 | tf_op jit(solution)/shard_map/ppermute | solution.py:592
  418.5 36.7 %collective-permute-start.56 = (bf16[384,2048]{1,0:T(8,128)(2,1)S(1)}, bf16[384,2048]{1,0:T(8,128)(2,1)}, u32[]{:S(2)}, u32[]{:S(2)}) collective-permute-start(bf16[384,2048]{1,0:T(8,128)(2,1)S(1)} %shard_map.380), channel_id=1, source_target_pairs={{0,4},{1,5},{2,6},{3,7},{4,0},{5,1},{6,2},{7,3},{8,12},{9,13},{10,... | collective-permute-start | bytes 4718600 | tf_op jit(solution)/shard_map/ppermute | solution.py:592
  420.6 37.4 %collective-permute-start.55 = (bf16[768,1024]{1,0:T(8,128)(2,1)S(1)}, bf16[768,1024]{1,0:T(8,128)(2,1)}, u32[]{:S(2)}, u32[]{:S(2)}) collective-permute-start(bf16[768,1024]{1,0:T(8,128)(2,1)S(1)} %shard_map.379), channel_id=1, source_target_pairs={{0,2},{1,3},{2,0},{3,1},{4,6},{5,7},{6,4},{7,5},{8,10},{9,11},{10,... | collective-permute-start | bytes 4718600 | tf_op jit(solution)/shard_map/ppermute | solution.py:592
  430.8 21.3 %collective-permute-start.59 = (bf16[2,384,384]{2,1,0:T(8,128)(2,1)S(1)}, bf16[2,384,384]{2,1,0:T(8,128)(2,1)}, u32[]{:S(2)}, u32[]{:S(2)}) collective-permute-start(bf16[2,384,384]{2,1,0:T(8,128)(2,1)S(1)} %dynamic-slice_bitcast_fusion.1), channel_id=1, source_target_pairs={{0,1},{1,0},{2,3},{3,2},{4,5},{5,4},{6,7},{7,6},{8,9},{9,8},{10,11... | collective-permute-start | bytes 1769480 | tf_op jit(solution)/shard_map/ppermute | solution.py:592
  431.8 23.1 %collective-permute-start.54 = (bf16[512,384]{1,0:T(8,128)(2,1)}, bf16[512,384]{1,0:T(8,128)(2,1)S(1)}, u32[]{:S(2)}, u32[]{:S(2)}) collective-permute-start(bf16[512,384]{1,0:T(8,128)(2,1)} %get-tuple-element.394), channel_id=1, source_target_pairs={{0,16},{1,17},{2,18},{3,19},{4,20},{5,21},{6,22},{7,23},{8,24},{9,... | collective-permute-start | bytes 1179656 | tf_op jit(solution)/shard_map/ppermute | solution.py:592
  434.4 52.2 %collective-permute-start.64 = (bf16[192,1024]{1,0:T(8,128)(2,1)}, bf16[192,1024]{1,0:T(8,128)(2,1)S(1)}, u32[]{:S(2)}, u32[]{:S(2)}) collective-permute-start(bf16[192,1024]{1,0:T(8,128)(2,1)} %add_convert_fusion.14), channel_id=1, source_target_pairs={{0,2},{1,3},{2,0},{3,1},{4,6},{5,7},{6,4},{7,5},{8,10},{9,11},{10,... | collective-permute-start | bytes 1179656 | tf_op jit(solution)/shard_map/ppermute | solution.py:592
  463.5 38.0 %collective-permute-start.62 = (bf16[384,1024]{1,0:T(8,128)(2,1)S(1)}, bf16[384,1024]{1,0:T(8,128)(2,1)S(1)}, u32[]{:S(2)}, u32[]{:S(2)}) collective-permute-start(bf16[384,1024]{1,0:T(8,128)(2,1)S(1)} %add_convert_fusion.3), channel_id=1, source_target_pairs={{0,2},{1,3},{2,0},{3,1},{4,6},{5,7},{6,4},{7,5},{8,10},{9,11},{10,... | collective-permute-start | bytes 2359304 | tf_op jit(solution)/shard_map/ppermute | solution.py:592
  469.8 31.6 %collective-permute-start.61 = (bf16[384,1024]{1,0:T(8,128)(2,1)S(1)}, bf16[384,1024]{1,0:T(8,128)(2,1)S(1)}, u32[]{:S(2)}, u32[]{:S(2)}) collective-permute-start(bf16[384,1024]{1,0:T(8,128)(2,1)S(1)} %add_convert_fusion.4), channel_id=1, source_target_pairs={{0,4},{1,5},{2,6},{3,7},{4,0},{5,1},{6,2},{7,3},{8,12},{9,13},{10,... | collective-permute-start | bytes 2359304 | tf_op jit(solution)/shard_map/ppermute | solution.py:592
  486.6 35.8 %collective-permute-start.73 = (bf16[192,768]{1,0:T(8,128)(2,1)}, bf16[192,768]{1,0:T(8,128)(2,1)}, u32[]{:S(2)}, u32[]{:S(2)}) collective-permute-start(bf16[192,768]{1,0:T(8,128)(2,1)} %get-tuple-element.448), channel_id=1, source_target_pairs={{0,4},{1,5},{2,6},{3,7},{4,0},{5,1},{6,2},{7,3},{8,12},{9,13},{10,... | collective-permute-start | bytes 884744 | tf_op jit(solution)/shard_map/ppermute | solution.py:592
  498.6 33.9 %collective-permute-start.74 = (bf16[256,1536]{1,0:T(8,128)(2,1)}, bf16[256,1536]{1,0:T(8,128)(2,1)}, u32[]{:S(2)}, u32[]{:S(2)}) collective-permute-start(bf16[256,1536]{1,0:T(8,128)(2,1)} %fusion.14), channel_id=1, source_target_pairs={{0,8},{1,9},{2,10},{3,11},{4,12},{5,13},{6,14},{7,15},{8,0},{9,1},... | collective-permute-start | bytes 2359304 | tf_op jit(solution)/shard_map/ppermute | solution.py:592
  503.0 29.5 %collective-permute-start.71 = (bf16[576,768]{1,0:T(8,128)(2,1)}, bf16[576,768]{1,0:T(8,128)(2,1)}, u32[]{:S(2)}, u32[]{:S(2)}) collective-permute-start(bf16[576,768]{1,0:T(8,128)(2,1)} %convolution_convert_fusion.11), channel_id=1, source_target_pairs={{0,4},{1,5},{2,6},{3,7},{4,0},{5,1},{6,2},{7,3},{8,12},{9,13},{10,... | collective-permute-start | bytes 2654216 | tf_op jit(solution)/shard_map/ppermute | solution.py:592
  504.7 27.8 %collective-permute-start.70 = (bf16[1152,384]{1,0:T(8,128)(2,1)}, bf16[1152,384]{1,0:T(8,128)(2,1)}, u32[]{:S(2)}, u32[]{:S(2)}) collective-permute-start(bf16[1152,384]{1,0:T(8,128)(2,1)} %convolution_convert_fusion.1), channel_id=1, source_target_pairs={{0,2},{1,3},{2,0},{3,1},{4,6},{5,7},{6,4},{7,5},{8,10},{9,11},{10,... | collective-permute-start | bytes 2654216 | tf_op jit(solution)/shard_map/ppermute | solution.py:592
  522.4 29.1 %collective-permute-start.77 = (bf16[192,1024]{1,0:T(8,128)(2,1)S(1)}, bf16[192,1024]{1,0:T(8,128)(2,1)}, u32[]{:S(2)}, u32[]{:S(2)}) collective-permute-start(bf16[192,1024]{1,0:T(8,128)(2,1)S(1)} %copy-done.149), channel_id=1, source_target_pairs={{0,16},{1,17},{2,18},{3,19},{4,20},{5,21},{6,22},{7,23},{8,24},{9,... | collective-permute-start | bytes 1179656 | tf_op jit(solution)/shard_map/ppermute | solution.py:592
  532.5 27.3 %collective-permute-start.69 = (bf16[192,1024]{1,0:T(8,128)(2,1)S(1)}, bf16[192,1024]{1,0:T(8,128)(2,1)S(1)}, u32[]{:S(2)}, u32[]{:S(2)}) collective-permute-start(bf16[192,1024]{1,0:T(8,128)(2,1)S(1)} %get-tuple-element.443), channel_id=1, source_target_pairs={{0,16},{1,17},{2,18},{3,19},{4,20},{5,21},{6,22},{7,23},{8,24},{9,... | collective-permute-start | bytes 1179656 | tf_op jit(solution)/shard_map/ppermute | solution.py:592
  538.5 21.2 %collective-permute-start.79 = (bf16[576,384]{1,0:T(8,128)(2,1)S(1)}, bf16[576,384]{1,0:T(8,128)(2,1)S(1)}, u32[]{:S(2)}, u32[]{:S(2)}) collective-permute-start(bf16[576,384]{1,0:T(8,128)(2,1)S(1)} %add_convert_fusion.9), channel_id=1, source_target_pairs={{0,2},{1,3},{2,0},{3,1},{4,6},{5,7},{6,4},{7,5},{8,10},{9,11},{10,... | collective-permute-start | bytes 1327112 | tf_op jit(solution)/shard_map/ppermute | solution.py:592
  539.3 20.5 %collective-permute-start.78 = (bf16[576,384]{1,0:T(8,128)(2,1)S(1)}, bf16[576,384]{1,0:T(8,128)(2,1)S(1)}, u32[]{:S(2)}, u32[]{:S(2)}) collective-permute-start(bf16[576,384]{1,0:T(8,128)(2,1)S(1)} %add_convert_fusion.10), channel_id=1, source_target_pairs={{0,4},{1,5},{2,6},{3,7},{4,0},{5,1},{6,2},{7,3},{8,12},{9,13},{10,... | collective-permute-start | bytes 1327112 | tf_op jit(solution)/shard_map/ppermute | solution.py:592
  564.8 30.6 %collective-permute-start.87 = (bf16[192,1024]{1,0:T(8,128)(2,1)}, bf16[192,1024]{1,0:T(8,128)(2,1)}, u32[]{:S(2)}, u32[]{:S(2)}) collective-permute-start(bf16[192,1024]{1,0:T(8,128)(2,1)} %get-tuple-element.483), channel_id=1, source_target_pairs={{0,16},{1,17},{2,18},{3,19},{4,20},{5,21},{6,22},{7,23},{8,24},{9,... | collective-permute-start | bytes 1179656 | tf_op jit(solution)/shard_map/ppermute | solution.py:592
  597.8 24.0 %collective-permute-start.86 = (bf16[576,384]{1,0:T(8,128)(2,1)S(1)}, bf16[576,384]{1,0:T(8,128)(2,1)S(1)}, u32[]{:S(2)}, u32[]{:S(2)}) collective-permute-start(bf16[576,384]{1,0:T(8,128)(2,1)S(1)} %broadcast_select_fusion.10), channel_id=1, source_target_pairs={{0,16},{1,17},{2,18},{3,19},{4,20},{5,21},{6,22},{7,23},{8,24},{9,... | collective-permute-start | bytes 1327112 | tf_op jit(solution)/shard_map/ppermute | solution.py:592
  (246 other events, 1839.5 us)

commit v4 on v3

--- a/solution.py
+++ b/solution.py
@@ -78,7 +78,7 @@
             scratch_shapes=[pltpu.SemaphoreType.DMA((2,))],
         ),
         out_shape=jax.ShapeDtypeStruct(shard.shape, shard.dtype),
-        compiler_params=pltpu.CompilerParams(vmem_limit_bytes=32 * 1024 * 1024),
+        compiler_params=pltpu.CompilerParams(vmem_limit_bytes=50 * 1024 * 1024),
         cost_estimate=SMALL_COST,
     )(index, shard, near, across, far)
 
@@ -341,7 +341,7 @@
             jax.ShapeDtypeStruct((rows * tokens, across), BF16),
             jax.ShapeDtypeStruct((across, rows * tokens), F32),
         ],
-        compiler_params=pltpu.CompilerParams(vmem_limit_bytes=48 * 1024 * 1024),
+        compiler_params=pltpu.CompilerParams(vmem_limit_bytes=34 * 1024 * 1024),
         cost_estimate=SMALL_COST,
     )(qkv, caps[0], caps[1], weight, cos_table, sin_table, marks, gains, tanh)
 
@@ -375,7 +375,7 @@
             whole(out_shape[4].shape),
         ],
         out_shape=out_shape,
-        compiler_params=pltpu.CompilerParams(vmem_limit_bytes=40 * 1024 * 1024),
+        compiler_params=pltpu.CompilerParams(vmem_limit_bytes=24 * 1024 * 1024),
         cost_estimate=SMALL_COST,
     )(qkv, cap, cos_table, sin_table, marks, gains, tanh, crossed, grad)
 
@@ -413,7 +413,7 @@
             out_specs=pl.BlockSpec((rows, width), lambda i, place: (0, i)),
         ),
         out_shape=jax.ShapeDtypeStruct((rows, count * width), BF16),
-        compiler_params=pltpu.CompilerParams(vmem_limit_bytes=40 * 1024 * 1024),
+        compiler_params=pltpu.CompilerParams(vmem_limit_bytes=26 * 1024 * 1024),
         cost_estimate=SMALL_COST,
     )(index, *lefts, *flat)
 
@@ -458,7 +458,7 @@
             jax.ShapeDtypeStruct((tokens, inner), BF16),
             jax.ShapeDtypeStruct((tokens, 2 * inner), BF16),
         ],
-        compiler_params=pltpu.CompilerParams(vmem_limit_bytes=40 * 1024 * 1024),
+        compiler_params=pltpu.CompilerParams(vmem_limit_bytes=52 * 1024 * 1024),
         cost_estimate=SMALL_COST,
     )(ffn_in, w_ffn, w_ffn, grad_branch, w_down)
 
@@ -469,6 +469,36 @@
         part = dot00(left[...], right[...])
         total = part if total is None else total + part
     refs[-1][...] = total.astype(BF16)
+
+
+def rows_kernel(*refs):
+    *pieces, out_ref = refs
+    at = 0
+    for group in range(0, len(pieces), 4):
+        near, far, near_right, far_right = pieces[group : group + 4]
+        total = dot00(near[...], near_right[...]) + dot00(far[...], far_right[...])
+        end = at + near_right.shape[1]
+        out_ref[:, at:end] = total.astype(BF16)
+        at = end
+
+
+def outer_rows(*groups):
+    block = 256
+    columns = sum(group[2].shape[1] for group in groups)
+    width = groups[0][0].shape[1]
+    specs = []
+    for near, far, near_right, far_right in groups:
+        specs += [pl.BlockSpec((left.shape[0], block), lambda i: (0, i)) for left in (near, far)]
+        specs += [pl.BlockSpec(right.shape, lambda i: (0, 0)) for right in (near_right, far_right)]
+    return pl.pallas_call(
+        rows_kernel,
+        grid=(width // block,),
+        in_specs=specs,
+        out_specs=pl.BlockSpec((block, columns), lambda i: (i, 0)),
+        out_shape=jax.ShapeDtypeStruct((width, columns), BF16),
+        compiler_params=pltpu.CompilerParams(vmem_limit_bytes=18 * 1024 * 1024),
+        cost_estimate=SMALL_COST,
+    )(*[piece for group in groups for piece in group])
 
 
 def outer_tokens(lefts, rights, left_block, blocks, right_block, right_blocks):
@@ -490,7 +520,7 @@
             out_specs=pl.BlockSpec((block, columns), lambda i, place: (i, 0)),
         ),
         out_shape=jax.ShapeDtypeStruct((blocks * block, columns), BF16),
-        compiler_params=pltpu.CompilerParams(vmem_limit_bytes=40 * 1024 * 1024),
+        compiler_params=pltpu.CompilerParams(vmem_limit_bytes=18 * 1024 * 1024),
         cost_estimate=SMALL_COST,
     )(index, *lefts, *rights)
 
@@ -537,7 +567,7 @@
             scratch_shapes=[pltpu.SemaphoreType.DMA((count,))],
         ),
         out_shape=jax.ShapeDtypeStruct((4 * rows, sum(widths)), near.dtype),
-        compiler_params=pltpu.CompilerParams(vmem_limit_bytes=32 * 1024 * 1024),
+        compiler_params=pltpu.CompilerParams(vmem_limit_bytes=50 * 1024 * 1024),
         cost_estimate=SMALL_COST,
     )(place_index, *shards, near, *pieces)
 
@@ -605,7 +635,7 @@
     def meet(self, flows, *values):
         waiting = [array for flow in flows for array in flow.waiting]
         arrived = self.arrive(*waiting, *values)
-        self.done(*arrived[len(waiting) :])
+        self.done(*(arrived[len(waiting) :] or arrived[:1]))
         at = 0
         for flow in flows:
             count = len(flow.waiting)
@@ -698,7 +728,7 @@
             yield step, (self.dp // step) % 2
             step //= 2
 
-    def spread(self, first, second, place, chunks=1, ahead=False):
+    def spread(self, first, second, place, chunks=1, ahead=False, hold=False):
         (step, keep), *lows = self.low_steps()
         side, low, kept = [], [], ()
         sents = [(first[0](1 - place, i), second[0](1 - keep, i)) for i in range(chunks)]
@@ -707,6 +737,10 @@
             kept += tuple(second[1](keep, i) for i in range(chunks))
         if ahead:
             sents = [(yield sents[0])]
+        if ahead == 2:
+            kept = first[1](place, 0), second[1](keep, 0)
+            arrived = yield tuple(sents[0]) + kept
+            sents, kept = [arrived[:2]], arrived[2:]
         for chunk in range(chunks):
             first_got = self.swap(sents[chunk][0], fsdp=2)
             operands = (self.operand,)
@@ -733,6 +767,8 @@
             sent_first, first = self.halves([joined(kept[:chunks]), joined(side)], 0, keep)
         second = [joined(kept[chunks:]), joined(low)]
         sent_second, second = self.halves(second, 1, place)
+        if hold:
+            sent_first, sent_second = yield sent_first, sent_second
         got = yield self.swap(sent_first, dp=step), self.swap(sent_second, fsdp=2)
         first.append(got[0])
         second.append(got[1])
@@ -764,8 +800,8 @@
                 [self.summed([self.part(array, index, 1) for array in value]) for value in (first, second)]
             )
 
-        value = yield from self.finish(both(self.core), both(1 - self.core), 2, True)
-        return [part.T for part in value]
+        (value,) = yield from self.finish(both(self.core), both(1 - self.core), 1, True)
+        return [part.T for part in jnp.split(value, 2, axis=0)]
 
     def split_back(self, by_side, by_low, count, parts, ahead=False):
         yield ()
@@ -778,7 +814,7 @@
         value = yield from self.finish(own, sent, parts)
         return [part.T for total in value for part in jnp.split(total, count // parts, axis=0)]
 
-    def rows_back(self, grad):
+    def rows_back(self, grad, hold=False):
         columns, rows = grad.shape
         value = grad.reshape(2, 2, columns // 4, rows)
         own = lax.dynamic_index_in_dim(value, self.core, 1, keepdims=False)
@@ -795,7 +831,7 @@
             return self.part(wide, index, 0)
 
         first, second = yield from self.spread(
-            (lambda *_: pieces[0], lambda *_: pieces[1]), (by_low, by_low), 0
+            (lambda *_: pieces[0], lambda *_: pieces[1]), (by_low, by_low), 0, hold=hold
         )
         first, second = self.summed(first), self.summed(second)
         sent = jnp.where(self.top == 0, second, first)
@@ -813,11 +849,10 @@
         for bit in (1, 2):
             value = value + self.swap(value, fsdp=bit)
         step = 1
-        while step < self.top_step:
+        while step < self.copies:
             value = value + self.swap(value, dp=step)
             step *= 2
-        got = self.swap(value, dp=step)
-        return lambda: value + self.held(got)
+        return value
 
 
 def layer(
@@ -1098,13 +1133,18 @@
     place.before = ()
     place.done(place.operand)
     attn_grad_far = jnp.concatenate([attn_grad_far, place.core_swap(attn_grad_far)], axis=0)
-    grad_down = outer_tokens(
-        (branch_near, branch_far), place.held((act_near, act_far)), 0, width // 256, 0, 1
-    )
-    down = Flow(place.rows_back(grad_down))
+    grad_rows = outer_rows(
+        (branch_near, branch_far, *place.held((act_near, act_far))),
+        (
+            attn_grad_near,
+            attn_grad_far,
+            mixed_near,
+            jnp.concatenate(mixed_blocks[2:], axis=0),
+        ),
+    )
+    down = Flow(place.rows_back(grad_rows))
+    attn_grad_far = after(attn_grad_far, grad_rows)
     far = heads_back(far_row, half, far_raw, far_crossed, attn_grad_far)
-    attn_grad_all = jnp.concatenate([attn_grad_near, attn_grad_far], axis=0)
-    mixed_all = jnp.concatenate(mixed_blocks, axis=0)
 
     def mix(grads, count):
         shaped = grads.reshape(count, place.low, -1, grads.shape[1])
@@ -1127,18 +1167,15 @@
     far[0], far[2] = place.meet([ffn, down], far[0], far[2])
     down.step(())
     cap_lefts += [mix(near[2], 2), mix(far[2], 2)]
-    cap = Flow(place.split_back(cap_by_side, cap_by_low, 2, 2))
+    cap = Flow(place.split_back(cap_by_side, cap_by_low, 2, 2, 2))
     cap.step(())
-    place.meet([ffn, down], *place.operands)
+    place.meet([ffn, down, cap])
+    place.meet([down, cap])
     place.done(place.before[0])
     place.before = ()
-    cap.step(())
-    cap_kept = cap.waiting[2:]
     branch_far_sum = far_sum(act_blocks, w_down, dot)
     branch_near_sum = near_sum(act_blocks, w_down, dot)
-    out = Flow(place.rows_back(dot_tokens(attn_grad_all, place.held(mixed_all)).astype(BF16)))
-    branch_near_sum, *_ = place.meet([ffn, cap, out], branch_near_sum, *cap_kept)
-    out.step(())
+    branch_near_sum, branch_far_sum = place.meet([ffn, cap], branch_near_sum, branch_far_sum)
     place.before = ()
     plain = (*jnp.split(near[1], 2, axis=0), *jnp.split(far[1], 2, axis=0))
     plain = place.held(plain)
@@ -1157,11 +1194,8 @@
 
     qkv = Flow(place.split_back(qkv_by_side, qkv_by_low, 3, 1, True))
     qkv.step(())
-    branch_far_sum, attn_near_sum = place.meet(
-        [ffn, cap, down, qkv], branch_far_sum, attn_near_sum
-    )
+    attn_far_sum, attn_near_sum = place.meet([cap, qkv, down], attn_far_sum, attn_near_sum)
     qkv.step(())
-    (attn_far_sum,) = place.meet([qkv, out], attn_far_sum)
     grad_attn_in = (attn_near_sum + attn_far_sum.astype(F32)).reshape(inputs.shape)
     grad_gain_in = jnp.sum(grad_attn_in * normed_in * scale_attn, axis=(0, 1))
     grad_mod_attn_scale = jnp.sum(grad_attn_in * normed_in * full_gain_attn, axis=1)
@@ -1176,10 +1210,6 @@
     grad_mod_ffn_gate = jnp.sum(upstream * ffn_branch, axis=1) * (
         1.0 - tanh_ffn[:, 0] * tanh_ffn[:, 0]
     )
-    grad_gain_in, input_grad, block_out = place.meet(
-        [cap, out, down, qkv], grad_gain_in, input_grad, block_out
-    )
-    place.before = ()
     head_part = jnp.zeros_like(full_head_gate)
     head_part = lax.dynamic_update_slice_in_dim(
         head_part, grad_head_gate, place.quarter * heads, axis=0
@@ -1193,11 +1223,13 @@
         head_part,
     )
     small_grads = jnp.concatenate(parts)
-    summed = place.total(after(small_grads, place.operand))
-    for flow in (ffn, down, cap, out, qkv):
-        for _ in range(4):
+    place.before = ()
+    summed = place.total(small_grads)
+    input_grad, block_out = place.meet([qkv, cap, down], input_grad, block_out)
+    (summed,) = place.meet([qkv, cap, down], summed)
+    for flow in (ffn, qkv, cap, down):
+        for _ in range(5):
             flow.step(flow.waiting)
-    summed = summed()
     modulation_grad = jnp.stack(
         [grad_mod_attn_scale, grad_mod_attn_gate, grad_mod_ffn_scale, grad_mod_ffn_gate], axis=1
     )
@@ -1221,11 +1253,11 @@
         cap.result[1],
         vectors[4],
         vectors[5],
-        out.result,
+        down.result[w_down.shape[0] :],
         vectors[1],
         ffn.result[0],
         ffn.result[1],
-        down.result,
+        down.result[: w_down.shape[0]],
     )
 
 

time: 632 us -> 622 us (0.984)
  other arithmetic: 75.5 us -> 60.8 us
  waiting for transfers between devices: 166 us -> 180 us
  Pallas kernels: 145 us -> 156 us
  matrix products: 52.4 us -> 42.8 us
  starting transfers between devices: 80.6 us -> 73.5 us
    ppermute x91 -> x83, waiting for transfers between devices: 166 us -> 180 us  [route(): value = lax.ppermute(value, ('dp', 'fsdp'), pairs)]
    pallas_call x3, Pallas kernels: 6.37 us -> 15 us  [join(): pl.pallas_call(functools.partial(join_kernel, widths, rows, chunks), grid...]
    ppermute x91 -> x83, starting transfers between devices: 80.6 us -> 73.5 us  [route(): value = lax.ppermute(value, ('dp', 'fsdp'), pairs)]
    pallas_call x0 -> x1, Pallas kernels: none -> 6.92 us  [outer_rows(): pl.pallas_call(rows_kernel, grid=(width // block,), in_specs=specs, out_s...]
    pallas_call x3, Pallas kernels: 42.5 us -> 35.8 us  [attend(): pl.pallas_call(functools.partial(forward_kernel, heads, size, half), grid...]
    pallas_call x9 -> x8, Pallas kernels: 21.4 us -> 16.5 us  [outer_tokens(): pl.pallas_call(functools.partial(outer_tokens_kernel, len(lefts)), grid_s...]
    convert_element_type x14 -> x11, other arithmetic: 18.4 us -> 13.7 us  [summed(): return sum((array.astype(F32) for array in arrays)).astype(BF16)]
    unnamed x418 -> x435, local copies, waits for them, and re-layouts: 46.7 us -> 46.1 us
  transfers between devices with their start and end apart: 91 -> 83, of which waited for: 28 -> 26; matrix products, arithmetic and copies ran while one was open for 27% -> 22% of each run, Pallas kernels for 22% -> 23%
where the time goes in v4:
time: 622 us; the launch traced here: 614 us
  waiting for transfers between devices  180 us (29%)
  Pallas kernels  156 us (25%)
  local copies, waits for them, and re-layouts  96.5 us (16%)
  starting transfers between devices  73.5 us (12%)
  other arithmetic  60.8 us (10%)
  matrix products  42.8 us (7%)
    ppermute x83, waiting for transfers between devices, route(): value = lax.ppermute(value, ('dp', 'fsdp'), pairs)  180 us
    ppermute x83, starting transfers between devices, route(): value = lax.ppermute(value, ('dp', 'fsdp'), pairs)  73.5 us
    unnamed x435, local copies, waits for them, and re-layouts  46.1 us
    pallas_call x3, Pallas kernels, attend(): pl.pallas_call(functools.partial(forward_kernel, heads, size, half), grid...  35.8 us
    pallas_call x2, Pallas kernels, attend_back(): pl.pallas_call(functools.partial(backward_kernel, heads, size), grid=(row...  29.7 us
    pallas_call x4, Pallas kernels, outer(): pl.pallas_call(functools.partial(outer_kernel, counts), grid_spec=pltpu.P...  23.8 us
    dot_general x13, matrix products, dot(): return jnp.einsum('tc,ce->te', left, right, preferred_element_type=F32)  23 us
    pallas_call x2, Pallas kernels, middle(): pl.pallas_call(functools.partial(middle_kernel, inner), grid=(steps,), in...  21.3 us
  transfers between devices with their start and end apart: 83, of which 26 were waited for; matrix products, arithmetic and copies ran while one was open for 22% of the time, Pallas kernels for 23%

profile of v4, /device:TPU:0, one launch (start us, length us, event | category | flops | bytes accessed | tf_op | source)
XLA Modules:
  0.0 613.8 jit_solution(13030633067407304325)
XLA Ops:
  5.0 2.6 collective-permute-start
  7.8 4.6 slice_bitcast_fusion.4
  19.4 8.7 %collective-permute-done.5 = bf16[2,822]{1,0:T(2,128)(2,1)S(1)} collective-permute-done((bf16[2,822]{1,0:T(2,128)(2,1)S(1)}, bf16[2,822]{1,0:T(2,128)(2,1)S(1)}, u32[]{:S(2)}, u32[]{:S(2)}) %collective-permute-start.5) | collective-permute-done | bytes 3320 | tf_op jit(solution)/shard_map/ppermute | solution.py:622
  29.5 8.6 %collective-permute-done.1 = bf16[128,4096]{1,0:T(8,128)(2,1)} collective-permute-done((bf16[128,4096]{1,0:T(8,128)(2,1)}, bf16[128,4096]{1,0:T(8,128)(2,1)}, u32[]{:S(2)}, u32[]{:S(2)}) %collective-permute-start.1) | collective-permute-done | bytes 1048608 | tf_op jit(solution)/shard_map/ppermute | solution.py:622
  43.5 18.9 %collective-permute-done.2.refs_3_ = bf16[512,768]{1,0:T(8,128)(2,1)} collective-permute-done((bf16[512,768]{1,0:T(8,128)(2,1)S(1)}, bf16[512,768]{1,0:T(8,128)(2,1)}, u32[]{:S(2)}, u32[]{:S(2)}) %collective-permute-start.2) | collective-permute-done | bytes 786464 | tf_op jit(solution)/shard_map/ppermute | solution.py:622
  70.3 3.5 shard_map.358
  76.8 9.3 %collective-permute-done.8.refs_4_ = bf16[512,768]{1,0:T(8,128)(2,1)S(1)} collective-permute-done((bf16[512,768]{1,0:T(8,128)(2,1)}, bf16[512,768]{1,0:T(8,128)(2,1)S(1)}, u32[]{:S(2)}, u32[]{:S(2)}) %collective-permute-start.8) | collective-permute-done | bytes 786464 | tf_op jit(solution)/shard_map/ppermute | solution.py:622
  86.5 5.2 collective-permute-done.9
  97.7 4.3 collective-permute-start.14
  108.8 5.8 fusion.68.qkv_ref
  114.7 9.9 %collective-permute-done.15.refs_6_ = bf16[512,768]{1,0:T(8,128)(2,1)S(1)} collective-permute-done((bf16[512,768]{1,0:T(8,128)(2,1)S(1)}, bf16[512,768]{1,0:T(8,128)(2,1)S(1)}, u32[]{:S(2)}, u32[]{:S(2)}) %collective-permute-start.15) | collective-permute-done | bytes 786464 | tf_op jit(solution)/shard_map/ppermute | solution.py:622
  125.4 3.3 collective-permute-done.16
  142.6 5.7 shard_map.359.weight_ref
  149.4 18.8 %shard_map.361 = (f32[1024,768]{1,0:T(8,128)S(1)}, bf16[512,384]{1,0:T(8,128)(2,1)S(1)}, f32[384,512]{1,0:T(8,128)S(1)}) custom-call(f32[1024,1152]{1,0:T(8,128)S(1)} %bitcast.178, bf16[512,4096]{1,0:T(8,128)(2,1)S(1)} %bitcast.172, bf16[512,4096]{1,0:T(8,128)(2,1)} %collective-permute-done.10.second_ref.refs_3_, bf16[4096,768]{1,0:T(8,128)(2,1)} %shard_map.359.weight_ref, ...), custom_call_target="tpu_custom_call" | custom-call | flops 1024 | bytes 1024 | tf_op jit(solution)/shard_map/pallas_call | solution.py:322
  186.9 2.8 copy-done.11
  189.7 9.3 %shard_map.360 = (f32[512,768]{1,0:T(8,128)S(1)}, bf16[256,384]{1,0:T(8,128)(2,1)S(1)}, f32[384,256]{1,0:T(8,128)S(1)}) custom-call(f32[1024,1152]{1,0:T(8,128)S(1)} %copy-done.10, bf16[256,4096]{1,0:T(8,128)(2,1)S(1)} %constant_dynamic-update-slice_fusion.first_ref.refs_4_, bf16[256,4096]{1,0:T(8,128)(2,1)} %collective-permute-done.18.second_ref.refs_5_, ...), custom_call_target="tpu_custom_call" | custom-call | flops 1024 | bytes 1024 | tf_op jit(solution)/shard_map/pallas_call | solution.py:322
  201.6 2.7 shard_map.363
  204.3 2.8 copy-done.12
  207.1 7.7 %shard_map.362 = (f32[512,768]{1,0:T(8,128)S(1)}, bf16[256,384]{1,0:T(8,128)(2,1)S(1)}, f32[384,256]{1,0:T(8,128)S(1)}) custom-call(f32[1024,1152]{1,0:T(8,128)S(1)} %bitcast.180, bf16[256,4096]{1,0:T(8,128)(2,1)S(1)} %copy-done.16, bf16[256,4096]{1,0:T(8,128)(2,1)S(1)} %copy-done.19, bf16[4096,768]{1,0:T(8,128)(2,1)S(1)} %copy-done.12, ...), custom_call_target="tpu_custom_call" | custom-call | flops 1024 | bytes 1024 | tf_op jit(solution)/shard_map/pallas_call | solution.py:322
  227.4 10.9 %collective-permute-done.34.refs_6_ = bf16[192,2048]{1,0:T(8,128)(2,1)S(1)} collective-permute-done((bf16[192,2048]{1,0:T(8,128)(2,1)}, bf16[192,2048]{1,0:T(8,128)(2,1)S(1)}, u32[]{:S(2)}, u32[]{:S(2)}) %collective-permute-start.34) | collective-permute-done | bytes 786464 | tf_op jit(solution)/shard_map/ppermute | solution.py:622
  238.3 5.9 shard_map.364.gate_ref.up_ref
  244.1 4.2 shard_map.365.down_ref
  260.9 10.7 %shard_map.366 = (bf16[512,1024]{1,0:T(8,128)(2,1)S(1)}, bf16[512,2048]{1,0:T(8,128)(2,1)}) custom-call(bf16[512,1536]{1,0:T(8,128)(2,1)} %pad_maximum_fusion.7.ffn_ref.refs_2_, bf16[1536,2048]{1,0:T(8,128)(2,1)} %shard_map.364.gate_ref.up_ref, bf16[1536,2048]{1,0:T(8,128)(2,1)} %shard_map.364.gate_ref.up_ref, ...), custom_call_target="tpu_custom_call" | custom-call | flops 1024 | bytes 1024 | tf_op jit(solution)/shard_map/pallas_call | solution.py:443
  279.6 10.6 %shard_map.367 = (bf16[512,1024]{1,0:T(8,128)(2,1)S(1)}, bf16[512,2048]{1,0:T(8,128)(2,1)}) custom-call(bf16[512,1536]{1,0:T(8,128)(2,1)} %copy-done.7, bf16[1536,2048]{1,0:T(8,128)(2,1)} %shard_map.364.gate_ref.up_ref, bf16[1536,2048]{1,0:T(8,128)(2,1)} %shard_map.364.gate_ref.up_ref, bf16[512,1536]{1,0:T(8,128)(2,1)} %copy-done.24, ...), custom_call_target="tpu_custom_call" | custom-call | flops 1024 | bytes 1024 | tf_op jit(solution)/shard_map/pallas_call | solution.py:443
  292.4 4.8 convolution_convert_fusion.5
  303.1 2.8 shard_map.368
  306.7 2.7 convolution_convert_fusion.4
  309.4 2.7 fusion.2
  330.1 3.1 convolution_add_fusion.6
  347.5 14.8 %shard_map.376 = (bf16[1152,512]{1,0:T(8,128)(2,1)S(1)}, bf16[512,1152]{1,0:T(8,128)(2,1)S(1)}, bf16[768,1024]{1,0:T(8,128)(2,1)S(1)}, f32[3,64,128]{2,1,0:T(8,128)S(1)}, f32[6,1,128]{2,1,0:T(1,128)S(1)}) custom-call(f32[1024,1152]{1,0:T(8,128)S(1)} %bitcast.182, f32[1024,768]{1,0:T(8,128)S(1)} %copy-done.37, f32[64,1024]{1,0:T(8,128)S(1)} %copy-done.29, ...), custom_call_target="tpu_custom_call" | custom-call | flops 1024 | bytes 1024 | tf_op jit(solution)/shard_map/pallas_call | solution.py:360
  366.8 6.9 %shard_map.377 = bf16[1536,1408]{1,0:T(8,128)(2,1)S(1)} custom-call(bf16[512,1536]{1,0:T(8,128)(2,1)S(1)} %copy-done.23, bf16[512,1536]{1,0:T(8,128)(2,1)S(1)} %copy-done.25, bf16[512,1024]{1,0:T(8,128)(2,1)S(1)} %copy-done.31, bf16[512,1024]{1,0:T(8,128)(2,1)S(1)} %copy-done.33, bf16[512,1536]{1,0:T(8,128)(2,1)S(1)} %pad_maximum_fusion.9.refs_4_, ...), custom_call_target="tpu_custom_call" | custom-call | flops 1024 | bytes 1024 | tf_op jit(solution)/shard_map/pallas_call | solution.py:493
  383.7 14.9 %shard_map.378 = (bf16[1152,512]{1,0:T(8,128)(2,1)S(1)}, bf16[512,1152]{1,0:T(8,128)(2,1)S(1)}, bf16[768,1024]{1,0:T(8,128)(2,1)S(1)}, f32[3,64,128]{2,1,0:T(8,128)S(1)}, f32[6,1,128]{2,1,0:T(1,128)S(1)}) custom-call(f32[1024,1152]{1,0:T(8,128)S(1)} %bitcast.182, f32[1024,768]{1,0:T(8,128)S(1)} %pad_maximum_fusion.1.cap_ref, f32[64,1024]{1,0:T(8,128)S(1)} %copy-done.29, ...), custom_call_target="tpu_custom_call" | custom-call | flops 1024 | bytes 1024 | tf_op jit(solution)/shard_map/pallas_call | solution.py:360
  411.4 6.2 %shard_map.380 = bf16[384,2048]{1,0:T(8,128)(2,1)S(1)} custom-call(s32[5]{0:T(128)S(1)} %copy-done.65, bf16[768,1024]{1,0:T(8,128)(2,1)S(1)} %bitcast.183, bf16[768,1024]{1,0:T(8,128)(2,1)S(1)} %bitcast.187, bf16[512,4096]{1,0:T(8,128)(2,1)S(1)} %bitcast.173, bf16[512,4096]{1,0:T(8,128)(2,1)} %collective-permute-done.10.second_ref.refs_3_, ...), custom_call_target="tpu_custom_call" | custom-call | flops 1024 | bytes 1024 | tf_op jit(solution)/shard_map/pallas_call | solution.py:404
  417.6 5.5 shard_map.379
  423.1 5.8 collective-permute-done.53
  436.6 6.2 %shard_map.382 = bf16[384,2048]{1,0:T(8,128)(2,1)S(1)} custom-call(s32[5]{0:T(128)S(1)} %stack.186.place_ref, bf16[768,1024]{1,0:T(8,128)(2,1)S(1)} %bitcast.185, bf16[768,1024]{1,0:T(8,128)(2,1)S(1)} %bitcast.189, bf16[512,4096]{1,0:T(8,128)(2,1)S(1)} %bitcast.175, bf16[512,4096]{1,0:T(8,128)(2,1)} %collective-permute-done.10.second_ref.refs_3_, ...), custom_call_target="tpu_custom_call" | custom-call | flops 1024 | bytes 1024 | tf_op jit(solution)/shard_map/pallas_call | solution.py:404
  442.8 6.0 shard_map.381
  450.8 2.6 collective-permute-start.54
  462.5 26.6 %collective-permute-done.54 = bf16[1024,384]{1,0:T(8,128)(2,1)S(1)} collective-permute-done((bf16[1024,384]{1,0:T(8,128)(2,1)S(1)}, bf16[1024,384]{1,0:T(8,128)(2,1)S(1)}, u32[]{:S(2)}, u32[]{:S(2)}) %collective-permute-start.54) | collective-permute-done | bytes 786464 | tf_op jit(solution)/shard_map/ppermute | solution.py:622
  489.1 4.3 collective-permute-done.61
  500.6 3.5 convolution_convert_fusion.1
  511.9 5.1 collective-permute-done.63
  518.4 10.2 %collective-permute-done.66 = bf16[256,1536]{1,0:T(8,128)(2,1)S(1)} collective-permute-done((bf16[256,1536]{1,0:T(8,128)(2,1)S(1)}, bf16[256,1536]{1,0:T(8,128)(2,1)S(1)}, u32[]{:S(2)}, u32[]{:S(2)}) %collective-permute-start.66) | collective-permute-done | bytes 786464 | tf_op jit(solution)/shard_map/ppermute | solution.py:622
  530.2 3.1 broadcast_select_fusion.1
  545.2 15.3 %collective-permute-done.77 = f32[3288]{0:T(1024)S(1)} collective-permute-done((f32[3288]{0:T(1024)S(1)}, f32[3288]{0:T(1024)S(1)}, u32[]{:S(2)}, u32[]{:S(2)}) %collective-permute-start.77) | collective-permute-done | bytes 13184 | tf_op jit(solution)/shard_map/ppermute | solution.py:622
  565.4 3.5 collective-permute-start.75
  575.3 10.6 %collective-permute-done.80 = f32[3288]{0:T(1024)S(1)} collective-permute-done((f32[3288]{0:T(1024)S(1)}, f32[3288]{0:T(1024)S(1)}, u32[]{:S(2)}, u32[]{:S(2)}) %collective-permute-start.80) | collective-permute-done | bytes 13184 | tf_op jit(solution)/shard_map/ppermute | solution.py:622
  594.2 18.2 %collective-permute-done.82 = bf16[576,384]{1,0:T(8,128)(2,1)S(1)} collective-permute-done((bf16[576,384]{1,0:T(8,128)(2,1)S(1)}, bf16[576,384]{1,0:T(8,128)(2,1)S(1)}, u32[]{:S(2)}, u32[]{:S(2)}) %collective-permute-start.82) | collective-permute-done | bytes 442400 | tf_op jit(solution)/shard_map/ppermute | solution.py:622
  (783 shorter events, 247.9 us)
Async XLA Ops:
  5.0 24.5 %collective-permute-start = (bf16[384,1152]{1,0:T(8,128)(2,1)}, bf16[384,1152]{1,0:T(8,128)(2,1)S(1)}, u32[]{:S(2)}, u32[]{:S(2)}) collective-permute-start(bf16[384,1152]{1,0:T(8,128)(2,1)} %pad_maximum_fusion.13), channel_id=1, source_target_pairs={{0,2},{1,3},{2,0},{3,1},{4,7},{5,6},{6,5},{7,4},{8,10},{9,11},{10,... | collective-permute-start | bytes 2654216 | tf_op jit(solution)/shard_map/ppermute | solution.py:622
  7.6 20.6 %collective-permute-start.10 = (bf16[512,4096]{1,0:T(8,128)(2,1)}, bf16[512,4096]{1,0:T(8,128)(2,1)}, u32[]{:S(2)}, u32[]{:S(2)}) collective-permute-start(bf16[512,4096]{1,0:T(8,128)(2,1)} %bitcast.171), channel_id=1, source_target_pairs={{0,1},{1,0},{2,3},{3,2},{4,5},{5,4},{6,7},{7,6},{8,9},{9,8},{10,11... | collective-permute-start | bytes 12582920 | tf_op jit(solution)/shard_map/ppermute | solution.py:622
  12.4 25.7 %collective-permute-start.1 = (bf16[128,4096]{1,0:T(8,128)(2,1)}, bf16[128,4096]{1,0:T(8,128)(2,1)}, u32[]{:S(2)}, u32[]{:S(2)}) collective-permute-start(bf16[128,4096]{1,0:T(8,128)(2,1)} %get-tuple-element.516), channel_id=1, source_target_pairs={{0,8},{1,9},{2,10},{3,11},{4,12},{5,13},{6,14},{7,15},{8,0},{9,1},... | collective-permute-start | bytes 3145736 | tf_op jit(solution)/shard_map/ppermute | solution.py:622
  38.1 24.3 %collective-permute-start.6 = (bf16[272,1536]{1,0:T(8,128)(2,1)S(1)}, bf16[272,1536]{1,0:T(8,128)(2,1)S(1)}, u32[]{:S(2)}, u32[]{:S(2)}) collective-permute-start(bf16[272,1536]{1,0:T(8,128)(2,1)S(1)} %pad_maximum_fusion.15), channel_id=1, source_target_pairs={{0,8},{1,9},{2,10},{3,11},{4,12},{5,13},{6,14},{7,15},{8,0},{9,1},... | collective-permute-start | bytes 2506760 | tf_op jit(solution)/shard_map/ppermute | solution.py:622
  39.7 22.7 %collective-permute-start.3 = (bf16[384,1152]{1,0:T(8,128)(2,1)S(1)}, bf16[384,1152]{1,0:T(8,128)(2,1)S(1)}, u32[]{:S(2)}, u32[]{:S(2)}) collective-permute-start(bf16[384,1152]{1,0:T(8,128)(2,1)S(1)} %collective-permute-done.refs_4_), channel_id=1, source_target_pairs={{0,4},{1,5},{2,6},{3,7},{4,0},{5,1},{6,2},{7,3},{8,12},{9,13},{10,... | collective-permute-start | bytes 2654216 | tf_op jit(solution)/shard_map/ppermute | solution.py:622
  41.3 22.1 %collective-permute-start.12 = (bf16[272,1536]{1,0:T(8,128)(2,1)S(1)}, bf16[272,1536]{1,0:T(8,128)(2,1)S(1)}, u32[]{:S(2)}, u32[]{:S(2)}) collective-permute-start(bf16[272,1536]{1,0:T(8,128)(2,1)S(1)} %pad_maximum_fusion.15), channel_id=1, source_target_pairs={{0,1},{1,0},{2,3},{3,2},{4,5},{5,4},{6,7},{7,6},{8,9},{9,8},{10,11... | collective-permute-start | bytes 2506760 | tf_op jit(solution)/shard_map/ppermute | solution.py:622
  42.5 19.9 %collective-permute-start.2 = (bf16[512,768]{1,0:T(8,128)(2,1)S(1)}, bf16[512,768]{1,0:T(8,128)(2,1)}, u32[]{:S(2)}, u32[]{:S(2)}) collective-permute-start(bf16[512,768]{1,0:T(8,128)(2,1)S(1)} %get-tuple-element.239), channel_id=1, source_target_pairs={{0,2},{1,3},{2,0},{3,1},{4,7},{5,6},{6,5},{7,4},{8,10},{9,11},{10,... | collective-permute-start | bytes 2359304 | tf_op jit(solution)/shard_map/ppermute | solution.py:622
  65.8 27.2 %collective-permute-start.17 = (bf16[1024,768]{1,0:T(8,128)(2,1)}, bf16[1024,768]{1,0:T(8,128)(2,1)}, u32[]{:S(2)}, u32[]{:S(2)}) collective-permute-start(bf16[1024,768]{1,0:T(8,128)(2,1)} %pad_maximum_fusion.5), channel_id=1, source_target_pairs={{0,1},{1,0},{2,3},{3,2},{4,5},{5,4},{6,7},{7,6},{8,9},{9,8},{10,11... | collective-permute-start | bytes 4718600 | tf_op jit(solution)/shard_map/ppermute | solution.py:622
  65.9 25.8 %collective-permute-start.9 = (bf16[128,4096]{1,0:T(8,128)(2,1)}, bf16[128,4096]{1,0:T(8,128)(2,1)}, u32[]{:S(2)}, u32[]{:S(2)}) collective-permute-start(bf16[128,4096]{1,0:T(8,128)(2,1)} %get-tuple-element.248), channel_id=1, source_target_pairs={{0,8},{1,9},{2,10},{3,11},{4,12},{5,13},{6,14},{7,15},{8,0},{9,1},... | collective-permute-start | bytes 3145736 | tf_op jit(solution)/shard_map/ppermute | solution.py:622
  97.7 31.0 %collective-permute-start.14 = (bf16[704,1536]{1,0:T(8,128)(2,1)}, bf16[704,1536]{1,0:T(8,128)(2,1)}, u32[]{:S(2)}, u32[]{:S(2)}) collective-permute-start(bf16[704,1536]{1,0:T(8,128)(2,1)} %pad_maximum_fusion.3), channel_id=1, source_target_pairs={{0,2},{2,1},{4,6},{6,5},{9,10},{11,9},{13,14},{15,13},{16,18},{18,... | collective-permute-start | bytes 6488072 | tf_op jit(solution)/shard_map/ppermute | solution.py:622
  106.2 22.6 %collective-permute-start.16 = (bf16[128,4096]{1,0:T(8,128)(2,1)S(1)}, bf16[128,4096]{1,0:T(8,128)(2,1)S(1)}, u32[]{:S(2)}, u32[]{:S(2)}) collective-permute-start(bf16[128,4096]{1,0:T(8,128)(2,1)S(1)} %copy-done.117), channel_id=1, source_target_pairs={{0,8},{1,9},{2,10},{3,11},{4,12},{5,13},{6,14},{7,15},{8,0},{9,1},... | collective-permute-start | bytes 3145736 | tf_op jit(solution)/shard_map/ppermute | solution.py:622
  107.1 24.3 %collective-permute-start.25 = (bf16[384,2048]{1,0:T(8,128)(2,1)S(1)}, bf16[384,2048]{1,0:T(8,128)(2,1)S(1)}, u32[]{:S(2)}, u32[]{:S(2)}) collective-permute-start(bf16[384,2048]{1,0:T(8,128)(2,1)S(1)} %pad_maximum_fusion.6), channel_id=1, source_target_pairs={{0,1},{1,0},{2,3},{3,2},{4,5},{5,4},{6,7},{7,6},{8,9},{9,8},{10,11... | collective-permute-start | bytes 4718600 | tf_op jit(solution)/shard_map/ppermute | solution.py:622
  128.7 41.2 %collective-permute-start.20 = (bf16[704,1536]{1,0:T(8,128)(2,1)}, bf16[704,1536]{1,0:T(8,128)(2,1)}, u32[]{:S(2)}, u32[]{:S(2)}) collective-permute-start(bf16[704,1536]{1,0:T(8,128)(2,1)} %collective-permute-done.14), channel_id=1, source_target_pairs={{1,5},{2,6},{5,1},{6,2},{9,13},{10,14},{13,9},{14,10},{17,21},{18,... | collective-permute-start | bytes 6488072 | tf_op jit(solution)/shard_map/ppermute | solution.py:622
  131.4 37.7 %collective-permute-start.26 = (bf16[384,1536]{1,0:T(8,128)(2,1)}, bf16[384,1536]{1,0:T(8,128)(2,1)}, u32[]{:S(2)}, u32[]{:S(2)}) collective-permute-start(bf16[384,1536]{1,0:T(8,128)(2,1)} %shard.2), channel_id=1, source_target_pairs={{2,3},{6,7},{9,8},{13,12},{18,19},{22,23},{25,24},{29,28}} | collective-permute-start | bytes 3538952 | tf_op jit(solution)/shard_map/ppermute | solution.py:622
  134.4 35.5 %collective-permute-start.21 = (bf16[128,4096]{1,0:T(8,128)(2,1)}, bf16[128,4096]{1,0:T(8,128)(2,1)}, u32[]{:S(2)}, u32[]{:S(2)}) collective-permute-start(bf16[128,4096]{1,0:T(8,128)(2,1)} %get-tuple-element.271), channel_id=1, source_target_pairs={{0,8},{1,9},{2,10},{3,11},{4,12},{5,13},{6,14},{7,15},{8,0},{9,1},... | collective-permute-start | bytes 3145736 | tf_op jit(solution)/shard_map/ppermute | solution.py:622
  137.5 32.4 %collective-permute-start.19 = (bf16[192,2048]{1,0:T(8,128)(2,1)}, bf16[192,2048]{1,0:T(8,128)(2,1)}, u32[]{:S(2)}, u32[]{:S(2)}) collective-permute-start(bf16[192,2048]{1,0:T(8,128)(2,1)} %get-tuple-element.269), channel_id=1, source_target_pairs={{0,2},{1,3},{2,0},{3,1},{4,7},{5,6},{6,5},{7,4},{8,10},{9,11},{10,... | collective-permute-start | bytes 2359304 | tf_op jit(solution)/shard_map/ppermute | solution.py:622
  177.4 38.1 %collective-permute-start.29 = (bf16[1024,1536]{1,0:T(8,128)(2,1)}, bf16[1024,1536]{1,0:T(8,128)(2,1)}, u32[]{:S(2)}, u32[]{:S(2)}) collective-permute-start(bf16[1024,1536]{1,0:T(8,128)(2,1)} %shard.3), channel_id=1, source_target_pairs={{2,3},{6,7},{9,8},{13,12},{18,19},{22,23},{25,24},{29,28}} | collective-permute-start | bytes 9437192 | tf_op jit(solution)/shard_map/ppermute | solution.py:622
  179.7 35.1 %collective-permute-start.24 = (bf16[256,1536]{1,0:T(8,128)(2,1)}, bf16[256,1536]{1,0:T(8,128)(2,1)}, u32[]{:S(2)}, u32[]{:S(2)}) collective-permute-start(bf16[256,1536]{1,0:T(8,128)(2,1)} %bitcast.19), channel_id=1, source_target_pairs={{0,8},{1,9},{2,10},{3,11},{4,12},{5,13},{6,14},{7,15},{8,0},{9,1},... | collective-permute-start | bytes 2359304 | tf_op jit(solution)/shard_map/ppermute | solution.py:622
  180.5 34.4 %collective-permute-start.23 = (bf16[192,2048]{1,0:T(8,128)(2,1)}, bf16[192,2048]{1,0:T(8,128)(2,1)}, u32[]{:S(2)}, u32[]{:S(2)}) collective-permute-start(bf16[192,2048]{1,0:T(8,128)(2,1)} %collective-permute-done.19.refs_3_), channel_id=1, source_target_pairs={{0,4},{1,5},{2,6},{3,7},{4,0},{5,1},{6,2},{7,3},{8,12},{9,13},{10,... | collective-permute-start | bytes 2359304 | tf_op jit(solution)/shard_map/ppermute | solution.py:622
  182.2 32.6 %collective-permute-start.22 = (bf16[192,2048]{1,0:T(8,128)(2,1)}, bf16[192,2048]{1,0:T(8,128)(2,1)}, u32[]{:S(2)}, u32[]{:S(2)}) collective-permute-start(bf16[192,2048]{1,0:T(8,128)(2,1)} %get-tuple-element.277), channel_id=1, source_target_pairs={{0,2},{1,3},{2,0},{3,1},{4,7},{5,6},{6,5},{7,4},{8,10},{9,11},{10,... | collective-permute-start | bytes 2359304 | tf_op jit(solution)/shard_map/ppermute | solution.py:622
  220.8 27.5 %collective-permute-start.33 = (bf16[256,1536]{1,0:T(8,128)(2,1)}, bf16[256,1536]{1,0:T(8,128)(2,1)S(1)}, u32[]{:S(2)}, u32[]{:S(2)}) collective-permute-start(bf16[256,1536]{1,0:T(8,128)(2,1)} %convolution_convert_fusion.6), channel_id=1, source_target_pairs={{0,1},{1,0},{2,3},{3,2},{4,5},{5,4},{6,7},{7,6},{8,9},{9,8},{10,11... | collective-permute-start | bytes 2359304 | tf_op jit(solution)/shard_map/ppermute | solution.py:622
  222.5 26.5 %collective-permute-start.31 = (bf16[256,1536]{1,0:T(8,128)(2,1)}, bf16[256,1536]{1,0:T(8,128)(2,1)}, u32[]{:S(2)}, u32[]{:S(2)}) collective-permute-start(bf16[256,1536]{1,0:T(8,128)(2,1)} %fusion), channel_id=1, source_target_pairs={{0,8},{1,9},{2,10},{3,11},{4,12},{5,13},{6,14},{7,15},{8,0},{9,1},... | collective-permute-start | bytes 2359304 | tf_op jit(solution)/shard_map/ppermute | solution.py:622
  253.0 20.1 %collective-permute-start.36 = (bf16[256,1536]{1,0:T(8,128)(2,1)S(1)}, bf16[256,1536]{1,0:T(8,128)(2,1)}, u32[]{:S(2)}, u32[]{:S(2)}) collective-permute-start(bf16[256,1536]{1,0:T(8,128)(2,1)S(1)} %bitcast.211), channel_id=1, source_target_pairs={{0,8},{1,9},{2,10},{3,11},{4,12},{5,13},{6,14},{7,15},{8,0},{9,1},... | collective-permute-start | bytes 2359304 | tf_op jit(solution)/shard_map/ppermute | solution.py:622
  302.0 31.3 %collective-permute-start.39 = (bf16[256,1536]{1,0:T(8,128)(2,1)}, bf16[256,1536]{1,0:T(8,128)(2,1)}, u32[]{:S(2)}, u32[]{:S(2)}) collective-permute-start(bf16[256,1536]{1,0:T(8,128)(2,1)} %shard_map.369), channel_id=1, source_target_pairs={{0,4},{1,5},{2,6},{3,7},{4,0},{5,1},{6,2},{7,3},{8,12},{9,13},{10,... | collective-permute-start | bytes 2359304 | tf_op jit(solution)/shard_map/ppermute | solution.py:622
  306.0 27.3 %collective-permute-start.38 = (bf16[512,768]{1,0:T(8,128)(2,1)}, bf16[512,768]{1,0:T(8,128)(2,1)}, u32[]{:S(2)}, u32[]{:S(2)}) collective-permute-start(bf16[512,768]{1,0:T(8,128)(2,1)} %shard_map.368), channel_id=1, source_target_pairs={{0,2},{1,3},{2,0},{3,1},{4,6},{5,7},{6,4},{7,5},{8,10},{9,11},{10,... | collective-permute-start | bytes 2359304 | tf_op jit(solution)/shard_map/ppermute | solution.py:622
  309.4 20.7 %collective-permute-start.42 = (bf16[256,1536]{1,0:T(8,128)(2,1)}, bf16[256,1536]{1,0:T(8,128)(2,1)}, u32[]{:S(2)}, u32[]{:S(2)}) collective-permute-start(bf16[256,1536]{1,0:T(8,128)(2,1)} %convolution_convert_fusion.4), channel_id=1, source_target_pairs={{0,1},{1,0},{2,3},{3,2},{4,5},{5,4},{6,7},{7,6},{8,9},{9,8},{10,11... | collective-permute-start | bytes 2359304 | tf_op jit(solution)/shard_map/ppermute | solution.py:622
  312.1 21.2 %collective-permute-start.41 = (bf16[256,1536]{1,0:T(8,128)(2,1)}, bf16[256,1536]{1,0:T(8,128)(2,1)}, u32[]{:S(2)}, u32[]{:S(2)}) collective-permute-start(bf16[256,1536]{1,0:T(8,128)(2,1)} %fusion.2), channel_id=1, source_target_pairs={{0,8},{1,9},{2,10},{3,11},{4,12},{5,13},{6,14},{7,15},{8,0},{9,1},... | collective-permute-start | bytes 2359304 | tf_op jit(solution)/shard_map/ppermute | solution.py:622
  340.4 21.9 %collective-permute-start.45 = (bf16[256,1536]{1,0:T(8,128)(2,1)S(1)}, bf16[256,1536]{1,0:T(8,128)(2,1)S(1)}, u32[]{:S(2)}, u32[]{:S(2)}) collective-permute-start(bf16[256,1536]{1,0:T(8,128)(2,1)S(1)} %bitcast.207), channel_id=1, source_target_pairs={{0,8},{1,9},{2,10},{3,11},{4,12},{5,13},{6,14},{7,15},{8,0},{9,1},... | collective-permute-start | bytes 2359304 | tf_op jit(solution)/shard_map/ppermute | solution.py:622
  341.1 21.2 %collective-permute-start.44 = (bf16[256,1536]{1,0:T(8,128)(2,1)S(1)}, bf16[256,1536]{1,0:T(8,128)(2,1)S(1)}, u32[]{:S(2)}, u32[]{:S(2)}) collective-permute-start(bf16[256,1536]{1,0:T(8,128)(2,1)S(1)} %shard_map.375), channel_id=1, source_target_pairs={{0,4},{1,5},{2,6},{3,7},{4,0},{5,1},{6,2},{7,3},{8,12},{9,13},{10,... | collective-permute-start | bytes 2359304 | tf_op jit(solution)/shard_map/ppermute | solution.py:622
  373.9 24.8 %collective-permute-start.50 = (bf16[2,384,1408]{2,1,0:T(8,128)(2,1)S(1)}, bf16[2,384,1408]{2,1,0:T(8,128)(2,1)}, u32[]{:S(2)}, u32[]{:S(2)}) collective-permute-start(bf16[2,384,1408]{2,1,0:T(8,128)(2,1)S(1)} %dynamic-slice_bitcast_fusion), channel_id=1, source_target_pairs={{0,1},{1,0},{2,3},{3,2},{4,5},{5,4},{6,7},{7,6},{8,9},{9,8},{10,11... | collective-permute-start | bytes 6488072 | tf_op jit(solution)/shard_map/ppermute | solution.py:622
  377.1 25.1 %collective-permute-start.48 = (bf16[512,768]{1,0:T(8,128)(2,1)}, bf16[512,768]{1,0:T(8,128)(2,1)}, u32[]{:S(2)}, u32[]{:S(2)}) collective-permute-start(bf16[512,768]{1,0:T(8,128)(2,1)} %add_convert_fusion.5), channel_id=1, source_target_pairs={{0,2},{1,3},{2,0},{3,1},{4,6},{5,7},{6,4},{7,5},{8,10},{9,11},{10,... | collective-permute-start | bytes 2359304 | tf_op jit(solution)/shard_map/ppermute | solution.py:622
  379.7 22.5 %collective-permute-start.47 = (bf16[512,768]{1,0:T(8,128)(2,1)}, bf16[512,768]{1,0:T(8,128)(2,1)}, u32[]{:S(2)}, u32[]{:S(2)}) collective-permute-start(bf16[512,768]{1,0:T(8,128)(2,1)} %add_convert_fusion.6), channel_id=1, source_target_pairs={{0,4},{1,5},{2,6},{3,7},{4,0},{5,1},{6,2},{7,3},{8,12},{9,13},{10,... | collective-permute-start | bytes 2359304 | tf_op jit(solution)/shard_map/ppermute | solution.py:622
  403.4 25.5 %collective-permute-start.53 = (bf16[192,2816]{1,0:T(8,128)(2,1)}, bf16[192,2816]{1,0:T(8,128)(2,1)}, u32[]{:S(2)}, u32[]{:S(2)}) collective-permute-start(bf16[192,2816]{1,0:T(8,128)(2,1)} %get-tuple-element.367), channel_id=1, source_target_pairs={{0,4},{1,5},{2,6},{3,7},{4,0},{5,1},{6,2},{7,3},{8,12},{9,13},{10,... | collective-permute-start | bytes 3244040 | tf_op jit(solution)/shard_map/ppermute | solution.py:622
  403.4 25.5 %collective-permute-start.52 = (bf16[384,1408]{1,0:T(8,128)(2,1)}, bf16[384,1408]{1,0:T(8,128)(2,1)}, u32[]{:S(2)}, u32[]{:S(2)}) collective-permute-start(bf16[384,1408]{1,0:T(8,128)(2,1)} %get-tuple-element.366), channel_id=1, source_target_pairs={{0,2},{1,3},{2,0},{3,1},{4,6},{5,7},{6,4},{7,5},{8,10},{9,11},{10,... | collective-permute-start | bytes 3244040 | tf_op jit(solution)/shard_map/ppermute | solution.py:622
  450.8 38.3 %collective-permute-start.54 = (bf16[1024,384]{1,0:T(8,128)(2,1)S(1)}, bf16[1024,384]{1,0:T(8,128)(2,1)S(1)}, u32[]{:S(2)}, u32[]{:S(2)}) collective-permute-start(bf16[1024,384]{1,0:T(8,128)(2,1)S(1)} %broadcast_select_fusion.6), channel_id=1, source_target_pairs={{0,16},{1,17},{2,18},{3,19},{4,20},{5,21},{6,22},{7,23},{8,24},{9,... | collective-permute-start | bytes 2359304 | tf_op jit(solution)/shard_map/ppermute | solution.py:622
  453.4 39.9 %collective-permute-start.58 = (bf16[384,2048]{1,0:T(8,128)(2,1)S(1)}, bf16[384,2048]{1,0:T(8,128)(2,1)S(1)}, u32[]{:S(2)}, u32[]{:S(2)}) collective-permute-start(bf16[384,2048]{1,0:T(8,128)(2,1)S(1)} %shard_map.380), channel_id=1, source_target_pairs={{0,4},{1,5},{2,6},{3,7},{4,0},{5,1},{6,2},{7,3},{8,12},{9,13},{10,... | collective-permute-start | bytes 4718600 | tf_op jit(solution)/shard_map/ppermute | solution.py:622
  453.7 39.6 %collective-permute-start.57 = (bf16[768,1024]{1,0:T(8,128)(2,1)S(1)}, bf16[768,1024]{1,0:T(8,128)(2,1)S(1)}, u32[]{:S(2)}, u32[]{:S(2)}) collective-permute-start(bf16[768,1024]{1,0:T(8,128)(2,1)S(1)} %shard_map.379), channel_id=1, source_target_pairs={{0,2},{1,3},{2,0},{3,1},{4,6},{5,7},{6,4},{7,5},{8,10},{9,11},{10,... | collective-permute-start | bytes 4718600 | tf_op jit(solution)/shard_map/ppermute | solution.py:622
  456.5 36.9 %collective-permute-start.61 = (bf16[256,1536]{1,0:T(8,128)(2,1)S(1)}, bf16[256,1536]{1,0:T(8,128)(2,1)S(1)}, u32[]{:S(2)}, u32[]{:S(2)}) collective-permute-start(bf16[256,1536]{1,0:T(8,128)(2,1)S(1)} %fusion.1), channel_id=1, source_target_pairs={{0,8},{1,9},{2,10},{3,11},{4,12},{5,13},{6,14},{7,15},{8,0},{9,1},... | collective-permute-start | bytes 2359304 | tf_op jit(solution)/shard_map/ppermute | solution.py:622
  460.4 51.5 %collective-permute-start.64 = (bf16[192,1408]{1,0:T(8,128)(2,1)S(1)}, bf16[192,1408]{1,0:T(8,128)(2,1)S(1)}, u32[]{:S(2)}, u32[]{:S(2)}) collective-permute-start(bf16[192,1408]{1,0:T(8,128)(2,1)S(1)} %get-tuple-element.408), channel_id=1, source_target_pairs={{0,16},{1,17},{2,18},{3,19},{4,20},{5,21},{6,22},{7,23},{8,24},{9,... | collective-permute-start | bytes 1622024 | tf_op jit(solution)/shard_map/ppermute | solution.py:622
  497.0 20.0 %collective-permute-start.63 = (bf16[384,1024]{1,0:T(8,128)(2,1)S(1)}, bf16[384,1024]{1,0:T(8,128)(2,1)S(1)}, u32[]{:S(2)}, u32[]{:S(2)}) collective-permute-start(bf16[384,1024]{1,0:T(8,128)(2,1)S(1)} %add_convert_fusion.3), channel_id=1, source_target_pairs={{0,2},{1,3},{2,0},{3,1},{4,6},{5,7},{6,4},{7,5},{8,10},{9,11},{10,... | collective-permute-start | bytes 2359304 | tf_op jit(solution)/shard_map/ppermute | solution.py:622
  506.4 22.2 %collective-permute-start.66 = (bf16[256,1536]{1,0:T(8,128)(2,1)S(1)}, bf16[256,1536]{1,0:T(8,128)(2,1)S(1)}, u32[]{:S(2)}, u32[]{:S(2)}) collective-permute-start(bf16[256,1536]{1,0:T(8,128)(2,1)S(1)} %fusion.3), channel_id=1, source_target_pairs={{0,8},{1,9},{2,10},{3,11},{4,12},{5,13},{6,14},{7,15},{8,0},{9,1},... | collective-permute-start | bytes 2359304 | tf_op jit(solution)/shard_map/ppermute | solution.py:622
  536.9 27.4 %collective-permute-start.72 = (bf16[192,1408]{1,0:T(8,128)(2,1)S(1)}, bf16[192,1408]{1,0:T(8,128)(2,1)S(1)}, u32[]{:S(2)}, u32[]{:S(2)}) collective-permute-start(bf16[192,1408]{1,0:T(8,128)(2,1)S(1)} %add_convert_fusion.7), channel_id=1, source_target_pairs={{0,0},{1,8},{2,2},{3,10},{4,4},{5,12},{6,6},{7,14},{8,1},{9,9},{10... | collective-permute-start | bytes 1622024 | tf_op jit(solution)/shard_map/ppermute | solution.py:622
  537.6 26.7 %collective-permute-start.69 = (bf16[576,768]{1,0:T(8,128)(2,1)S(1)}, bf16[576,768]{1,0:T(8,128)(2,1)S(1)}, u32[]{:S(2)}, u32[]{:S(2)}) collective-permute-start(bf16[576,768]{1,0:T(8,128)(2,1)S(1)} %copy-done.197), channel_id=1, source_target_pairs={{0,4},{1,5},{2,6},{3,7},{4,0},{5,1},{6,2},{7,3},{8,12},{9,13},{10,... | collective-permute-start | bytes 2654216 | tf_op jit(solution)/shard_map/ppermute | solution.py:622
  537.9 26.3 %collective-permute-start.68 = (bf16[1152,384]{1,0:T(8,128)(2,1)S(1)}, bf16[1152,384]{1,0:T(8,128)(2,1)S(1)}, u32[]{:S(2)}, u32[]{:S(2)}) collective-permute-start(bf16[1152,384]{1,0:T(8,128)(2,1)S(1)} %copy-done.196), channel_id=1, source_target_pairs={{0,2},{1,3},{2,0},{3,1},{4,6},{5,7},{6,4},{7,5},{8,10},{9,11},{10,... | collective-permute-start | bytes 2654216 | tf_op jit(solution)/shard_map/ppermute | solution.py:622
  538.6 21.9 %collective-permute-start.77 = (f32[3288]{0:T(1024)S(1)}, f32[3288]{0:T(1024)S(1)}, u32[]{:S(2)}, u32[]{:S(2)}) collective-permute-start(f32[3288]{0:T(1024)S(1)} %add.493), channel_id=1, source_target_pairs={{0,2},{1,3},{2,0},{3,1},{4,6},{5,7},{6,4},{7,5},{8,10},{9,11},{10,... | collective-permute-start | bytes 39464 | tf_op jit(solution)/shard_map/ppermute | solution.py:622
  541.1 23.2 %collective-permute-start.71 = (bf16[192,1024]{1,0:T(8,128)(2,1)S(1)}, bf16[192,1024]{1,0:T(8,128)(2,1)S(1)}, u32[]{:S(2)}, u32[]{:S(2)}) collective-permute-start(bf16[192,1024]{1,0:T(8,128)(2,1)S(1)} %get-tuple-element.433), channel_id=1, source_target_pairs={{0,16},{1,17},{2,18},{3,19},{4,20},{5,21},{6,22},{7,23},{8,24},{9,... | collective-permute-start | bytes 1179656 | tf_op jit(solution)/shard_map/ppermute | solution.py:622
  565.4 20.4 %collective-permute-start.75 = (bf16[192,1024]{1,0:T(8,128)(2,1)}, bf16[192,1024]{1,0:T(8,128)(2,1)}, u32[]{:S(2)}, u32[]{:S(2)}) collective-permute-start(bf16[192,1024]{1,0:T(8,128)(2,1)} %get-tuple-element.445), channel_id=1, source_target_pairs={{0,16},{1,17},{2,18},{3,19},{4,20},{5,21},{6,22},{7,23},{8,24},{9,... | collective-permute-start | bytes 1179656 | tf_op jit(solution)/shard_map/ppermute | solution.py:622
  589.9 22.5 %collective-permute-start.82 = (bf16[576,384]{1,0:T(8,128)(2,1)S(1)}, bf16[576,384]{1,0:T(8,128)(2,1)S(1)}, u32[]{:S(2)}, u32[]{:S(2)}) collective-permute-start(bf16[576,384]{1,0:T(8,128)(2,1)S(1)} %broadcast_select_fusion.10), channel_id=1, source_target_pairs={{0,16},{1,17},{2,18},{3,19},{4,20},{5,21},{6,22},{7,23},{8,24},{9,... | collective-permute-start | bytes 1327112 | tf_op jit(solution)/shard_map/ppermute | solution.py:622
  (248 other events, 2002.8 us)

commit v5 on v4

--- a/solution.py
+++ b/solution.py
@@ -845,13 +845,9 @@
         (got,) = yield (self.route(value, turn),)
         return got.astype(F32).T
 
-    def total(self, value):
-        for bit in (1, 2):
-            value = value + self.swap(value, fsdp=bit)
-        step = 1
-        while step < self.copies:
-            value = value + self.swap(value, dp=step)
-            step *= 2
+    def total(self, value, axis, steps):
+        for step in steps:
+            value = value + self.swap(value, **{axis: step})
         return value
 
 
@@ -890,8 +886,9 @@
     qkv_shards, cap_shards, ffn_shards = (w_query, w_key, w_value), (w_cap_key, w_cap_value), (w_gate, w_up)
     qkv_sent, qkv_near = place.cut_columns(qkv_shards)
     qkv_side = place.side_swap(qkv_sent)
-    cap_pieces = [caption[0, : cap_tokens // 2], caption[0, cap_tokens // 2 :]]
-    cap_pieces += [caption[1, : cap_tokens // 2], caption[1, cap_tokens // 2 :]]
+    later = after(caption, qkv_sent)
+    cap_pieces = [caption[0, : cap_tokens // 2], later[0, cap_tokens // 2 :]]
+    cap_pieces += [later[1, : cap_tokens // 2], later[1, cap_tokens // 2 :]]
     far_pieces = [place.team_swap(cap_pieces[0])]
 
     small = (gain_attn, gain_ffn, gain_query, gain_key, gain_cap_key, head_gate)
@@ -1173,10 +1170,6 @@
     place.meet([down, cap])
     place.done(place.before[0])
     place.before = ()
-    branch_far_sum = far_sum(act_blocks, w_down, dot)
-    branch_near_sum = near_sum(act_blocks, w_down, dot)
-    branch_near_sum, branch_far_sum = place.meet([ffn, cap], branch_near_sum, branch_far_sum)
-    place.before = ()
     plain = (*jnp.split(near[1], 2, axis=0), *jnp.split(far[1], 2, axis=0))
     plain = place.held(plain)
     attn_far_sum = far_sum(plain, w_qkv, dot_back)
@@ -1192,9 +1185,11 @@
     def qkv_by_low(index, _):
         return dot(place.part(place.held(turned), index, 0), low_rows).astype(BF16)
 
+    attn_near_sum, attn_far_sum = place.meet([ffn, cap], attn_near_sum, attn_far_sum)
+    place.before = ()
+    place.done(place.operand)
+    attn_near_sum, attn_far_sum = place.held((attn_near_sum, attn_far_sum))
     qkv = Flow(place.split_back(qkv_by_side, qkv_by_low, 3, 1, True))
-    qkv.step(())
-    attn_far_sum, attn_near_sum = place.meet([cap, qkv, down], attn_far_sum, attn_near_sum)
     qkv.step(())
     grad_attn_in = (attn_near_sum + attn_far_sum.astype(F32)).reshape(inputs.shape)
     grad_gain_in = jnp.sum(grad_attn_in * normed_in * scale_attn, axis=(0, 1))
@@ -1205,11 +1200,6 @@
     gate_parts = near[4] + far[4]
     gain_parts = jnp.sum(near[3] + far[3], axis=2)
     grad_head_gate = jnp.sum(gate_parts, axis=(1, 2)) * (1.0 - head_tanh * head_tanh)
-    ffn_branch = (branch_near_sum + branch_far_sum.astype(F32)).reshape(inputs.shape)
-    block_out = (hidden + tanh_ffn * ffn_branch).astype(BF16)
-    grad_mod_ffn_gate = jnp.sum(upstream * ffn_branch, axis=1) * (
-        1.0 - tanh_ffn[:, 0] * tanh_ffn[:, 0]
-    )
     head_part = jnp.zeros_like(full_head_gate)
     head_part = lax.dynamic_update_slice_in_dim(
         head_part, grad_head_gate, place.quarter * heads, axis=0
@@ -1222,23 +1212,34 @@
         gain_parts[2],
         head_part,
     )
-    small_grads = jnp.concatenate(parts)
+    summed = place.total(jnp.concatenate(parts), "fsdp", (1, 2))
+    branch_far_sum = far_sum(act_blocks, w_down, dot)
+    branch_near_sum = near_sum(act_blocks, w_down, dot)
+    summed, input_grad = place.meet([down, qkv, cap], summed, input_grad)
     place.before = ()
-    summed = place.total(small_grads)
-    input_grad, block_out = place.meet([qkv, cap, down], input_grad, block_out)
-    (summed,) = place.meet([qkv, cap, down], summed)
+    qkv.step(())
+    steps = [1 << i for i in range(place.copies.bit_length() - 1)]
+    summed = place.total(summed, "dp", steps[:-2])
+    summed, branch_near_sum = place.meet([qkv, cap, down], summed, branch_near_sum)
+    place.before = ()
+    summed = place.total(summed, "dp", steps[-2:])
+    summed, branch_far_sum = place.meet([qkv, cap, down], summed, branch_far_sum)
+    ffn_branch = (branch_near_sum + branch_far_sum.astype(F32)).reshape(inputs.shape)
+    block_out = (hidden + tanh_ffn * ffn_branch).astype(BF16)
+    grad_mod_ffn_gate = jnp.sum(upstream * ffn_branch, axis=1) * (
+        1.0 - tanh_ffn[:, 0] * tanh_ffn[:, 0]
+    )
     for flow in (ffn, qkv, cap, down):
         for _ in range(5):
             flow.step(flow.waiting)
-    modulation_grad = jnp.stack(
-        [grad_mod_attn_scale, grad_mod_attn_gate, grad_mod_ffn_scale, grad_mod_ffn_gate], axis=1
-    )
-
     vectors, at = [], 0
     for vector in parts:
         length = vector.shape[0] // place.shards
         vectors.append(lax.dynamic_slice_in_dim(summed, at + place.fsdp * length, length))
         at += vector.shape[0]
+    modulation_grad = jnp.stack(
+        [grad_mod_attn_scale, grad_mod_attn_gate, grad_mod_ffn_scale, grad_mod_ffn_gate], axis=1
+    )
     return (
         block_out,
         input_grad,

time: 622 us -> 622 us (level)
  waiting for transfers between devices: 180 us -> 164 us
  local copies, waits for them, and re-layouts: 96.5 us -> 105 us
    ppermute x83, waiting for transfers between devices: 180 us -> 164 us  [route(): value = lax.ppermute(value, ('dp', 'fsdp'), pairs)]
    unnamed x435 -> x407, local copies, waits for them, and re-layouts: 46.1 us -> 51.1 us
  transfers between devices with their start and end apart: 83 -> 83, of which waited for: 26 -> 25; matrix products, arithmetic and copies ran while one was open for 22% -> 24% of each run, Pallas kernels for 23% -> 23%
where the time goes in v5:
time: 622 us; the launch traced here: 612 us
  waiting for transfers between devices  164 us (26%)
  Pallas kernels  156 us (25%)
  local copies, waits for them, and re-layouts  105 us (17%)
  starting transfers between devices  74 us (12%)
  other arithmetic  60 us (10%)
  matrix products  48.9 us (8%)
    ppermute x83, waiting for transfers between devices, route(): value = lax.ppermute(value, ('dp', 'fsdp'), pairs)  164 us
    ppermute x83, starting transfers between devices, route(): value = lax.ppermute(value, ('dp', 'fsdp'), pairs)  74 us
    unnamed x407, local copies, waits for them, and re-layouts  51.1 us
    pallas_call x3, Pallas kernels, attend(): pl.pallas_call(functools.partial(forward_kernel, heads, size, half), grid...  35.8 us
    pallas_call x2, Pallas kernels, attend_back(): pl.pallas_call(functools.partial(backward_kernel, heads, size), grid=(row...  29.7 us
    dot_general x13, matrix products, dot(): return jnp.einsum('tc,ce->te', left, right, preferred_element_type=F32)  29.1 us
    pallas_call x4, Pallas kernels, outer(): pl.pallas_call(functools.partial(outer_kernel, counts), grid_spec=pltpu.P...  23.9 us
    pallas_call x2, Pallas kernels, middle(): pl.pallas_call(functools.partial(middle_kernel, inner), grid=(steps,), in...  21.2 us
  transfers between devices with their start and end apart: 83, of which 25 were waited for; matrix products, arithmetic and copies ran while one was open for 24% of the time, Pallas kernels for 23%

profile of v5, /device:TPU:0, one launch (start us, length us, event | category | flops | bytes accessed | tf_op | source)
XLA Modules:
  0.0 611.6 jit_solution(1403566709979326674)
XLA Ops:
  15.7 2.9 constant_dynamic-slice_fusion.6
  18.7 9.4 %collective-permute-done.5 = bf16[2,822]{1,0:T(2,128)(2,1)S(1)} collective-permute-done((bf16[2,822]{1,0:T(2,128)(2,1)S(1)}, bf16[2,822]{1,0:T(2,128)(2,1)S(1)}, u32[]{:S(2)}, u32[]{:S(2)}) %collective-permute-start.5) | collective-permute-done | bytes 3320 | tf_op jit(solution)/shard_map/ppermute | solution.py:622
  29.5 6.4 %collective-permute-done.1 = bf16[128,4096]{1,0:T(8,128)(2,1)} collective-permute-done((bf16[128,4096]{1,0:T(8,128)(2,1)}, bf16[128,4096]{1,0:T(8,128)(2,1)}, u32[]{:S(2)}, u32[]{:S(2)}) %collective-permute-start.1) | collective-permute-done | bytes 1048608 | tf_op jit(solution)/shard_map/ppermute | solution.py:622
  41.3 18.9 %collective-permute-done.2.refs_3_ = bf16[512,768]{1,0:T(8,128)(2,1)} collective-permute-done((bf16[512,768]{1,0:T(8,128)(2,1)S(1)}, bf16[512,768]{1,0:T(8,128)(2,1)}, u32[]{:S(2)}, u32[]{:S(2)}) %collective-permute-start.2) | collective-permute-done | bytes 786464 | tf_op jit(solution)/shard_map/ppermute | solution.py:622
  69.8 3.5 shard_map.358
  76.2 9.5 %collective-permute-done.8.refs_4_ = bf16[512,768]{1,0:T(8,128)(2,1)S(1)} collective-permute-done((bf16[512,768]{1,0:T(8,128)(2,1)}, bf16[512,768]{1,0:T(8,128)(2,1)S(1)}, u32[]{:S(2)}, u32[]{:S(2)}) %collective-permute-start.8) | collective-permute-done | bytes 786464 | tf_op jit(solution)/shard_map/ppermute | solution.py:622
  85.8 5.4 collective-permute-done.9
  97.2 4.2 collective-permute-start.14
  108.4 5.8 fusion.68.qkv_ref
  114.2 9.9 %collective-permute-done.15.refs_6_ = bf16[512,768]{1,0:T(8,128)(2,1)S(1)} collective-permute-done((bf16[512,768]{1,0:T(8,128)(2,1)S(1)}, bf16[512,768]{1,0:T(8,128)(2,1)S(1)}, u32[]{:S(2)}, u32[]{:S(2)}) %collective-permute-start.15) | collective-permute-done | bytes 786464 | tf_op jit(solution)/shard_map/ppermute | solution.py:622
  125.0 3.3 collective-permute-done.16
  142.1 5.7 shard_map.359.weight_ref
  149.0 18.8 %shard_map.361 = (f32[1024,768]{1,0:T(8,128)S(1)}, bf16[512,384]{1,0:T(8,128)(2,1)S(1)}, f32[384,512]{1,0:T(8,128)S(1)}) custom-call(f32[1024,1152]{1,0:T(8,128)S(1)} %bitcast.178, bf16[512,4096]{1,0:T(8,128)(2,1)S(1)} %bitcast.172, bf16[512,4096]{1,0:T(8,128)(2,1)} %collective-permute-done.10.second_ref.refs_3_, bf16[4096,768]{1,0:T(8,128)(2,1)} %shard_map.359.weight_ref, ...), custom_call_target="tpu_custom_call" | custom-call | flops 1024 | bytes 1024 | tf_op jit(solution)/shard_map/pallas_call | solution.py:322
  186.5 2.8 copy-done.12
  189.3 9.3 %shard_map.360 = (f32[512,768]{1,0:T(8,128)S(1)}, bf16[256,384]{1,0:T(8,128)(2,1)S(1)}, f32[384,256]{1,0:T(8,128)S(1)}) custom-call(f32[1024,1152]{1,0:T(8,128)S(1)} %copy-done.11, bf16[256,4096]{1,0:T(8,128)(2,1)S(1)} %constant_dynamic-update-slice_fusion.first_ref.refs_4_, bf16[256,4096]{1,0:T(8,128)(2,1)} %collective-permute-done.18.second_ref.refs_5_, ...), custom_call_target="tpu_custom_call" | custom-call | flops 1024 | bytes 1024 | tf_op jit(solution)/shard_map/pallas_call | solution.py:322
  201.2 2.7 shard_map.363
  204.0 2.8 copy-done.13
  206.7 7.7 %shard_map.362 = (f32[512,768]{1,0:T(8,128)S(1)}, bf16[256,384]{1,0:T(8,128)(2,1)S(1)}, f32[384,256]{1,0:T(8,128)S(1)}) custom-call(f32[1024,1152]{1,0:T(8,128)S(1)} %bitcast.180, bf16[256,4096]{1,0:T(8,128)(2,1)S(1)} %copy-done.17, bf16[256,4096]{1,0:T(8,128)(2,1)S(1)} %copy-done.20, bf16[4096,768]{1,0:T(8,128)(2,1)S(1)} %copy-done.13, ...), custom_call_target="tpu_custom_call" | custom-call | flops 1024 | bytes 1024 | tf_op jit(solution)/shard_map/pallas_call | solution.py:322
  227.1 10.8 %collective-permute-done.34.refs_6_ = bf16[192,2048]{1,0:T(8,128)(2,1)S(1)} collective-permute-done((bf16[192,2048]{1,0:T(8,128)(2,1)}, bf16[192,2048]{1,0:T(8,128)(2,1)S(1)}, u32[]{:S(2)}, u32[]{:S(2)}) %collective-permute-start.34) | collective-permute-done | bytes 786464 | tf_op jit(solution)/shard_map/ppermute | solution.py:622
  237.9 5.9 shard_map.364.gate_ref.up_ref
  243.8 4.2 shard_map.365.down_ref
  260.8 10.7 %shard_map.366 = (bf16[512,1024]{1,0:T(8,128)(2,1)S(1)}, bf16[512,2048]{1,0:T(8,128)(2,1)}) custom-call(bf16[512,1536]{1,0:T(8,128)(2,1)} %pad_maximum_fusion.7.ffn_ref.refs_2_, bf16[1536,2048]{1,0:T(8,128)(2,1)} %shard_map.364.gate_ref.up_ref, bf16[1536,2048]{1,0:T(8,128)(2,1)} %shard_map.364.gate_ref.up_ref, ...), custom_call_target="tpu_custom_call" | custom-call | flops 1024 | bytes 1024 | tf_op jit(solution)/shard_map/pallas_call | solution.py:443
  279.5 10.5 %shard_map.367 = (bf16[512,1024]{1,0:T(8,128)(2,1)S(1)}, bf16[512,2048]{1,0:T(8,128)(2,1)}) custom-call(bf16[512,1536]{1,0:T(8,128)(2,1)} %copy-done.8, bf16[1536,2048]{1,0:T(8,128)(2,1)} %shard_map.364.gate_ref.up_ref, bf16[1536,2048]{1,0:T(8,128)(2,1)} %shard_map.364.gate_ref.up_ref, bf16[512,1536]{1,0:T(8,128)(2,1)} %copy-done.25, ...), custom_call_target="tpu_custom_call" | custom-call | flops 1024 | bytes 1024 | tf_op jit(solution)/shard_map/pallas_call | solution.py:443
  292.2 4.8 convolution_convert_fusion.5
  302.9 2.9 shard_map.368
  306.4 2.7 convolution_convert_fusion.4
  309.2 2.7 fusion.2
  329.9 3.1 convolution_add_fusion.6
  346.8 14.8 %shard_map.376 = (bf16[1152,512]{1,0:T(8,128)(2,1)S(1)}, bf16[512,1152]{1,0:T(8,128)(2,1)S(1)}, bf16[768,1024]{1,0:T(8,128)(2,1)S(1)}, f32[3,64,128]{2,1,0:T(8,128)S(1)}, f32[6,1,128]{2,1,0:T(1,128)S(1)}) custom-call(f32[1024,1152]{1,0:T(8,128)S(1)} %bitcast.182, f32[1024,768]{1,0:T(8,128)S(1)} %copy-done.38, f32[64,1024]{1,0:T(8,128)S(1)} %copy-done.30, ...), custom_call_target="tpu_custom_call" | custom-call | flops 1024 | bytes 1024 | tf_op jit(solution)/shard_map/pallas_call | solution.py:360
  366.1 6.9 %shard_map.377 = bf16[1536,1408]{1,0:T(8,128)(2,1)S(1)} custom-call(bf16[512,1536]{1,0:T(8,128)(2,1)S(1)} %copy-done.24, bf16[512,1536]{1,0:T(8,128)(2,1)S(1)} %copy-done.26, bf16[512,1024]{1,0:T(8,128)(2,1)S(1)} %copy-done.32, bf16[512,1024]{1,0:T(8,128)(2,1)S(1)} %copy-done.34, bf16[512,1536]{1,0:T(8,128)(2,1)S(1)} %pad_maximum_fusion.9.refs_4_, ...), custom_call_target="tpu_custom_call" | custom-call | flops 1024 | bytes 1024 | tf_op jit(solution)/shard_map/pallas_call | solution.py:493
  383.0 14.9 %shard_map.378 = (bf16[1152,512]{1,0:T(8,128)(2,1)S(1)}, bf16[512,1152]{1,0:T(8,128)(2,1)S(1)}, bf16[768,1024]{1,0:T(8,128)(2,1)S(1)}, f32[3,64,128]{2,1,0:T(8,128)S(1)}, f32[6,1,128]{2,1,0:T(1,128)S(1)}) custom-call(f32[1024,1152]{1,0:T(8,128)S(1)} %bitcast.182, f32[1024,768]{1,0:T(8,128)S(1)} %pad_maximum_fusion.1.cap_ref, f32[64,1024]{1,0:T(8,128)S(1)} %copy-done.30, ...), custom_call_target="tpu_custom_call" | custom-call | flops 1024 | bytes 1024 | tf_op jit(solution)/shard_map/pallas_call | solution.py:360
  410.8 6.2 %shard_map.380 = bf16[384,2048]{1,0:T(8,128)(2,1)S(1)} custom-call(s32[5]{0:T(128)S(1)} %copy-done.66, bf16[768,1024]{1,0:T(8,128)(2,1)S(1)} %bitcast.183, bf16[768,1024]{1,0:T(8,128)(2,1)S(1)} %bitcast.187, bf16[512,4096]{1,0:T(8,128)(2,1)S(1)} %bitcast.173, bf16[512,4096]{1,0:T(8,128)(2,1)} %collective-permute-done.10.second_ref.refs_3_, ...), custom_call_target="tpu_custom_call" | custom-call | flops 1024 | bytes 1024 | tf_op jit(solution)/shard_map/pallas_call | solution.py:404
  417.0 5.5 shard_map.379
  422.5 5.7 collective-permute-done.53
  436.5 6.2 %shard_map.382 = bf16[384,2048]{1,0:T(8,128)(2,1)S(1)} custom-call(s32[5]{0:T(128)S(1)} %stack.186.place_ref, bf16[768,1024]{1,0:T(8,128)(2,1)S(1)} %bitcast.185, bf16[768,1024]{1,0:T(8,128)(2,1)S(1)} %bitcast.189, bf16[512,4096]{1,0:T(8,128)(2,1)S(1)} %bitcast.175, bf16[512,4096]{1,0:T(8,128)(2,1)} %collective-permute-done.10.second_ref.refs_3_, ...), custom_call_target="tpu_custom_call" | custom-call | flops 1024 | bytes 1024 | tf_op jit(solution)/shard_map/pallas_call | solution.py:404
  442.7 6.0 shard_map.381
  459.9 2.8 broadcast_select_fusion.7
  464.7 25.9 %collective-permute-done.57 = bf16[1024,384]{1,0:T(8,128)(2,1)S(1)} collective-permute-done((bf16[1024,384]{1,0:T(8,128)(2,1)S(1)}, bf16[1024,384]{1,0:T(8,128)(2,1)S(1)}, u32[]{:S(2)}, u32[]{:S(2)}) %collective-permute-start.57) | collective-permute-done | bytes 786464 | tf_op jit(solution)/shard_map/ppermute | solution.py:622
  490.6 4.7 collective-permute-done.62
  509.4 3.9 convolution_convert_fusion.3
  513.3 3.6 convolution_convert_fusion.1
  529.3 3.2 broadcast_select_fusion.1
  543.5 3.5 collective-permute-start.80
  549.2 7.8 %collective-permute-done.68 = bf16[576,768]{1,0:T(8,128)(2,1)S(1)} collective-permute-done((bf16[576,768]{1,0:T(8,128)(2,1)S(1)}, bf16[576,768]{1,0:T(8,128)(2,1)S(1)}, u32[]{:S(2)}, u32[]{:S(2)}) %collective-permute-start.68) | collective-permute-done | bytes 884768 | tf_op jit(solution)/shard_map/ppermute | solution.py:622
  557.5 3.9 collective-permute-done.72
  567.1 11.4 %collective-permute-done.78 = f32[3288]{0:T(1024)S(1)} collective-permute-done((f32[3288]{0:T(1024)S(1)}, f32[3288]{0:T(1024)S(1)}, u32[]{:S(2)}, u32[]{:S(2)}) %collective-permute-start.78) | collective-permute-done | bytes 13184 | tf_op jit(solution)/shard_map/ppermute | solution.py:622
  580.3 2.8 collective-permute-done.79
  590.8 19.5 %collective-permute-done.82 = bf16[576,384]{1,0:T(8,128)(2,1)S(1)} collective-permute-done((bf16[576,384]{1,0:T(8,128)(2,1)S(1)}, bf16[576,384]{1,0:T(8,128)(2,1)S(1)}, u32[]{:S(2)}, u32[]{:S(2)}) %collective-permute-start.82) | collective-permute-done | bytes 442400 | tf_op jit(solution)/shard_map/ppermute | solution.py:622
  (756 shorter events, 261.3 us)
Async XLA Ops:
  5.0 24.5 %collective-permute-start = (bf16[384,1152]{1,0:T(8,128)(2,1)}, bf16[384,1152]{1,0:T(8,128)(2,1)S(1)}, u32[]{:S(2)}, u32[]{:S(2)}) collective-permute-start(bf16[384,1152]{1,0:T(8,128)(2,1)} %pad_maximum_fusion.13), channel_id=1, source_target_pairs={{0,2},{1,3},{2,0},{3,1},{4,7},{5,6},{6,5},{7,4},{8,10},{9,11},{10,... | collective-permute-start | bytes 2654216 | tf_op jit(solution)/shard_map/ppermute | solution.py:622
  7.6 20.7 %collective-permute-start.10 = (bf16[512,4096]{1,0:T(8,128)(2,1)}, bf16[512,4096]{1,0:T(8,128)(2,1)}, u32[]{:S(2)}, u32[]{:S(2)}) collective-permute-start(bf16[512,4096]{1,0:T(8,128)(2,1)} %bitcast.171), channel_id=1, source_target_pairs={{0,1},{1,0},{2,3},{3,2},{4,5},{5,4},{6,7},{7,6},{8,9},{9,8},{10,11... | collective-permute-start | bytes 12582920 | tf_op jit(solution)/shard_map/ppermute | solution.py:622
  10.2 25.7 %collective-permute-start.1 = (bf16[128,4096]{1,0:T(8,128)(2,1)}, bf16[128,4096]{1,0:T(8,128)(2,1)}, u32[]{:S(2)}, u32[]{:S(2)}) collective-permute-start(bf16[128,4096]{1,0:T(8,128)(2,1)} %slice_bitcast_fusion.7), channel_id=1, source_target_pairs={{0,8},{1,9},{2,10},{3,11},{4,12},{5,13},{6,14},{7,15},{8,0},{9,1},... | collective-permute-start | bytes 3145736 | tf_op jit(solution)/shard_map/ppermute | solution.py:622
  35.9 24.3 %collective-permute-start.6 = (bf16[272,1536]{1,0:T(8,128)(2,1)S(1)}, bf16[272,1536]{1,0:T(8,128)(2,1)S(1)}, u32[]{:S(2)}, u32[]{:S(2)}) collective-permute-start(bf16[272,1536]{1,0:T(8,128)(2,1)S(1)} %pad_maximum_fusion.15), channel_id=1, source_target_pairs={{0,8},{1,9},{2,10},{3,11},{4,12},{5,13},{6,14},{7,15},{8,0},{9,1},... | collective-permute-start | bytes 2506760 | tf_op jit(solution)/shard_map/ppermute | solution.py:622
  37.5 22.7 %collective-permute-start.3 = (bf16[384,1152]{1,0:T(8,128)(2,1)S(1)}, bf16[384,1152]{1,0:T(8,128)(2,1)S(1)}, u32[]{:S(2)}, u32[]{:S(2)}) collective-permute-start(bf16[384,1152]{1,0:T(8,128)(2,1)S(1)} %collective-permute-done.refs_4_), channel_id=1, source_target_pairs={{0,4},{1,5},{2,6},{3,7},{4,0},{5,1},{6,2},{7,3},{8,12},{9,13},{10,... | collective-permute-start | bytes 2654216 | tf_op jit(solution)/shard_map/ppermute | solution.py:622
  39.1 22.1 %collective-permute-start.12 = (bf16[272,1536]{1,0:T(8,128)(2,1)S(1)}, bf16[272,1536]{1,0:T(8,128)(2,1)S(1)}, u32[]{:S(2)}, u32[]{:S(2)}) collective-permute-start(bf16[272,1536]{1,0:T(8,128)(2,1)S(1)} %pad_maximum_fusion.15), channel_id=1, source_target_pairs={{0,1},{1,0},{2,3},{3,2},{4,5},{5,4},{6,7},{7,6},{8,9},{9,8},{10,11... | collective-permute-start | bytes 2506760 | tf_op jit(solution)/shard_map/ppermute | solution.py:622
  40.3 19.9 %collective-permute-start.2 = (bf16[512,768]{1,0:T(8,128)(2,1)S(1)}, bf16[512,768]{1,0:T(8,128)(2,1)}, u32[]{:S(2)}, u32[]{:S(2)}) collective-permute-start(bf16[512,768]{1,0:T(8,128)(2,1)S(1)} %get-tuple-element.243), channel_id=1, source_target_pairs={{0,2},{1,3},{2,0},{3,1},{4,7},{5,6},{6,5},{7,4},{8,10},{9,11},{10,... | collective-permute-start | bytes 2359304 | tf_op jit(solution)/shard_map/ppermute | solution.py:622
  63.6 29.0 %collective-permute-start.17 = (bf16[1024,768]{1,0:T(8,128)(2,1)}, bf16[1024,768]{1,0:T(8,128)(2,1)}, u32[]{:S(2)}, u32[]{:S(2)}) collective-permute-start(bf16[1024,768]{1,0:T(8,128)(2,1)} %pad_maximum_fusion.5), channel_id=1, source_target_pairs={{0,1},{1,0},{2,3},{3,2},{4,5},{5,4},{6,7},{7,6},{8,9},{9,8},{10,11... | collective-permute-start | bytes 4718600 | tf_op jit(solution)/shard_map/ppermute | solution.py:622
  65.5 25.7 %collective-permute-start.9 = (bf16[128,4096]{1,0:T(8,128)(2,1)}, bf16[128,4096]{1,0:T(8,128)(2,1)}, u32[]{:S(2)}, u32[]{:S(2)}) collective-permute-start(bf16[128,4096]{1,0:T(8,128)(2,1)} %get-tuple-element.253), channel_id=1, source_target_pairs={{0,8},{1,9},{2,10},{3,11},{4,12},{5,13},{6,14},{7,15},{8,0},{9,1},... | collective-permute-start | bytes 3145736 | tf_op jit(solution)/shard_map/ppermute | solution.py:622
  97.2 31.1 %collective-permute-start.14 = (bf16[704,1536]{1,0:T(8,128)(2,1)}, bf16[704,1536]{1,0:T(8,128)(2,1)}, u32[]{:S(2)}, u32[]{:S(2)}) collective-permute-start(bf16[704,1536]{1,0:T(8,128)(2,1)} %pad_maximum_fusion.3), channel_id=1, source_target_pairs={{0,2},{2,1},{4,6},{6,5},{9,10},{11,9},{13,14},{15,13},{16,18},{18,... | collective-permute-start | bytes 6488072 | tf_op jit(solution)/shard_map/ppermute | solution.py:622
  105.7 22.6 %collective-permute-start.16 = (bf16[128,4096]{1,0:T(8,128)(2,1)S(1)}, bf16[128,4096]{1,0:T(8,128)(2,1)S(1)}, u32[]{:S(2)}, u32[]{:S(2)}) collective-permute-start(bf16[128,4096]{1,0:T(8,128)(2,1)S(1)} %copy-done.117), channel_id=1, source_target_pairs={{0,8},{1,9},{2,10},{3,11},{4,12},{5,13},{6,14},{7,15},{8,0},{9,1},... | collective-permute-start | bytes 3145736 | tf_op jit(solution)/shard_map/ppermute | solution.py:622
  106.6 24.4 %collective-permute-start.25 = (bf16[384,2048]{1,0:T(8,128)(2,1)S(1)}, bf16[384,2048]{1,0:T(8,128)(2,1)S(1)}, u32[]{:S(2)}, u32[]{:S(2)}) collective-permute-start(bf16[384,2048]{1,0:T(8,128)(2,1)S(1)} %pad_maximum_fusion.6), channel_id=1, source_target_pairs={{0,1},{1,0},{2,3},{3,2},{4,5},{5,4},{6,7},{7,6},{8,9},{9,8},{10,11... | collective-permute-start | bytes 4718600 | tf_op jit(solution)/shard_map/ppermute | solution.py:622
  128.3 41.2 %collective-permute-start.20 = (bf16[704,1536]{1,0:T(8,128)(2,1)}, bf16[704,1536]{1,0:T(8,128)(2,1)}, u32[]{:S(2)}, u32[]{:S(2)}) collective-permute-start(bf16[704,1536]{1,0:T(8,128)(2,1)} %collective-permute-done.14), channel_id=1, source_target_pairs={{1,5},{2,6},{5,1},{6,2},{9,13},{10,14},{13,9},{14,10},{17,21},{18,... | collective-permute-start | bytes 6488072 | tf_op jit(solution)/shard_map/ppermute | solution.py:622
  131.0 37.7 %collective-permute-start.26 = (bf16[384,1536]{1,0:T(8,128)(2,1)}, bf16[384,1536]{1,0:T(8,128)(2,1)}, u32[]{:S(2)}, u32[]{:S(2)}) collective-permute-start(bf16[384,1536]{1,0:T(8,128)(2,1)} %shard.2), channel_id=1, source_target_pairs={{2,3},{6,7},{9,8},{13,12},{18,19},{22,23},{25,24},{29,28}} | collective-permute-start | bytes 3538952 | tf_op jit(solution)/shard_map/ppermute | solution.py:622
  134.0 35.5 %collective-permute-start.21 = (bf16[128,4096]{1,0:T(8,128)(2,1)}, bf16[128,4096]{1,0:T(8,128)(2,1)}, u32[]{:S(2)}, u32[]{:S(2)}) collective-permute-start(bf16[128,4096]{1,0:T(8,128)(2,1)} %get-tuple-element.276), channel_id=1, source_target_pairs={{0,8},{1,9},{2,10},{3,11},{4,12},{5,13},{6,14},{7,15},{8,0},{9,1},... | collective-permute-start | bytes 3145736 | tf_op jit(solution)/shard_map/ppermute | solution.py:622
  137.1 32.4 %collective-permute-start.19 = (bf16[192,2048]{1,0:T(8,128)(2,1)}, bf16[192,2048]{1,0:T(8,128)(2,1)}, u32[]{:S(2)}, u32[]{:S(2)}) collective-permute-start(bf16[192,2048]{1,0:T(8,128)(2,1)} %get-tuple-element.274), channel_id=1, source_target_pairs={{0,2},{1,3},{2,0},{3,1},{4,7},{5,6},{6,5},{7,4},{8,10},{9,11},{10,... | collective-permute-start | bytes 2359304 | tf_op jit(solution)/shard_map/ppermute | solution.py:622
  177.1 38.1 %collective-permute-start.29 = (bf16[1024,1536]{1,0:T(8,128)(2,1)}, bf16[1024,1536]{1,0:T(8,128)(2,1)}, u32[]{:S(2)}, u32[]{:S(2)}) collective-permute-start(bf16[1024,1536]{1,0:T(8,128)(2,1)} %shard.3), channel_id=1, source_target_pairs={{2,3},{6,7},{9,8},{13,12},{18,19},{22,23},{25,24},{29,28}} | collective-permute-start | bytes 9437192 | tf_op jit(solution)/shard_map/ppermute | solution.py:622
  179.4 35.1 %collective-permute-start.24 = (bf16[256,1536]{1,0:T(8,128)(2,1)}, bf16[256,1536]{1,0:T(8,128)(2,1)}, u32[]{:S(2)}, u32[]{:S(2)}) collective-permute-start(bf16[256,1536]{1,0:T(8,128)(2,1)} %bitcast.18), channel_id=1, source_target_pairs={{0,8},{1,9},{2,10},{3,11},{4,12},{5,13},{6,14},{7,15},{8,0},{9,1},... | collective-permute-start | bytes 2359304 | tf_op jit(solution)/shard_map/ppermute | solution.py:622
  180.1 34.4 %collective-permute-start.23 = (bf16[192,2048]{1,0:T(8,128)(2,1)}, bf16[192,2048]{1,0:T(8,128)(2,1)}, u32[]{:S(2)}, u32[]{:S(2)}) collective-permute-start(bf16[192,2048]{1,0:T(8,128)(2,1)} %collective-permute-done.19.refs_3_), channel_id=1, source_target_pairs={{0,4},{1,5},{2,6},{3,7},{4,0},{5,1},{6,2},{7,3},{8,12},{9,13},{10,... | collective-permute-start | bytes 2359304 | tf_op jit(solution)/shard_map/ppermute | solution.py:622
  181.8 32.7 %collective-permute-start.22 = (bf16[192,2048]{1,0:T(8,128)(2,1)}, bf16[192,2048]{1,0:T(8,128)(2,1)}, u32[]{:S(2)}, u32[]{:S(2)}) collective-permute-start(bf16[192,2048]{1,0:T(8,128)(2,1)} %get-tuple-element.282), channel_id=1, source_target_pairs={{0,2},{1,3},{2,0},{3,1},{4,7},{5,6},{6,5},{7,4},{8,10},{9,11},{10,... | collective-permute-start | bytes 2359304 | tf_op jit(solution)/shard_map/ppermute | solution.py:622
  218.0 19.9 %collective-permute-start.34 = (bf16[192,2048]{1,0:T(8,128)(2,1)}, bf16[192,2048]{1,0:T(8,128)(2,1)S(1)}, u32[]{:S(2)}, u32[]{:S(2)}) collective-permute-start(bf16[192,2048]{1,0:T(8,128)(2,1)} %collective-permute-done.22.refs_5_), channel_id=1, source_target_pairs={{0,4},{1,5},{2,6},{3,7},{4,0},{5,1},{6,2},{7,3},{8,12},{9,13},{10,... | collective-permute-start | bytes 2359304 | tf_op jit(solution)/shard_map/ppermute | solution.py:622
  220.4 27.5 %collective-permute-start.33 = (bf16[256,1536]{1,0:T(8,128)(2,1)}, bf16[256,1536]{1,0:T(8,128)(2,1)S(1)}, u32[]{:S(2)}, u32[]{:S(2)}) collective-permute-start(bf16[256,1536]{1,0:T(8,128)(2,1)} %convolution_convert_fusion.6), channel_id=1, source_target_pairs={{0,1},{1,0},{2,3},{3,2},{4,5},{5,4},{6,7},{7,6},{8,9},{9,8},{10,11... | collective-permute-start | bytes 2359304 | tf_op jit(solution)/shard_map/ppermute | solution.py:622
  222.1 26.5 %collective-permute-start.31 = (bf16[256,1536]{1,0:T(8,128)(2,1)}, bf16[256,1536]{1,0:T(8,128)(2,1)}, u32[]{:S(2)}, u32[]{:S(2)}) collective-permute-start(bf16[256,1536]{1,0:T(8,128)(2,1)} %fusion), channel_id=1, source_target_pairs={{0,8},{1,9},{2,10},{3,11},{4,12},{5,13},{6,14},{7,15},{8,0},{9,1},... | collective-permute-start | bytes 2359304 | tf_op jit(solution)/shard_map/ppermute | solution.py:622
  252.7 20.1 %collective-permute-start.36 = (bf16[256,1536]{1,0:T(8,128)(2,1)S(1)}, bf16[256,1536]{1,0:T(8,128)(2,1)}, u32[]{:S(2)}, u32[]{:S(2)}) collective-permute-start(bf16[256,1536]{1,0:T(8,128)(2,1)S(1)} %bitcast.211), channel_id=1, source_target_pairs={{0,8},{1,9},{2,10},{3,11},{4,12},{5,13},{6,14},{7,15},{8,0},{9,1},... | collective-permute-start | bytes 2359304 | tf_op jit(solution)/shard_map/ppermute | solution.py:622
  301.8 31.3 %collective-permute-start.39 = (bf16[256,1536]{1,0:T(8,128)(2,1)}, bf16[256,1536]{1,0:T(8,128)(2,1)}, u32[]{:S(2)}, u32[]{:S(2)}) collective-permute-start(bf16[256,1536]{1,0:T(8,128)(2,1)} %shard_map.369), channel_id=1, source_target_pairs={{0,4},{1,5},{2,6},{3,7},{4,0},{5,1},{6,2},{7,3},{8,12},{9,13},{10,... | collective-permute-start | bytes 2359304 | tf_op jit(solution)/shard_map/ppermute | solution.py:622
  305.8 27.3 %collective-permute-start.38 = (bf16[512,768]{1,0:T(8,128)(2,1)}, bf16[512,768]{1,0:T(8,128)(2,1)}, u32[]{:S(2)}, u32[]{:S(2)}) collective-permute-start(bf16[512,768]{1,0:T(8,128)(2,1)} %shard_map.368), channel_id=1, source_target_pairs={{0,2},{1,3},{2,0},{3,1},{4,6},{5,7},{6,4},{7,5},{8,10},{9,11},{10,... | collective-permute-start | bytes 2359304 | tf_op jit(solution)/shard_map/ppermute | solution.py:622
  309.2 20.8 %collective-permute-start.42 = (bf16[256,1536]{1,0:T(8,128)(2,1)}, bf16[256,1536]{1,0:T(8,128)(2,1)}, u32[]{:S(2)}, u32[]{:S(2)}) collective-permute-start(bf16[256,1536]{1,0:T(8,128)(2,1)} %convolution_convert_fusion.4), channel_id=1, source_target_pairs={{0,1},{1,0},{2,3},{3,2},{4,5},{5,4},{6,7},{7,6},{8,9},{9,8},{10,11... | collective-permute-start | bytes 2359304 | tf_op jit(solution)/shard_map/ppermute | solution.py:622
  311.9 21.2 %collective-permute-start.41 = (bf16[256,1536]{1,0:T(8,128)(2,1)}, bf16[256,1536]{1,0:T(8,128)(2,1)}, u32[]{:S(2)}, u32[]{:S(2)}) collective-permute-start(bf16[256,1536]{1,0:T(8,128)(2,1)} %fusion.2), channel_id=1, source_target_pairs={{0,8},{1,9},{2,10},{3,11},{4,12},{5,13},{6,14},{7,15},{8,0},{9,1},... | collective-permute-start | bytes 2359304 | tf_op jit(solution)/shard_map/ppermute | solution.py:622
  339.7 21.9 %collective-permute-start.45 = (bf16[256,1536]{1,0:T(8,128)(2,1)S(1)}, bf16[256,1536]{1,0:T(8,128)(2,1)S(1)}, u32[]{:S(2)}, u32[]{:S(2)}) collective-permute-start(bf16[256,1536]{1,0:T(8,128)(2,1)S(1)} %bitcast.207), channel_id=1, source_target_pairs={{0,8},{1,9},{2,10},{3,11},{4,12},{5,13},{6,14},{7,15},{8,0},{9,1},... | collective-permute-start | bytes 2359304 | tf_op jit(solution)/shard_map/ppermute | solution.py:622
  340.4 21.2 %collective-permute-start.44 = (bf16[256,1536]{1,0:T(8,128)(2,1)S(1)}, bf16[256,1536]{1,0:T(8,128)(2,1)S(1)}, u32[]{:S(2)}, u32[]{:S(2)}) collective-permute-start(bf16[256,1536]{1,0:T(8,128)(2,1)S(1)} %shard_map.375), channel_id=1, source_target_pairs={{0,4},{1,5},{2,6},{3,7},{4,0},{5,1},{6,2},{7,3},{8,12},{9,13},{10,... | collective-permute-start | bytes 2359304 | tf_op jit(solution)/shard_map/ppermute | solution.py:622
  373.2 24.8 %collective-permute-start.50 = (bf16[2,384,1408]{2,1,0:T(8,128)(2,1)S(1)}, bf16[2,384,1408]{2,1,0:T(8,128)(2,1)}, u32[]{:S(2)}, u32[]{:S(2)}) collective-permute-start(bf16[2,384,1408]{2,1,0:T(8,128)(2,1)S(1)} %dynamic-slice_bitcast_fusion), channel_id=1, source_target_pairs={{0,1},{1,0},{2,3},{3,2},{4,5},{5,4},{6,7},{7,6},{8,9},{9,8},{10,11... | collective-permute-start | bytes 6488072 | tf_op jit(solution)/shard_map/ppermute | solution.py:622
  376.5 25.0 %collective-permute-start.48 = (bf16[512,768]{1,0:T(8,128)(2,1)}, bf16[512,768]{1,0:T(8,128)(2,1)}, u32[]{:S(2)}, u32[]{:S(2)}) collective-permute-start(bf16[512,768]{1,0:T(8,128)(2,1)} %add_convert_fusion.5), channel_id=1, source_target_pairs={{0,2},{1,3},{2,0},{3,1},{4,6},{5,7},{6,4},{7,5},{8,10},{9,11},{10,... | collective-permute-start | bytes 2359304 | tf_op jit(solution)/shard_map/ppermute | solution.py:622
  379.0 22.5 %collective-permute-start.47 = (bf16[512,768]{1,0:T(8,128)(2,1)}, bf16[512,768]{1,0:T(8,128)(2,1)}, u32[]{:S(2)}, u32[]{:S(2)}) collective-permute-start(bf16[512,768]{1,0:T(8,128)(2,1)} %add_convert_fusion.6), channel_id=1, source_target_pairs={{0,4},{1,5},{2,6},{3,7},{4,0},{5,1},{6,2},{7,3},{8,12},{9,13},{10,... | collective-permute-start | bytes 2359304 | tf_op jit(solution)/shard_map/ppermute | solution.py:622
  402.7 25.5 %collective-permute-start.53 = (bf16[192,2816]{1,0:T(8,128)(2,1)}, bf16[192,2816]{1,0:T(8,128)(2,1)}, u32[]{:S(2)}, u32[]{:S(2)}) collective-permute-start(bf16[192,2816]{1,0:T(8,128)(2,1)} %get-tuple-element.372), channel_id=1, source_target_pairs={{0,4},{1,5},{2,6},{3,7},{4,0},{5,1},{6,2},{7,3},{8,12},{9,13},{10,... | collective-permute-start | bytes 3244040 | tf_op jit(solution)/shard_map/ppermute | solution.py:622
  402.7 25.5 %collective-permute-start.52 = (bf16[384,1408]{1,0:T(8,128)(2,1)}, bf16[384,1408]{1,0:T(8,128)(2,1)}, u32[]{:S(2)}, u32[]{:S(2)}) collective-permute-start(bf16[384,1408]{1,0:T(8,128)(2,1)} %get-tuple-element.371), channel_id=1, source_target_pairs={{0,2},{1,3},{2,0},{3,1},{4,6},{5,7},{6,4},{7,5},{8,10},{9,11},{10,... | collective-permute-start | bytes 3244040 | tf_op jit(solution)/shard_map/ppermute | solution.py:622
  452.3 38.3 %collective-permute-start.57 = (bf16[1024,384]{1,0:T(8,128)(2,1)S(1)}, bf16[1024,384]{1,0:T(8,128)(2,1)S(1)}, u32[]{:S(2)}, u32[]{:S(2)}) collective-permute-start(bf16[1024,384]{1,0:T(8,128)(2,1)S(1)} %broadcast_select_fusion.4), channel_id=1, source_target_pairs={{0,16},{1,17},{2,18},{3,19},{4,20},{5,21},{6,22},{7,23},{8,24},{9,... | collective-permute-start | bytes 2359304 | tf_op jit(solution)/shard_map/ppermute | solution.py:622
  455.0 40.3 %collective-permute-start.59 = (bf16[384,2048]{1,0:T(8,128)(2,1)S(1)}, bf16[384,2048]{1,0:T(8,128)(2,1)S(1)}, u32[]{:S(2)}, u32[]{:S(2)}) collective-permute-start(bf16[384,2048]{1,0:T(8,128)(2,1)S(1)} %shard_map.380), channel_id=1, source_target_pairs={{0,4},{1,5},{2,6},{3,7},{4,0},{5,1},{6,2},{7,3},{8,12},{9,13},{10,... | collective-permute-start | bytes 4718600 | tf_op jit(solution)/shard_map/ppermute | solution.py:622
  455.3 40.0 %collective-permute-start.58 = (bf16[768,1024]{1,0:T(8,128)(2,1)S(1)}, bf16[768,1024]{1,0:T(8,128)(2,1)S(1)}, u32[]{:S(2)}, u32[]{:S(2)}) collective-permute-start(bf16[768,1024]{1,0:T(8,128)(2,1)S(1)} %shard_map.379), channel_id=1, source_target_pairs={{0,2},{1,3},{2,0},{3,1},{4,6},{5,7},{6,4},{7,5},{8,10},{9,11},{10,... | collective-permute-start | bytes 4718600 | tf_op jit(solution)/shard_map/ppermute | solution.py:622
  458.4 36.9 %collective-permute-start.62 = (bf16[256,1536]{1,0:T(8,128)(2,1)S(1)}, bf16[256,1536]{1,0:T(8,128)(2,1)S(1)}, u32[]{:S(2)}, u32[]{:S(2)}) collective-permute-start(bf16[256,1536]{1,0:T(8,128)(2,1)S(1)} %fusion.3), channel_id=1, source_target_pairs={{0,8},{1,9},{2,10},{3,11},{4,12},{5,13},{6,14},{7,15},{8,0},{9,1},... | collective-permute-start | bytes 2359304 | tf_op jit(solution)/shard_map/ppermute | solution.py:622
  462.7 63.1 %collective-permute-start.56 = (bf16[192,1408]{1,0:T(8,128)(2,1)}, bf16[192,1408]{1,0:T(8,128)(2,1)}, u32[]{:S(2)}, u32[]{:S(2)}) collective-permute-start(bf16[192,1408]{1,0:T(8,128)(2,1)} %get-tuple-element.393), channel_id=1, source_target_pairs={{0,16},{1,17},{2,18},{3,19},{4,20},{5,21},{6,22},{7,23},{8,24},{9,... | collective-permute-start | bytes 1622024 | tf_op jit(solution)/shard_map/ppermute | solution.py:622
  496.8 30.8 %collective-permute-start.64 = (bf16[384,1024]{1,0:T(8,128)(2,1)}, bf16[384,1024]{1,0:T(8,128)(2,1)}, u32[]{:S(2)}, u32[]{:S(2)}) collective-permute-start(bf16[384,1024]{1,0:T(8,128)(2,1)} %add_convert_fusion.4), channel_id=1, source_target_pairs={{0,2},{1,3},{2,0},{3,1},{4,6},{5,7},{6,4},{7,5},{8,10},{9,11},{10,... | collective-permute-start | bytes 2359304 | tf_op jit(solution)/shard_map/ppermute | solution.py:622
  507.7 19.8 %collective-permute-start.63 = (bf16[384,1024]{1,0:T(8,128)(2,1)}, bf16[384,1024]{1,0:T(8,128)(2,1)}, u32[]{:S(2)}, u32[]{:S(2)}) collective-permute-start(bf16[384,1024]{1,0:T(8,128)(2,1)} %add_convert_fusion.3), channel_id=1, source_target_pairs={{0,4},{1,5},{2,6},{3,7},{4,0},{5,1},{6,2},{7,3},{8,12},{9,13},{10,... | collective-permute-start | bytes 2359304 | tf_op jit(solution)/shard_map/ppermute | solution.py:622
  535.2 21.7 %collective-permute-start.68 = (bf16[576,768]{1,0:T(8,128)(2,1)S(1)}, bf16[576,768]{1,0:T(8,128)(2,1)S(1)}, u32[]{:S(2)}, u32[]{:S(2)}) collective-permute-start(bf16[576,768]{1,0:T(8,128)(2,1)S(1)} %copy-done.183), channel_id=1, source_target_pairs={{0,4},{1,5},{2,6},{3,7},{4,0},{5,1},{6,2},{7,3},{8,12},{9,13},{10,... | collective-permute-start | bytes 2654216 | tf_op jit(solution)/shard_map/ppermute | solution.py:622
  535.6 21.9 %collective-permute-start.67 = (bf16[1152,384]{1,0:T(8,128)(2,1)S(1)}, bf16[1152,384]{1,0:T(8,128)(2,1)S(1)}, u32[]{:S(2)}, u32[]{:S(2)}) collective-permute-start(bf16[1152,384]{1,0:T(8,128)(2,1)S(1)} %copy-done.182), channel_id=1, source_target_pairs={{0,2},{1,3},{2,0},{3,1},{4,6},{5,7},{6,4},{7,5},{8,10},{9,11},{10,... | collective-permute-start | bytes 2654216 | tf_op jit(solution)/shard_map/ppermute | solution.py:622
  541.1 20.3 %collective-permute-start.72 = (bf16[192,1024]{1,0:T(8,128)(2,1)S(1)}, bf16[192,1024]{1,0:T(8,128)(2,1)S(1)}, u32[]{:S(2)}, u32[]{:S(2)}) collective-permute-start(bf16[192,1024]{1,0:T(8,128)(2,1)S(1)} %get-tuple-element.441), channel_id=1, source_target_pairs={{0,16},{1,17},{2,18},{3,19},{4,20},{5,21},{6,22},{7,23},{8,24},{9,... | collective-permute-start | bytes 1179656 | tf_op jit(solution)/shard_map/ppermute | solution.py:622
  543.5 39.6 %collective-permute-start.80 = (bf16[256,1536]{1,0:T(8,128)(2,1)S(1)}, bf16[256,1536]{1,0:T(8,128)(2,1)S(1)}, u32[]{:S(2)}, u32[]{:S(2)}) collective-permute-start(bf16[256,1536]{1,0:T(8,128)(2,1)S(1)} %fusion.1), channel_id=1, source_target_pairs={{0,8},{1,9},{2,10},{3,11},{4,12},{5,13},{6,14},{7,15},{8,0},{9,1},... | collective-permute-start | bytes 2359304 | tf_op jit(solution)/shard_map/ppermute | solution.py:622
  561.4 21.7 %collective-permute-start.77 = (bf16[192,1024]{1,0:T(8,128)(2,1)S(1)}, bf16[192,1024]{1,0:T(8,128)(2,1)S(1)}, u32[]{:S(2)}, u32[]{:S(2)}) collective-permute-start(bf16[192,1024]{1,0:T(8,128)(2,1)S(1)} %get-tuple-element.454), channel_id=1, source_target_pairs={{0,16},{1,17},{2,18},{3,19},{4,20},{5,21},{6,22},{7,23},{8,24},{9,... | collective-permute-start | bytes 1179656 | tf_op jit(solution)/shard_map/ppermute | solution.py:622
  588.3 22.0 %collective-permute-start.82 = (bf16[576,384]{1,0:T(8,128)(2,1)S(1)}, bf16[576,384]{1,0:T(8,128)(2,1)S(1)}, u32[]{:S(2)}, u32[]{:S(2)}) collective-permute-start(bf16[576,384]{1,0:T(8,128)(2,1)S(1)} %broadcast_select_fusion.10), channel_id=1, source_target_pairs={{0,16},{1,17},{2,18},{3,19},{4,20},{5,21},{6,22},{7,23},{8,24},{9,... | collective-permute-start | bytes 1327112 | tf_op jit(solution)/shard_map/ppermute | solution.py:622
  (234 other events, 1878.3 us)
